TPU v7x, 32 devices: a whole 2x2x4 slice. The times are simulated.
32 devices in a mesh: date: 8 (over z, y), rng: 4 (over x, core).
Axes of the slice: x: 2, y: 2, z: 4, core: 2. Of those that a mesh axis runs over, the one named last changes fastest.
Arguments:
- slc: bfloat16 [8, 2, 64, 4096], P('date', None, None, 'rng'), may hold values from -9 to 9
- ref_date: int32 [1], replicated, may hold values from 0 to 7
- int_offset: int32 [8, 1, 64], P('date', None, 'rng'), may hold values from -4 to 4
- frac_offset: float32 [8, 1, 64], P('date', None, 'rng'), may hold values from 0 to 1
- partners: int32 [8, 4], P('date'), may hold values from 0 to 1, as said below
Outputs:
- surface: float32 [8, 1, 64, 1024], P('date', None, 'rng')
- coherence: bfloat16 [8, 4, 64, 4096], P('date', None, None, 'rng')
Inputs may be any that keep to these rules, and one draw needn't show every extreme that they name: `partners`: each row holds 2 to 4 ones.
All inputs are finite; a program needn't handle non-finite values.
Results may differ from a plain program's by a relative error of at most 0.009.
Values may be sent and summed in bfloat16 or wider, within the bound.
No kernel may reach another device: no remote copies, remote signals or barrier semaphores. Data moves between devices by JAX's collectives and lax.ppermute only.
A program may use at most 64 MiB of HBM per device.

v0:
```python
import jax
import jax.numpy as jnp
import numpy as np
from jax import lax
from jax.experimental import pallas as pl
from jax.experimental.pallas import tpu as pltpu
from jax.sharding import PartitionSpec as P

BLK = 64
OVS = 2
LAGS = 32
SPAN = 4
BOXA = 5
BOXR = 19
TAPS = 8
LANES = 128
PAD = 16
EDGE = 32
F32 = jnp.float32
BF16 = jnp.bfloat16
HIGHEST = lax.Precision.HIGHEST
VMEM = pl.BlockSpec(memory_space=pltpu.VMEM)
SMEM = pl.BlockSpec(memory_space=pltpu.SMEM)


def dot(a, b):
    return jnp.dot(a, b, preferred_element_type=F32)


def iota(shape, dim):
    return lax.broadcasted_iota(jnp.int32, shape, dim)


def band(table):
    top = 96
    rows = 2 * LANES - top
    step = iota((rows, LANES), 0) + top - iota((rows, LANES), 1) - (LANES - PAD - 3)
    step = step.astype(F32) - table[TAPS : TAPS + 1, :]
    out = jnp.zeros((rows, LANES), F32)
    for tap in range(TAPS):
        out = jnp.where(step == float(tap), table[tap : tap + 1, :], out)
    return jnp.concatenate([jnp.zeros((top, LANES), BF16), out.astype(BF16)], axis=0)


def prep_kernel(slc_ref, off_ref, frac_ref, res_ref, amp_ref, low_ref, high_ref):
    _, rows, cols = slc_ref.shape
    blocks = cols // BLK
    tiles = cols // LANES
    real = slc_ref[0].astype(F32)
    imag = slc_ref[1].astype(F32)
    amp_ref[...] = jnp.sqrt(real * real + imag * imag + 1e-06).astype(BF16)
    dist = iota((TAPS, blocks), 0).astype(F32) - 3.0 - frac_ref[...]
    arg = jnp.pi * dist
    sinc = jnp.where(arg == 0.0, 1.0, jnp.sin(arg) / jnp.where(arg == 0.0, 1.0, arg))
    weights = sinc * (0.5 + 0.5 * jnp.cos(arg / 4.0))
    shifts = jnp.broadcast_to(off_ref[...].astype(F32), (TAPS, blocks))
    small = jnp.concatenate([weights, shifts], axis=0).astype(BF16)
    place = (iota((blocks, cols), 1) - PAD) >> 6 == iota((blocks, cols), 0)
    table = dot(small, place.astype(BF16))
    ends = iota((blocks, 2 * LANES), 0) == jnp.where(iota((blocks, 2 * LANES), 1) < LANES, 0, blocks - 1)
    ends = dot(small, ends.astype(BF16)).astype(BF16)
    low_ref[0 : 2 * rows, :] = slc_ref[:, :, 0:LANES].reshape(2 * rows, LANES)
    low_ref[2 * rows :, :] = ends[:, 0:LANES]
    high_ref[0 : 2 * rows, :] = slc_ref[:, :, cols - LANES :].reshape(2 * rows, LANES)
    high_ref[2 * rows :, :] = ends[:, LANES:]
    for p in range(tiles):
        taps = band(table[:, p * LANES : (p + 1) * LANES])
        if p == 0:
            window, taps = slc_ref[:, :, 0:LANES], taps[LANES:]
        else:
            window = slc_ref[:, :, (p - 1) * LANES : (p + 1) * LANES]
        out = dot(window.reshape(2 * rows, window.shape[2]), taps)
        res_ref[:, :, p * LANES : (p + 1) * LANES] = out.astype(BF16).reshape(2, rows, LANES)


def edge_kernel(low_ref, high_ref, left_ref, right_ref, out_ref):
    rows = out_ref.shape[0]
    lane = iota((2 * TAPS, LANES), 1)

    def tile(before, after):
        table = jnp.where(lane < PAD, before[2 * rows :, :].astype(F32), after[2 * rows :, :].astype(F32))
        window = jnp.concatenate([before[0 : 2 * rows, :], after[0 : 2 * rows, :]], axis=1)
        return dot(window, band(table))

    first = tile(left_ref, low_ref)
    last = pltpu.roll(tile(high_ref, right_ref), EDGE, 1)
    lane = iota((2 * rows, LANES), 1)
    both = jnp.where(lane < EDGE, first, jnp.where(lane < 2 * EDGE, last, 0.0))
    out_ref[...] = (both[0:rows] + pltpu.roll(both[rows:], 2 * EDGE, 1)).astype(BF16)


def range_box():
    gap = iota((2 * LANES, LANES), 0) - iota((2 * LANES, LANES), 1) - PAD
    return (jnp.abs(gap) <= BOXR // 2).astype(BF16)


def line_box(field):
    rows, lanes = field.shape
    base = jnp.concatenate([field, jnp.zeros((8, lanes), F32)], axis=0)
    two = base + pltpu.roll(base, 1, 0)
    four = two + pltpu.roll(two, 2, 0)
    five = four + pltpu.roll(base, 4, 0)
    return pltpu.roll(five, rows + 8 - BOXA // 2, 0)[0:rows]


def extended(main_ref, edge_ref, p):
    tiles = main_ref.shape[2] // LANES
    if 0 < p < tiles:
        return tuple(main_ref[c, :, p * LANES : (p + 1) * LANES].astype(F32) for c in range(2))
    edge = edge_ref[...].astype(F32)
    lane = iota(edge.shape, 1)
    if p == 0:
        inner = [main_ref[c, :, 0:LANES].astype(F32) for c in range(2)]
        outer = [edge, pltpu.roll(edge, LANES - 2 * EDGE, 1)]
    else:
        inner = [jnp.zeros(edge.shape, F32)] * 2
        outer = [pltpu.roll(edge, LANES - EDGE, 1), pltpu.roll(edge, LANES - 3 * EDGE, 1)]
    return tuple(jnp.where(lane < EDGE, o, i) for o, i in zip(outer, inner))


def coherence_kernel(count, *refs):
    flag_ref, own_ref, own_edge_ref = refs[0:3]
    others = refs[3 : 3 + 2 * count]
    out_ref, fields_ref = refs[3 + 2 * count :]
    _, rows, cols = own_ref.shape
    tiles = cols // LANES
    for p in range(tiles + 1):
        lanes = slice(p * LANES, (p + 1) * LANES)
        own_r, own_i = extended(own_ref, own_edge_ref, p)
        fields_ref[0:rows, lanes] = (own_r * own_r + own_i * own_i).astype(BF16)
        for h in range(count):
            r, i = extended(others[2 * h], others[2 * h + 1], p)
            at = rows * (1 + 3 * h)
            fields_ref[at : at + rows, lanes] = (own_r * r + own_i * i).astype(BF16)
            fields_ref[at + rows : at + 2 * rows, lanes] = (own_i * r - own_r * i).astype(BF16)
            fields_ref[at + 2 * rows : at + 3 * rows, lanes] = (r * r + i * i).astype(BF16)
    box = range_box()
    for p in range(tiles):
        sums = dot(fields_ref[:, p * LANES : (p + 2) * LANES], box)
        own = line_box(sums[0:rows])
        for h in range(count):
            at = rows * (1 + 3 * h)
            re = line_box(sums[at : at + rows])
            im = line_box(sums[at + rows : at + 2 * rows])
            partner = line_box(sums[at + 2 * rows : at + 3 * rows])
            value = flag_ref[0, h].astype(F32) * (re * re + im * im) / (own * partner + 1e-06)
            out_ref[h, :, p * LANES : (p + 1) * LANES] = value.astype(BF16)


def split(table):
    high = table.astype(BF16)
    return high, (table - high.astype(np.float32)).astype(BF16)


def twice(table):
    zero = np.zeros_like(table)
    return np.block([[table, zero], [zero, table]])


def surface_tables():
    index = np.arange(BLK)
    angle = 2.0 * np.pi / BLK * (index[:, None] * index[None, :] % BLK)
    cosine, sine = np.cos(angle).astype(np.float32), np.sin(angle).astype(np.float32)
    signed = np.where(index < BLK // 2, index, index - BLK)
    upsampled = OVS * BLK
    lag_phase = (np.arange(LAGS) - LAGS // 2)[:, None] * signed[None, :] % upsampled
    lag_angle = 2.0 * np.pi / upsampled * lag_phase
    lag_cos, lag_sin = np.cos(lag_angle).astype(np.float32), np.sin(lag_angle).astype(np.float32)
    high, low = split(np.concatenate([cosine, -sine], axis=0))
    first = np.concatenate([high, low, high], axis=1)
    second = np.concatenate(split(np.concatenate([twice(cosine), twice(sine)], axis=1)), axis=0)
    per = LANES // LAGS
    order = np.arange(LAGS).reshape(LAGS // per, per).T.reshape(-1)
    left = np.block([[lag_cos[order], -lag_sin[order]], [lag_sin[order], lag_cos[order]]])
    third = np.concatenate(split(left), axis=1)
    spread = [twice(np.tile(table.T, (1, per))) for table in (lag_cos, -lag_sin)]
    fourth = np.concatenate(split(np.concatenate(spread, axis=0)), axis=0)
    return first, second, third, fourth


def surface_kernel(own_ref, ref_ref, first_ref, second_ref, third_ref, fourth_ref, out_ref, rows_ref, out_scr):
    size, cols = own_ref.shape
    tiles = cols // LANES
    group = (iota((LANES, LANES), 0) >> 6 == iota((LANES, LANES), 1) >> 6).astype(F32)
    sources = (own_ref, ref_ref)

    def tile_of(s, p):
        return sources[s][:, p * LANES : (p + 1) * LANES].astype(F32)

    for s in range(2):
        for p in range(tiles):
            rows_ref[s * tiles + p : s * tiles + p + 1, :] = jnp.sum(tile_of(s, p), axis=0, keepdims=True)
    mean = jnp.dot(rows_ref[...], group, precision=HIGHEST) / (BLK * BLK)
    centered = []
    for s in range(2):
        for p in range(tiles):
            value = tile_of(s, p) - mean[s * tiles + p : s * tiles + p + 1, :]
            rows_ref[s * tiles + p : s * tiles + p + 1, :] = jnp.sum(value * value, axis=0, keepdims=True)
            centered.append(value)
    energy = jnp.dot(rows_ref[...], group, precision=HIGHEST)
    scale = 1.0 / (BLK * jnp.sqrt(energy[0:tiles] * energy[tiles:] + 1e-06))

    def spectrum(value):
        high = value.astype(BF16)
        low = (value - high.astype(F32)).astype(BF16)
        f = dot(first_ref[...], jnp.concatenate([high, high, low], axis=0)).astype(BF16)
        s = dot(jnp.concatenate([f, f], axis=1), second_ref[...])
        return (
            s[0:size, 0:LANES] + s[size:, LANES:],
            s[size:, 0:LANES] - s[0:size, LANES:],
        )

    lag_rows = [[] for _ in range(LANES // LAGS)]
    for p in range(tiles):
        own_r, own_i = spectrum(centered[p])
        ref_r, ref_i = spectrum(centered[tiles + p])
        by = scale[p : p + 1, :]
        cross = jnp.concatenate(
            [(own_r * ref_r + own_i * ref_i) * by, (own_i * ref_r - own_r * ref_i) * by], axis=0
        ).astype(BF16)
        lags = dot(third_ref[...], jnp.concatenate([cross, cross], axis=0))
        for q in range(LANES // LAGS):
            part = [lags[ri * LAGS + q * 8 : ri * LAGS + q * 8 + 8] for ri in range(2)]
            lag_rows[q].append(jnp.concatenate(part, axis=1))
    lhs = jnp.concatenate([row for rows in lag_rows for row in rows], axis=0).astype(BF16)
    result = dot(jnp.concatenate([lhs, lhs], axis=1), fourth_ref[...])
    height = 8 * tiles
    quarter = iota((height, 2 * LANES), 1) % LANES // LAGS
    total = result[0:height]
    for q in range(1, LANES // LAGS):
        total = jnp.where(quarter == q, result[q * height : (q + 1) * height], total)
    for p in range(tiles):
        for jj in range(2):
            at = (2 * p + jj) * 8
            out_scr[at : at + 8, :] = total[p * 8 : p * 8 + 8, jj * LANES : (jj + 1) * LANES]
    for a in range(8):
        out_ref[:, a * LANES : (a + 1) * LANES] = out_scr[pl.ds(a, 2 * tiles, stride=8), :]


def shifted(value, axis, steps):
    count = lax.axis_size(axis)
    pairs = [(s, s - steps) for s in range(count) if 0 <= s - steps < count]
    return lax.ppermute(value, axis, pairs)


def from_root(value, axis, root):
    count = lax.axis_size(axis)
    value = jnp.where(lax.axis_index(axis) == root, value, jnp.zeros_like(value))
    if count & (count - 1):
        return lax.psum(value, axis)
    step = 1
    while step < count:
        value = jnp.maximum(value, lax.ppermute(value, axis, [(s, s ^ step) for s in range(count)]))
        step *= 2
    return value


def cost(flops, size):
    return pl.CostEstimate(flops=flops, bytes_accessed=size, transcendentals=0)


def body(slc, ref_date, int_offset, frac_offset, partners):
    own = slc[0]
    _, rows, cols = own.shape
    sds = jax.ShapeDtypeStruct
    payload = sds((2 * rows + 2 * TAPS, LANES), BF16)
    main, amp, low, high = pl.pallas_call(
        prep_kernel,
        out_shape=(sds(own.shape, BF16), sds((rows, cols), BF16), payload, payload),
        in_specs=[VMEM] * 3,
        out_specs=(VMEM,) * 4,
        cost_estimate=cost(2 * 128 * 256 * cols, 1 << 20),
        name="prepare",
    )(own, int_offset[0], frac_offset[0])
    right = shifted(low, "rng", 1)
    left = shifted(high, "rng", -1)
    two = shifted(main, "date", 2)
    one = shifted(main, "date", 1)
    edge = pl.pallas_call(
        edge_kernel,
        out_shape=sds((rows, LANES), BF16),
        in_specs=[VMEM] * 4,
        out_specs=VMEM,
        name="edges",
    )(low, high, left, right)
    mains = [one, two, shifted(two, "date", 1), shifted(two, "date", 2)]
    edges = [shifted(edge, "date", h) for h in range(1, SPAN + 1)]
    ref_amp = from_root(amp, "date", ref_date[0])
    tables = [jnp.asarray(t) for t in surface_tables()]
    surface = pl.pallas_call(
        surface_kernel,
        out_shape=sds((cols // BLK, LAGS * LAGS), F32),
        in_specs=[VMEM] * 6,
        out_specs=VMEM,
        scratch_shapes=[
            pltpu.VMEM((2 * cols // LANES, LANES), F32),
            pltpu.VMEM((8 * cols // BLK, LANES), F32),
        ],
        name="surface",
    )(amp, ref_amp, *tables)
    operands = [v for pair in zip(mains, edges) for v in pair]
    coherence = pl.pallas_call(
        lambda *refs: coherence_kernel(SPAN, *refs),
        out_shape=sds((SPAN, rows, cols), BF16),
        in_specs=[SMEM] + [VMEM] * (2 + 2 * SPAN),
        out_specs=VMEM,
        scratch_shapes=[pltpu.VMEM(((1 + 3 * SPAN) * rows, cols + LANES), BF16)],
        name="coherence",
    )(partners, main, edge, *operands)
    return (surface[None, None], coherence[None])


def solution(mesh):
    in_specs = (
        P("date", None, None, "rng"),
        P(),
        P("date", None, "rng"),
        P("date", None, "rng"),
        P("date", None),
    )
    out_specs = (P("date", None, "rng", None), P("date", None, None, "rng"))
    return jax.shard_map(body, mesh=mesh, in_specs=in_specs, out_specs=out_specs, check_vma=False)
```

profile of v0, /device:TPU:26, one launch (start us, length us, event | category | flops | bytes accessed | tf_op | source)
XLA Modules:
  0.0 67.5 jit_solution(2557373571853605733)
XLA Ops:
  1.3 2.5 %prepare.1 = (bf16[2,64,1024]{2,1,0:T(8,128)(2,1)}, bf16[64,1024]{1,0:T(8,128)(2,1)}, bf16[144,128]{1,0:T(8,128)(2,1)}, bf16[144,128]{1,0:T(8,128)(2,1)}) custom-call(bf16[2,64,1024]{2,1,0:T(8,128)(2,1)} %bitcast.8, s32[1,16]{1,0:T(1,128)} %bitcast.10, f32[1,16]{1,0:T(1,128)} %bitcast.11), custom_call_target="tpu_custom_call" | custom-call | flops 67108864 | bytes 1048576 | tf_op jit(solution)/shard_map/prepare/pallas_call | solution.py:267
  3.8 0.0 copy-start.1
  3.8 1.6 %collective-permute-start = (bf16[64,1024]{1,0:T(8,128)(2,1)S(1)}, bf16[64,1024]{1,0:T(8,128)(2,1)S(1)}, u32[]{:S(2)}, u32[]{:S(2)}) collective-permute-start(bf16[64,1024]{1,0:T(8,128)(2,1)S(1)} %broadcast_select_fusion), channel_id=1, source_target_pairs={{0,4},{4,0},{8,12},{12,8},{16,20},{20,16},{24,28},{28,24},{1,5},{5... | collective-permute-start | bytes 393224 | tf_op jit(solution)/shard_map/ppermute | solution.py:253
  5.4 2.4 %collective-permute-start.7 = (bf16[2,64,1024]{2,1,0:T(8,128)(2,1)}, bf16[2,64,1024]{2,1,0:T(8,128)(2,1)S(1)}, u32[]{:S(2)}, u32[]{:S(2)}) collective-permute-start(bf16[2,64,1024]{2,1,0:T(8,128)(2,1)} %get-tuple-element.7.refs_1_), channel_id=1, source_target_pairs={{8,0},{12,4},{16,8},{20,12},{24,16},{28,20},{9,1},{13,5},{17,9},{2... | collective-permute-start | bytes 786440 | tf_op jit(solution)/shard_map/ppermute | solution.py:243
  7.8 1.4 %collective-permute-done = bf16[64,1024]{1,0:T(8,128)(2,1)S(1)} collective-permute-done((bf16[64,1024]{1,0:T(8,128)(2,1)S(1)}, bf16[64,1024]{1,0:T(8,128)(2,1)S(1)}, u32[]{:S(2)}, u32[]{:S(2)}) %collective-permute-start) | collective-permute-done | bytes 131104 | tf_op jit(solution)/shard_map/ppermute | solution.py:253
  9.1 0.0 copy-done
  9.2 0.0 copy-start.6
  9.2 0.0 copy-start.7
  9.2 0.5 collective-permute-start.1
  9.7 0.0 copy-done.1
  9.7 4.4 %collective-permute-start.5 = (bf16[2,64,1024]{2,1,0:T(8,128)(2,1)S(1)}, bf16[2,64,1024]{2,1,0:T(8,128)(2,1)S(1)}, u32[]{:S(2)}, u32[]{:S(2)}) collective-permute-start(bf16[2,64,1024]{2,1,0:T(8,128)(2,1)S(1)} %copy-done.1), channel_id=1, source_target_pairs={{4,0},{8,4},{12,8},{16,12},{20,16},{24,20},{28,24},{5,1},{9,5},{13... | collective-permute-start | bytes 786440 | tf_op jit(solution)/shard_map/ppermute | solution.py:243
  14.1 0.7 %collective-permute-done.7.refs_5_ = bf16[2,64,1024]{2,1,0:T(8,128)(2,1)S(1)} collective-permute-done((bf16[2,64,1024]{2,1,0:T(8,128)(2,1)}, bf16[2,64,1024]{2,1,0:T(8,128)(2,1)S(1)}, u32[]{:S(2)}, u32[]{:S(2)}) %collective-permute-start.7) | collective-permute-done | bytes 262176 | tf_op jit(solution)/shard_map/ppermute | solution.py:243
  14.8 4.3 %collective-permute-start.11 = (bf16[2,64,1024]{2,1,0:T(8,128)(2,1)S(1)}, bf16[2,64,1024]{2,1,0:T(8,128)(2,1)S(1)}, u32[]{:S(2)}, u32[]{:S(2)}) collective-permute-start(bf16[2,64,1024]{2,1,0:T(8,128)(2,1)S(1)} %collective-permute-done.7.refs_5_), channel_id=1, source_target_pairs={{8,0},{12,4},{16,8},{20,12},{24,16},{28,20},{9,1},{13,5},{17,9},{2... | collective-permute-start | bytes 786440 | tf_op jit(solution)/shard_map/ppermute | solution.py:243
  19.1 1.9 %collective-permute-start.9 = (bf16[2,64,1024]{2,1,0:T(8,128)(2,1)S(1)}, bf16[2,64,1024]{2,1,0:T(8,128)(2,1)S(1)}, u32[]{:S(2)}, u32[]{:S(2)}) collective-permute-start(bf16[2,64,1024]{2,1,0:T(8,128)(2,1)S(1)} %collective-permute-done.7.refs_5_), channel_id=1, source_target_pairs={{4,0},{8,4},{12,8},{16,12},{20,16},{24,20},{28,24},{5,1},{9,5},{13... | collective-permute-start | bytes 786440 | tf_op jit(solution)/shard_map/ppermute | solution.py:243
  21.0 0.0 collective-permute-done.1
  21.1 0.4 collective-permute-start.2
  21.5 0.0 copy-done.6
  21.5 1.9 %collective-permute-start.4 = (bf16[144,128]{1,0:T(8,128)(2,1)S(1)}, bf16[144,128]{1,0:T(8,128)(2,1)S(1)}, u32[]{:S(2)}, u32[]{:S(2)}) collective-permute-start(bf16[144,128]{1,0:T(8,128)(2,1)S(1)} %copy-done.6), channel_id=1, source_target_pairs={{1,0},{2,1},{3,2},{5,4},{6,5},{7,6},{9,8},{10,9},{11,10},{13,12},{... | collective-permute-start | bytes 110600 | tf_op jit(solution)/shard_map/ppermute | solution.py:243
  23.4 1.6 %collective-permute-done.4.right_ref = bf16[144,128]{1,0:T(8,128)(2,1)S(1)} collective-permute-done((bf16[144,128]{1,0:T(8,128)(2,1)S(1)}, bf16[144,128]{1,0:T(8,128)(2,1)S(1)}, u32[]{:S(2)}, u32[]{:S(2)}) %collective-permute-start.4) | collective-permute-done | bytes 36896 | tf_op jit(solution)/shard_map/ppermute | solution.py:243
  25.0 0.0 copy-done.7
  25.0 1.9 %collective-permute-start.3 = (bf16[144,128]{1,0:T(8,128)(2,1)S(1)}, bf16[144,128]{1,0:T(8,128)(2,1)S(1)}, u32[]{:S(2)}, u32[]{:S(2)}) collective-permute-start(bf16[144,128]{1,0:T(8,128)(2,1)S(1)} %copy-done.7), channel_id=1, source_target_pairs={{0,1},{1,2},{2,3},{4,5},{5,6},{6,7},{8,9},{9,10},{10,11},{12,13},{... | collective-permute-start | bytes 110600 | tf_op jit(solution)/shard_map/ppermute | solution.py:243
  26.9 3.7 %collective-permute-done.3.left_ref = bf16[144,128]{1,0:T(8,128)(2,1)S(1)} collective-permute-done((bf16[144,128]{1,0:T(8,128)(2,1)S(1)}, bf16[144,128]{1,0:T(8,128)(2,1)S(1)}, u32[]{:S(2)}, u32[]{:S(2)}) %collective-permute-start.3) | collective-permute-done | bytes 36896 | tf_op jit(solution)/shard_map/ppermute | solution.py:243
  30.6 0.0 copy-done.8
  30.6 0.6 copy-done.9
  31.2 1.8 %edges.1.refs_2_ = bf16[64,128]{1,0:T(8,128)(2,1)} custom-call(bf16[144,128]{1,0:T(8,128)(2,1)} %get-tuple-element.8.low_ref, bf16[144,128]{1,0:T(8,128)(2,1)} %get-tuple-element.9.high_ref, bf16[144,128]{1,0:T(8,128)(2,1)} %copy-done.9, bf16[144,128]{1,0:T(8,128)(2,1)} %copy-done.8), custom_call_target="tpu_custom_call" | custom-call | tf_op jit(solution)/shard_map/edges/pallas_call | solution.py:279
  33.0 0.0 copy-done.2
  33.0 4.2 %collective-permute-start.12 = (bf16[64,128]{1,0:T(8,128)(2,1)}, bf16[64,128]{1,0:T(8,128)(2,1)S(1)}, u32[]{:S(2)}, u32[]{:S(2)}) collective-permute-start(bf16[64,128]{1,0:T(8,128)(2,1)} %edges.1.refs_2_), channel_id=1, source_target_pairs={{16,0},{20,4},{24,8},{28,12},{17,1},{21,5},{25,9},{29,13},{18,2},{... | collective-permute-start | bytes 49160 | tf_op jit(solution)/shard_map/ppermute | solution.py:243
  37.2 1.6 %collective-permute-done.12.refs_10_ = bf16[64,128]{1,0:T(8,128)(2,1)S(1)} collective-permute-done((bf16[64,128]{1,0:T(8,128)(2,1)}, bf16[64,128]{1,0:T(8,128)(2,1)S(1)}, u32[]{:S(2)}, u32[]{:S(2)}) %collective-permute-start.12) | collective-permute-done | bytes 16416 | tf_op jit(solution)/shard_map/ppermute | solution.py:243
  38.8 7.0 %collective-permute-start.10 = (bf16[64,128]{1,0:T(8,128)(2,1)}, bf16[64,128]{1,0:T(8,128)(2,1)S(1)}, u32[]{:S(2)}, u32[]{:S(2)}) collective-permute-start(bf16[64,128]{1,0:T(8,128)(2,1)} %edges.1.refs_2_), channel_id=1, source_target_pairs={{12,0},{16,4},{20,8},{24,12},{28,16},{13,1},{17,5},{21,9},{25,13},... | collective-permute-start | bytes 49160 | tf_op jit(solution)/shard_map/ppermute | solution.py:243
  45.8 1.6 %collective-permute-done.10.refs_8_ = bf16[64,128]{1,0:T(8,128)(2,1)S(1)} collective-permute-done((bf16[64,128]{1,0:T(8,128)(2,1)}, bf16[64,128]{1,0:T(8,128)(2,1)S(1)}, u32[]{:S(2)}, u32[]{:S(2)}) %collective-permute-start.10) | collective-permute-done | bytes 16416 | tf_op jit(solution)/shard_map/ppermute | solution.py:243
  47.5 2.1 %collective-permute-start.8 = (bf16[64,128]{1,0:T(8,128)(2,1)}, bf16[64,128]{1,0:T(8,128)(2,1)S(1)}, u32[]{:S(2)}, u32[]{:S(2)}) collective-permute-start(bf16[64,128]{1,0:T(8,128)(2,1)} %edges.1.refs_2_), channel_id=1, source_target_pairs={{8,0},{12,4},{16,8},{20,12},{24,16},{28,20},{9,1},{13,5},{17,9},{2... | collective-permute-start | bytes 49160 | tf_op jit(solution)/shard_map/ppermute | solution.py:243
  49.6 0.0 collective-permute-done.2
  49.6 6.4 %collective-permute-start.6 = (bf16[64,128]{1,0:T(8,128)(2,1)}, bf16[64,128]{1,0:T(8,128)(2,1)S(1)}, u32[]{:S(2)}, u32[]{:S(2)}) collective-permute-start(bf16[64,128]{1,0:T(8,128)(2,1)} %edges.1.refs_2_), channel_id=1, source_target_pairs={{4,0},{8,4},{12,8},{16,12},{20,16},{24,20},{28,24},{5,1},{9,5},{13... | collective-permute-start | bytes 49160 | tf_op jit(solution)/shard_map/ppermute | solution.py:243
  56.0 0.7 %max.11.ref_ref = bf16[64,1024]{1,0:T(8,128)(2,1)} maximum(bf16[64,1024]{1,0:T(8,128)(2,1)S(1)} %max.10, bf16[64,1024]{1,0:T(8,128)(2,1)S(1)} %collective-permute-done.2) | non-fusion elementwise | flops 65536 | bytes 393216 | tf_op jit(solution)/shard_map/max | solution.py:253
  56.6 0.0 copy-done.10
  56.7 4.5 %surface.1 = f32[16,1024]{1,0:T(8,128)} custom-call(bf16[64,1024]{1,0:T(8,128)(2,1)} %get-tuple-element.6.own_ref, bf16[64,1024]{1,0:T(8,128)(2,1)} %max.11.ref_ref, bf16[128,192]{1,0:T(8,128)(2,1)} %constant.16.clone.first_ref, bf16[256,256]{1,0:T(8,128)(2,1)} %constant.17.clone.second_ref, bf16[64,256]{1,0:T(8,128)(2,1)} %constant.18.clone.third_ref, ...), custom_call_target="tpu_custom_call" | custom-call | tf_op jit(solution)/shard_map/surface/pallas_call | solution.py:290
  61.2 0.0 collective-permute-done.8.refs_6_
  61.2 0.0 collective-permute-done.6.refs_4_
  61.2 0.0 collective-permute-done.5.refs_3_
  61.2 0.0 collective-permute-done.11.refs_9_
  61.2 0.0 copy-start.4
  61.2 0.0 collective-permute-done.9.refs_7_
  61.2 0.5 copy-done.12
  61.8 0.0 copy-done.13
  61.8 0.1 copy-done.3
  61.9 0.1 copy-done.4
  62.0 0.7 %copy-done.5 = bf16[2,64,1024]{2,1,0:T(8,128)(2,1)} copy-done((bf16[2,64,1024]{2,1,0:T(8,128)(2,1)}, bf16[2,64,1024]{2,1,0:T(8,128)(2,1)S(1)}, u32[]{:S(2)}) %copy-start.5) | copy-done | bytes 262168
  62.7 4.9 %coherence.1 = bf16[4,64,1024]{2,1,0:T(8,128)(2,1)} custom-call(s32[1,4]{1,0:T(1,128)} %refs_0_.1, bf16[2,64,1024]{2,1,0:T(8,128)(2,1)} %get-tuple-element.7.refs_1_, bf16[64,128]{1,0:T(8,128)(2,1)} %edges.1.refs_2_, bf16[2,64,1024]{2,1,0:T(8,128)(2,1)} %copy-done.3, bf16[64,128]{1,0:T(8,128)(2,1)} %copy-done.13, bf16[2,64,1024]{2,1,0:T(8,128)(2,1)} %copy-done.2, ...), custom_call_target="tpu_custom_call" | custom-call | tf_op jit(solution)/shard_map/coherence/pallas_call | solution.py:302
  (14 shorter events, 0.1 us)
Async XLA Ops:
  3.8 5.3 %copy-start = (bf16[64,1024]{1,0:T(8,128)(2,1)S(1)}, bf16[64,1024]{1,0:T(8,128)(2,1)}, u32[]{:S(2)}) copy-start(bf16[64,1024]{1,0:T(8,128)(2,1)} %get-tuple-element.6.own_ref) | copy-start | bytes 393220
  3.8 5.9 %copy-start.1 = (bf16[2,64,1024]{2,1,0:T(8,128)(2,1)S(1)}, bf16[2,64,1024]{2,1,0:T(8,128)(2,1)}, u32[]{:S(2)}) copy-start(bf16[2,64,1024]{2,1,0:T(8,128)(2,1)} %get-tuple-element.7.refs_1_) | copy-start | bytes 786436
  3.8 5.3 %collective-permute-start = (bf16[64,1024]{1,0:T(8,128)(2,1)S(1)}, bf16[64,1024]{1,0:T(8,128)(2,1)S(1)}, u32[]{:S(2)}, u32[]{:S(2)}) collective-permute-start(bf16[64,1024]{1,0:T(8,128)(2,1)S(1)} %broadcast_select_fusion), channel_id=1, source_target_pairs={{0,4},{4,0},{8,12},{12,8},{16,20},{20,16},{24,28},{28,24},{1,5},{5... | collective-permute-start | bytes 393224 | tf_op jit(solution)/shard_map/ppermute | solution.py:253
  5.4 9.4 %collective-permute-start.7 = (bf16[2,64,1024]{2,1,0:T(8,128)(2,1)}, bf16[2,64,1024]{2,1,0:T(8,128)(2,1)S(1)}, u32[]{:S(2)}, u32[]{:S(2)}) collective-permute-start(bf16[2,64,1024]{2,1,0:T(8,128)(2,1)} %get-tuple-element.7.refs_1_), channel_id=1, source_target_pairs={{8,0},{12,4},{16,8},{20,12},{24,16},{28,20},{9,1},{13,5},{17,9},{2... | collective-permute-start | bytes 786440 | tf_op jit(solution)/shard_map/ppermute | solution.py:243
  9.2 12.3 %copy-start.6 = (bf16[144,128]{1,0:T(8,128)(2,1)S(1)}, bf16[144,128]{1,0:T(8,128)(2,1)}, u32[]{:S(2)}) copy-start(bf16[144,128]{1,0:T(8,128)(2,1)} %get-tuple-element.8.low_ref) | copy-start | bytes 110596
  9.2 15.8 %copy-start.7 = (bf16[144,128]{1,0:T(8,128)(2,1)S(1)}, bf16[144,128]{1,0:T(8,128)(2,1)}, u32[]{:S(2)}) copy-start(bf16[144,128]{1,0:T(8,128)(2,1)} %get-tuple-element.9.high_ref) | copy-start | bytes 110596
  9.2 11.9 %collective-permute-start.1 = (bf16[64,1024]{1,0:T(8,128)(2,1)S(1)}, bf16[64,1024]{1,0:T(8,128)(2,1)S(1)}, u32[]{:S(2)}, u32[]{:S(2)}) collective-permute-start(bf16[64,1024]{1,0:T(8,128)(2,1)S(1)} %fusion), channel_id=1, source_target_pairs={{0,8},{4,12},{8,0},{12,4},{16,24},{20,28},{24,16},{28,20},{1,9},{5... | collective-permute-start | bytes 393224 | tf_op jit(solution)/shard_map/ppermute | solution.py:253
  9.7 51.5 %collective-permute-start.5 = (bf16[2,64,1024]{2,1,0:T(8,128)(2,1)S(1)}, bf16[2,64,1024]{2,1,0:T(8,128)(2,1)S(1)}, u32[]{:S(2)}, u32[]{:S(2)}) collective-permute-start(bf16[2,64,1024]{2,1,0:T(8,128)(2,1)S(1)} %copy-done.1), channel_id=1, source_target_pairs={{4,0},{8,4},{12,8},{16,12},{20,16},{24,20},{28,24},{5,1},{9,5},{13... | collective-permute-start | bytes 786440 | tf_op jit(solution)/shard_map/ppermute | solution.py:243
  14.8 18.2 %copy-start.2 = (bf16[2,64,1024]{2,1,0:T(8,128)(2,1)}, bf16[2,64,1024]{2,1,0:T(8,128)(2,1)S(1)}, u32[]{:S(2)}) copy-start(bf16[2,64,1024]{2,1,0:T(8,128)(2,1)S(1)} %collective-permute-done.7.refs_5_) | copy-start | bytes 786436
  14.8 46.4 %collective-permute-start.11 = (bf16[2,64,1024]{2,1,0:T(8,128)(2,1)S(1)}, bf16[2,64,1024]{2,1,0:T(8,128)(2,1)S(1)}, u32[]{:S(2)}, u32[]{:S(2)}) collective-permute-start(bf16[2,64,1024]{2,1,0:T(8,128)(2,1)S(1)} %collective-permute-done.7.refs_5_), channel_id=1, source_target_pairs={{8,0},{12,4},{16,8},{20,12},{24,16},{28,20},{9,1},{13,5},{17,9},{2... | collective-permute-start | bytes 786440 | tf_op jit(solution)/shard_map/ppermute | solution.py:243
  19.1 42.1 %collective-permute-start.9 = (bf16[2,64,1024]{2,1,0:T(8,128)(2,1)S(1)}, bf16[2,64,1024]{2,1,0:T(8,128)(2,1)S(1)}, u32[]{:S(2)}, u32[]{:S(2)}) collective-permute-start(bf16[2,64,1024]{2,1,0:T(8,128)(2,1)S(1)} %collective-permute-done.7.refs_5_), channel_id=1, source_target_pairs={{4,0},{8,4},{12,8},{16,12},{20,16},{24,20},{28,24},{5,1},{9,5},{13... | collective-permute-start | bytes 786440 | tf_op jit(solution)/shard_map/ppermute | solution.py:243
  21.1 28.5 %collective-permute-start.2 = (bf16[64,1024]{1,0:T(8,128)(2,1)S(1)}, bf16[64,1024]{1,0:T(8,128)(2,1)S(1)}, u32[]{:S(2)}, u32[]{:S(2)}) collective-permute-start(bf16[64,1024]{1,0:T(8,128)(2,1)S(1)} %max.10), channel_id=1, source_target_pairs={{0,16},{4,20},{8,24},{12,28},{16,0},{20,4},{24,8},{28,12},{1,17},{... | collective-permute-start | bytes 393224 | tf_op jit(solution)/shard_map/ppermute | solution.py:253
  21.5 3.5 %collective-permute-start.4 = (bf16[144,128]{1,0:T(8,128)(2,1)S(1)}, bf16[144,128]{1,0:T(8,128)(2,1)S(1)}, u32[]{:S(2)}, u32[]{:S(2)}) collective-permute-start(bf16[144,128]{1,0:T(8,128)(2,1)S(1)} %copy-done.6), channel_id=1, source_target_pairs={{1,0},{2,1},{3,2},{5,4},{6,5},{7,6},{9,8},{10,9},{11,10},{13,12},{... | collective-permute-start | bytes 110600 | tf_op jit(solution)/shard_map/ppermute | solution.py:243
  25.0 5.6 %copy-start.8 = (bf16[144,128]{1,0:T(8,128)(2,1)}, bf16[144,128]{1,0:T(8,128)(2,1)S(1)}, u32[]{:S(2)}) copy-start(bf16[144,128]{1,0:T(8,128)(2,1)S(1)} %collective-permute-done.4.right_ref) | copy-start | bytes 110596
  25.0 5.6 %collective-permute-start.3 = (bf16[144,128]{1,0:T(8,128)(2,1)S(1)}, bf16[144,128]{1,0:T(8,128)(2,1)S(1)}, u32[]{:S(2)}, u32[]{:S(2)}) collective-permute-start(bf16[144,128]{1,0:T(8,128)(2,1)S(1)} %copy-done.7), channel_id=1, source_target_pairs={{0,1},{1,2},{2,3},{4,5},{5,6},{6,7},{8,9},{9,10},{10,11},{12,13},{... | collective-permute-start | bytes 110600 | tf_op jit(solution)/shard_map/ppermute | solution.py:243
  30.6 0.6 copy-start.9
  33.0 5.8 %collective-permute-start.12 = (bf16[64,128]{1,0:T(8,128)(2,1)}, bf16[64,128]{1,0:T(8,128)(2,1)S(1)}, u32[]{:S(2)}, u32[]{:S(2)}) collective-permute-start(bf16[64,128]{1,0:T(8,128)(2,1)} %edges.1.refs_2_), channel_id=1, source_target_pairs={{16,0},{20,4},{24,8},{28,12},{17,1},{21,5},{25,9},{29,13},{18,2},{... | collective-permute-start | bytes 49160 | tf_op jit(solution)/shard_map/ppermute | solution.py:243
  38.8 17.8 %copy-start.10 = (bf16[64,128]{1,0:T(8,128)(2,1)}, bf16[64,128]{1,0:T(8,128)(2,1)S(1)}, u32[]{:S(2)}) copy-start(bf16[64,128]{1,0:T(8,128)(2,1)S(1)} %collective-permute-done.12.refs_10_) | copy-start | bytes 49156
  38.8 8.7 %collective-permute-start.10 = (bf16[64,128]{1,0:T(8,128)(2,1)}, bf16[64,128]{1,0:T(8,128)(2,1)S(1)}, u32[]{:S(2)}, u32[]{:S(2)}) collective-permute-start(bf16[64,128]{1,0:T(8,128)(2,1)} %edges.1.refs_2_), channel_id=1, source_target_pairs={{12,0},{16,4},{20,8},{24,12},{28,16},{13,1},{17,5},{21,9},{25,13},... | collective-permute-start | bytes 49160 | tf_op jit(solution)/shard_map/ppermute | solution.py:243
  47.5 9.2 %copy-start.11 = (bf16[64,128]{1,0:T(8,128)(2,1)}, bf16[64,128]{1,0:T(8,128)(2,1)S(1)}, u32[]{:S(2)}) copy-start(bf16[64,128]{1,0:T(8,128)(2,1)S(1)} %collective-permute-done.10.refs_8_) | copy-start | bytes 49156
  47.5 13.7 %collective-permute-start.8 = (bf16[64,128]{1,0:T(8,128)(2,1)}, bf16[64,128]{1,0:T(8,128)(2,1)S(1)}, u32[]{:S(2)}, u32[]{:S(2)}) collective-permute-start(bf16[64,128]{1,0:T(8,128)(2,1)} %edges.1.refs_2_), channel_id=1, source_target_pairs={{8,0},{12,4},{16,8},{20,12},{24,16},{28,20},{9,1},{13,5},{17,9},{2... | collective-permute-start | bytes 49160 | tf_op jit(solution)/shard_map/ppermute | solution.py:243
  49.6 11.6 %collective-permute-start.6 = (bf16[64,128]{1,0:T(8,128)(2,1)}, bf16[64,128]{1,0:T(8,128)(2,1)S(1)}, u32[]{:S(2)}, u32[]{:S(2)}) collective-permute-start(bf16[64,128]{1,0:T(8,128)(2,1)} %edges.1.refs_2_), channel_id=1, source_target_pairs={{4,0},{8,4},{12,8},{16,12},{20,16},{24,20},{28,24},{5,1},{9,5},{13... | collective-permute-start | bytes 49160 | tf_op jit(solution)/shard_map/ppermute | solution.py:243
  61.2 0.6 copy-start.12
  61.2 0.6 copy-start.13
  61.2 0.7 %copy-start.3 = (bf16[2,64,1024]{2,1,0:T(8,128)(2,1)}, bf16[2,64,1024]{2,1,0:T(8,128)(2,1)S(1)}, u32[]{:S(2)}) copy-start(bf16[2,64,1024]{2,1,0:T(8,128)(2,1)S(1)} %collective-permute-done.5.refs_3_) | copy-start | bytes 786436
  61.2 0.8 %copy-start.4 = (bf16[2,64,1024]{2,1,0:T(8,128)(2,1)}, bf16[2,64,1024]{2,1,0:T(8,128)(2,1)S(1)}, u32[]{:S(2)}) copy-start(bf16[2,64,1024]{2,1,0:T(8,128)(2,1)S(1)} %collective-permute-done.11.refs_9_) | copy-start | bytes 786436
  62.0 0.7 %copy-start.5 = (bf16[2,64,1024]{2,1,0:T(8,128)(2,1)}, bf16[2,64,1024]{2,1,0:T(8,128)(2,1)S(1)}, u32[]{:S(2)}) copy-start(bf16[2,64,1024]{2,1,0:T(8,128)(2,1)S(1)} %collective-permute-done.9.refs_7_) | copy-start | bytes 786436
where the time goes:
time: 68 us; the launch traced here: 67.5 us
  starting transfers between devices  39 us (57%)
  Pallas kernels  13.6 us (20%)
  waiting for transfers between devices  10.6 us (16%)
  local copies, waits for them, and re-layouts  2.11 us (3%)
  between operations  1.49 us (2%)
  other arithmetic  0.76 us (1%)
    ppermute x10, starting transfers between devices, shifted(): return lax.ppermute(value, axis, pairs)  36.5 us
    ppermute x10, waiting for transfers between devices, shifted(): return lax.ppermute(value, axis, pairs)  9.24 us
    pallas_call x1, Pallas kernels, body(): pl.pallas_call(lambda *refs: coherence_kernel(SPAN, *refs), out_shape=sds...  4.85 us
    pallas_call x1, Pallas kernels, body(): pl.pallas_call(surface_kernel, out_shape=sds((cols // BLK, LAGS * LAGS),...  4.5 us
    pallas_call x1, Pallas kernels, body(): pl.pallas_call(prep_kernel, out_shape=(sds(own.shape, BF16), sds((rows, c...  2.51 us
    ppermute x3, starting transfers between devices, from_root(): lax.ppermute(value, axis, [(s, s ^ step) for s in range(count)])  2.49 us
    unnamed x28, local copies, waits for them, and re-layouts  2.11 us
    pallas_call x1, Pallas kernels, body(): pl.pallas_call(edge_kernel, out_shape=sds((rows, LANES), BF16), in_specs=...  1.77 us
  transfers between devices with their start and end apart: 13, of which 6 were waited for; matrix products, arithmetic and copies ran while one was open for 1% of the time, Pallas kernels for 9%

commit v1 on v0

--- a/solution.py
+++ b/solution.py
@@ -21,6 +21,7 @@
 HIGHEST = lax.Precision.HIGHEST
 VMEM = pl.BlockSpec(memory_space=pltpu.VMEM)
 SMEM = pl.BlockSpec(memory_space=pltpu.SMEM)
+PARAMS = pltpu.CompilerParams(vmem_limit_bytes=8 << 20)
 
 
 def dot(a, b):
@@ -70,12 +71,16 @@
         else:
             window = slc_ref[:, :, (p - 1) * LANES : (p + 1) * LANES]
         out = dot(window.reshape(2 * rows, window.shape[2]), taps)
-        res_ref[:, :, p * LANES : (p + 1) * LANES] = out.astype(BF16).reshape(2, rows, LANES)
-
-
-def edge_kernel(low_ref, high_ref, left_ref, right_ref, out_ref):
-    rows = out_ref.shape[0]
+        res_ref[p] = out[0:rows].astype(BF16)
+        res_ref[tiles + p] = out[rows:].astype(BF16)
+
+
+def edge_kernel(keep_ref, low_ref, high_ref, left_ref, right_ref, out_ref):
+    rows = out_ref.shape[1]
     lane = iota((2 * TAPS, LANES), 1)
+    outside = [keep_ref[0, k] == 0 for k in range(2)]
+    left_ref = jnp.where(outside[0], jnp.zeros_like(left_ref), left_ref[...])
+    right_ref = jnp.where(outside[1], jnp.zeros_like(right_ref), right_ref[...])
 
     def tile(before, after):
         table = jnp.where(lane < PAD, before[2 * rows :, :].astype(F32), after[2 * rows :, :].astype(F32))
@@ -86,7 +91,7 @@
     last = pltpu.roll(tile(high_ref, right_ref), EDGE, 1)
     lane = iota((2 * rows, LANES), 1)
     both = jnp.where(lane < EDGE, first, jnp.where(lane < 2 * EDGE, last, 0.0))
-    out_ref[...] = (both[0:rows] + pltpu.roll(both[rows:], 2 * EDGE, 1)).astype(BF16)
+    out_ref[0] = (both[0:rows] + pltpu.roll(both[rows:], 2 * EDGE, 1)).astype(BF16)
 
 
 def range_box():
@@ -104,13 +109,13 @@
 
 
 def extended(main_ref, edge_ref, p):
-    tiles = main_ref.shape[2] // LANES
+    tiles = main_ref.shape[0] // 2
     if 0 < p < tiles:
-        return tuple(main_ref[c, :, p * LANES : (p + 1) * LANES].astype(F32) for c in range(2))
-    edge = edge_ref[...].astype(F32)
+        return tuple(main_ref[c * tiles + p].astype(F32) for c in range(2))
+    edge = edge_ref[0].astype(F32)
     lane = iota(edge.shape, 1)
     if p == 0:
-        inner = [main_ref[c, :, 0:LANES].astype(F32) for c in range(2)]
+        inner = [main_ref[c * tiles].astype(F32) for c in range(2)]
         outer = [edge, pltpu.roll(edge, LANES - 2 * EDGE, 1)]
     else:
         inner = [jnp.zeros(edge.shape, F32)] * 2
@@ -118,33 +123,53 @@
     return tuple(jnp.where(lane < EDGE, o, i) for o, i in zip(outer, inner))
 
 
-def coherence_kernel(count, *refs):
-    flag_ref, own_ref, own_edge_ref = refs[0:3]
-    others = refs[3 : 3 + 2 * count]
-    out_ref, fields_ref = refs[3 + 2 * count :]
-    _, rows, cols = own_ref.shape
+def pair_kernel(first, flag_ref, own_ref, own_edge_ref, main_ref, edge_ref, *refs):
+    if first:
+        out_ref, power_ref, fields_ref = refs
+    else:
+        power_ref, out_ref, fields_ref = refs
+    rows, cols = out_ref.shape
     tiles = cols // LANES
     for p in range(tiles + 1):
         lanes = slice(p * LANES, (p + 1) * LANES)
         own_r, own_i = extended(own_ref, own_edge_ref, p)
-        fields_ref[0:rows, lanes] = (own_r * own_r + own_i * own_i).astype(BF16)
-        for h in range(count):
-            r, i = extended(others[2 * h], others[2 * h + 1], p)
-            at = rows * (1 + 3 * h)
-            fields_ref[at : at + rows, lanes] = (own_r * r + own_i * i).astype(BF16)
-            fields_ref[at + rows : at + 2 * rows, lanes] = (own_i * r - own_r * i).astype(BF16)
-            fields_ref[at + 2 * rows : at + 3 * rows, lanes] = (r * r + i * i).astype(BF16)
+        r, i = extended(main_ref, edge_ref, p)
+        fields_ref[0:rows, lanes] = (own_r * r + own_i * i).astype(BF16)
+        fields_ref[rows : 2 * rows, lanes] = (own_i * r - own_r * i).astype(BF16)
+        fields_ref[2 * rows : 3 * rows, lanes] = (r * r + i * i).astype(BF16)
+        if first:
+            fields_ref[3 * rows :, lanes] = (own_r * own_r + own_i * own_i).astype(BF16)
     box = range_box()
+    flag = flag_ref[0].astype(F32)
     for p in range(tiles):
+        lanes = slice(p * LANES, (p + 1) * LANES)
         sums = dot(fields_ref[:, p * LANES : (p + 2) * LANES], box)
-        own = line_box(sums[0:rows])
-        for h in range(count):
-            at = rows * (1 + 3 * h)
-            re = line_box(sums[at : at + rows])
-            im = line_box(sums[at + rows : at + 2 * rows])
-            partner = line_box(sums[at + 2 * rows : at + 3 * rows])
-            value = flag_ref[0, h].astype(F32) * (re * re + im * im) / (own * partner + 1e-06)
-            out_ref[h, :, p * LANES : (p + 1) * LANES] = value.astype(BF16)
+        if first:
+            power_ref[:, lanes] = line_box(sums[3 * rows :])
+        re = line_box(sums[0:rows])
+        im = line_box(sums[rows : 2 * rows])
+        partner = line_box(sums[2 * rows : 3 * rows])
+        value = flag * (re * re + im * im) / (power_ref[:, lanes] * partner + 1e-06)
+        out_ref[:, lanes] = value.astype(BF16)
+
+
+def first_kernel(*refs):
+    pair_kernel(True, *refs)
+
+
+def next_kernel(*refs):
+    pair_kernel(False, *refs)
+
+
+def last_kernel(odd_ref, flag_ref, own_ref, own_edge_ref, main_ref, edge_ref, power_ref, *refs):
+    two_ref, cross_ref, four_ref, out_ref, tail_ref, fields_ref = refs
+    pair_kernel(False, flag_ref, own_ref, own_edge_ref, main_ref, edge_ref, power_ref, tail_ref, fields_ref)
+    odd = odd_ref[0] == 1
+    tail, cross = tail_ref[...], cross_ref[...]
+    out_ref[0] = jnp.where(odd, cross, tail)
+    out_ref[1] = two_ref[...]
+    out_ref[2] = jnp.where(odd, tail, cross)
+    out_ref[3] = four_ref[...]
 
 
 def split(table):
@@ -239,8 +264,20 @@
 
 def shifted(value, axis, steps):
     count = lax.axis_size(axis)
-    pairs = [(s, s - steps) for s in range(count) if 0 <= s - steps < count]
-    return lax.ppermute(value, axis, pairs)
+    return lax.ppermute(value, axis, [(s, (s - steps) % count) for s in range(count)])
+
+
+def swapped(value, axis, step):
+    return lax.ppermute(value, axis, [(s, s ^ step) for s in range(lax.axis_size(axis))])
+
+
+def two_later(value, axis):
+    count = lax.axis_size(axis)
+    middle = {s: s + 2 if s % 4 > 1 else s - 2 for s in range(2, count - 2)}
+    middle.update({0: 1, 1: 0, count - 2: count - 1, count - 1: count - 2})
+    inner = lax.ppermute(value, axis, sorted(middle.items()))
+    outer = swapped(value, axis, 2)
+    return jnp.where(lax.axis_index(axis) % 4 < 2, outer, inner)
 
 
 def from_root(value, axis, root):
@@ -248,10 +285,10 @@
     value = jnp.where(lax.axis_index(axis) == root, value, jnp.zeros_like(value))
     if count & (count - 1):
         return lax.psum(value, axis)
-    step = 1
-    while step < count:
-        value = jnp.maximum(value, lax.ppermute(value, axis, [(s, s ^ step) for s in range(count)]))
-        step *= 2
+    step = count // 2
+    while step:
+        value = jnp.maximum(value, swapped(value, axis, step))
+        step //= 2
     return value
 
 
@@ -262,29 +299,38 @@
 def body(slc, ref_date, int_offset, frac_offset, partners):
     own = slc[0]
     _, rows, cols = own.shape
+    tiles = cols // LANES
     sds = jax.ShapeDtypeStruct
     payload = sds((2 * rows + 2 * TAPS, LANES), BF16)
     main, amp, low, high = pl.pallas_call(
         prep_kernel,
-        out_shape=(sds(own.shape, BF16), sds((rows, cols), BF16), payload, payload),
+        out_shape=(sds((2 * tiles, rows, LANES), BF16), sds((rows, cols), BF16), payload, payload),
         in_specs=[VMEM] * 3,
         out_specs=(VMEM,) * 4,
-        cost_estimate=cost(2 * 128 * 256 * cols, 1 << 20),
+        compiler_params=PARAMS,
         name="prepare",
     )(own, int_offset[0], frac_offset[0])
+    at = lax.axis_index("rng")
+    keep = jnp.stack([at > 0, at < lax.axis_size("rng") - 1]).astype(jnp.int32)[None]
+    ahead = lax.axis_index("date") + 1 + jnp.arange(SPAN, dtype=jnp.int32)
+    flags = jnp.where(ahead < lax.axis_size("date"), partners[0], 0)
+    odd = lax.axis_index("date") % 2
+    beside = swapped(main, "date", 1)
+    two = two_later(main, "date")
+    cross = swapped(two, "date", 1)
+    four = two_later(two, "date")
+    four_cross = swapped(four, "date", 1)
     right = shifted(low, "rng", 1)
     left = shifted(high, "rng", -1)
-    two = shifted(main, "date", 2)
-    one = shifted(main, "date", 1)
     edge = pl.pallas_call(
         edge_kernel,
-        out_shape=sds((rows, LANES), BF16),
-        in_specs=[VMEM] * 4,
+        out_shape=sds((1, rows, LANES), BF16),
+        in_specs=[SMEM] + [VMEM] * 4,
         out_specs=VMEM,
+        compiler_params=PARAMS,
         name="edges",
-    )(low, high, left, right)
-    mains = [one, two, shifted(two, "date", 1), shifted(two, "date", 2)]
-    edges = [shifted(edge, "date", h) for h in range(1, SPAN + 1)]
+    )(keep, low, high, left, right)
+    one_edge, two_edge, three_edge, four_edge = [shifted(edge, "date", h) for h in range(1, SPAN + 1)]
     ref_amp = from_root(amp, "date", ref_date[0])
     tables = [jnp.asarray(t) for t in surface_tables()]
     surface = pl.pallas_call(
@@ -296,17 +342,48 @@
             pltpu.VMEM((2 * cols // LANES, LANES), F32),
             pltpu.VMEM((8 * cols // BLK, LANES), F32),
         ],
+        compiler_params=PARAMS,
         name="surface",
     )(amp, ref_amp, *tables)
-    operands = [v for pair in zip(mains, edges) for v in pair]
-    coherence = pl.pallas_call(
-        lambda *refs: coherence_kernel(SPAN, *refs),
-        out_shape=sds((SPAN, rows, cols), BF16),
-        in_specs=[SMEM] + [VMEM] * (2 + 2 * SPAN),
-        out_specs=VMEM,
-        scratch_shapes=[pltpu.VMEM(((1 + 3 * SPAN) * rows, cols + LANES), BF16)],
-        name="coherence",
-    )(partners, main, edge, *operands)
+
+    def pair(kernel, name, flag, partner, partner_edge, extra, out_shape, fields, scratch=()):
+        return pl.pallas_call(
+            kernel,
+            out_shape=out_shape,
+            in_specs=[SMEM] * (2 if name == "last" else 1) + [VMEM] * (4 + len(extra)),
+            out_specs=jax.tree.map(lambda _: VMEM, out_shape),
+            scratch_shapes=[*scratch, pltpu.VMEM((fields * rows, cols + LANES), BF16)],
+            compiler_params=PARAMS,
+            name=name,
+        )(*([odd[None]] if name == "last" else []), flag, main, edge, partner, partner_edge, *extra)
+
+    field = sds((rows, cols), BF16)
+    even = odd == 0
+    coh_two, power = pair(
+        first_kernel, "first", flags[1:2], two, two_edge, (), (field, sds((rows, cols), F32)), 4
+    )
+    coh_cross = pair(
+        next_kernel,
+        "cross",
+        jnp.where(even, flags[2:3], flags[0:1]),
+        cross,
+        jnp.where(even, three_edge, one_edge),
+        (power,),
+        field,
+        3,
+    )
+    coh_four = pair(next_kernel, "four", flags[3:4], four, four_edge, (power,), field, 3)
+    coherence = pair(
+        last_kernel,
+        "last",
+        jnp.where(even, flags[0:1], flags[2:3]),
+        jnp.where(even, beside, four_cross),
+        jnp.where(even, one_edge, three_edge),
+        (power, coh_two, coh_cross, coh_four),
+        sds((SPAN, rows, cols), BF16),
+        3,
+        (pltpu.VMEM((rows, cols), BF16),),
+    )
     return (surface[None, None], coherence[None])
 
 

time: 68 us -> 51.1 us (0.75)
  the two profiles are of different devices: /device:TPU:26 before, /device:TPU:0 now
where the time goes in v1:
time: 51.1 us; the launch traced here: 50.8 us
  starting transfers between devices  26.1 us (51%)
  Pallas kernels  10.1 us (20%)
  waiting for transfers between devices  7.42 us (15%)
  between operations  3.97 us (8%)
  local copies, waits for them, and re-layouts  2.96 us (6%)
    ppermute x8, starting transfers between devices, swapped(): lax.ppermute(value, axis, [(s, s ^ step) for s in range(lax.axis_size(axi...  13.9 us
    ppermute x6, starting transfers between devices, shifted(): lax.ppermute(value, axis, [(s, (s - steps) % count) for s in range(count)])  9.18 us
    ppermute x8, waiting for transfers between devices, swapped(): lax.ppermute(value, axis, [(s, s ^ step) for s in range(lax.axis_size(axi...  6.35 us
    pallas_call x4, Pallas kernels, pair(): pl.pallas_call(kernel, out_shape=out_shape, in_specs=[SMEM] * (2 if name...  4.96 us
    pallas_call x1, Pallas kernels, body(): pl.pallas_call(surface_kernel, out_shape=sds((cols // BLK, LAGS * LAGS),...  3.3 us
    ppermute x2, starting transfers between devices, two_later(): inner = lax.ppermute(value, axis, sorted(middle.items()))  3.04 us
    unnamed x16, local copies, waits for them, and re-layouts  2.28 us
    ppermute x2, waiting for transfers between devices, two_later(): inner = lax.ppermute(value, axis, sorted(middle.items()))  1.06 us
  transfers between devices with their start and end apart: 16, of which 4 were waited for; matrix products, arithmetic and copies ran while one was open for 2% of the time, Pallas kernels for 15%

profile of v1, /device:TPU:0, one launch (start us, length us, event | category | flops | bytes accessed | tf_op | source)
XLA Modules:
  0.0 50.8 jit_solution(6727832119568581664)
XLA Ops:
  0.6 0.6 %copy-done.5 = s32[1,1,16]{2,1,0:T(1,128)S(1)} copy-done((s32[1,1,16]{2,1,0:T(1,128)S(1)}, s32[1,1,16]{2,1,0:T(1,128)}, u32[]{:S(2)}) %copy-start.5) | copy-done | bytes 88
  1.3 0.0 copy-done.6
  1.3 0.9 %copy-done.1 = bf16[1,2,64,1024]{3,2,1,0:T(8,128)(2,1)S(1)} copy-done((bf16[1,2,64,1024]{3,2,1,0:T(8,128)(2,1)S(1)}, bf16[1,2,64,1024]{3,2,1,0:T(8,128)(2,1)}, u32[]{:S(2)}) %copy-start.1) | copy-done | bytes 262168
  2.3 0.9 %prepare.1 = (bf16[16,64,128]{2,1,0:T(8,128)(2,1)S(1)}, bf16[64,1024]{1,0:T(8,128)(2,1)S(1)}, bf16[144,128]{1,0:T(8,128)(2,1)S(1)}, bf16[144,128]{1,0:T(8,128)(2,1)S(1)}) custom-call(bf16[2,64,1024]{2,1,0:T(8,128)(2,1)S(1)} %bitcast.13, s32[1,16]{1,0:T(1,128)S(1)} %bitcast.14, f32[1,16]{1,0:T(1,128)S(1)} %bitcast.15), custom_call_target="tpu_custom_call" | custom-call | tf_op jit(solution)/shard_map/prepare/pallas_call | solution.py:305
  3.2 3.1 %collective-permute-start.6 = (bf16[16,64,128]{2,1,0:T(8,128)(2,1)S(1)}, bf16[16,64,128]{2,1,0:T(8,128)(2,1)S(1)}, u32[]{:S(2)}, u32[]{:S(2)}) collective-permute-start(bf16[16,64,128]{2,1,0:T(8,128)(2,1)S(1)} %get-tuple-element.9.refs_1_.own_ref), channel_id=1, source_target_pairs={{0,8},{4,12},{8,0},{12,4},{16,24},{20,28},{24,16},{28,20},{1,9},{5... | collective-permute-start | bytes 786440 | tf_op jit(solution)/shard_map/ppermute | solution.py:271
  6.3 1.5 %collective-permute-start.7 = (bf16[16,64,128]{2,1,0:T(8,128)(2,1)S(1)}, bf16[16,64,128]{2,1,0:T(8,128)(2,1)S(1)}, u32[]{:S(2)}, u32[]{:S(2)}) collective-permute-start(bf16[16,64,128]{2,1,0:T(8,128)(2,1)S(1)} %get-tuple-element.9.refs_1_.own_ref), channel_id=1, source_target_pairs={{0,4},{4,0},{8,16},{12,20},{16,8},{20,12},{24,28},{28,24},{1,5},{5... | collective-permute-start | bytes 786440 | tf_op jit(solution)/shard_map/ppermute | solution.py:278
  8.5 1.1 %collective-permute-start = (bf16[64,1024]{1,0:T(8,128)(2,1)S(1)}, bf16[64,1024]{1,0:T(8,128)(2,1)S(1)}, u32[]{:S(2)}, u32[]{:S(2)}) collective-permute-start(bf16[64,1024]{1,0:T(8,128)(2,1)S(1)} %broadcast_select_fusion.3), channel_id=1, source_target_pairs={{0,16},{4,20},{8,24},{12,28},{16,0},{20,4},{24,8},{28,12},{1,17},{... | collective-permute-start | bytes 393224 | tf_op jit(solution)/shard_map/ppermute | solution.py:271
  9.6 0.0 collective-permute-start.3
  9.6 1.7 %collective-permute-start.4 = (bf16[144,128]{1,0:T(8,128)(2,1)S(1)}, bf16[144,128]{1,0:T(8,128)(2,1)S(1)}, u32[]{:S(2)}, u32[]{:S(2)}) collective-permute-start(bf16[144,128]{1,0:T(8,128)(2,1)S(1)} %get-tuple-element.10.low_ref), channel_id=1, source_target_pairs={{0,3},{1,0},{2,1},{3,2},{4,7},{5,4},{6,5},{7,6},{8,11},{9,8},{10,9... | collective-permute-start | bytes 110600 | tf_op jit(solution)/shard_map/ppermute | solution.py:267
  11.4 0.7 %copy-done.7 = s32[1,4]{1,0:T(1,128)S(1)} copy-done((s32[1,4]{1,0:T(1,128)S(1)}, s32[1,4]{1,0:T(1,128)}, u32[]{:S(2)}) %copy-start.7) | copy-done | bytes 40
  12.0 1.0 %collective-permute-done.6 = bf16[16,64,128]{2,1,0:T(8,128)(2,1)S(1)} collective-permute-done((bf16[16,64,128]{2,1,0:T(8,128)(2,1)S(1)}, bf16[16,64,128]{2,1,0:T(8,128)(2,1)S(1)}, u32[]{:S(2)}, u32[]{:S(2)}) %collective-permute-start.6) | collective-permute-done | bytes 262176 | tf_op jit(solution)/shard_map/ppermute | solution.py:271
  13.0 1.1 %collective-permute-done.7 = bf16[16,64,128]{2,1,0:T(8,128)(2,1)S(1)} collective-permute-done((bf16[16,64,128]{2,1,0:T(8,128)(2,1)S(1)}, bf16[16,64,128]{2,1,0:T(8,128)(2,1)S(1)}, u32[]{:S(2)}, u32[]{:S(2)}) %collective-permute-start.7) | collective-permute-done | bytes 262176 | tf_op jit(solution)/shard_map/ppermute | solution.py:278
  14.1 5.4 %collective-permute-start.8 = (bf16[16,64,128]{2,1,0:T(8,128)(2,1)S(1)}, bf16[16,64,128]{2,1,0:T(8,128)(2,1)S(1)}, u32[]{:S(2)}, u32[]{:S(2)}) collective-permute-start(bf16[16,64,128]{2,1,0:T(8,128)(2,1)S(1)} %broadcast_select_fusion.1.refs_3_), channel_id=1, source_target_pairs={{0,8},{4,12},{8,0},{12,4},{16,24},{20,28},{24,16},{28,20},{1,9},{5... | collective-permute-start | bytes 786440 | tf_op jit(solution)/shard_map/ppermute | solution.py:271
  19.5 1.5 %collective-permute-start.9 = (bf16[16,64,128]{2,1,0:T(8,128)(2,1)S(1)}, bf16[16,64,128]{2,1,0:T(8,128)(2,1)S(1)}, u32[]{:S(2)}, u32[]{:S(2)}) collective-permute-start(bf16[16,64,128]{2,1,0:T(8,128)(2,1)S(1)} %broadcast_select_fusion.1.refs_3_), channel_id=1, source_target_pairs={{0,4},{4,0},{8,16},{12,20},{16,8},{20,12},{24,28},{28,24},{1,5},{5... | collective-permute-start | bytes 786440 | tf_op jit(solution)/shard_map/ppermute | solution.py:278
  21.1 0.1 add_convert_fusion.keep_ref
  21.1 0.0 collective-permute-done.3.left_ref
  21.1 0.5 collective-permute-start.5
  21.6 0.0 collective-permute-done.4.right_ref
  21.6 0.9 %edges.1.refs_2_.own_edge_ref = bf16[1,64,128]{2,1,0:T(8,128)(2,1)S(1)} custom-call(s32[1,2]{1,0:T(1,128)S(1)} %add_convert_fusion.keep_ref, bf16[144,128]{1,0:T(8,128)(2,1)S(1)} %get-tuple-element.10.low_ref, bf16[144,128]{1,0:T(8,128)(2,1)S(1)} %get-tuple-element.11.high_ref, bf16[144,128]{1,0:T(8,128)(2,1)S(1)} %collective-permute-done.3.left_ref, ...), custom_call_target="tpu_custom_call" | custom-call | tf_op jit(solution)/shard_map/edges/pallas_call | solution.py:325
  22.5 1.1 %collective-permute-start.12 = (bf16[1,64,128]{2,1,0:T(8,128)(2,1)S(1)}, bf16[1,64,128]{2,1,0:T(8,128)(2,1)S(1)}, u32[]{:S(2)}, u32[]{:S(2)}) collective-permute-start(bf16[1,64,128]{2,1,0:T(8,128)(2,1)S(1)} %edges.1.refs_2_.own_edge_ref), channel_id=1, source_target_pairs={{0,20},{4,24},{8,28},{12,0},{16,4},{20,8},{24,12},{28,16},{1,21},{... | collective-permute-start | bytes 49160 | tf_op jit(solution)/shard_map/ppermute | solution.py:267
  23.6 0.0 collective-permute-done
  23.6 2.9 %collective-permute-start.11 = (bf16[1,64,128]{2,1,0:T(8,128)(2,1)S(1)}, bf16[1,64,128]{2,1,0:T(8,128)(2,1)S(1)}, u32[]{:S(2)}, u32[]{:S(2)}) collective-permute-start(bf16[1,64,128]{2,1,0:T(8,128)(2,1)S(1)} %edges.1.refs_2_.own_edge_ref), channel_id=1, source_target_pairs={{0,28},{4,0},{8,4},{12,8},{16,12},{20,16},{24,20},{28,24},{1,29},{... | collective-permute-start | bytes 49160 | tf_op jit(solution)/shard_map/ppermute | solution.py:267
  26.6 0.0 collective-permute-done.8
  26.6 1.5 %collective-permute-start.13 = (bf16[1,64,128]{2,1,0:T(8,128)(2,1)S(1)}, bf16[1,64,128]{2,1,0:T(8,128)(2,1)S(1)}, u32[]{:S(2)}, u32[]{:S(2)}) collective-permute-start(bf16[1,64,128]{2,1,0:T(8,128)(2,1)S(1)} %edges.1.refs_2_.own_edge_ref), channel_id=1, source_target_pairs={{0,24},{4,28},{8,0},{12,4},{16,8},{20,12},{24,16},{28,20},{1,25},{... | collective-permute-start | bytes 49160 | tf_op jit(solution)/shard_map/ppermute | solution.py:267
  28.1 0.0 collective-permute-done.9
  28.1 0.6 %collective-permute-start.1 = (bf16[64,1024]{1,0:T(8,128)(2,1)S(1)}, bf16[64,1024]{1,0:T(8,128)(2,1)S(1)}, u32[]{:S(2)}, u32[]{:S(2)}) collective-permute-start(bf16[64,1024]{1,0:T(8,128)(2,1)S(1)} %fusion.1), channel_id=1, source_target_pairs={{0,8},{4,12},{8,0},{12,4},{16,24},{20,28},{24,16},{28,20},{1,9},{5... | collective-permute-start | bytes 393224 | tf_op jit(solution)/shard_map/ppermute | solution.py:271
  28.7 0.0 collective-permute-done.12
  28.7 1.0 %collective-permute-start.14 = (bf16[16,64,128]{2,1,0:T(8,128)(2,1)S(1)}, bf16[16,64,128]{2,1,0:T(8,128)(2,1)S(1)}, u32[]{:S(2)}, u32[]{:S(2)}) collective-permute-start(bf16[16,64,128]{2,1,0:T(8,128)(2,1)S(1)} %broadcast_select_fusion.1.refs_3_), channel_id=1, source_target_pairs={{0,4},{4,0},{8,12},{12,8},{16,20},{20,16},{24,28},{28,24},{1,5},{5... | collective-permute-start | bytes 786440 | tf_op jit(solution)/shard_map/ppermute | solution.py:271
  29.8 3.3 %collective-permute-done.1 = bf16[64,1024]{1,0:T(8,128)(2,1)S(1)} collective-permute-done((bf16[64,1024]{1,0:T(8,128)(2,1)S(1)}, bf16[64,1024]{1,0:T(8,128)(2,1)S(1)}, u32[]{:S(2)}, u32[]{:S(2)}) %collective-permute-start.1) | collective-permute-done | bytes 131104 | tf_op jit(solution)/shard_map/ppermute | solution.py:271
  33.1 0.7 %collective-permute-start.10 = (bf16[16,64,128]{2,1,0:T(8,128)(2,1)S(1)}, bf16[16,64,128]{2,1,0:T(8,128)(2,1)S(1)}, u32[]{:S(2)}, u32[]{:S(2)}) collective-permute-start(bf16[16,64,128]{2,1,0:T(8,128)(2,1)S(1)} %broadcast_select_fusion.refs_3_), channel_id=1, source_target_pairs={{0,4},{4,0},{8,12},{12,8},{16,20},{20,16},{24,28},{28,24},{1,5},{5... | collective-permute-start | bytes 786440 | tf_op jit(solution)/shard_map/ppermute | solution.py:271
  33.8 0.7 %fusion = (s32[1]{0:T(128)}, s32[1]{0:T(128)}, s32[1]{0:T(128)}, s32[1]{0:T(128)}) fusion(s32[4]{0:T(128)S(1)} %compare_select_fusion), kind=kLoop, calls=%fused_computation.8 | loop fusion | bytes 32 | tf_op jit(solution)/shard_map/slice | solution.py:375
  37.0 0.0 collective-permute-done.11
  37.0 1.9 %collective-permute-start.15 = (bf16[1,64,128]{2,1,0:T(8,128)(2,1)S(1)}, bf16[1,64,128]{2,1,0:T(8,128)(2,1)S(1)}, u32[]{:S(2)}, u32[]{:S(2)}) collective-permute-start(bf16[1,64,128]{2,1,0:T(8,128)(2,1)S(1)} %edges.1.refs_2_.own_edge_ref), channel_id=1, source_target_pairs={{0,16},{4,20},{8,24},{12,28},{16,0},{20,4},{24,8},{28,12},{1,17},{... | collective-permute-start | bytes 49160 | tf_op jit(solution)/shard_map/ppermute | solution.py:267
  38.9 0.0 collective-permute-done.13.refs_4_
  38.9 1.4 %collective-permute-start.2 = (bf16[64,1024]{1,0:T(8,128)(2,1)S(1)}, bf16[64,1024]{1,0:T(8,128)(2,1)S(1)}, u32[]{:S(2)}, u32[]{:S(2)}) collective-permute-start(bf16[64,1024]{1,0:T(8,128)(2,1)S(1)} %max.10), channel_id=1, source_target_pairs={{0,4},{4,0},{8,12},{12,8},{16,20},{20,16},{24,28},{28,24},{1,5},{5... | collective-permute-start | bytes 393224 | tf_op jit(solution)/shard_map/ppermute | solution.py:271
  40.3 0.0 copy-start.4
  40.3 1.5 %first.1 = (bf16[64,1024]{1,0:T(8,128)(2,1)S(1)}, f32[64,1024]{1,0:T(8,128)S(1)}) custom-call(s32[1]{0:T(128)} %get-tuple-element.17.refs_0_, bf16[16,64,128]{2,1,0:T(8,128)(2,1)S(1)} %get-tuple-element.9.refs_1_.own_ref, bf16[1,64,128]{2,1,0:T(8,128)(2,1)S(1)} %edges.1.refs_2_.own_edge_ref, bf16[16,64,128]{2,1,0:T(8,128)(2,1)S(1)} %broadcast_select_fusion.1.refs_3_, ...), custom_call_target="tpu_custom_call" | custom-call | tf_op jit(solution)/shard_map/first/pallas_call | solution.py:350
  41.8 0.0 copy-start
  41.8 0.0 copy-start.2
  41.8 2.0 %collective-permute-done.2 = bf16[64,1024]{1,0:T(8,128)(2,1)S(1)} collective-permute-done((bf16[64,1024]{1,0:T(8,128)(2,1)S(1)}, bf16[64,1024]{1,0:T(8,128)(2,1)S(1)}, u32[]{:S(2)}, u32[]{:S(2)}) %collective-permute-start.2) | collective-permute-done | bytes 131104 | tf_op jit(solution)/shard_map/ppermute | solution.py:271
  44.0 3.3 %surface.1 = f32[16,1024]{1,0:T(8,128)} custom-call(bf16[64,1024]{1,0:T(8,128)(2,1)S(1)} %get-tuple-element.8.own_ref, bf16[64,1024]{1,0:T(8,128)(2,1)S(1)} %max.11.ref_ref, bf16[128,192]{1,0:T(8,128)(2,1)S(1)} %copy-done.3, bf16[256,256]{1,0:T(8,128)(2,1)S(1)} %copy-done.2, bf16[64,256]{1,0:T(8,128)(2,1)S(1)} %copy-done.4, bf16[512,256]{1,0:T(8,128)(2,1)S(1)} %copy-done), custom_call_target="tpu_custom_call" | custom-call | tf_op jit(solution)/shard_map/surface/pallas_call | solution.py:336
  47.3 0.0 collective-permute-done.15.refs_4_
  47.3 1.3 %four.1.refs_2_ = bf16[64,1024]{1,0:T(8,128)(2,1)S(1)} custom-call(s32[1]{0:T(128)} %get-tuple-element.16.refs_0_, bf16[16,64,128]{2,1,0:T(8,128)(2,1)S(1)} %get-tuple-element.9.refs_1_.own_ref, bf16[1,64,128]{2,1,0:T(8,128)(2,1)S(1)} %edges.1.refs_2_.own_edge_ref, bf16[16,64,128]{2,1,0:T(8,128)(2,1)S(1)} %broadcast_select_fusion.refs_3_, ...), custom_call_target="tpu_custom_call" | custom-call | tf_op jit(solution)/shard_map/four/pallas_call | solution.py:350
  48.6 0.0 collective-permute-done.14.refs_3_
  48.6 0.7 %cross.1.refs_1_ = bf16[64,1024]{1,0:T(8,128)(2,1)S(1)} custom-call(s32[1]{0:T(128)S(6)} %select_n.81.refs_0_, bf16[16,64,128]{2,1,0:T(8,128)(2,1)S(1)} %get-tuple-element.9.refs_1_.own_ref, bf16[1,64,128]{2,1,0:T(8,128)(2,1)S(1)} %edges.1.refs_2_.own_edge_ref, bf16[16,64,128]{2,1,0:T(8,128)(2,1)S(1)} %collective-permute-done.14.refs_3_, ...), custom_call_target="tpu_custom_call" | custom-call | tf_op jit(solution)/shard_map/cross/pallas_call | solution.py:350
  49.3 0.0 collective-permute-done.5
  49.3 0.0 collective-permute-done.10
  49.3 1.5 %last.1 = bf16[4,64,1024]{2,1,0:T(8,128)(2,1)} custom-call(s32[1]{0:T(128)} %bitcast.5.odd_ref, s32[1]{0:T(128)S(6)} %select_n.72.flag_ref, bf16[16,64,128]{2,1,0:T(8,128)(2,1)S(1)} %get-tuple-element.9.refs_1_.own_ref, bf16[1,64,128]{2,1,0:T(8,128)(2,1)S(1)} %edges.1.refs_2_.own_edge_ref, bf16[16,64,128]{2,1,0:T(8,128)(2,1)S(1)} %broadcast_select_fusion.2.main_ref, ...), custom_call_target="tpu_custom_call" | custom-call | tf_op jit(solution)/shard_map/last/pallas_call | solution.py:350
  (18 shorter events, 0.2 us)
Async XLA Ops:
  0.6 0.7 %copy-start.5 = (s32[1,1,16]{2,1,0:T(1,128)S(1)}, s32[1,1,16]{2,1,0:T(1,128)}, u32[]{:S(2)}) copy-start(s32[1,1,16]{2,1,0:T(1,128)} %param.11) | copy-start | bytes 196
  0.6 0.7 %copy-start.6 = (f32[1,1,16]{2,1,0:T(1,128)S(1)}, f32[1,1,16]{2,1,0:T(1,128)}, u32[]{:S(2)}) copy-start(f32[1,1,16]{2,1,0:T(1,128)} %param.12) | copy-start | bytes 196
  1.3 0.9 %copy-start.1 = (bf16[1,2,64,1024]{3,2,1,0:T(8,128)(2,1)S(1)}, bf16[1,2,64,1024]{3,2,1,0:T(8,128)(2,1)}, u32[]{:S(2)}) copy-start(bf16[1,2,64,1024]{3,2,1,0:T(8,128)(2,1)} %param.9) | copy-start | bytes 786436
  3.2 9.8 %collective-permute-start.6 = (bf16[16,64,128]{2,1,0:T(8,128)(2,1)S(1)}, bf16[16,64,128]{2,1,0:T(8,128)(2,1)S(1)}, u32[]{:S(2)}, u32[]{:S(2)}) collective-permute-start(bf16[16,64,128]{2,1,0:T(8,128)(2,1)S(1)} %get-tuple-element.9.refs_1_.own_ref), channel_id=1, source_target_pairs={{0,8},{4,12},{8,0},{12,4},{16,24},{20,28},{24,16},{28,20},{1,9},{5... | collective-permute-start | bytes 786440 | tf_op jit(solution)/shard_map/ppermute | solution.py:271
  6.3 7.8 %collective-permute-start.7 = (bf16[16,64,128]{2,1,0:T(8,128)(2,1)S(1)}, bf16[16,64,128]{2,1,0:T(8,128)(2,1)S(1)}, u32[]{:S(2)}, u32[]{:S(2)}) collective-permute-start(bf16[16,64,128]{2,1,0:T(8,128)(2,1)S(1)} %get-tuple-element.9.refs_1_.own_ref), channel_id=1, source_target_pairs={{0,4},{4,0},{8,16},{12,20},{16,8},{20,12},{24,28},{28,24},{1,5},{5... | collective-permute-start | bytes 786440 | tf_op jit(solution)/shard_map/ppermute | solution.py:278
  8.5 15.1 %collective-permute-start = (bf16[64,1024]{1,0:T(8,128)(2,1)S(1)}, bf16[64,1024]{1,0:T(8,128)(2,1)S(1)}, u32[]{:S(2)}, u32[]{:S(2)}) collective-permute-start(bf16[64,1024]{1,0:T(8,128)(2,1)S(1)} %broadcast_select_fusion.3), channel_id=1, source_target_pairs={{0,16},{4,20},{8,24},{12,28},{16,0},{20,4},{24,8},{28,12},{1,17},{... | collective-permute-start | bytes 393224 | tf_op jit(solution)/shard_map/ppermute | solution.py:271
  9.6 11.5 %collective-permute-start.3 = (bf16[144,128]{1,0:T(8,128)(2,1)S(1)}, bf16[144,128]{1,0:T(8,128)(2,1)S(1)}, u32[]{:S(2)}, u32[]{:S(2)}) collective-permute-start(bf16[144,128]{1,0:T(8,128)(2,1)S(1)} %get-tuple-element.11.high_ref), channel_id=1, source_target_pairs={{0,1},{1,2},{2,3},{3,0},{4,5},{5,6},{6,7},{7,4},{8,9},{9,10},{10,1... | collective-permute-start | bytes 110600 | tf_op jit(solution)/shard_map/ppermute | solution.py:267
  9.6 12.0 %collective-permute-start.4 = (bf16[144,128]{1,0:T(8,128)(2,1)S(1)}, bf16[144,128]{1,0:T(8,128)(2,1)S(1)}, u32[]{:S(2)}, u32[]{:S(2)}) collective-permute-start(bf16[144,128]{1,0:T(8,128)(2,1)S(1)} %get-tuple-element.10.low_ref), channel_id=1, source_target_pairs={{0,3},{1,0},{2,1},{3,2},{4,7},{5,4},{6,5},{7,6},{8,11},{9,8},{10,9... | collective-permute-start | bytes 110600 | tf_op jit(solution)/shard_map/ppermute | solution.py:267
  11.4 0.7 %copy-start.7 = (s32[1,4]{1,0:T(1,128)S(1)}, s32[1,4]{1,0:T(1,128)}, u32[]{:S(2)}) copy-start(s32[1,4]{1,0:T(1,128)} %param.13) | copy-start | bytes 52
  14.1 12.5 %collective-permute-start.8 = (bf16[16,64,128]{2,1,0:T(8,128)(2,1)S(1)}, bf16[16,64,128]{2,1,0:T(8,128)(2,1)S(1)}, u32[]{:S(2)}, u32[]{:S(2)}) collective-permute-start(bf16[16,64,128]{2,1,0:T(8,128)(2,1)S(1)} %broadcast_select_fusion.1.refs_3_), channel_id=1, source_target_pairs={{0,8},{4,12},{8,0},{12,4},{16,24},{20,28},{24,16},{28,20},{1,9},{5... | collective-permute-start | bytes 786440 | tf_op jit(solution)/shard_map/ppermute | solution.py:271
  19.5 8.6 %collective-permute-start.9 = (bf16[16,64,128]{2,1,0:T(8,128)(2,1)S(1)}, bf16[16,64,128]{2,1,0:T(8,128)(2,1)S(1)}, u32[]{:S(2)}, u32[]{:S(2)}) collective-permute-start(bf16[16,64,128]{2,1,0:T(8,128)(2,1)S(1)} %broadcast_select_fusion.1.refs_3_), channel_id=1, source_target_pairs={{0,4},{4,0},{8,16},{12,20},{16,8},{20,12},{24,28},{28,24},{1,5},{5... | collective-permute-start | bytes 786440 | tf_op jit(solution)/shard_map/ppermute | solution.py:278
  21.1 28.1 %collective-permute-start.5 = (bf16[16,64,128]{2,1,0:T(8,128)(2,1)S(1)}, bf16[16,64,128]{2,1,0:T(8,128)(2,1)S(1)}, u32[]{:S(2)}, u32[]{:S(2)}) collective-permute-start(bf16[16,64,128]{2,1,0:T(8,128)(2,1)S(1)} %get-tuple-element.9.refs_1_.own_ref), channel_id=1, source_target_pairs={{0,4},{4,0},{8,12},{12,8},{16,20},{20,16},{24,28},{28,24},{1,5},{5... | collective-permute-start | bytes 786440 | tf_op jit(solution)/shard_map/ppermute | solution.py:271
  22.5 6.2 %collective-permute-start.12 = (bf16[1,64,128]{2,1,0:T(8,128)(2,1)S(1)}, bf16[1,64,128]{2,1,0:T(8,128)(2,1)S(1)}, u32[]{:S(2)}, u32[]{:S(2)}) collective-permute-start(bf16[1,64,128]{2,1,0:T(8,128)(2,1)S(1)} %edges.1.refs_2_.own_edge_ref), channel_id=1, source_target_pairs={{0,20},{4,24},{8,28},{12,0},{16,4},{20,8},{24,12},{28,16},{1,21},{... | collective-permute-start | bytes 49160 | tf_op jit(solution)/shard_map/ppermute | solution.py:267
  23.6 13.4 %collective-permute-start.11 = (bf16[1,64,128]{2,1,0:T(8,128)(2,1)S(1)}, bf16[1,64,128]{2,1,0:T(8,128)(2,1)S(1)}, u32[]{:S(2)}, u32[]{:S(2)}) collective-permute-start(bf16[1,64,128]{2,1,0:T(8,128)(2,1)S(1)} %edges.1.refs_2_.own_edge_ref), channel_id=1, source_target_pairs={{0,28},{4,0},{8,4},{12,8},{16,12},{20,16},{24,20},{28,24},{1,29},{... | collective-permute-start | bytes 49160 | tf_op jit(solution)/shard_map/ppermute | solution.py:267
  26.6 12.3 %collective-permute-start.13 = (bf16[1,64,128]{2,1,0:T(8,128)(2,1)S(1)}, bf16[1,64,128]{2,1,0:T(8,128)(2,1)S(1)}, u32[]{:S(2)}, u32[]{:S(2)}) collective-permute-start(bf16[1,64,128]{2,1,0:T(8,128)(2,1)S(1)} %edges.1.refs_2_.own_edge_ref), channel_id=1, source_target_pairs={{0,24},{4,28},{8,0},{12,4},{16,8},{20,12},{24,16},{28,20},{1,25},{... | collective-permute-start | bytes 49160 | tf_op jit(solution)/shard_map/ppermute | solution.py:267
  28.1 5.0 %collective-permute-start.1 = (bf16[64,1024]{1,0:T(8,128)(2,1)S(1)}, bf16[64,1024]{1,0:T(8,128)(2,1)S(1)}, u32[]{:S(2)}, u32[]{:S(2)}) collective-permute-start(bf16[64,1024]{1,0:T(8,128)(2,1)S(1)} %fusion.1), channel_id=1, source_target_pairs={{0,8},{4,12},{8,0},{12,4},{16,24},{20,28},{24,16},{28,20},{1,9},{5... | collective-permute-start | bytes 393224 | tf_op jit(solution)/shard_map/ppermute | solution.py:271
  28.7 19.8 %collective-permute-start.14 = (bf16[16,64,128]{2,1,0:T(8,128)(2,1)S(1)}, bf16[16,64,128]{2,1,0:T(8,128)(2,1)S(1)}, u32[]{:S(2)}, u32[]{:S(2)}) collective-permute-start(bf16[16,64,128]{2,1,0:T(8,128)(2,1)S(1)} %broadcast_select_fusion.1.refs_3_), channel_id=1, source_target_pairs={{0,4},{4,0},{8,12},{12,8},{16,20},{20,16},{24,28},{28,24},{1,5},{5... | collective-permute-start | bytes 786440 | tf_op jit(solution)/shard_map/ppermute | solution.py:271
  33.1 16.2 %collective-permute-start.10 = (bf16[16,64,128]{2,1,0:T(8,128)(2,1)S(1)}, bf16[16,64,128]{2,1,0:T(8,128)(2,1)S(1)}, u32[]{:S(2)}, u32[]{:S(2)}) collective-permute-start(bf16[16,64,128]{2,1,0:T(8,128)(2,1)S(1)} %broadcast_select_fusion.refs_3_), channel_id=1, source_target_pairs={{0,4},{4,0},{8,12},{12,8},{16,20},{20,16},{24,28},{28,24},{1,5},{5... | collective-permute-start | bytes 786440 | tf_op jit(solution)/shard_map/ppermute | solution.py:271
  37.0 10.2 %collective-permute-start.15 = (bf16[1,64,128]{2,1,0:T(8,128)(2,1)S(1)}, bf16[1,64,128]{2,1,0:T(8,128)(2,1)S(1)}, u32[]{:S(2)}, u32[]{:S(2)}) collective-permute-start(bf16[1,64,128]{2,1,0:T(8,128)(2,1)S(1)} %edges.1.refs_2_.own_edge_ref), channel_id=1, source_target_pairs={{0,16},{4,20},{8,24},{12,28},{16,0},{20,4},{24,8},{28,12},{1,17},{... | collective-permute-start | bytes 49160 | tf_op jit(solution)/shard_map/ppermute | solution.py:267
  38.9 5.0 %collective-permute-start.2 = (bf16[64,1024]{1,0:T(8,128)(2,1)S(1)}, bf16[64,1024]{1,0:T(8,128)(2,1)S(1)}, u32[]{:S(2)}, u32[]{:S(2)}) collective-permute-start(bf16[64,1024]{1,0:T(8,128)(2,1)S(1)} %max.10), channel_id=1, source_target_pairs={{0,4},{4,0},{8,12},{12,8},{16,20},{20,16},{24,28},{28,24},{1,5},{5... | collective-permute-start | bytes 393224 | tf_op jit(solution)/shard_map/ppermute | solution.py:271
  40.3 3.6 %copy-start.3 = (bf16[128,192]{1,0:T(8,128)(2,1)S(1)}, bf16[128,192]{1,0:T(8,128)(2,1)}, u32[]{:S(2)}) copy-start(bf16[128,192]{1,0:T(8,128)(2,1)} %constant.49.clone.first_ref) | copy-start | bytes 147460
  40.3 3.6 %copy-start.4 = (bf16[64,256]{1,0:T(8,128)(2,1)S(1)}, bf16[64,256]{1,0:T(8,128)(2,1)}, u32[]{:S(2)}) copy-start(bf16[64,256]{1,0:T(8,128)(2,1)} %constant.51.clone.third_ref) | copy-start | bytes 98308
  41.8 2.1 %copy-start = (bf16[512,256]{1,0:T(8,128)(2,1)S(1)}, bf16[512,256]{1,0:T(8,128)(2,1)}, u32[]{:S(2)}) copy-start(bf16[512,256]{1,0:T(8,128)(2,1)} %constant.52.clone.fourth_ref) | copy-start | bytes 786436
  41.8 2.1 %copy-start.2 = (bf16[256,256]{1,0:T(8,128)(2,1)S(1)}, bf16[256,256]{1,0:T(8,128)(2,1)}, u32[]{:S(2)}) copy-start(bf16[256,256]{1,0:T(8,128)(2,1)} %constant.50.clone.second_ref) | copy-start | bytes 393220

commit v2 on v0

v2 whole, which is shorter than its diff:
```python
import functools

import jax
import jax.numpy as jnp
import numpy as np
from jax import lax
from jax.experimental import pallas as pl
from jax.experimental.pallas import tpu as pltpu
from jax.sharding import PartitionSpec as P

BLK = 64
OVS = 2
LAGS = 32
SPAN = 4
BOXA = 5
BOXR = 19
TAPS = 8
LANES = 128
PAD = 16
EDGE = 32
HROWS = 16
F32 = jnp.float32
BF16 = jnp.bfloat16
HIGHEST = lax.Precision.HIGHEST
VMEM = pl.BlockSpec(memory_space=pltpu.VMEM)
SMEM = pl.BlockSpec(memory_space=pltpu.SMEM)
PARAMS = pltpu.CompilerParams(vmem_limit_bytes=8 << 20)


def dot(a, b):
    return jnp.dot(a, b, preferred_element_type=F32)


def iota(shape, dim):
    return lax.broadcasted_iota(jnp.int32, shape, dim)


def band(table):
    top = 96
    rows = 2 * LANES - top
    step = iota((rows, LANES), 0) + top - iota((rows, LANES), 1) - (LANES - PAD - 3)
    step = step.astype(F32) - table[TAPS : TAPS + 1, :]
    out = jnp.zeros((rows, LANES), F32)
    for tap in range(TAPS):
        out = jnp.where(step == float(tap), table[tap : tap + 1, :], out)
    return jnp.concatenate([jnp.zeros((top, LANES), BF16), out.astype(BF16)], axis=0)


def amplitude(real, imag):
    real, imag = real.astype(F32), imag.astype(F32)
    return jnp.sqrt(real * real + imag * imag + 1e-06).astype(BF16)


EVEN, LEFT, RIGHT, PICK = 4, 5, 6, 8


def prep_kernel(
    own_hbm, off_hbm, frac_hbm, ref_hbm, partners_hbm, own_ref, cond_ref, taps_ref, low_ref, high_ref, *scratch
):
    off_ref, frac_ref, ref_ref, partners_ref, sems = scratch
    sources = (own_hbm, off_hbm, frac_hbm, ref_hbm, partners_hbm)
    targets = (own_ref, off_ref, frac_ref, ref_ref, partners_ref)
    copies = [pltpu.make_async_copy(s, t, sems.at[k]) for k, (s, t) in enumerate(zip(sources, targets))]
    for copy in copies:
        copy.start()
    for copy in copies[1:]:
        copy.wait()
    rows, cols = own_ref.shape[0] // 2, own_ref.shape[1]
    blocks = cols // BLK
    date, dates = lax.axis_index("date"), lax.axis_size("date")
    place, places = lax.axis_index("rng"), lax.axis_size("rng")
    values = [jnp.where(date + 1 + h < dates, partners_ref[0, h], 0) for h in range(SPAN)]
    values += [1 - date % 2, (place > 0).astype(jnp.int32), (place < places - 1).astype(jnp.int32), jnp.int32(0)]
    beside = date + 1 - 2 * (date % 2)
    held = [date, beside, date + 2, beside + 2, date + 4, beside + 4]
    found = [(lax.rem(h, dates) == ref_ref[0]).astype(jnp.int32) for h in held]
    values += found
    row = iota(cond_ref.shape, 0)
    cond = jnp.zeros(cond_ref.shape, jnp.int32)
    for k, value in enumerate(values):
        cond = jnp.where(row == k, value, cond)
    cond_ref[...] = cond.astype(F32)
    dist = iota((TAPS, blocks), 0).astype(F32) - 3.0 - frac_ref[...]
    arg = jnp.pi * dist
    sinc = jnp.where(arg == 0.0, 1.0, jnp.sin(arg) / jnp.where(arg == 0.0, 1.0, arg))
    weights = sinc * (0.5 + 0.5 * jnp.cos(arg / 4.0))
    shifts = jnp.broadcast_to(off_ref[...].astype(F32), (TAPS, blocks))
    small = jnp.concatenate([weights, shifts], axis=0).astype(BF16)
    block, lane = iota((blocks, LANES), 0), iota((blocks, LANES), 1)
    taps_ref[...] = dot(small, (lane == block + 1).astype(BF16)).astype(BF16)
    low_ref[2 * rows :, :] = dot(small, (block == 0).astype(BF16)).astype(BF16)
    high_ref[2 * rows :, :] = dot(small, (block == blocks - 1).astype(BF16)).astype(BF16)
    copies[0].wait()
    low_ref[0 : 2 * rows, :] = own_ref[:, 0:LANES]
    high_ref[0 : 2 * rows, :] = own_ref[:, cols - LANES :]


def join_kernel(cond_ref, own_ref, beside_ref, halo_ref, two_ref, two_halo_ref, amp_ref, both_ref, all_ref):
    rows = amp_ref.shape[0]
    mine, other = cond_ref[PICK : PICK + 1, 0:1] > 0.0, cond_ref[PICK + 1 : PICK + 2, 0:1] > 0.0
    value = jnp.where(other, beside_ref[...].astype(F32), own_ref[...].astype(F32))
    value = amplitude(value[0:rows], value[rows:])
    amp_ref[...] = jnp.where(mine | other, value.astype(F32), 0.0).astype(BF16)
    width = two_halo_ref.shape[1]
    for ref in (both_ref, all_ref):
        ref[0 : 2 * rows, :] = two_ref[...]
        ref[2 * rows : 2 * rows + HROWS, 0:width] = two_halo_ref[...]
        ref[2 * rows : 2 * rows + HROWS, width:] = jnp.zeros((HROWS, ref.shape[1] - width), BF16)
    all_ref[2 * rows + HROWS :, 0:width] = halo_ref[...]
    all_ref[2 * rows + HROWS :, width:] = jnp.zeros((HROWS, all_ref.shape[1] - width), BF16)


def halo_kernel(blocks, cond_ref, taps_ref, left_ref, right_ref, out_ref):
    left = jnp.where(cond_ref[LEFT : LEFT + 1, :] > 0.0, left_ref[...].astype(F32), 0.0)
    right = jnp.where(cond_ref[RIGHT : RIGHT + 1, :] > 0.0, right_ref[...].astype(F32), 0.0)
    rows = (left.shape[0] - HROWS) // 2
    lane = iota((2 * rows, LANES), 1)
    both = jnp.where(lane < EDGE, pltpu.roll(left[0 : 2 * rows], EDGE, 1), pltpu.roll(right[0 : 2 * rows], EDGE, 1))
    both = jnp.where(lane < 2 * EDGE, both, 0.0)
    both = (both[0:rows] + pltpu.roll(both[rows:], 2 * EDGE, 1)).astype(BF16)
    groups = rows // HROWS
    for k in range(groups):
        out_ref[:, k * LANES : (k + 1) * LANES] = both[k * HROWS : (k + 1) * HROWS]
    lane = iota((HROWS, LANES), 1)
    taps = jnp.where(lane == 0, left[2 * rows :], taps_ref[...].astype(F32))
    out_ref[:, groups * LANES : (groups + 1) * LANES] = jnp.where(
        lane == blocks + 1, right[2 * rows :], taps
    ).astype(BF16)


def resample(main_ref, halo_ref, use):
    rows, cols = main_ref.shape[0] // 2, main_ref.shape[1]
    tiles = cols // LANES
    groups = rows // HROWS
    edge = jnp.concatenate([halo_ref[:, k * LANES : (k + 1) * LANES] for k in range(groups)], axis=0).astype(F32)
    edge = [pltpu.roll(edge, LANES - EDGE, 1), pltpu.roll(edge, EDGE, 1)]
    edge = jnp.concatenate(edge, axis=0).astype(BF16)
    shape = (LANES, cols + LANES)
    place = ((iota(shape, 1) - PAD) >> 6) + 1 == iota(shape, 0)
    table = dot(halo_ref[:, groups * LANES : (groups + 1) * LANES], place.astype(BF16))
    for p in range(tiles + 1):
        if p == 0:
            window = jnp.concatenate([edge, main_ref[:, 0:LANES]], axis=1)
        elif p == tiles:
            window = jnp.concatenate([main_ref[:, cols - LANES :], edge], axis=1)
        else:
            window = main_ref[:, (p - 1) * LANES : (p + 1) * LANES]
        out = dot(window, band(table[:, p * LANES : (p + 1) * LANES])).astype(BF16)
        use(p, out[0:rows], out[rows:])


def range_box():
    gap = iota((2 * LANES, LANES), 0) - iota((2 * LANES, LANES), 1) - PAD
    return (jnp.abs(gap) <= BOXR // 2).astype(BF16)


def line_box(field):
    rows, lanes = field.shape
    base = jnp.concatenate([field, jnp.zeros((8, lanes), F32)], axis=0)
    two = base + pltpu.roll(base, 1, 0)
    four = two + pltpu.roll(two, 2, 0)
    five = four + pltpu.roll(base, 4, 0)
    return pltpu.roll(five, rows + 8 - BOXA // 2, 0)[0:rows]


def own_kernel(main_ref, halo_ref, ext_ref, power_ref, fields_ref):
    rows, cols = power_ref.shape

    def use(p, real, imag):
        lanes = slice(p * LANES, (p + 1) * LANES)
        ext_ref[0:rows, lanes] = real
        ext_ref[rows:, lanes] = imag
        real, imag = real.astype(F32), imag.astype(F32)
        fields_ref[:, lanes] = (real * real + imag * imag).astype(BF16)

    resample(main_ref, halo_ref, use)
    box = range_box()
    for p in range(cols // LANES):
        lanes = slice(p * LANES, (p + 1) * LANES)
        power_ref[:, lanes] = line_box(dot(fields_ref[:, p * LANES : (p + 2) * LANES], box))


def pair(flag, ext_ref, power_ref, main_ref, halo_ref, out_ref, fields_ref):
    rows, cols = out_ref.shape

    def use(p, real, imag):
        lanes = slice(p * LANES, (p + 1) * LANES)
        own_r, own_i = ext_ref[0:rows, lanes].astype(F32), ext_ref[rows:, lanes].astype(F32)
        r, i = real.astype(F32), imag.astype(F32)
        fields_ref[0:rows, lanes] = (own_r * r + own_i * i).astype(BF16)
        fields_ref[rows : 2 * rows, lanes] = (own_i * r - own_r * i).astype(BF16)
        fields_ref[2 * rows :, lanes] = (r * r + i * i).astype(BF16)

    resample(main_ref, halo_ref, use)
    box = range_box()
    for p in range(cols // LANES):
        lanes = slice(p * LANES, (p + 1) * LANES)
        sums = dot(fields_ref[:, p * LANES : (p + 2) * LANES], box)
        re = line_box(sums[0:rows])
        im = line_box(sums[rows : 2 * rows])
        partner = line_box(sums[2 * rows :])
        value = flag * (re * re + im * im) / (power_ref[:, lanes] * partner + 1e-06)
        out_ref[:, lanes] = value.astype(BF16)


def two_kernel(cond_ref, ext_ref, power_ref, main_ref, halo_ref, out_ref, fields_ref):
    pair(cond_ref[1:2, :], ext_ref, power_ref, main_ref, halo_ref, out_ref, fields_ref)


def joined(ref, rows):
    return ref.at[0 : 2 * rows], ref.at[2 * rows : 2 * rows + HROWS]


def four_kernel(cond_ref, ext_ref, power_ref, both_ref, out_ref, fields_ref):
    pair(cond_ref[3:4, :], ext_ref, power_ref, *joined(both_ref, out_ref.shape[0]), out_ref, fields_ref)


def cross_kernel(cond_ref, ext_ref, power_ref, both_ref, out_ref, fields_ref):
    flag = jnp.where(cond_ref[EVEN : EVEN + 1, :] > 0.0, cond_ref[2:3, :], cond_ref[0:1, :])
    pair(flag, ext_ref, power_ref, *joined(both_ref, out_ref.shape[0]), out_ref, fields_ref)


def split(table):
    high = table.astype(BF16)
    return high, (table - high.astype(np.float32)).astype(BF16)


def twice(table):
    zero = np.zeros_like(table)
    return np.block([[table, zero], [zero, table]])


def surface_tables():
    index = np.arange(BLK)
    angle = 2.0 * np.pi / BLK * (index[:, None] * index[None, :] % BLK)
    cosine, sine = np.cos(angle).astype(np.float32), np.sin(angle).astype(np.float32)
    signed = np.where(index < BLK // 2, index, index - BLK)
    upsampled = OVS * BLK
    lag_phase = (np.arange(LAGS) - LAGS // 2)[:, None] * signed[None, :] % upsampled
    lag_angle = 2.0 * np.pi / upsampled * lag_phase
    lag_cos, lag_sin = np.cos(lag_angle).astype(np.float32), np.sin(lag_angle).astype(np.float32)
    high, low = split(np.concatenate([cosine, -sine], axis=0))
    first = np.concatenate([high, low, high], axis=1)
    second = np.concatenate(split(np.concatenate([twice(cosine), twice(sine)], axis=1)), axis=0)
    per = LANES // LAGS
    order = np.arange(LAGS).reshape(LAGS // per, per).T.reshape(-1)
    left = np.block([[lag_cos[order], -lag_sin[order]], [lag_sin[order], lag_cos[order]]])
    third = np.concatenate(split(left), axis=1)
    spread = [twice(np.tile(table.T, (1, per))) for table in (lag_cos, -lag_sin)]
    fourth = np.concatenate(split(np.concatenate(spread, axis=0)), axis=0)
    return first, second, third, fourth


def spectrum(amp_ref, rows_ref, first_ref, second_ref, use):
    size, cols = amp_ref.shape
    tiles = cols // LANES
    group = (iota((LANES, LANES), 0) >> 6 == iota((LANES, LANES), 1) >> 6).astype(F32)
    values = [amp_ref[:, p * LANES : (p + 1) * LANES].astype(F32) for p in range(tiles)]
    for p, value in enumerate(values):
        rows_ref[p : p + 1, :] = jnp.sum(value, axis=0, keepdims=True)
    mean = jnp.dot(rows_ref[...], group, precision=HIGHEST) / (BLK * BLK)
    for p, value in enumerate(values):
        value = value - mean[p : p + 1, :]
        rows_ref[p : p + 1, :] = jnp.sum(value * value, axis=0, keepdims=True)
        high = value.astype(BF16)
        low = (value - high.astype(F32)).astype(BF16)
        f = dot(first_ref[...], jnp.concatenate([high, high, low], axis=0)).astype(BF16)
        s = dot(jnp.concatenate([f, f], axis=1), second_ref[...])
        use(p, s[0:size, 0:LANES] + s[size:, LANES:], s[size:, 0:LANES] - s[0:size, LANES:])
    return jnp.dot(rows_ref[...], group, precision=HIGHEST)


def spectrum_kernel(own_ref, first_ref, second_ref, spec_ref, energy_ref, amp_ref, rows_ref):
    size = amp_ref.shape[0]
    amp_ref[...] = amplitude(own_ref[0:size, :], own_ref[size:, :])

    def use(p, real, imag):
        lanes = slice(p * LANES, (p + 1) * LANES)
        spec_ref[0:size, lanes] = real
        spec_ref[size:, lanes] = imag

    energy_ref[...] = spectrum(amp_ref, rows_ref, first_ref, second_ref, use)


def last_kernel(
    cond_ref,
    ext_ref,
    power_ref,
    last_ref,
    last_halo_ref,
    coh_two_ref,
    coh_cross_ref,
    coh_four_ref,
    *refs,
):
    samples, before_ref, refs = refs[0:6], refs[6], refs[7:]
    spec_ref, energy_ref, first_ref, second_ref, third_ref, fourth_ref, coh_hbm, surface_hbm = refs[0:8]
    tail_ref, fields_ref, amp_ref, rows_ref, cross_ref, out_scr, out_ref, sems = refs[8:]
    odd = lax.axis_index("date") % 2
    copies = [
        pltpu.make_async_copy(coh_two_ref, coh_hbm.at[1], sems.at[0]),
        pltpu.make_async_copy(coh_four_ref, coh_hbm.at[3], sems.at[1]),
        pltpu.make_async_copy(coh_cross_ref, coh_hbm.at[2 - 2 * odd], sems.at[2]),
        pltpu.make_async_copy(tail_ref, coh_hbm.at[2 * odd], sems.at[3]),
        pltpu.make_async_copy(out_ref, surface_hbm, sems.at[4]),
    ]
    for copy in copies[0:3]:
        copy.start()
    flag = jnp.where(cond_ref[EVEN : EVEN + 1, :] > 0.0, cond_ref[0:1, :], cond_ref[2:3, :])
    pair(flag, ext_ref, power_ref, last_ref, last_halo_ref, tail_ref, fields_ref)
    copies[3].start()
    size, cols = amp_ref.shape
    tiles = cols // LANES
    picks = [cond_ref[PICK + k : PICK + k + 1, 0:1] > 0.0 for k in range(len(samples))]
    value = samples[0][...].astype(F32)
    for pick, ref in zip(picks[1:], samples[1:]):
        value = jnp.where(pick, ref[0 : 2 * size, :].astype(F32), value)
    found = functools.reduce(jnp.logical_or, picks)
    value = amplitude(value[0:size], value[size:]).astype(F32)
    amp_ref[...] = jnp.where(found, value, before_ref[...].astype(F32)).astype(BF16)

    def use(p, ref_r, ref_i):
        lanes = slice(p * LANES, (p + 1) * LANES)
        own_r, own_i = spec_ref[0:size, lanes], spec_ref[size:, lanes]
        cross_ref[0:size, lanes] = own_r * ref_r + own_i * ref_i
        cross_ref[size:, lanes] = own_i * ref_r - own_r * ref_i

    energy = spectrum(amp_ref, rows_ref, first_ref, second_ref, use)
    scale = 1.0 / (BLK * jnp.sqrt(energy_ref[...] * energy + 1e-06))
    lag_rows = [[] for _ in range(LANES // LAGS)]
    for p in range(tiles):
        cross = (cross_ref[:, p * LANES : (p + 1) * LANES] * scale[p : p + 1, :]).astype(BF16)
        lags = dot(third_ref[...], jnp.concatenate([cross, cross], axis=0))
        for q in range(LANES // LAGS):
            part = [lags[ri * LAGS + q * 8 : ri * LAGS + q * 8 + 8] for ri in range(2)]
            lag_rows[q].append(jnp.concatenate(part, axis=1))
    lhs = jnp.concatenate([row for rows in lag_rows for row in rows], axis=0).astype(BF16)
    result = dot(jnp.concatenate([lhs, lhs], axis=1), fourth_ref[...])
    height = 8 * tiles
    quarter = iota((height, 2 * LANES), 1) % LANES // LAGS
    total = result[0:height]
    for q in range(1, LANES // LAGS):
        total = jnp.where(quarter == q, result[q * height : (q + 1) * height], total)
    for p in range(tiles):
        for jj in range(2):
            at = (2 * p + jj) * 8
            out_scr[at : at + 8, :] = total[p * 8 : p * 8 + 8, jj * LANES : (jj + 1) * LANES]
    for a in range(8):
        out_ref[:, a * LANES : (a + 1) * LANES] = out_scr[pl.ds(a, 2 * tiles, stride=8), :]
    copies[4].start()
    for copy in copies:
        copy.wait()


def shifted(value, axis, steps):
    count = lax.axis_size(axis)
    return lax.ppermute(value, axis, [(s, (s - steps) % count) for s in range(count)])


def swapped(value, axis, step):
    return lax.ppermute(value, axis, [(s, s ^ step) for s in range(lax.axis_size(axis))])


def spread(value, axis):
    count = lax.axis_size(axis)
    step = 2
    while step < count:
        value = jnp.maximum(value, swapped(value, axis, step))
        step *= 2
    return value


def call(kernel, name, out_shape, operands, scratch=()):
    return pl.pallas_call(
        kernel,
        out_shape=out_shape,
        in_specs=[VMEM] * len(operands),
        out_specs=jax.tree.map(lambda _: VMEM, out_shape),
        scratch_shapes=[pltpu.VMEM(*s) for s in scratch],
        compiler_params=PARAMS,
        name=name,
    )(*operands)


def body(slc, ref_date, int_offset, frac_offset, partners):
    sds = jax.ShapeDtypeStruct
    _, _, rows, cols = slc.shape
    tiles = cols // LANES
    dates = lax.axis_size("date")
    even = lax.axis_index("date") % 2 == 0
    field, samples = sds((rows, cols), BF16), sds((2 * rows, cols), BF16)
    payload = sds((2 * rows + HROWS, LANES), BF16)
    own, cond, taps, low, high = pl.pallas_call(
        prep_kernel,
        out_shape=(samples, sds((16, LANES), F32), sds((HROWS, LANES), BF16), payload, payload),
        in_specs=[pl.BlockSpec(memory_space=pl.ANY)] * 5,
        out_specs=(VMEM,) * 5,
        scratch_shapes=[
            pltpu.VMEM(int_offset.shape[1:], jnp.int32),
            pltpu.VMEM(frac_offset.shape[1:], F32),
            pltpu.SMEM(ref_date.shape, jnp.int32),
            pltpu.SMEM(partners.shape, jnp.int32),
            pltpu.SemaphoreType.DMA((5,)),
        ],
        compiler_params=PARAMS,
        name="prepare",
    )(slc.reshape(2 * rows, cols), int_offset[0], frac_offset[0], ref_date, partners)
    beside = swapped(own, "date", 1)
    two = shifted(own, "date", 2)
    right = shifted(low, "rng", 1)
    left = shifted(high, "rng", -1)
    width = (rows // HROWS + 1) * LANES
    halo = call(
        functools.partial(halo_kernel, cols // BLK), "halo", sds((HROWS, width), BF16), (cond, taps, left, right)
    )
    two_halo = shifted(halo, "date", 2)
    pair_amp, both, everything = call(
        join_kernel,
        "join",
        (field, sds((2 * rows + HROWS, cols), BF16), sds((2 * rows + 2 * HROWS, cols), BF16)),
        (cond, own, beside, halo, two, two_halo),
    )
    cross = swapped(everything, "date", 1)
    four = shifted(both, "date", 2)
    before = shifted(pair_amp, "date", -2) if dates == 8 else spread(pair_amp, "date")
    across = lax.ppermute(both, "date", [(s, (s - 2) % dates ^ 1) for s in range(dates)])
    first, second, third, fourth = [jnp.asarray(t) for t in surface_tables()]
    spec, energy = call(
        spectrum_kernel,
        "spectrum",
        (sds((2 * rows, cols), F32), sds((tiles, LANES), F32)),
        (own, first, second),
        [((rows, cols), BF16), ((tiles, LANES), F32)],
    )
    fields = ((3 * rows, cols + LANES), BF16)
    ext, power = call(
        own_kernel,
        "own",
        (sds((2 * rows, cols + LANES), BF16), sds((rows, cols), F32)),
        (own, halo),
        [((rows, cols + LANES), BF16)],
    )
    coh_two = call(two_kernel, "two", field, (cond, ext, power, two, two_halo), [fields])
    coh_cross = call(cross_kernel, "cross", field, (cond, ext, power, cross), [fields])
    coh_four = call(four_kernel, "four", field, (cond, ext, power, four), [fields])
    last = jnp.where(even, beside, across[0 : 2 * rows])
    last_halo = jnp.where(even, cross[2 * rows + HROWS :], across[2 * rows :])
    operands = (
        *(cond, ext, power, last, last_halo, coh_two, coh_cross, coh_four),
        *(own, beside, two, cross, four, across, before),
        *(spec, energy, first, second, third, fourth),
    )
    lags = (cols // BLK, LAGS * LAGS)
    coherence, surface = pl.pallas_call(
        last_kernel,
        out_shape=(sds((SPAN, rows, cols), BF16), sds(lags, F32)),
        in_specs=[VMEM] * len(operands),
        out_specs=(pl.BlockSpec(memory_space=pl.ANY),) * 2,
        scratch_shapes=[
            pltpu.VMEM((rows, cols), BF16),
            pltpu.VMEM(*fields),
            pltpu.VMEM((rows, cols), BF16),
            pltpu.VMEM((tiles, LANES), F32),
            pltpu.VMEM((2 * rows, cols), F32),
            pltpu.VMEM((8 * cols // BLK, LANES), F32),
            pltpu.VMEM(lags, F32),
            pltpu.SemaphoreType.DMA((5,)),
        ],
        compiler_params=PARAMS,
        name="last",
    )(*operands)
    return (surface[None, None], coherence[None])


def solution(mesh):
    in_specs = (
        P("date", None, None, "rng"),
        P(),
        P("date", None, "rng"),
        P("date", None, "rng"),
        P("date", None),
    )
    out_specs = (P("date", None, "rng", None), P("date", None, None, "rng"))
    return jax.shard_map(body, mesh=mesh, in_specs=in_specs, out_specs=out_specs, check_vma=False)
```

time: 68 us -> 42.7 us (0.63)
  the two profiles are of different devices: /device:TPU:26 before, /device:TPU:0 now
where the time goes in v2:
time: 42.7 us; the launch traced here: 42.4 us
  starting transfers between devices  14.7 us (34%)
  waiting for transfers between devices  13 us (30%)
  Pallas kernels  11 us (26%)
  local copies, waits for them, and re-layouts  2.34 us (5%)
  between operations  1.4 us (3%)
    ppermute x6, starting transfers between devices, shifted(): lax.ppermute(value, axis, [(s, (s - steps) % count) for s in range(count)])  11.6 us
    pallas_call x7, Pallas kernels, call(): pl.pallas_call(kernel, out_shape=out_shape, in_specs=[VMEM] * len(operand...  6.51 us
    ppermute x6, waiting for transfers between devices, shifted(): lax.ppermute(value, axis, [(s, (s - steps) % count) for s in range(count)])  5.58 us
    ppermute x1, waiting for transfers between devices, body(): lax.ppermute(both, 'date', [(s, (s - 2) % dates ^ 1) for s in range(dates)])  4.85 us
    pallas_call x1, Pallas kernels, body(): pl.pallas_call(last_kernel, out_shape=(sds((SPAN, rows, cols), BF16), sds...  3.65 us
    ppermute x2, starting transfers between devices, swapped(): lax.ppermute(value, axis, [(s, s ^ step) for s in range(lax.axis_size(axi...  3.04 us
    ppermute x2, waiting for transfers between devices, swapped(): lax.ppermute(value, axis, [(s, s ^ step) for s in range(lax.axis_size(axi...  2.6 us
    unnamed x16, local copies, waits for them, and re-layouts  2.34 us
  transfers between devices with their start and end apart: 9, of which 5 were waited for; matrix products, arithmetic and copies ran while one was open for 0% of the time, Pallas kernels for 15%

profile of v2, /device:TPU:0, one launch (start us, length us, event | category | flops | bytes accessed | tf_op | source)
XLA Modules:
  0.0 42.4 jit_solution(13960439991211225510)
XLA Ops:
  1.3 0.0 copy-start.5
  1.3 0.0 copy-start.6
  1.3 0.0 copy-start.7
  1.3 0.6 %copy-done.5 = s32[1,1,16]{2,1,0:T(1,128)S(1)} copy-done((s32[1,1,16]{2,1,0:T(1,128)S(1)}, s32[1,1,16]{2,1,0:T(1,128)}, u32[]{:S(2)}) %copy-start.5) | copy-done | bytes 88
  1.9 0.0 copy-done.6
  1.9 0.0 copy-done.7
  2.0 0.0 copy-start.3
  2.0 0.9 %copy-done.3 = bf16[1,2,64,1024]{3,2,1,0:T(8,128)(2,1)S(1)} copy-done((bf16[1,2,64,1024]{3,2,1,0:T(8,128)(2,1)S(1)}, bf16[1,2,64,1024]{3,2,1,0:T(8,128)(2,1)}, u32[]{:S(2)}) %copy-start.3) | copy-done | bytes 262168
  2.9 0.8 %prepare.1 = (bf16[128,1024]{1,0:T(8,128)(2,1)S(1)}, f32[16,128]{1,0:T(8,128)S(1)}, bf16[16,128]{1,0:T(8,128)(2,1)S(1)}, bf16[144,128]{1,0:T(8,128)(2,1)S(1)}, bf16[144,128]{1,0:T(8,128)(2,1)S(1)}) custom-call(bf16[128,1024]{1,0:T(8,128)(2,1)S(1)} %bitcast.5, s32[1,16]{1,0:T(1,128)S(1)} %bitcast.6, f32[1,16]{1,0:T(1,128)S(1)} %bitcast.7, ...), custom_call_target="tpu_custom_call" | custom-call | tf_op jit(solution)/shard_map/prepare/pallas_call | solution.py:393
  3.7 5.1 %collective-permute-start.3 = (bf16[128,1024]{1,0:T(8,128)(2,1)S(1)}, bf16[128,1024]{1,0:T(8,128)(2,1)S(1)}, u32[]{:S(2)}, u32[]{:S(2)}) collective-permute-start(bf16[128,1024]{1,0:T(8,128)(2,1)S(1)} %get-tuple-element.17.main_ref.own_ref.refs_0_), channel_id=1, source_target_pairs={{0,24},{4,28},{8,0},{12,4},{16,8},{20,12},{24,16},{28,20},{1,25},{... | collective-permute-start | bytes 786440 | tf_op jit(solution)/shard_map/ppermute | solution.py:357
  8.8 1.5 %collective-permute-start.2 = (bf16[128,1024]{1,0:T(8,128)(2,1)S(1)}, bf16[128,1024]{1,0:T(8,128)(2,1)S(1)}, u32[]{:S(2)}, u32[]{:S(2)}) collective-permute-start(bf16[128,1024]{1,0:T(8,128)(2,1)S(1)} %get-tuple-element.17.main_ref.own_ref.refs_0_), channel_id=1, source_target_pairs={{0,4},{4,0},{8,12},{12,8},{16,20},{20,16},{24,28},{28,24},{1,5},{5... | collective-permute-start | bytes 786440 | tf_op jit(solution)/shard_map/ppermute | solution.py:361
  10.3 0.0 collective-permute-start
  10.4 1.7 %collective-permute-start.1 = (bf16[144,128]{1,0:T(8,128)(2,1)S(1)}, bf16[144,128]{1,0:T(8,128)(2,1)S(1)}, u32[]{:S(2)}, u32[]{:S(2)}) collective-permute-start(bf16[144,128]{1,0:T(8,128)(2,1)S(1)} %get-tuple-element.20), channel_id=1, source_target_pairs={{0,3},{1,0},{2,1},{3,2},{4,7},{5,4},{6,5},{7,6},{8,11},{9,8},{10,9... | collective-permute-start | bytes 110600 | tf_op jit(solution)/shard_map/ppermute | solution.py:357
  12.1 1.6 %collective-permute-done.left_ref = bf16[144,128]{1,0:T(8,128)(2,1)S(1)} collective-permute-done((bf16[144,128]{1,0:T(8,128)(2,1)S(1)}, bf16[144,128]{1,0:T(8,128)(2,1)S(1)}, u32[]{:S(2)}, u32[]{:S(2)}) %collective-permute-start) | collective-permute-done | bytes 36896 | tf_op jit(solution)/shard_map/ppermute | solution.py:357
  13.7 0.0 collective-permute-done.1.right_ref
  13.7 0.2 halo.1.halo_ref
  13.9 0.0 copy-start
  13.9 0.5 %collective-permute-start.4 = (bf16[16,640]{1,0:T(8,128)(2,1)S(1)}, bf16[16,640]{1,0:T(8,128)(2,1)S(1)}, u32[]{:S(2)}, u32[]{:S(2)}) collective-permute-start(bf16[16,640]{1,0:T(8,128)(2,1)S(1)} %halo.1.halo_ref), channel_id=1, source_target_pairs={{0,24},{4,28},{8,0},{12,4},{16,8},{20,12},{24,16},{28,20},{1,25},{... | collective-permute-start | bytes 61448 | tf_op jit(solution)/shard_map/ppermute | solution.py:357
  14.4 3.3 %collective-permute-done.4.two_halo_ref.halo_ref = bf16[16,640]{1,0:T(8,128)(2,1)S(1)} collective-permute-done((bf16[16,640]{1,0:T(8,128)(2,1)S(1)}, bf16[16,640]{1,0:T(8,128)(2,1)S(1)}, u32[]{:S(2)}, u32[]{:S(2)}) %collective-permute-start.4) | collective-permute-done | bytes 20512 | tf_op jit(solution)/shard_map/ppermute | solution.py:357
  17.7 0.0 collective-permute-done.3.two_ref.main_ref.refs_2_
  17.7 0.0 collective-permute-done.2.beside_ref.refs_1_
  17.7 0.0 copy-start.1
  17.7 0.3 join.1
  18.0 2.3 %collective-permute-start.7 = (bf16[144,1024]{1,0:T(8,128)(2,1)S(1)}, bf16[144,1024]{1,0:T(8,128)(2,1)S(1)}, u32[]{:S(2)}, u32[]{:S(2)}) collective-permute-start(bf16[144,1024]{1,0:T(8,128)(2,1)S(1)} %get-tuple-element.23), channel_id=1, source_target_pairs={{0,24},{4,28},{8,0},{12,4},{16,8},{20,12},{24,16},{28,20},{1,25},{... | collective-permute-start | bytes 884744 | tf_op jit(solution)/shard_map/ppermute | solution.py:357
  20.3 0.0 collective-permute-start.5
  20.3 1.5 %collective-permute-start.6 = (bf16[160,1024]{1,0:T(8,128)(2,1)S(1)}, bf16[160,1024]{1,0:T(8,128)(2,1)S(1)}, u32[]{:S(2)}, u32[]{:S(2)}) collective-permute-start(bf16[160,1024]{1,0:T(8,128)(2,1)S(1)} %get-tuple-element.24), channel_id=1, source_target_pairs={{0,4},{4,0},{8,12},{12,8},{16,20},{20,16},{24,28},{28,24},{1,5},{5... | collective-permute-start | bytes 983048 | tf_op jit(solution)/shard_map/ppermute | solution.py:361
  21.8 0.0 copy-done
  21.8 0.0 copy-done.1
  21.8 1.2 %spectrum.1 = (f32[128,1024]{1,0:T(8,128)S(1)}, f32[8,128]{1,0:T(8,128)S(1)}) custom-call(bf16[128,1024]{1,0:T(8,128)(2,1)S(1)} %get-tuple-element.17.main_ref.own_ref.refs_0_, bf16[128,192]{1,0:T(8,128)(2,1)S(1)} %copy-done.1, bf16[256,256]{1,0:T(8,128)(2,1)S(1)} %copy-done), custom_call_target="tpu_custom_call" | custom-call | tf_op jit(solution)/shard_map/spectrum/pallas_call | solution.py:374
  23.0 1.0 %own.1 = (bf16[128,1152]{1,0:T(8,128)(2,1)S(1)}, f32[64,1024]{1,0:T(8,128)S(1)}) custom-call(bf16[128,1024]{1,0:T(8,128)(2,1)S(1)} %get-tuple-element.17.main_ref.own_ref.refs_0_, bf16[16,640]{1,0:T(8,128)(2,1)S(1)} %halo.1.halo_ref), custom_call_target="tpu_custom_call" | custom-call | tf_op jit(solution)/shard_map/own/pallas_call | solution.py:374
  24.0 2.0 %collective-permute-start.8 = (bf16[64,1024]{1,0:T(8,128)(2,1)S(1)}, bf16[64,1024]{1,0:T(8,128)(2,1)S(1)}, u32[]{:S(2)}, u32[]{:S(2)}) collective-permute-start(bf16[64,1024]{1,0:T(8,128)(2,1)S(1)} %get-tuple-element.25), channel_id=1, source_target_pairs={{0,8},{4,12},{8,16},{12,20},{16,24},{20,28},{24,0},{28,4},{1,9},{5... | collective-permute-start | bytes 393224 | tf_op jit(solution)/shard_map/ppermute | solution.py:357
  26.0 1.3 %two.1.coh_two_ref = bf16[64,1024]{1,0:T(8,128)(2,1)S(1)} custom-call(f32[16,128]{1,0:T(8,128)S(1)} %get-tuple-element.16.cond_ref, bf16[128,1152]{1,0:T(8,128)(2,1)S(1)} %get-tuple-element.21.ext_ref, f32[64,1024]{1,0:T(8,128)S(1)} %get-tuple-element.22.power_ref, bf16[128,1024]{1,0:T(8,128)(2,1)S(1)} %collective-permute-done.3.two_ref.main_ref.refs_2_, ...), custom_call_target="tpu_custom_call" | custom-call | tf_op jit(solution)/shard_map/two/pallas_call | solution.py:374
  27.3 0.6 %collective-permute-done.7.both_ref.refs_4_ = bf16[144,1024]{1,0:T(8,128)(2,1)S(1)} collective-permute-done((bf16[144,1024]{1,0:T(8,128)(2,1)S(1)}, bf16[144,1024]{1,0:T(8,128)(2,1)S(1)}, u32[]{:S(2)}, u32[]{:S(2)}) %collective-permute-start.7) | collective-permute-done | bytes 294944 | tf_op jit(solution)/shard_map/ppermute | solution.py:357
  27.9 1.3 %four.1.coh_four_ref = bf16[64,1024]{1,0:T(8,128)(2,1)S(1)} custom-call(f32[16,128]{1,0:T(8,128)S(1)} %get-tuple-element.16.cond_ref, bf16[128,1152]{1,0:T(8,128)(2,1)S(1)} %get-tuple-element.21.ext_ref, f32[64,1024]{1,0:T(8,128)S(1)} %get-tuple-element.22.power_ref, bf16[144,1024]{1,0:T(8,128)(2,1)S(1)} %collective-permute-done.7.both_ref.refs_4_), custom_call_target="tpu_custom_call" | custom-call | tf_op jit(solution)/shard_map/four/pallas_call | solution.py:374
  29.2 4.9 %collective-permute-done.5.refs_5_ = bf16[144,1024]{1,0:T(8,128)(2,1)S(1)} collective-permute-done((bf16[144,1024]{1,0:T(8,128)(2,1)S(1)}, bf16[144,1024]{1,0:T(8,128)(2,1)S(1)}, u32[]{:S(2)}, u32[]{:S(2)}) %collective-permute-start.5) | collective-permute-done | bytes 294944 | tf_op jit(solution)/shard_map/ppermute | solution.py:426
  34.1 2.6 %collective-permute-done.6.both_ref.refs_3_ = bf16[160,1024]{1,0:T(8,128)(2,1)S(1)} collective-permute-done((bf16[160,1024]{1,0:T(8,128)(2,1)S(1)}, bf16[160,1024]{1,0:T(8,128)(2,1)S(1)}, u32[]{:S(2)}, u32[]{:S(2)}) %collective-permute-start.6) | collective-permute-done | bytes 327712 | tf_op jit(solution)/shard_map/ppermute | solution.py:361
  36.7 0.0 copy-start.2
  36.7 1.3 %cross.1.coh_cross_ref = bf16[64,1024]{1,0:T(8,128)(2,1)S(1)} custom-call(f32[16,128]{1,0:T(8,128)S(1)} %get-tuple-element.16.cond_ref, bf16[128,1152]{1,0:T(8,128)(2,1)S(1)} %get-tuple-element.21.ext_ref, f32[64,1024]{1,0:T(8,128)S(1)} %get-tuple-element.22.power_ref, bf16[160,1024]{1,0:T(8,128)(2,1)S(1)} %collective-permute-done.6.both_ref.refs_3_), custom_call_target="tpu_custom_call" | custom-call | tf_op jit(solution)/shard_map/cross/pallas_call | solution.py:374
  38.0 0.0 copy-start.4
  38.1 0.0 collective-permute-done.8.refs_6_
  38.1 0.0 copy-done.2
  38.1 0.7 %copy-done.4 = bf16[64,256]{1,0:T(8,128)(2,1)S(1)} copy-done((bf16[64,256]{1,0:T(8,128)(2,1)S(1)}, bf16[64,256]{1,0:T(8,128)(2,1)}, u32[]{:S(2)}) %copy-start.4) | copy-done | bytes 32792
  38.8 3.7 %last.1 = (bf16[4,64,1024]{2,1,0:T(8,128)(2,1)}, f32[16,1024]{1,0:T(8,128)}) custom-call(f32[16,128]{1,0:T(8,128)S(1)} %get-tuple-element.16.cond_ref, bf16[128,1152]{1,0:T(8,128)(2,1)S(1)} %get-tuple-element.21.ext_ref, f32[64,1024]{1,0:T(8,128)S(1)} %get-tuple-element.22.power_ref, bf16[128,1024]{1,0:T(8,128)(2,1)S(1)} %slice_select_fusion.last_ref, ...), custom_call_target="tpu_custom_call" | custom-call | tf_op jit(solution)/shard_map/last/pallas_call | solution.py:454
  (2 shorter events, 0.0 us)
Async XLA Ops:
  1.3 0.7 %copy-start.5 = (s32[1,1,16]{2,1,0:T(1,128)S(1)}, s32[1,1,16]{2,1,0:T(1,128)}, u32[]{:S(2)}) copy-start(s32[1,1,16]{2,1,0:T(1,128)} %param.11) | copy-start | bytes 196
  1.3 0.7 %copy-start.6 = (f32[1,1,16]{2,1,0:T(1,128)S(1)}, f32[1,1,16]{2,1,0:T(1,128)}, u32[]{:S(2)}) copy-start(f32[1,1,16]{2,1,0:T(1,128)} %param.12) | copy-start | bytes 196
  1.3 0.7 %copy-start.7 = (s32[1,4]{1,0:T(1,128)S(1)}, s32[1,4]{1,0:T(1,128)}, u32[]{:S(2)}) copy-start(s32[1,4]{1,0:T(1,128)} %partners_hbm.1) | copy-start | bytes 52
  2.0 0.9 %copy-start.3 = (bf16[1,2,64,1024]{3,2,1,0:T(8,128)(2,1)S(1)}, bf16[1,2,64,1024]{3,2,1,0:T(8,128)(2,1)}, u32[]{:S(2)}) copy-start(bf16[1,2,64,1024]{3,2,1,0:T(8,128)(2,1)} %param.9) | copy-start | bytes 786436
  3.7 14.0 %collective-permute-start.3 = (bf16[128,1024]{1,0:T(8,128)(2,1)S(1)}, bf16[128,1024]{1,0:T(8,128)(2,1)S(1)}, u32[]{:S(2)}, u32[]{:S(2)}) collective-permute-start(bf16[128,1024]{1,0:T(8,128)(2,1)S(1)} %get-tuple-element.17.main_ref.own_ref.refs_0_), channel_id=1, source_target_pairs={{0,24},{4,28},{8,0},{12,4},{16,8},{20,12},{24,16},{28,20},{1,25},{... | collective-permute-start | bytes 786440 | tf_op jit(solution)/shard_map/ppermute | solution.py:357
  8.8 8.9 %collective-permute-start.2 = (bf16[128,1024]{1,0:T(8,128)(2,1)S(1)}, bf16[128,1024]{1,0:T(8,128)(2,1)S(1)}, u32[]{:S(2)}, u32[]{:S(2)}) collective-permute-start(bf16[128,1024]{1,0:T(8,128)(2,1)S(1)} %get-tuple-element.17.main_ref.own_ref.refs_0_), channel_id=1, source_target_pairs={{0,4},{4,0},{8,12},{12,8},{16,20},{20,16},{24,28},{28,24},{1,5},{5... | collective-permute-start | bytes 786440 | tf_op jit(solution)/shard_map/ppermute | solution.py:361
  10.3 3.4 %collective-permute-start = (bf16[144,128]{1,0:T(8,128)(2,1)S(1)}, bf16[144,128]{1,0:T(8,128)(2,1)S(1)}, u32[]{:S(2)}, u32[]{:S(2)}) collective-permute-start(bf16[144,128]{1,0:T(8,128)(2,1)S(1)} %get-tuple-element.19), channel_id=1, source_target_pairs={{0,1},{1,2},{2,3},{3,0},{4,5},{5,6},{6,7},{7,4},{8,9},{9,10},{10,1... | collective-permute-start | bytes 110600 | tf_op jit(solution)/shard_map/ppermute | solution.py:357
  10.4 3.4 %collective-permute-start.1 = (bf16[144,128]{1,0:T(8,128)(2,1)S(1)}, bf16[144,128]{1,0:T(8,128)(2,1)S(1)}, u32[]{:S(2)}, u32[]{:S(2)}) collective-permute-start(bf16[144,128]{1,0:T(8,128)(2,1)S(1)} %get-tuple-element.20), channel_id=1, source_target_pairs={{0,3},{1,0},{2,1},{3,2},{4,7},{5,4},{6,5},{7,6},{8,11},{9,8},{10,9... | collective-permute-start | bytes 110600 | tf_op jit(solution)/shard_map/ppermute | solution.py:357
  13.9 8.0 %copy-start = (bf16[256,256]{1,0:T(8,128)(2,1)S(1)}, bf16[256,256]{1,0:T(8,128)(2,1)}, u32[]{:S(2)}) copy-start(bf16[256,256]{1,0:T(8,128)(2,1)} %constant.29.clone.second_ref.refs_10_) | copy-start | bytes 393220
  13.9 3.8 %collective-permute-start.4 = (bf16[16,640]{1,0:T(8,128)(2,1)S(1)}, bf16[16,640]{1,0:T(8,128)(2,1)S(1)}, u32[]{:S(2)}, u32[]{:S(2)}) collective-permute-start(bf16[16,640]{1,0:T(8,128)(2,1)S(1)} %halo.1.halo_ref), channel_id=1, source_target_pairs={{0,24},{4,28},{8,0},{12,4},{16,8},{20,12},{24,16},{28,20},{1,25},{... | collective-permute-start | bytes 61448 | tf_op jit(solution)/shard_map/ppermute | solution.py:357
  17.7 4.2 %copy-start.1 = (bf16[128,192]{1,0:T(8,128)(2,1)S(1)}, bf16[128,192]{1,0:T(8,128)(2,1)}, u32[]{:S(2)}) copy-start(bf16[128,192]{1,0:T(8,128)(2,1)} %constant.28.clone.first_ref.refs_9_) | copy-start | bytes 147460
  18.0 9.9 %collective-permute-start.7 = (bf16[144,1024]{1,0:T(8,128)(2,1)S(1)}, bf16[144,1024]{1,0:T(8,128)(2,1)S(1)}, u32[]{:S(2)}, u32[]{:S(2)}) collective-permute-start(bf16[144,1024]{1,0:T(8,128)(2,1)S(1)} %get-tuple-element.23), channel_id=1, source_target_pairs={{0,24},{4,28},{8,0},{12,4},{16,8},{20,12},{24,16},{28,20},{1,25},{... | collective-permute-start | bytes 884744 | tf_op jit(solution)/shard_map/ppermute | solution.py:357
  20.3 13.8 %collective-permute-start.5 = (bf16[144,1024]{1,0:T(8,128)(2,1)S(1)}, bf16[144,1024]{1,0:T(8,128)(2,1)S(1)}, u32[]{:S(2)}, u32[]{:S(2)}) collective-permute-start(bf16[144,1024]{1,0:T(8,128)(2,1)S(1)} %get-tuple-element.23), channel_id=1, source_target_pairs={{0,28},{4,24},{8,4},{12,0},{16,12},{20,8},{24,20},{28,16},{1,29},{... | collective-permute-start | bytes 884744 | tf_op jit(solution)/shard_map/ppermute | solution.py:426
  20.3 16.4 %collective-permute-start.6 = (bf16[160,1024]{1,0:T(8,128)(2,1)S(1)}, bf16[160,1024]{1,0:T(8,128)(2,1)S(1)}, u32[]{:S(2)}, u32[]{:S(2)}) collective-permute-start(bf16[160,1024]{1,0:T(8,128)(2,1)S(1)} %get-tuple-element.24), channel_id=1, source_target_pairs={{0,4},{4,0},{8,12},{12,8},{16,20},{20,16},{24,28},{28,24},{1,5},{5... | collective-permute-start | bytes 983048 | tf_op jit(solution)/shard_map/ppermute | solution.py:361
  24.0 14.0 %collective-permute-start.8 = (bf16[64,1024]{1,0:T(8,128)(2,1)S(1)}, bf16[64,1024]{1,0:T(8,128)(2,1)S(1)}, u32[]{:S(2)}, u32[]{:S(2)}) collective-permute-start(bf16[64,1024]{1,0:T(8,128)(2,1)S(1)} %get-tuple-element.25), channel_id=1, source_target_pairs={{0,8},{4,12},{8,16},{12,20},{16,24},{20,28},{24,0},{28,4},{1,9},{5... | collective-permute-start | bytes 393224 | tf_op jit(solution)/shard_map/ppermute | solution.py:357
  36.7 1.3 %copy-start.2 = (bf16[512,256]{1,0:T(8,128)(2,1)S(1)}, bf16[512,256]{1,0:T(8,128)(2,1)}, u32[]{:S(2)}) copy-start(bf16[512,256]{1,0:T(8,128)(2,1)} %constant.31.clone.refs_12_) | copy-start | bytes 786436
  38.0 0.8 %copy-start.4 = (bf16[64,256]{1,0:T(8,128)(2,1)S(1)}, bf16[64,256]{1,0:T(8,128)(2,1)}, u32[]{:S(2)}) copy-start(bf16[64,256]{1,0:T(8,128)(2,1)} %constant.30.clone.refs_11_) | copy-start | bytes 98308

commit v3 on v2

--- a/solution.py
+++ b/solution.py
@@ -72,9 +72,9 @@
     values = [jnp.where(date + 1 + h < dates, partners_ref[0, h], 0) for h in range(SPAN)]
     values += [1 - date % 2, (place > 0).astype(jnp.int32), (place < places - 1).astype(jnp.int32), jnp.int32(0)]
     beside = date + 1 - 2 * (date % 2)
-    held = [date, beside, date + 2, beside + 2, date + 4, beside + 4]
+    held = [date, beside, date + 2, date + 4, beside + 2, beside + 4]
     found = [(lax.rem(h, dates) == ref_ref[0]).astype(jnp.int32) for h in held]
-    values += found
+    values += found[0:4] + [(found[4] + found[5]) * int(dates == 8)]
     row = iota(cond_ref.shape, 0)
     cond = jnp.zeros(cond_ref.shape, jnp.int32)
     for k, value in enumerate(values):
@@ -95,19 +95,18 @@
     high_ref[0 : 2 * rows, :] = own_ref[:, cols - LANES :]
 
 
-def join_kernel(cond_ref, own_ref, beside_ref, halo_ref, two_ref, two_halo_ref, amp_ref, both_ref, all_ref):
+def candidate_kernel(first, cond_ref, a_ref, b_ref, amp_ref):
     rows = amp_ref.shape[0]
-    mine, other = cond_ref[PICK : PICK + 1, 0:1] > 0.0, cond_ref[PICK + 1 : PICK + 2, 0:1] > 0.0
-    value = jnp.where(other, beside_ref[...].astype(F32), own_ref[...].astype(F32))
+    at = PICK + first
+    a, b = cond_ref[at : at + 1, 0:1] > 0.0, cond_ref[at + 1 : at + 2, 0:1] > 0.0
+    value = jnp.where(b, b_ref[...].astype(F32), a_ref[...].astype(F32))
     value = amplitude(value[0:rows], value[rows:])
-    amp_ref[...] = jnp.where(mine | other, value.astype(F32), 0.0).astype(BF16)
-    width = two_halo_ref.shape[1]
-    for ref in (both_ref, all_ref):
-        ref[0 : 2 * rows, :] = two_ref[...]
-        ref[2 * rows : 2 * rows + HROWS, 0:width] = two_halo_ref[...]
-        ref[2 * rows : 2 * rows + HROWS, width:] = jnp.zeros((HROWS, ref.shape[1] - width), BF16)
-    all_ref[2 * rows + HROWS :, 0:width] = halo_ref[...]
-    all_ref[2 * rows + HROWS :, width:] = jnp.zeros((HROWS, all_ref.shape[1] - width), BF16)
+    amp_ref[...] = jnp.where(a | b, value.astype(F32), 0.0).astype(BF16)
+
+
+def pass_kernel(earlier_ref, in_ref, out_ref):
+    del earlier_ref
+    out_ref[...] = in_ref[...]
 
 
 def halo_kernel(blocks, cond_ref, taps_ref, left_ref, right_ref, out_ref):
@@ -163,15 +162,38 @@
     return pltpu.roll(five, rows + 8 - BOXA // 2, 0)[0:rows]
 
 
-def own_kernel(main_ref, halo_ref, ext_ref, power_ref, fields_ref):
+def keep_tile(ext_ref, p, real, imag):
+    rows, lanes = real.shape[0], slice(p * LANES, (p + 1) * LANES)
+    ext_ref[0:rows, lanes] = real
+    ext_ref[rows:, lanes] = imag
+
+
+def power_tile(fields_ref, p, real, imag):
+    real, imag = real.astype(F32), imag.astype(F32)
+    fields_ref[:, p * LANES : (p + 1) * LANES] = (real * real + imag * imag).astype(BF16)
+
+
+def cross_tile(fields_ref, ext_ref, p, real, imag):
+    rows, lanes = real.shape[0], slice(p * LANES, (p + 1) * LANES)
+    own_r, own_i = ext_ref[0:rows, lanes].astype(F32), ext_ref[rows:, lanes].astype(F32)
+    r, i = real.astype(F32), imag.astype(F32)
+    fields_ref[0:rows, lanes] = (own_r * r + own_i * i).astype(BF16)
+    fields_ref[rows : 2 * rows, lanes] = (own_i * r - own_r * i).astype(BF16)
+
+
+def coherence(sums, own, partner):
+    rows = own.shape[0]
+    re, im = line_box(sums[0:rows]), line_box(sums[rows : 2 * rows])
+    return ((re * re + im * im) / (own * partner + 1e-06)).astype(BF16)
+
+
+def own_kernel(earlier_ref, main_ref, halo_ref, ext_ref, power_ref, fields_ref):
+    del earlier_ref
     rows, cols = power_ref.shape
 
     def use(p, real, imag):
-        lanes = slice(p * LANES, (p + 1) * LANES)
-        ext_ref[0:rows, lanes] = real
-        ext_ref[rows:, lanes] = imag
-        real, imag = real.astype(F32), imag.astype(F32)
-        fields_ref[:, lanes] = (real * real + imag * imag).astype(BF16)
+        keep_tile(ext_ref, p, real, imag)
+        power_tile(fields_ref, p, real, imag)
 
     resample(main_ref, halo_ref, use)
     box = range_box()
@@ -180,44 +202,47 @@
         power_ref[:, lanes] = line_box(dot(fields_ref[:, p * LANES : (p + 2) * LANES], box))
 
 
-def pair(flag, ext_ref, power_ref, main_ref, halo_ref, out_ref, fields_ref):
+def pair_kernel(own_ref, own_power_ref, main_ref, halo_ref, ext_ref, power_ref, out_ref, fields_ref):
     rows, cols = out_ref.shape
 
     def use(p, real, imag):
-        lanes = slice(p * LANES, (p + 1) * LANES)
-        own_r, own_i = ext_ref[0:rows, lanes].astype(F32), ext_ref[rows:, lanes].astype(F32)
-        r, i = real.astype(F32), imag.astype(F32)
-        fields_ref[0:rows, lanes] = (own_r * r + own_i * i).astype(BF16)
-        fields_ref[rows : 2 * rows, lanes] = (own_i * r - own_r * i).astype(BF16)
-        fields_ref[2 * rows :, lanes] = (r * r + i * i).astype(BF16)
+        keep_tile(ext_ref, p, real, imag)
+        power_tile(fields_ref.at[2 * rows :], p, real, imag)
+        cross_tile(fields_ref, own_ref, p, real, imag)
 
     resample(main_ref, halo_ref, use)
     box = range_box()
     for p in range(cols // LANES):
         lanes = slice(p * LANES, (p + 1) * LANES)
         sums = dot(fields_ref[:, p * LANES : (p + 2) * LANES], box)
-        re = line_box(sums[0:rows])
-        im = line_box(sums[rows : 2 * rows])
-        partner = line_box(sums[2 * rows :])
-        value = flag * (re * re + im * im) / (power_ref[:, lanes] * partner + 1e-06)
-        out_ref[:, lanes] = value.astype(BF16)
-
-
-def two_kernel(cond_ref, ext_ref, power_ref, main_ref, halo_ref, out_ref, fields_ref):
-    pair(cond_ref[1:2, :], ext_ref, power_ref, main_ref, halo_ref, out_ref, fields_ref)
-
-
-def joined(ref, rows):
-    return ref.at[0 : 2 * rows], ref.at[2 * rows : 2 * rows + HROWS]
-
-
-def four_kernel(cond_ref, ext_ref, power_ref, both_ref, out_ref, fields_ref):
-    pair(cond_ref[3:4, :], ext_ref, power_ref, *joined(both_ref, out_ref.shape[0]), out_ref, fields_ref)
-
-
-def cross_kernel(cond_ref, ext_ref, power_ref, both_ref, out_ref, fields_ref):
-    flag = jnp.where(cond_ref[EVEN : EVEN + 1, :] > 0.0, cond_ref[2:3, :], cond_ref[0:1, :])
-    pair(flag, ext_ref, power_ref, *joined(both_ref, out_ref.shape[0]), out_ref, fields_ref)
+        power = line_box(sums[2 * rows :])
+        power_ref[:, lanes] = power
+        out_ref[:, lanes] = coherence(sums, own_power_ref[:, lanes], power)
+
+
+def again_kernel(own_ref, own_power_ref, ext_ref, power_ref, out_ref, fields_ref):
+    rows, cols = out_ref.shape
+    for p in range(cols // LANES + 1):
+        lanes = slice(p * LANES, (p + 1) * LANES)
+        cross_tile(fields_ref, own_ref, p, ext_ref[0:rows, lanes], ext_ref[rows:, lanes])
+    box = range_box()
+    for p in range(cols // LANES):
+        lanes = slice(p * LANES, (p + 1) * LANES)
+        sums = dot(fields_ref[:, p * LANES : (p + 2) * LANES], box)
+        out_ref[:, lanes] = coherence(sums, own_power_ref[:, lanes], power_ref[:, lanes])
+
+
+def place_kernel(cond_ref, beside_ref, two_ref, four_ref, near_ref, far_ref, out_ref):
+    even = cond_ref[EVEN : EVEN + 1, 0:1] > 0.0
+    near = near_ref[...].astype(F32)
+    fields = [
+        jnp.where(even, beside_ref[...].astype(F32), near),
+        two_ref[...].astype(F32),
+        jnp.where(even, near, far_ref[...].astype(F32)),
+        four_ref[...].astype(F32),
+    ]
+    for h, value in enumerate(fields):
+        out_ref[h] = (value * cond_ref[h : h + 1, 0:1]).astype(BF16)
 
 
 def split(table):
@@ -270,7 +295,8 @@
     return jnp.dot(rows_ref[...], group, precision=HIGHEST)
 
 
-def spectrum_kernel(own_ref, first_ref, second_ref, spec_ref, energy_ref, amp_ref, rows_ref):
+def spectrum_kernel(own_ref, first_ref, second_ref, third_ref, fourth_ref, spec_ref, energy_ref, amp_ref, rows_ref):
+    del third_ref, fourth_ref
     size = amp_ref.shape[0]
     amp_ref[...] = amplitude(own_ref[0:size, :], own_ref[size:, :])
 
@@ -282,42 +308,20 @@
     energy_ref[...] = spectrum(amp_ref, rows_ref, first_ref, second_ref, use)
 
 
-def last_kernel(
-    cond_ref,
-    ext_ref,
-    power_ref,
-    last_ref,
-    last_halo_ref,
-    coh_two_ref,
-    coh_cross_ref,
-    coh_four_ref,
-    *refs,
-):
-    samples, before_ref, refs = refs[0:6], refs[6], refs[7:]
-    spec_ref, energy_ref, first_ref, second_ref, third_ref, fourth_ref, coh_hbm, surface_hbm = refs[0:8]
-    tail_ref, fields_ref, amp_ref, rows_ref, cross_ref, out_scr, out_ref, sems = refs[8:]
-    odd = lax.axis_index("date") % 2
-    copies = [
-        pltpu.make_async_copy(coh_two_ref, coh_hbm.at[1], sems.at[0]),
-        pltpu.make_async_copy(coh_four_ref, coh_hbm.at[3], sems.at[1]),
-        pltpu.make_async_copy(coh_cross_ref, coh_hbm.at[2 - 2 * odd], sems.at[2]),
-        pltpu.make_async_copy(tail_ref, coh_hbm.at[2 * odd], sems.at[3]),
-        pltpu.make_async_copy(out_ref, surface_hbm, sems.at[4]),
-    ]
-    for copy in copies[0:3]:
-        copy.start()
-    flag = jnp.where(cond_ref[EVEN : EVEN + 1, :] > 0.0, cond_ref[0:1, :], cond_ref[2:3, :])
-    pair(flag, ext_ref, power_ref, last_ref, last_halo_ref, tail_ref, fields_ref)
-    copies[3].start()
+def surface_kernel(cond_ref, *refs):
+    samples, across_ref, before_ref, refs = refs[0:4], refs[4], refs[5], refs[6:]
+    spec_ref, energy_ref, first_ref, second_ref, third_ref, fourth_ref, out_ref = refs[0:7]
+    amp_ref, rows_ref, cross_ref, out_scr = refs[7:]
     size, cols = amp_ref.shape
     tiles = cols // LANES
-    picks = [cond_ref[PICK + k : PICK + k + 1, 0:1] > 0.0 for k in range(len(samples))]
+    picks = [cond_ref[PICK + k : PICK + k + 1, 0:1] > 0.0 for k in range(len(samples) + 1)]
     value = samples[0][...].astype(F32)
-    for pick, ref in zip(picks[1:], samples[1:]):
-        value = jnp.where(pick, ref[0 : 2 * size, :].astype(F32), value)
-    found = functools.reduce(jnp.logical_or, picks)
+    for pick, ref in zip(picks[1:4], samples[1:]):
+        value = jnp.where(pick, ref[...].astype(F32), value)
+    found = functools.reduce(jnp.logical_or, picks[0:4])
     value = amplitude(value[0:size], value[size:]).astype(F32)
-    amp_ref[...] = jnp.where(found, value, before_ref[...].astype(F32)).astype(BF16)
+    other = jnp.where(picks[4], across_ref[...].astype(F32), before_ref[...].astype(F32))
+    amp_ref[...] = jnp.where(found, value, other).astype(BF16)
 
     def use(p, ref_r, ref_i):
         lanes = slice(p * LANES, (p + 1) * LANES)
@@ -347,9 +351,6 @@
             out_scr[at : at + 8, :] = total[p * 8 : p * 8 + 8, jj * LANES : (jj + 1) * LANES]
     for a in range(8):
         out_ref[:, a * LANES : (a + 1) * LANES] = out_scr[pl.ds(a, 2 * tiles, stride=8), :]
-    copies[4].start()
-    for copy in copies:
-        copy.wait()
 
 
 def shifted(value, axis, steps):
@@ -393,7 +394,7 @@
     own, cond, taps, low, high = pl.pallas_call(
         prep_kernel,
         out_shape=(samples, sds((16, LANES), F32), sds((HROWS, LANES), BF16), payload, payload),
-        in_specs=[pl.BlockSpec(memory_space=pl.ANY)] * 5,
+        in_specs=[pl.BlockSpec(memory_space=pltpu.HBM)] * 5,
         out_specs=(VMEM,) * 5,
         scratch_shapes=[
             pltpu.VMEM(int_offset.shape[1:], jnp.int32),
@@ -405,71 +406,62 @@
         compiler_params=PARAMS,
         name="prepare",
     )(slc.reshape(2 * rows, cols), int_offset[0], frac_offset[0], ref_date, partners)
-    beside = swapped(own, "date", 1)
-    two = shifted(own, "date", 2)
+    beside = swapped(slc.reshape(2 * rows, cols), "date", 1)
+    two = shifted(slc.reshape(2 * rows, cols), "date", 2)
     right = shifted(low, "rng", 1)
     left = shifted(high, "rng", -1)
     width = (rows // HROWS + 1) * LANES
     halo = call(
         functools.partial(halo_kernel, cols // BLK), "halo", sds((HROWS, width), BF16), (cond, taps, left, right)
     )
+    two = call(pass_kernel, "pass", samples, (halo, two))
+    four = shifted(two, "date", 2)
+    beside_halo = swapped(halo, "date", 1)
     two_halo = shifted(halo, "date", 2)
-    pair_amp, both, everything = call(
-        join_kernel,
-        "join",
-        (field, sds((2 * rows + HROWS, cols), BF16), sds((2 * rows + 2 * HROWS, cols), BF16)),
-        (cond, own, beside, halo, two, two_halo),
-    )
-    cross = swapped(everything, "date", 1)
-    four = shifted(both, "date", 2)
-    before = shifted(pair_amp, "date", -2) if dates == 8 else spread(pair_amp, "date")
-    across = lax.ppermute(both, "date", [(s, (s - 2) % dates ^ 1) for s in range(dates)])
+    four_halo = shifted(halo, "date", 4)
+    amp = call(functools.partial(candidate_kernel, 0), "candidate", field, (cond, own, beside))
+    before = shifted(amp, "date", -2) if dates == 8 else spread(amp, "date")
+    later = call(functools.partial(candidate_kernel, 2), "later", field, (cond, two, four))
+    across = swapped(later, "date", 1)
     first, second, third, fourth = [jnp.asarray(t) for t in surface_tables()]
     spec, energy = call(
         spectrum_kernel,
         "spectrum",
         (sds((2 * rows, cols), F32), sds((tiles, LANES), F32)),
-        (own, first, second),
+        (own, first, second, third, fourth),
         [((rows, cols), BF16), ((tiles, LANES), F32)],
     )
-    fields = ((3 * rows, cols + LANES), BF16)
-    ext, power = call(
-        own_kernel,
-        "own",
-        (sds((2 * rows, cols + LANES), BF16), sds((rows, cols), F32)),
-        (own, halo),
-        [((rows, cols + LANES), BF16)],
-    )
-    coh_two = call(two_kernel, "two", field, (cond, ext, power, two, two_halo), [fields])
-    coh_cross = call(cross_kernel, "cross", field, (cond, ext, power, cross), [fields])
-    coh_four = call(four_kernel, "four", field, (cond, ext, power, four), [fields])
-    last = jnp.where(even, beside, across[0 : 2 * rows])
-    last_halo = jnp.where(even, cross[2 * rows + HROWS :], across[2 * rows :])
-    operands = (
-        *(cond, ext, power, last, last_halo, coh_two, coh_cross, coh_four),
-        *(own, beside, two, cross, four, across, before),
-        *(spec, energy, first, second, third, fourth),
-    )
-    lags = (cols // BLK, LAGS * LAGS)
-    coherence, surface = pl.pallas_call(
-        last_kernel,
-        out_shape=(sds((SPAN, rows, cols), BF16), sds(lags, F32)),
-        in_specs=[VMEM] * len(operands),
-        out_specs=(pl.BlockSpec(memory_space=pl.ANY),) * 2,
-        scratch_shapes=[
-            pltpu.VMEM((rows, cols), BF16),
-            pltpu.VMEM(*fields),
-            pltpu.VMEM((rows, cols), BF16),
-            pltpu.VMEM((tiles, LANES), F32),
-            pltpu.VMEM((2 * rows, cols), F32),
-            pltpu.VMEM((8 * cols // BLK, LANES), F32),
-            pltpu.VMEM(lags, F32),
-            pltpu.SemaphoreType.DMA((5,)),
+    resampled = (sds((2 * rows, cols + LANES), BF16), sds((rows, cols), F32))
+    scratch = [[((k * rows, cols + LANES), BF16)] for k in range(4)]
+    own_ext = call(own_kernel, "own", resampled, (amp, own, halo), scratch[1])
+    *beside_ext, coh_beside = call(
+        pair_kernel, "beside", (*resampled, field), (*own_ext, beside, beside_halo), scratch[3]
+    )
+    *two_ext, coh_near = call(pair_kernel, "near", (*resampled, field), (*beside_ext, two, two_halo), scratch[3])
+    near = swapped(coh_near, "date", 1)
+    coh_two = call(again_kernel, "two", field, (*own_ext, *two_ext), scratch[2])
+    *four_ext, coh_far = call(pair_kernel, "far", (*resampled, field), (*beside_ext, four, four_halo), scratch[3])
+    far = swapped(coh_far, "date", 1)
+    coh_four = call(again_kernel, "four", field, (*own_ext, *four_ext), scratch[2])
+    surface = call(
+        surface_kernel,
+        "surface",
+        sds((cols // BLK, LAGS * LAGS), F32),
+        (cond, own, beside, two, four, across, before, spec, energy, first, second, third, fourth),
+        [
+            ((rows, cols), BF16),
+            ((tiles, LANES), F32),
+            ((2 * rows, cols), F32),
+            ((8 * cols // BLK, LANES), F32),
         ],
-        compiler_params=PARAMS,
-        name="last",
-    )(*operands)
-    return (surface[None, None], coherence[None])
+    )
+    fields = call(
+        place_kernel,
+        "place",
+        sds((SPAN, rows, cols), BF16),
+        (cond, coh_beside, coh_two, coh_four, near, far),
+    )
+    return (surface[None, None], fields[None])
 
 
 def solution(mesh):

time: 42.7 us -> 35.4 us (0.83)
  waiting for transfers between devices: 13 us -> 1.83 us
  starting transfers between devices: 14.7 us -> 19 us
  local copies, waits for them, and re-layouts: 2.34 us -> 0.68 us
  Pallas kernels: 11 us -> 12.3 us
    ppermute x6 -> x7, waiting for transfers between devices: 5.58 us -> 0.72 us  [shifted(): lax.ppermute(value, axis, [(s, (s - steps) % count) for s in range(count)])]
    ppermute x1 -> x0, waiting for transfers between devices: 4.85 us -> none  [body(): lax.ppermute(both, 'date', [(s, (s - 2) % dates ^ 1) for s in range(dates)])]
    pallas_call x7 -> x13, Pallas kernels: 6.51 us -> 11.3 us  [call(): pl.pallas_call(kernel, out_shape=out_shape, in_specs=[VMEM] * len(operand...]
    ppermute x2 -> x5, starting transfers between devices: 3.04 us -> 6.78 us  [swapped(): lax.ppermute(value, axis, [(s, s ^ step) for s in range(lax.axis_size(axi...]
    pallas_call x1 -> x0, Pallas kernels: 3.65 us -> none  [body(): pl.pallas_call(last_kernel, out_shape=(sds((SPAN, rows, cols), BF16), sds...]
    unnamed x16 -> x14, local copies, waits for them, and re-layouts: 2.34 us -> 0.68 us
    ppermute x2 -> x5, waiting for transfers between devices: 2.6 us -> 1.11 us  [swapped(): lax.ppermute(value, axis, [(s, s ^ step) for s in range(lax.axis_size(axi...]
    ppermute x6 -> x7, starting transfers between devices: 11.6 us -> 12.2 us  [shifted(): lax.ppermute(value, axis, [(s, (s - steps) % count) for s in range(count)])]
  transfers between devices with their start and end apart: 9 -> 12, of which waited for: 5 -> 4; matrix products, arithmetic and copies ran while one was open for 0% -> 0% of each run, Pallas kernels for 15% -> 32%
where the time goes in v3:
time: 35.4 us; the launch traced here: 35.2 us
  starting transfers between devices  19 us (54%)
  Pallas kernels  12.3 us (35%)
  waiting for transfers between devices  1.83 us (5%)
  between operations  1.44 us (4%)
  local copies, waits for them, and re-layouts  0.68 us (2%)
    ppermute x7, starting transfers between devices, shifted(): lax.ppermute(value, axis, [(s, (s - steps) % count) for s in range(count)])  12.2 us
    pallas_call x13, Pallas kernels, call(): pl.pallas_call(kernel, out_shape=out_shape, in_specs=[VMEM] * len(operand...  11.3 us
    ppermute x5, starting transfers between devices, swapped(): lax.ppermute(value, axis, [(s, s ^ step) for s in range(lax.axis_size(axi...  6.78 us
    ppermute x5, waiting for transfers between devices, swapped(): lax.ppermute(value, axis, [(s, s ^ step) for s in range(lax.axis_size(axi...  1.11 us
    pallas_call x1, Pallas kernels, body(): pl.pallas_call(prep_kernel, out_shape=(samples, sds((16, LANES), F32), sd...  1.01 us
    ppermute x7, waiting for transfers between devices, shifted(): lax.ppermute(value, axis, [(s, (s - steps) % count) for s in range(count)])  0.72 us
  transfers between devices with their start and end apart: 12, of which 4 were waited for; matrix products, arithmetic and copies ran while one was open for 0% of the time, Pallas kernels for 32%

profile of v3, /device:TPU:0, one launch (start us, length us, event | category | flops | bytes accessed | tf_op | source)
XLA Modules:
  0.0 35.2 jit_solution(15474862273898148801)
XLA Ops:
  0.6 5.1 %collective-permute-start.3 = (bf16[128,1024]{1,0:T(8,128)(2,1)}, bf16[128,1024]{1,0:T(8,128)(2,1)S(1)}, u32[]{:S(2)}, u32[]{:S(2)}) collective-permute-start(bf16[128,1024]{1,0:T(8,128)(2,1)} %bitcast.own_hbm), channel_id=1, source_target_pairs={{0,24},{4,28},{8,0},{12,4},{16,8},{20,12},{24,16},{28,20},{1,25},{... | collective-permute-start | bytes 786440 | tf_op jit(solution)/shard_map/ppermute | solution.py:358
  6.4 0.0 copy-start.4
  6.4 0.0 copy-start.5
  6.4 0.0 copy-start.6
  6.4 0.6 %copy-done.4 = s32[1,1,16]{2,1,0:T(1,128)S(1)} copy-done((s32[1,1,16]{2,1,0:T(1,128)S(1)}, s32[1,1,16]{2,1,0:T(1,128)}, u32[]{:S(2)}) %copy-start.4) | copy-done | bytes 88
  7.0 0.0 copy-done.5
  7.1 0.0 copy-done.6
  7.1 1.0 %prepare.1 = (bf16[128,1024]{1,0:T(8,128)(2,1)S(1)}, f32[16,128]{1,0:T(8,128)S(1)}, bf16[16,128]{1,0:T(8,128)(2,1)S(1)}, bf16[144,128]{1,0:T(8,128)(2,1)S(1)}, bf16[144,128]{1,0:T(8,128)(2,1)S(1)}) custom-call(bf16[128,1024]{1,0:T(8,128)(2,1)} %bitcast.own_hbm, s32[1,16]{1,0:T(1,128)S(1)} %bitcast.5, f32[1,16]{1,0:T(1,128)S(1)} %bitcast.6, ...), custom_call_target="tpu_custom_call" | custom-call | tf_op jit(solution)/shard_map/prepare/pallas_call | solution.py:394
  8.1 0.1 collective-permute-start.1
  8.2 1.7 %collective-permute-start.2 = (bf16[144,128]{1,0:T(8,128)(2,1)S(1)}, bf16[144,128]{1,0:T(8,128)(2,1)S(1)}, u32[]{:S(2)}, u32[]{:S(2)}) collective-permute-start(bf16[144,128]{1,0:T(8,128)(2,1)S(1)} %get-tuple-element.24), channel_id=1, source_target_pairs={{0,3},{1,0},{2,1},{3,2},{4,7},{5,4},{6,5},{7,6},{8,11},{9,8},{10,9... | collective-permute-start | bytes 110600 | tf_op jit(solution)/shard_map/ppermute | solution.py:358
  9.9 1.5 %collective-permute-start = (bf16[128,1024]{1,0:T(8,128)(2,1)}, bf16[128,1024]{1,0:T(8,128)(2,1)S(1)}, u32[]{:S(2)}, u32[]{:S(2)}) collective-permute-start(bf16[128,1024]{1,0:T(8,128)(2,1)} %bitcast.own_hbm), channel_id=1, source_target_pairs={{0,4},{4,0},{8,12},{12,8},{16,20},{20,16},{24,28},{28,24},{1,5},{5... | collective-permute-start | bytes 786440 | tf_op jit(solution)/shard_map/ppermute | solution.py:362
  11.4 0.1 collective-permute-done.1.left_ref
  11.5 0.0 collective-permute-done.2.right_ref
  11.5 0.2 halo.1.earlier_ref.halo_ref
  11.7 0.0 collective-permute-done.3.in_ref
  11.7 4.2 %collective-permute-start.4 = (bf16[128,1024]{1,0:T(8,128)(2,1)S(1)}, bf16[128,1024]{1,0:T(8,128)(2,1)S(1)}, u32[]{:S(2)}, u32[]{:S(2)}) collective-permute-start(bf16[128,1024]{1,0:T(8,128)(2,1)S(1)} %pass.1.a_ref.refs_2_.main_ref), channel_id=1, source_target_pairs={{0,24},{4,28},{8,0},{12,4},{16,8},{20,12},{24,16},{28,20},{1,25},{... | collective-permute-start | bytes 786440 | tf_op jit(solution)/shard_map/ppermute | solution.py:358
  15.9 1.5 %collective-permute-start.7 = (bf16[16,640]{1,0:T(8,128)(2,1)S(1)}, bf16[16,640]{1,0:T(8,128)(2,1)S(1)}, u32[]{:S(2)}, u32[]{:S(2)}) collective-permute-start(bf16[16,640]{1,0:T(8,128)(2,1)S(1)} %halo.1.earlier_ref.halo_ref), channel_id=1, source_target_pairs={{0,4},{4,0},{8,12},{12,8},{16,20},{20,16},{24,28},{28,24},{1,5},{5... | collective-permute-start | bytes 61448 | tf_op jit(solution)/shard_map/ppermute | solution.py:362
  17.4 0.1 collective-permute-start.8
  17.5 0.0 collective-permute-start.9
  17.5 0.9 %collective-permute-done.b_ref.refs_1_.main_ref = bf16[128,1024]{1,0:T(8,128)(2,1)S(1)} collective-permute-done((bf16[128,1024]{1,0:T(8,128)(2,1)}, bf16[128,1024]{1,0:T(8,128)(2,1)S(1)}, u32[]{:S(2)}, u32[]{:S(2)}) %collective-permute-start) | collective-permute-done | bytes 262176 | tf_op jit(solution)/shard_map/ppermute | solution.py:362
  18.4 0.3 candidate.1.earlier_ref
  18.7 1.1 %collective-permute-start.6 = (bf16[64,1024]{1,0:T(8,128)(2,1)S(1)}, bf16[64,1024]{1,0:T(8,128)(2,1)S(1)}, u32[]{:S(2)}, u32[]{:S(2)}) collective-permute-start(bf16[64,1024]{1,0:T(8,128)(2,1)S(1)} %candidate.1.earlier_ref), channel_id=1, source_target_pairs={{0,8},{4,12},{8,16},{12,20},{16,24},{20,28},{24,0},{28,4},{1,9},{5... | collective-permute-start | bytes 393224 | tf_op jit(solution)/shard_map/ppermute | solution.py:358
  19.8 1.0 %own.1 = (bf16[128,1152]{1,0:T(8,128)(2,1)S(1)}, f32[64,1024]{1,0:T(8,128)S(1)}) custom-call(bf16[64,1024]{1,0:T(8,128)(2,1)S(1)} %candidate.1.earlier_ref, bf16[128,1024]{1,0:T(8,128)(2,1)S(1)} %get-tuple-element.21.a_ref.own_ref.refs_0_.main_ref, bf16[16,640]{1,0:T(8,128)(2,1)S(1)} %halo.1.earlier_ref.halo_ref), custom_call_target="tpu_custom_call" | custom-call | tf_op jit(solution)/shard_map/own/pallas_call | solution.py:375
  20.7 0.0 collective-permute-done.7.halo_ref
  20.8 1.3 %beside.1 = (bf16[128,1152]{1,0:T(8,128)(2,1)S(1)}, f32[64,1024]{1,0:T(8,128)S(1)}, bf16[64,1024]{1,0:T(8,128)(2,1)S(1)}) custom-call(bf16[128,1152]{1,0:T(8,128)(2,1)S(1)} %get-tuple-element.27.own_ref, f32[64,1024]{1,0:T(8,128)S(1)} %get-tuple-element.28.own_power_ref, bf16[128,1024]{1,0:T(8,128)(2,1)S(1)} %collective-permute-done.b_ref.refs_1_.main_ref, ...), custom_call_target="tpu_custom_call" | custom-call | tf_op jit(solution)/shard_map/beside/pallas_call | solution.py:375
  22.1 0.6 %collective-permute-done.8.halo_ref = bf16[16,640]{1,0:T(8,128)(2,1)S(1)} collective-permute-done((bf16[16,640]{1,0:T(8,128)(2,1)S(1)}, bf16[16,640]{1,0:T(8,128)(2,1)S(1)}, u32[]{:S(2)}, u32[]{:S(2)}) %collective-permute-start.8) | collective-permute-done | bytes 20512 | tf_op jit(solution)/shard_map/ppermute | solution.py:358
  22.7 1.3 %near.1 = (bf16[128,1152]{1,0:T(8,128)(2,1)S(1)}, f32[64,1024]{1,0:T(8,128)S(1)}, bf16[64,1024]{1,0:T(8,128)(2,1)S(1)}) custom-call(bf16[128,1152]{1,0:T(8,128)(2,1)S(1)} %get-tuple-element.30.own_ref, f32[64,1024]{1,0:T(8,128)S(1)} %get-tuple-element.31.own_power_ref, bf16[128,1024]{1,0:T(8,128)(2,1)S(1)} %pass.1.a_ref.refs_2_.main_ref, ...), custom_call_target="tpu_custom_call" | custom-call | tf_op jit(solution)/shard_map/near/pallas_call | solution.py:375
  24.0 0.0 collective-permute-done.4.b_ref.refs_3_.main_ref
  24.0 0.3 later.1
  24.3 1.6 %collective-permute-start.5 = (bf16[64,1024]{1,0:T(8,128)(2,1)S(1)}, bf16[64,1024]{1,0:T(8,128)(2,1)S(1)}, u32[]{:S(2)}, u32[]{:S(2)}) collective-permute-start(bf16[64,1024]{1,0:T(8,128)(2,1)S(1)} %later.1), channel_id=1, source_target_pairs={{0,4},{4,0},{8,12},{12,8},{16,20},{20,16},{24,28},{28,24},{1,5},{5... | collective-permute-start | bytes 393224 | tf_op jit(solution)/shard_map/ppermute | solution.py:362
  25.9 0.0 copy-start
  25.9 0.6 %collective-permute-start.10 = (bf16[64,1024]{1,0:T(8,128)(2,1)S(1)}, bf16[64,1024]{1,0:T(8,128)(2,1)S(1)}, u32[]{:S(2)}, u32[]{:S(2)}) collective-permute-start(bf16[64,1024]{1,0:T(8,128)(2,1)S(1)} %get-tuple-element.36), channel_id=1, source_target_pairs={{0,4},{4,0},{8,12},{12,8},{16,20},{20,16},{24,28},{28,24},{1,5},{5... | collective-permute-start | bytes 393224 | tf_op jit(solution)/shard_map/ppermute | solution.py:362
  26.4 0.0 collective-permute-done.9.halo_ref
  26.4 1.3 %far.1 = (bf16[128,1152]{1,0:T(8,128)(2,1)S(1)}, f32[64,1024]{1,0:T(8,128)S(1)}, bf16[64,1024]{1,0:T(8,128)(2,1)S(1)}) custom-call(bf16[128,1152]{1,0:T(8,128)(2,1)S(1)} %get-tuple-element.30.own_ref, f32[64,1024]{1,0:T(8,128)S(1)} %get-tuple-element.31.own_power_ref, bf16[128,1024]{1,0:T(8,128)(2,1)S(1)} %collective-permute-done.4.b_ref.refs_3_.main_ref, ...), custom_call_target="tpu_custom_call" | custom-call | tf_op jit(solution)/shard_map/far/pallas_call | solution.py:375
  27.8 1.6 %collective-permute-start.11 = (bf16[64,1024]{1,0:T(8,128)(2,1)S(1)}, bf16[64,1024]{1,0:T(8,128)(2,1)S(1)}, u32[]{:S(2)}, u32[]{:S(2)}) collective-permute-start(bf16[64,1024]{1,0:T(8,128)(2,1)S(1)} %get-tuple-element.37), channel_id=1, source_target_pairs={{0,4},{4,0},{8,12},{12,8},{16,20},{20,16},{24,28},{28,24},{1,5},{5... | collective-permute-start | bytes 393224 | tf_op jit(solution)/shard_map/ppermute | solution.py:362
  29.3 0.0 copy-done
  29.3 0.0 copy-done.1
  29.4 0.0 copy-done.2
  29.4 0.0 copy-done.3
  29.4 1.2 %spectrum.1 = (f32[128,1024]{1,0:T(8,128)S(1)}, f32[8,128]{1,0:T(8,128)S(1)}) custom-call(bf16[128,1024]{1,0:T(8,128)(2,1)S(1)} %get-tuple-element.21.a_ref.own_ref.refs_0_.main_ref, bf16[128,192]{1,0:T(8,128)(2,1)S(1)} %copy-done.2, bf16[256,256]{1,0:T(8,128)(2,1)S(1)} %copy-done.1, bf16[64,256]{1,0:T(8,128)(2,1)S(1)} %copy-done.3, bf16[512,256]{1,0:T(8,128)(2,1)S(1)} %copy-done), custom_call_target="tpu_custom_call" | custom-call | tf_op jit(solution)/shard_map/spectrum/pallas_call | solution.py:375
  30.6 0.5 %two.1.two_ref = bf16[64,1024]{1,0:T(8,128)(2,1)S(1)} custom-call(bf16[128,1152]{1,0:T(8,128)(2,1)S(1)} %get-tuple-element.27.own_ref, f32[64,1024]{1,0:T(8,128)S(1)} %get-tuple-element.28.own_power_ref, bf16[128,1152]{1,0:T(8,128)(2,1)S(1)} %get-tuple-element.32.ext_ref, f32[64,1024]{1,0:T(8,128)S(1)} %get-tuple-element.33.power_ref), custom_call_target="tpu_custom_call" | custom-call | tf_op jit(solution)/shard_map/two/pallas_call | solution.py:375
  31.1 0.5 %four.1.four_ref = bf16[64,1024]{1,0:T(8,128)(2,1)S(1)} custom-call(bf16[128,1152]{1,0:T(8,128)(2,1)S(1)} %get-tuple-element.27.own_ref, f32[64,1024]{1,0:T(8,128)S(1)} %get-tuple-element.28.own_power_ref, bf16[128,1152]{1,0:T(8,128)(2,1)S(1)} %get-tuple-element.34.ext_ref, f32[64,1024]{1,0:T(8,128)S(1)} %get-tuple-element.35.power_ref), custom_call_target="tpu_custom_call" | custom-call | tf_op jit(solution)/shard_map/four/pallas_call | solution.py:375
  31.5 0.0 collective-permute-done.6.refs_5_
  31.6 0.0 collective-permute-done.5.refs_4_
  31.6 2.5 %surface.1 = f32[16,1024]{1,0:T(8,128)} custom-call(f32[16,128]{1,0:T(8,128)S(1)} %get-tuple-element.20.cond_ref, bf16[128,1024]{1,0:T(8,128)(2,1)S(1)} %get-tuple-element.21.a_ref.own_ref.refs_0_.main_ref, bf16[128,1024]{1,0:T(8,128)(2,1)S(1)} %collective-permute-done.b_ref.refs_1_.main_ref, bf16[128,1024]{1,0:T(8,128)(2,1)S(1)} %pass.1.a_ref.refs_2_.main_ref, ...), custom_call_target="tpu_custom_call" | custom-call | tf_op jit(solution)/shard_map/surface/pallas_call | solution.py:375
  34.1 0.0 collective-permute-done.10.near_ref
  34.1 0.2 collective-permute-done.11.far_ref
  34.3 1.0 %place.1 = bf16[4,64,1024]{2,1,0:T(8,128)(2,1)} custom-call(f32[16,128]{1,0:T(8,128)S(1)} %get-tuple-element.20.cond_ref, bf16[64,1024]{1,0:T(8,128)(2,1)S(1)} %get-tuple-element.29.beside_ref, bf16[64,1024]{1,0:T(8,128)(2,1)S(1)} %two.1.two_ref, bf16[64,1024]{1,0:T(8,128)(2,1)S(1)} %four.1.four_ref, bf16[64,1024]{1,0:T(8,128)(2,1)S(1)} %collective-permute-done.10.near_ref, ...), custom_call_target="tpu_custom_call" | custom-call | tf_op jit(solution)/shard_map/place/pallas_call | solution.py:375
  (4 shorter events, 0.0 us)
Async XLA Ops:
  0.6 11.0 %collective-permute-start.3 = (bf16[128,1024]{1,0:T(8,128)(2,1)}, bf16[128,1024]{1,0:T(8,128)(2,1)S(1)}, u32[]{:S(2)}, u32[]{:S(2)}) collective-permute-start(bf16[128,1024]{1,0:T(8,128)(2,1)} %bitcast.own_hbm), channel_id=1, source_target_pairs={{0,24},{4,28},{8,0},{12,4},{16,8},{20,12},{24,16},{28,20},{1,25},{... | collective-permute-start | bytes 786440 | tf_op jit(solution)/shard_map/ppermute | solution.py:358
  6.4 0.7 %copy-start.4 = (s32[1,1,16]{2,1,0:T(1,128)S(1)}, s32[1,1,16]{2,1,0:T(1,128)}, u32[]{:S(2)}) copy-start(s32[1,1,16]{2,1,0:T(1,128)} %param.11) | copy-start | bytes 196
  6.4 0.7 %copy-start.5 = (f32[1,1,16]{2,1,0:T(1,128)S(1)}, f32[1,1,16]{2,1,0:T(1,128)}, u32[]{:S(2)}) copy-start(f32[1,1,16]{2,1,0:T(1,128)} %param.12) | copy-start | bytes 196
  6.4 0.7 %copy-start.6 = (s32[1,4]{1,0:T(1,128)S(1)}, s32[1,4]{1,0:T(1,128)}, u32[]{:S(2)}) copy-start(s32[1,4]{1,0:T(1,128)} %partners_hbm.1) | copy-start | bytes 52
  8.1 3.4 %collective-permute-start.1 = (bf16[144,128]{1,0:T(8,128)(2,1)S(1)}, bf16[144,128]{1,0:T(8,128)(2,1)S(1)}, u32[]{:S(2)}, u32[]{:S(2)}) collective-permute-start(bf16[144,128]{1,0:T(8,128)(2,1)S(1)} %get-tuple-element.23), channel_id=1, source_target_pairs={{0,1},{1,2},{2,3},{3,0},{4,5},{5,6},{6,7},{7,4},{8,9},{9,10},{10,1... | collective-permute-start | bytes 110600 | tf_op jit(solution)/shard_map/ppermute | solution.py:358
  8.2 3.4 %collective-permute-start.2 = (bf16[144,128]{1,0:T(8,128)(2,1)S(1)}, bf16[144,128]{1,0:T(8,128)(2,1)S(1)}, u32[]{:S(2)}, u32[]{:S(2)}) collective-permute-start(bf16[144,128]{1,0:T(8,128)(2,1)S(1)} %get-tuple-element.24), channel_id=1, source_target_pairs={{0,3},{1,0},{2,1},{3,2},{4,7},{5,4},{6,5},{7,6},{8,11},{9,8},{10,9... | collective-permute-start | bytes 110600 | tf_op jit(solution)/shard_map/ppermute | solution.py:358
  9.9 8.5 %collective-permute-start = (bf16[128,1024]{1,0:T(8,128)(2,1)}, bf16[128,1024]{1,0:T(8,128)(2,1)S(1)}, u32[]{:S(2)}, u32[]{:S(2)}) collective-permute-start(bf16[128,1024]{1,0:T(8,128)(2,1)} %bitcast.own_hbm), channel_id=1, source_target_pairs={{0,4},{4,0},{8,12},{12,8},{16,20},{20,16},{24,28},{28,24},{1,5},{5... | collective-permute-start | bytes 786440 | tf_op jit(solution)/shard_map/ppermute | solution.py:362
  11.7 12.3 %collective-permute-start.4 = (bf16[128,1024]{1,0:T(8,128)(2,1)S(1)}, bf16[128,1024]{1,0:T(8,128)(2,1)S(1)}, u32[]{:S(2)}, u32[]{:S(2)}) collective-permute-start(bf16[128,1024]{1,0:T(8,128)(2,1)S(1)} %pass.1.a_ref.refs_2_.main_ref), channel_id=1, source_target_pairs={{0,24},{4,28},{8,0},{12,4},{16,8},{20,12},{24,16},{28,20},{1,25},{... | collective-permute-start | bytes 786440 | tf_op jit(solution)/shard_map/ppermute | solution.py:358
  15.9 4.9 %collective-permute-start.7 = (bf16[16,640]{1,0:T(8,128)(2,1)S(1)}, bf16[16,640]{1,0:T(8,128)(2,1)S(1)}, u32[]{:S(2)}, u32[]{:S(2)}) collective-permute-start(bf16[16,640]{1,0:T(8,128)(2,1)S(1)} %halo.1.earlier_ref.halo_ref), channel_id=1, source_target_pairs={{0,4},{4,0},{8,12},{12,8},{16,20},{20,16},{24,28},{28,24},{1,5},{5... | collective-permute-start | bytes 61448 | tf_op jit(solution)/shard_map/ppermute | solution.py:362
  17.4 5.3 %collective-permute-start.8 = (bf16[16,640]{1,0:T(8,128)(2,1)S(1)}, bf16[16,640]{1,0:T(8,128)(2,1)S(1)}, u32[]{:S(2)}, u32[]{:S(2)}) collective-permute-start(bf16[16,640]{1,0:T(8,128)(2,1)S(1)} %halo.1.earlier_ref.halo_ref), channel_id=1, source_target_pairs={{0,24},{4,28},{8,0},{12,4},{16,8},{20,12},{24,16},{28,20},{1,25},{... | collective-permute-start | bytes 61448 | tf_op jit(solution)/shard_map/ppermute | solution.py:358
  17.5 9.0 %collective-permute-start.9 = (bf16[16,640]{1,0:T(8,128)(2,1)S(1)}, bf16[16,640]{1,0:T(8,128)(2,1)S(1)}, u32[]{:S(2)}, u32[]{:S(2)}) collective-permute-start(bf16[16,640]{1,0:T(8,128)(2,1)S(1)} %halo.1.earlier_ref.halo_ref), channel_id=1, source_target_pairs={{0,16},{4,20},{8,24},{12,28},{16,0},{20,4},{24,8},{28,12},{1,17},{... | collective-permute-start | bytes 61448 | tf_op jit(solution)/shard_map/ppermute | solution.py:358
  18.7 12.9 %collective-permute-start.6 = (bf16[64,1024]{1,0:T(8,128)(2,1)S(1)}, bf16[64,1024]{1,0:T(8,128)(2,1)S(1)}, u32[]{:S(2)}, u32[]{:S(2)}) collective-permute-start(bf16[64,1024]{1,0:T(8,128)(2,1)S(1)} %candidate.1.earlier_ref), channel_id=1, source_target_pairs={{0,8},{4,12},{8,16},{12,20},{16,24},{20,28},{24,0},{28,4},{1,9},{5... | collective-permute-start | bytes 393224 | tf_op jit(solution)/shard_map/ppermute | solution.py:358
  24.3 7.3 %collective-permute-start.5 = (bf16[64,1024]{1,0:T(8,128)(2,1)S(1)}, bf16[64,1024]{1,0:T(8,128)(2,1)S(1)}, u32[]{:S(2)}, u32[]{:S(2)}) collective-permute-start(bf16[64,1024]{1,0:T(8,128)(2,1)S(1)} %later.1), channel_id=1, source_target_pairs={{0,4},{4,0},{8,12},{12,8},{16,20},{20,16},{24,28},{28,24},{1,5},{5... | collective-permute-start | bytes 393224 | tf_op jit(solution)/shard_map/ppermute | solution.py:362
  25.9 3.5 %copy-start = (bf16[512,256]{1,0:T(8,128)(2,1)S(1)}, bf16[512,256]{1,0:T(8,128)(2,1)}, u32[]{:S(2)}) copy-start(bf16[512,256]{1,0:T(8,128)(2,1)} %constant.11.clone.fourth_ref.refs_11_) | copy-start | bytes 786436
  25.9 3.5 %copy-start.1 = (bf16[256,256]{1,0:T(8,128)(2,1)S(1)}, bf16[256,256]{1,0:T(8,128)(2,1)}, u32[]{:S(2)}) copy-start(bf16[256,256]{1,0:T(8,128)(2,1)} %constant.9.clone.second_ref.refs_9_) | copy-start | bytes 393220
  25.9 3.5 %copy-start.2 = (bf16[128,192]{1,0:T(8,128)(2,1)S(1)}, bf16[128,192]{1,0:T(8,128)(2,1)}, u32[]{:S(2)}) copy-start(bf16[128,192]{1,0:T(8,128)(2,1)} %constant.8.clone.first_ref.refs_8_) | copy-start | bytes 147460
  25.9 3.5 %copy-start.3 = (bf16[64,256]{1,0:T(8,128)(2,1)S(1)}, bf16[64,256]{1,0:T(8,128)(2,1)}, u32[]{:S(2)}) copy-start(bf16[64,256]{1,0:T(8,128)(2,1)} %constant.10.clone.third_ref.refs_10_) | copy-start | bytes 98308
  25.9 8.2 %collective-permute-start.10 = (bf16[64,1024]{1,0:T(8,128)(2,1)S(1)}, bf16[64,1024]{1,0:T(8,128)(2,1)S(1)}, u32[]{:S(2)}, u32[]{:S(2)}) collective-permute-start(bf16[64,1024]{1,0:T(8,128)(2,1)S(1)} %get-tuple-element.36), channel_id=1, source_target_pairs={{0,4},{4,0},{8,12},{12,8},{16,20},{20,16},{24,28},{28,24},{1,5},{5... | collective-permute-start | bytes 393224 | tf_op jit(solution)/shard_map/ppermute | solution.py:362
  27.8 6.5 %collective-permute-start.11 = (bf16[64,1024]{1,0:T(8,128)(2,1)S(1)}, bf16[64,1024]{1,0:T(8,128)(2,1)S(1)}, u32[]{:S(2)}, u32[]{:S(2)}) collective-permute-start(bf16[64,1024]{1,0:T(8,128)(2,1)S(1)} %get-tuple-element.37), channel_id=1, source_target_pairs={{0,4},{4,0},{8,12},{12,8},{16,20},{20,16},{24,28},{28,24},{1,5},{5... | collective-permute-start | bytes 393224 | tf_op jit(solution)/shard_map/ppermute | solution.py:362

commit v4 on v3

--- a/solution.py
+++ b/solution.py
@@ -55,17 +55,17 @@
 
 
 def prep_kernel(
-    own_hbm, off_hbm, frac_hbm, ref_hbm, partners_hbm, own_ref, cond_ref, taps_ref, low_ref, high_ref, *scratch
+    own_hbm, off_hbm, frac_hbm, partners_hbm, ref_ref, own_ref, cond_ref, taps_ref, low_ref, high_ref, *scratch
 ):
-    off_ref, frac_ref, ref_ref, partners_ref, sems = scratch
-    sources = (own_hbm, off_hbm, frac_hbm, ref_hbm, partners_hbm)
-    targets = (own_ref, off_ref, frac_ref, ref_ref, partners_ref)
+    off_ref, frac_ref, partners_ref, sems = scratch
+    sources = (own_hbm, off_hbm, frac_hbm, partners_hbm)
+    targets = (own_ref.at[0 : own_hbm.shape[0]], off_ref, frac_ref, partners_ref)
     copies = [pltpu.make_async_copy(s, t, sems.at[k]) for k, (s, t) in enumerate(zip(sources, targets))]
     for copy in copies:
         copy.start()
     for copy in copies[1:]:
         copy.wait()
-    rows, cols = own_ref.shape[0] // 2, own_ref.shape[1]
+    rows, cols = own_hbm.shape[0] // 2, own_ref.shape[1]
     blocks = cols // BLK
     date, dates = lax.axis_index("date"), lax.axis_size("date")
     place, places = lax.axis_index("rng"), lax.axis_size("rng")
@@ -91,22 +91,24 @@
     low_ref[2 * rows :, :] = dot(small, (block == 0).astype(BF16)).astype(BF16)
     high_ref[2 * rows :, :] = dot(small, (block == blocks - 1).astype(BF16)).astype(BF16)
     copies[0].wait()
-    low_ref[0 : 2 * rows, :] = own_ref[:, 0:LANES]
-    high_ref[0 : 2 * rows, :] = own_ref[:, cols - LANES :]
+    low_ref[0 : 2 * rows, :] = own_ref[0 : 2 * rows, 0:LANES]
+    high_ref[0 : 2 * rows, :] = own_ref[0 : 2 * rows, cols - LANES :]
 
 
 def candidate_kernel(first, cond_ref, a_ref, b_ref, amp_ref):
     rows = amp_ref.shape[0]
     at = PICK + first
     a, b = cond_ref[at : at + 1, 0:1] > 0.0, cond_ref[at + 1 : at + 2, 0:1] > 0.0
-    value = jnp.where(b, b_ref[...].astype(F32), a_ref[...].astype(F32))
+    value = jnp.where(b, b_ref[0 : 2 * rows, :].astype(F32), a_ref[0 : 2 * rows, :].astype(F32))
     value = amplitude(value[0:rows], value[rows:])
     amp_ref[...] = jnp.where(a | b, value.astype(F32), 0.0).astype(BF16)
 
 
-def pass_kernel(earlier_ref, in_ref, out_ref):
-    del earlier_ref
-    out_ref[...] = in_ref[...]
+def join_kernel(halo_ref, main_ref, both_ref):
+    rows, width = main_ref.shape[0], halo_ref.shape[1]
+    both_ref[0:rows, :] = main_ref[...]
+    both_ref[rows:, 0:width] = halo_ref[...]
+    both_ref[rows:, width:] = jnp.zeros((HROWS, both_ref.shape[1] - width), BF16)
 
 
 def halo_kernel(blocks, cond_ref, taps_ref, left_ref, right_ref, out_ref):
@@ -128,7 +130,9 @@
 
 
 def resample(main_ref, halo_ref, use):
-    rows, cols = main_ref.shape[0] // 2, main_ref.shape[1]
+    rows, cols = main_ref.shape[0] // (2 * HROWS) * HROWS, main_ref.shape[1]
+    rows -= rows % BLK
+    main_ref, halo_ref = main_ref.at[0 : 2 * rows], halo_ref.at[halo_ref.shape[0] - HROWS :]
     tiles = cols // LANES
     groups = rows // HROWS
     edge = jnp.concatenate([halo_ref[:, k * LANES : (k + 1) * LANES] for k in range(groups)], axis=0).astype(F32)
@@ -220,6 +224,11 @@
         out_ref[:, lanes] = coherence(sums, own_power_ref[:, lanes], power)
 
 
+def beside_kernel(earlier_ref, *refs):
+    del earlier_ref
+    pair_kernel(*refs)
+
+
 def again_kernel(own_ref, own_power_ref, ext_ref, power_ref, out_ref, fields_ref):
     rows, cols = out_ref.shape
     for p in range(cols // LANES + 1):
@@ -232,17 +241,25 @@
         out_ref[:, lanes] = coherence(sums, own_power_ref[:, lanes], power_ref[:, lanes])
 
 
-def place_kernel(cond_ref, beside_ref, two_ref, four_ref, near_ref, far_ref, out_ref):
+def place_kernel(
+    cond_ref, surface_ref, beside_ref, two_ref, four_ref, near_ref, far_ref, surface_hbm, out_hbm, out_ref, sems
+):
+    copies = [pltpu.make_async_copy(surface_ref, surface_hbm, sems.at[SPAN])]
+    copies += [pltpu.make_async_copy(out_ref.at[h], out_hbm.at[h], sems.at[h]) for h in range(SPAN)]
+    copies[0].start()
     even = cond_ref[EVEN : EVEN + 1, 0:1] > 0.0
     near = near_ref[...].astype(F32)
     fields = [
-        jnp.where(even, beside_ref[...].astype(F32), near),
-        two_ref[...].astype(F32),
-        jnp.where(even, near, far_ref[...].astype(F32)),
-        four_ref[...].astype(F32),
+        lambda: jnp.where(even, beside_ref[...].astype(F32), near),
+        lambda: two_ref[...].astype(F32),
+        lambda: jnp.where(even, near, far_ref[...].astype(F32)),
+        lambda: four_ref[...].astype(F32),
     ]
     for h, value in enumerate(fields):
-        out_ref[h] = (value * cond_ref[h : h + 1, 0:1]).astype(BF16)
+        out_ref[h] = (value() * cond_ref[h : h + 1, 0:1]).astype(BF16)
+        copies[1 + h].start()
+    for copy in copies:
+        copy.wait()
 
 
 def split(table):
@@ -284,21 +301,27 @@
     for p, value in enumerate(values):
         rows_ref[p : p + 1, :] = jnp.sum(value, axis=0, keepdims=True)
     mean = jnp.dot(rows_ref[...], group, precision=HIGHEST) / (BLK * BLK)
+    parts = [[], []]
     for p, value in enumerate(values):
         value = value - mean[p : p + 1, :]
         rows_ref[p : p + 1, :] = jnp.sum(value * value, axis=0, keepdims=True)
-        high = value.astype(BF16)
-        low = (value - high.astype(F32)).astype(BF16)
-        f = dot(first_ref[...], jnp.concatenate([high, high, low], axis=0)).astype(BF16)
-        s = dot(jnp.concatenate([f, f], axis=1), second_ref[...])
-        use(p, s[0:size, 0:LANES] + s[size:, LANES:], s[size:, 0:LANES] - s[0:size, LANES:])
+        parts[0].append(value.astype(BF16))
+        parts[1].append((value - parts[0][p].astype(F32)).astype(BF16))
+    high, low = (jnp.concatenate(part, axis=1) for part in parts)
+    f = dot(first_ref[...], jnp.concatenate([high, high, low], axis=0)).astype(BF16)
+    f = jnp.concatenate([f[:, p * LANES : (p + 1) * LANES] for p in range(tiles)], axis=0)
+    s = dot(jnp.concatenate([f, f], axis=1), second_ref[...])
+    for p in range(tiles):
+        at = 2 * size * p
+        top, bottom = s[at : at + size], s[at + size : at + 2 * size]
+        use(p, top[:, 0:LANES] + bottom[:, LANES:], bottom[:, 0:LANES] - top[:, LANES:])
     return jnp.dot(rows_ref[...], group, precision=HIGHEST)
 
 
 def spectrum_kernel(own_ref, first_ref, second_ref, third_ref, fourth_ref, spec_ref, energy_ref, amp_ref, rows_ref):
     del third_ref, fourth_ref
     size = amp_ref.shape[0]
-    amp_ref[...] = amplitude(own_ref[0:size, :], own_ref[size:, :])
+    amp_ref[...] = amplitude(own_ref[0:size, :], own_ref[size : 2 * size, :])
 
     def use(p, real, imag):
         lanes = slice(p * LANES, (p + 1) * LANES)
@@ -315,9 +338,9 @@
     size, cols = amp_ref.shape
     tiles = cols // LANES
     picks = [cond_ref[PICK + k : PICK + k + 1, 0:1] > 0.0 for k in range(len(samples) + 1)]
-    value = samples[0][...].astype(F32)
+    value = samples[0][0 : 2 * size, :].astype(F32)
     for pick, ref in zip(picks[1:4], samples[1:]):
-        value = jnp.where(pick, ref[...].astype(F32), value)
+        value = jnp.where(pick, ref[0 : 2 * size, :].astype(F32), value)
     found = functools.reduce(jnp.logical_or, picks[0:4])
     value = amplitude(value[0:size], value[size:]).astype(F32)
     other = jnp.where(picks[4], across_ref[...].astype(F32), before_ref[...].astype(F32))
@@ -332,11 +355,13 @@
     energy = spectrum(amp_ref, rows_ref, first_ref, second_ref, use)
     scale = 1.0 / (BLK * jnp.sqrt(energy_ref[...] * energy + 1e-06))
     lag_rows = [[] for _ in range(LANES // LAGS)]
+    cross = [cross_ref[:, p * LANES : (p + 1) * LANES] * scale[p : p + 1, :] for p in range(tiles)]
+    cross = jnp.concatenate([value.astype(BF16) for value in cross], axis=1)
+    lags = dot(third_ref[...], jnp.concatenate([cross, cross], axis=0))
     for p in range(tiles):
-        cross = (cross_ref[:, p * LANES : (p + 1) * LANES] * scale[p : p + 1, :]).astype(BF16)
-        lags = dot(third_ref[...], jnp.concatenate([cross, cross], axis=0))
         for q in range(LANES // LAGS):
-            part = [lags[ri * LAGS + q * 8 : ri * LAGS + q * 8 + 8] for ri in range(2)]
+            at = [ri * LAGS + q * 8 for ri in range(2)]
+            part = [lags[k : k + 8, p * LANES : (p + 1) * LANES] for k in at]
             lag_rows[q].append(jnp.concatenate(part, axis=1))
     lhs = jnp.concatenate([row for rows in lag_rows for row in rows], axis=0).astype(BF16)
     result = dot(jnp.concatenate([lhs, lhs], axis=1), fourth_ref[...])
@@ -391,22 +416,23 @@
     even = lax.axis_index("date") % 2 == 0
     field, samples = sds((rows, cols), BF16), sds((2 * rows, cols), BF16)
     payload = sds((2 * rows + HROWS, LANES), BF16)
+    inputs = (slc.reshape(2 * rows, cols), int_offset[0], frac_offset[0], partners)
+    inputs = [pltpu.with_memory_space_constraint(v, pltpu.HBM) for v in inputs]
     own, cond, taps, low, high = pl.pallas_call(
         prep_kernel,
-        out_shape=(samples, sds((16, LANES), F32), sds((HROWS, LANES), BF16), payload, payload),
-        in_specs=[pl.BlockSpec(memory_space=pltpu.HBM)] * 5,
+        out_shape=(sds((2 * rows + 32, cols), BF16), sds((16, LANES), F32), sds((HROWS, LANES), BF16), payload, payload),
+        in_specs=[pl.BlockSpec(memory_space=pltpu.HBM)] * 4 + [SMEM],
         out_specs=(VMEM,) * 5,
         scratch_shapes=[
             pltpu.VMEM(int_offset.shape[1:], jnp.int32),
             pltpu.VMEM(frac_offset.shape[1:], F32),
-            pltpu.SMEM(ref_date.shape, jnp.int32),
             pltpu.SMEM(partners.shape, jnp.int32),
-            pltpu.SemaphoreType.DMA((5,)),
+            pltpu.SemaphoreType.DMA((4,)),
         ],
         compiler_params=PARAMS,
         name="prepare",
-    )(slc.reshape(2 * rows, cols), int_offset[0], frac_offset[0], ref_date, partners)
-    beside = swapped(slc.reshape(2 * rows, cols), "date", 1)
+    )(*inputs, ref_date)
+    beside = swapped(own, "date", 1)
     two = shifted(slc.reshape(2 * rows, cols), "date", 2)
     right = shifted(low, "rng", 1)
     left = shifted(high, "rng", -1)
@@ -414,10 +440,9 @@
     halo = call(
         functools.partial(halo_kernel, cols // BLK), "halo", sds((HROWS, width), BF16), (cond, taps, left, right)
     )
-    two = call(pass_kernel, "pass", samples, (halo, two))
-    four = shifted(two, "date", 2)
+    joined = sds((2 * rows + HROWS, cols), BF16)
+    four = shifted(call(join_kernel, "join", joined, (halo, two)), "date", 2)
     beside_halo = swapped(halo, "date", 1)
-    two_halo = shifted(halo, "date", 2)
     four_halo = shifted(halo, "date", 4)
     amp = call(functools.partial(candidate_kernel, 0), "candidate", field, (cond, own, beside))
     before = shifted(amp, "date", -2) if dates == 8 else spread(amp, "date")
@@ -435,9 +460,9 @@
     scratch = [[((k * rows, cols + LANES), BF16)] for k in range(4)]
     own_ext = call(own_kernel, "own", resampled, (amp, own, halo), scratch[1])
     *beside_ext, coh_beside = call(
-        pair_kernel, "beside", (*resampled, field), (*own_ext, beside, beside_halo), scratch[3]
+        beside_kernel, "beside", (*resampled, field), (energy, *own_ext, beside, beside_halo), scratch[3]
     )
-    *two_ext, coh_near = call(pair_kernel, "near", (*resampled, field), (*beside_ext, two, two_halo), scratch[3])
+    *two_ext, coh_near = call(pair_kernel, "near", (*resampled, field), (*beside_ext, two, four), scratch[3])
     near = swapped(coh_near, "date", 1)
     coh_two = call(again_kernel, "two", field, (*own_ext, *two_ext), scratch[2])
     *four_ext, coh_far = call(pair_kernel, "far", (*resampled, field), (*beside_ext, four, four_halo), scratch[3])
@@ -455,12 +480,16 @@
             ((8 * cols // BLK, LANES), F32),
         ],
     )
-    fields = call(
+    operands = (cond, surface, coh_beside, coh_two, coh_four, near, far)
+    surface, fields = pl.pallas_call(
         place_kernel,
-        "place",
-        sds((SPAN, rows, cols), BF16),
-        (cond, coh_beside, coh_two, coh_four, near, far),
-    )
+        out_shape=(sds(surface.shape, F32), sds((SPAN, rows, cols), BF16)),
+        in_specs=[VMEM] * len(operands),
+        out_specs=(pl.BlockSpec(memory_space=pl.ANY),) * 2,
+        scratch_shapes=[pltpu.VMEM((SPAN, rows, cols), BF16), pltpu.SemaphoreType.DMA((SPAN + 1,))],
+        compiler_params=PARAMS,
+        name="place",
+    )(*operands)
     return (surface[None, None], fields[None])
 
 

time: 35.4 us -> 35 us (0.989)
  waiting for transfers between devices: 1.83 us -> 4.01 us
  Pallas kernels: 12.3 us -> 11.2 us
  starting transfers between devices: 19 us -> 18.1 us
  local copies, waits for them, and re-layouts: 0.68 us -> 0.02 us
    pallas_call x13 -> x12, Pallas kernels: 11.3 us -> 9.26 us  [call(): pl.pallas_call(kernel, out_shape=out_shape, in_specs=[VMEM] * len(operand...]
    ppermute x7 -> x6, waiting for transfers between devices: 0.72 us -> 1.94 us  [shifted(): lax.ppermute(value, axis, [(s, (s - steps) % count) for s in range(count)])]
    ppermute x5, waiting for transfers between devices: 1.11 us -> 2.07 us  [swapped(): lax.ppermute(value, axis, [(s, s ^ step) for s in range(lax.axis_size(axi...]
    pallas_call x1 -> x2, Pallas kernels: 1.01 us -> 1.95 us  [the longest x1 1.03 us: body(): pl.pallas_call(prep_kernel, out_shape=(sds((2 * rows + 32, cols), BF16),...]
    ppermute x7 -> x6, starting transfers between devices: 12.2 us -> 11.3 us  [shifted(): lax.ppermute(value, axis, [(s, (s - steps) % count) for s in range(count)])]
    unnamed x14 -> x8, local copies, waits for them, and re-layouts: 0.68 us -> 0.02 us
  transfers between devices with their start and end apart: 12 -> 11, of which waited for: 4 -> 6; matrix products, arithmetic and copies ran while one was open for 0% -> 0% of each run, Pallas kernels for 32% -> 30%
where the time goes in v4:
time: 35 us; the launch traced here: 34.8 us
  starting transfers between devices  18.1 us (52%)
  Pallas kernels  11.2 us (32%)
  waiting for transfers between devices  4.01 us (11%)
  between operations  1.44 us (4%)
    ppermute x6, starting transfers between devices, shifted(): lax.ppermute(value, axis, [(s, (s - steps) % count) for s in range(count)])  11.3 us
    pallas_call x12, Pallas kernels, call(): pl.pallas_call(kernel, out_shape=out_shape, in_specs=[VMEM] * len(operand...  9.26 us
    ppermute x5, starting transfers between devices, swapped(): lax.ppermute(value, axis, [(s, s ^ step) for s in range(lax.axis_size(axi...  6.82 us
    ppermute x5, waiting for transfers between devices, swapped(): lax.ppermute(value, axis, [(s, s ^ step) for s in range(lax.axis_size(axi...  2.07 us
    ppermute x6, waiting for transfers between devices, shifted(): lax.ppermute(value, axis, [(s, (s - steps) % count) for s in range(count)])  1.94 us
    pallas_call x1, Pallas kernels, body(): pl.pallas_call(prep_kernel, out_shape=(sds((2 * rows + 32, cols), BF16),...  1.03 us
    pallas_call x1, Pallas kernels, body(): pl.pallas_call(place_kernel, out_shape=(sds(surface.shape, F32), sds((SPA...  0.93 us
  transfers between devices with their start and end apart: 11, of which 6 were waited for; matrix products, arithmetic and copies ran while one was open for 0% of the time, Pallas kernels for 30%

profile of v4, /device:TPU:0, one launch (start us, length us, event | category | flops | bytes accessed | tf_op | source)
XLA Modules:
  0.0 34.8 jit_solution(10545137300933877942)
XLA Ops:
  0.6 5.1 %collective-permute-start.1 = (bf16[128,1024]{1,0:T(8,128)(2,1)}, bf16[128,1024]{1,0:T(8,128)(2,1)S(1)}, u32[]{:S(2)}, u32[]{:S(2)}) collective-permute-start(bf16[128,1024]{1,0:T(8,128)(2,1)} %bitcast.5), channel_id=1, source_target_pairs={{0,24},{4,28},{8,0},{12,4},{16,8},{20,12},{24,16},{28,20},{1,25},{... | collective-permute-start | bytes 786440 | tf_op jit(solution)/shard_map/ppermute | solution.py:383
  6.4 1.0 %prepare.1 = (bf16[160,1024]{1,0:T(8,128)(2,1)S(1)}, f32[16,128]{1,0:T(8,128)S(1)}, bf16[16,128]{1,0:T(8,128)(2,1)S(1)}, bf16[144,128]{1,0:T(8,128)(2,1)S(1)}, bf16[144,128]{1,0:T(8,128)(2,1)S(1)}) custom-call(bf16[128,1024]{1,0:T(8,128)(2,1)} %bitcast.6, s32[1,16]{1,0:T(1,128)} %bitcast.7, f32[1,16]{1,0:T(1,128)} %bitcast.8, s32[1,4]{1,0:T(1,128)} %partners_hbm.1, ...), custom_call_target="tpu_custom_call" | custom-call | tf_op jit(solution)/shard_map/prepare/pallas_call | solution.py:421
  7.4 0.1 collective-permute-start.2
  7.5 1.7 %collective-permute-start.3 = (bf16[144,128]{1,0:T(8,128)(2,1)S(1)}, bf16[144,128]{1,0:T(8,128)(2,1)S(1)}, u32[]{:S(2)}, u32[]{:S(2)}) collective-permute-start(bf16[144,128]{1,0:T(8,128)(2,1)S(1)} %get-tuple-element.26), channel_id=1, source_target_pairs={{0,3},{1,0},{2,1},{3,2},{4,7},{5,4},{6,5},{7,6},{8,11},{9,8},{10,9... | collective-permute-start | bytes 110600 | tf_op jit(solution)/shard_map/ppermute | solution.py:383
  9.2 1.5 %collective-permute-start = (bf16[160,1024]{1,0:T(8,128)(2,1)S(1)}, bf16[160,1024]{1,0:T(8,128)(2,1)S(1)}, u32[]{:S(2)}, u32[]{:S(2)}) collective-permute-start(bf16[160,1024]{1,0:T(8,128)(2,1)S(1)} %get-tuple-element.23.a_ref.own_ref.refs_0_.main_ref), channel_id=1, source_target_pairs={{0,4},{4,0},{8,12},{12,8},{16,20},{20,16},{24,28},{28,24},{1,5},{5... | collective-permute-start | bytes 983048 | tf_op jit(solution)/shard_map/ppermute | solution.py:387
  10.7 0.1 collective-permute-done.2.left_ref
  10.9 0.0 collective-permute-done.3.right_ref
  10.9 0.1 halo.1.halo_ref
  11.0 0.0 copy-start
  11.0 0.0 copy-start.1
  11.0 0.0 copy-start.2
  11.0 0.0 copy-start.3
  11.0 0.6 %collective-permute-done.1.main_ref.a_ref.refs_2_ = bf16[128,1024]{1,0:T(8,128)(2,1)S(1)} collective-permute-done((bf16[128,1024]{1,0:T(8,128)(2,1)}, bf16[128,1024]{1,0:T(8,128)(2,1)S(1)}, u32[]{:S(2)}, u32[]{:S(2)}) %collective-permute-start.1) | collective-permute-done | bytes 262176 | tf_op jit(solution)/shard_map/ppermute | solution.py:383
  11.6 4.2 %collective-permute-start.4 = (bf16[144,1024]{1,0:T(8,128)(2,1)S(1)}, bf16[144,1024]{1,0:T(8,128)(2,1)S(1)}, u32[]{:S(2)}, u32[]{:S(2)}) collective-permute-start(bf16[144,1024]{1,0:T(8,128)(2,1)S(1)} %join.1), channel_id=1, source_target_pairs={{0,24},{4,28},{8,0},{12,4},{16,8},{20,12},{24,16},{28,20},{1,25},{... | collective-permute-start | bytes 884744 | tf_op jit(solution)/shard_map/ppermute | solution.py:383
  15.9 1.5 %collective-permute-start.7 = (bf16[16,640]{1,0:T(8,128)(2,1)S(1)}, bf16[16,640]{1,0:T(8,128)(2,1)S(1)}, u32[]{:S(2)}, u32[]{:S(2)}) collective-permute-start(bf16[16,640]{1,0:T(8,128)(2,1)S(1)} %halo.1.halo_ref), channel_id=1, source_target_pairs={{0,4},{4,0},{8,12},{12,8},{16,20},{20,16},{24,28},{28,24},{1,5},{5... | collective-permute-start | bytes 61448 | tf_op jit(solution)/shard_map/ppermute | solution.py:387
  17.4 0.0 collective-permute-start.8
  17.4 0.0 copy-done
  17.4 0.0 copy-done.1
  17.4 0.0 copy-done.2
  17.4 0.0 copy-done.3
  17.4 1.0 %spectrum.1 = (f32[128,1024]{1,0:T(8,128)S(1)}, f32[8,128]{1,0:T(8,128)S(1)}) custom-call(bf16[160,1024]{1,0:T(8,128)(2,1)S(1)} %get-tuple-element.23.a_ref.own_ref.refs_0_.main_ref, bf16[128,192]{1,0:T(8,128)(2,1)S(1)} %copy-done.2, bf16[256,256]{1,0:T(8,128)(2,1)S(1)} %copy-done.1, bf16[64,256]{1,0:T(8,128)(2,1)S(1)} %copy-done.3, bf16[512,256]{1,0:T(8,128)(2,1)S(1)} %copy-done), custom_call_target="tpu_custom_call" | custom-call | tf_op jit(solution)/shard_map/spectrum/pallas_call | solution.py:400
  18.4 0.5 %collective-permute-done.b_ref.refs_1_.refs_2_ = bf16[160,1024]{1,0:T(8,128)(2,1)S(1)} collective-permute-done((bf16[160,1024]{1,0:T(8,128)(2,1)S(1)}, bf16[160,1024]{1,0:T(8,128)(2,1)S(1)}, u32[]{:S(2)}, u32[]{:S(2)}) %collective-permute-start) | collective-permute-done | bytes 327712 | tf_op jit(solution)/shard_map/ppermute | solution.py:387
  18.9 0.3 candidate.1.earlier_ref
  19.2 0.2 collective-permute-start.6
  19.4 1.0 %own.1 = (bf16[128,1152]{1,0:T(8,128)(2,1)S(1)}, f32[64,1024]{1,0:T(8,128)S(1)}) custom-call(bf16[64,1024]{1,0:T(8,128)(2,1)S(1)} %candidate.1.earlier_ref, bf16[160,1024]{1,0:T(8,128)(2,1)S(1)} %get-tuple-element.23.a_ref.own_ref.refs_0_.main_ref, bf16[16,640]{1,0:T(8,128)(2,1)S(1)} %halo.1.halo_ref), custom_call_target="tpu_custom_call" | custom-call | tf_op jit(solution)/shard_map/own/pallas_call | solution.py:400
  20.4 0.0 collective-permute-done.7.refs_3_
  20.4 1.3 %beside.1 = (bf16[128,1152]{1,0:T(8,128)(2,1)S(1)}, f32[64,1024]{1,0:T(8,128)S(1)}, bf16[64,1024]{1,0:T(8,128)(2,1)S(1)}) custom-call(f32[8,128]{1,0:T(8,128)S(1)} %get-tuple-element.28.refs_7_.earlier_ref, bf16[128,1152]{1,0:T(8,128)(2,1)S(1)} %get-tuple-element.29.refs_0_.own_ref, f32[64,1024]{1,0:T(8,128)S(1)} %get-tuple-element.30.refs_1_.own_power_ref, ...), custom_call_target="tpu_custom_call" | custom-call | tf_op jit(solution)/shard_map/beside/pallas_call | solution.py:400
  21.7 1.2 %collective-permute-done.4.b_ref.refs_3_.halo_ref.main_ref = bf16[144,1024]{1,0:T(8,128)(2,1)S(1)} collective-permute-done((bf16[144,1024]{1,0:T(8,128)(2,1)S(1)}, bf16[144,1024]{1,0:T(8,128)(2,1)S(1)}, u32[]{:S(2)}, u32[]{:S(2)}) %collective-permute-start.4) | collective-permute-done | bytes 294944 | tf_op jit(solution)/shard_map/ppermute | solution.py:383
  22.9 0.3 later.1
  23.2 1.6 %collective-permute-start.5 = (bf16[64,1024]{1,0:T(8,128)(2,1)S(1)}, bf16[64,1024]{1,0:T(8,128)(2,1)S(1)}, u32[]{:S(2)}, u32[]{:S(2)}) collective-permute-start(bf16[64,1024]{1,0:T(8,128)(2,1)S(1)} %later.1), channel_id=1, source_target_pairs={{0,4},{4,0},{8,12},{12,8},{16,20},{20,16},{24,28},{28,24},{1,5},{5... | collective-permute-start | bytes 393224 | tf_op jit(solution)/shard_map/ppermute | solution.py:387
  24.8 1.3 %near.1 = (bf16[128,1152]{1,0:T(8,128)(2,1)S(1)}, f32[64,1024]{1,0:T(8,128)S(1)}, bf16[64,1024]{1,0:T(8,128)(2,1)S(1)}) custom-call(bf16[128,1152]{1,0:T(8,128)(2,1)S(1)} %get-tuple-element.32.own_ref, f32[64,1024]{1,0:T(8,128)S(1)} %get-tuple-element.33.own_power_ref, bf16[128,1024]{1,0:T(8,128)(2,1)S(1)} %collective-permute-done.1.main_ref.a_ref.refs_2_, ...), custom_call_target="tpu_custom_call" | custom-call | tf_op jit(solution)/shard_map/near/pallas_call | solution.py:400
  26.2 0.5 %collective-permute-start.9 = (bf16[64,1024]{1,0:T(8,128)(2,1)S(1)}, bf16[64,1024]{1,0:T(8,128)(2,1)S(1)}, u32[]{:S(2)}, u32[]{:S(2)}) collective-permute-start(bf16[64,1024]{1,0:T(8,128)(2,1)S(1)} %get-tuple-element.38), channel_id=1, source_target_pairs={{0,4},{4,0},{8,12},{12,8},{16,20},{20,16},{24,28},{28,24},{1,5},{5... | collective-permute-start | bytes 393224 | tf_op jit(solution)/shard_map/ppermute | solution.py:387
  26.7 0.0 collective-permute-done.8.halo_ref
  26.7 1.3 %far.1 = (bf16[128,1152]{1,0:T(8,128)(2,1)S(1)}, f32[64,1024]{1,0:T(8,128)S(1)}, bf16[64,1024]{1,0:T(8,128)(2,1)S(1)}) custom-call(bf16[128,1152]{1,0:T(8,128)(2,1)S(1)} %get-tuple-element.32.own_ref, f32[64,1024]{1,0:T(8,128)S(1)} %get-tuple-element.33.own_power_ref, bf16[144,1024]{1,0:T(8,128)(2,1)S(1)} %collective-permute-done.4.b_ref.refs_3_.halo_ref.main_ref, ...), custom_call_target="tpu_custom_call" | custom-call | tf_op jit(solution)/shard_map/far/pallas_call | solution.py:400
  28.0 1.6 %collective-permute-start.10 = (bf16[64,1024]{1,0:T(8,128)(2,1)S(1)}, bf16[64,1024]{1,0:T(8,128)(2,1)S(1)}, u32[]{:S(2)}, u32[]{:S(2)}) collective-permute-start(bf16[64,1024]{1,0:T(8,128)(2,1)S(1)} %get-tuple-element.39), channel_id=1, source_target_pairs={{0,4},{4,0},{8,12},{12,8},{16,20},{20,16},{24,28},{28,24},{1,5},{5... | collective-permute-start | bytes 393224 | tf_op jit(solution)/shard_map/ppermute | solution.py:387
  29.6 0.5 %two.1.two_ref = bf16[64,1024]{1,0:T(8,128)(2,1)S(1)} custom-call(bf16[128,1152]{1,0:T(8,128)(2,1)S(1)} %get-tuple-element.29.refs_0_.own_ref, f32[64,1024]{1,0:T(8,128)S(1)} %get-tuple-element.30.refs_1_.own_power_ref, bf16[128,1152]{1,0:T(8,128)(2,1)S(1)} %get-tuple-element.34.ext_ref, f32[64,1024]{1,0:T(8,128)S(1)} %get-tuple-element.35.power_ref), custom_call_target="tpu_custom_call" | custom-call | tf_op jit(solution)/shard_map/two/pallas_call | solution.py:400
  30.1 0.5 %four.1.four_ref = bf16[64,1024]{1,0:T(8,128)(2,1)S(1)} custom-call(bf16[128,1152]{1,0:T(8,128)(2,1)S(1)} %get-tuple-element.29.refs_0_.own_ref, f32[64,1024]{1,0:T(8,128)S(1)} %get-tuple-element.30.refs_1_.own_power_ref, bf16[128,1152]{1,0:T(8,128)(2,1)S(1)} %get-tuple-element.36.ext_ref, f32[64,1024]{1,0:T(8,128)S(1)} %get-tuple-element.37.power_ref), custom_call_target="tpu_custom_call" | custom-call | tf_op jit(solution)/shard_map/four/pallas_call | solution.py:400
  30.6 0.0 collective-permute-done.6.refs_5_
  30.6 0.0 collective-permute-done.5.refs_4_
  30.6 1.7 %surface.1.surface_ref = f32[16,1024]{1,0:T(8,128)S(1)} custom-call(f32[16,128]{1,0:T(8,128)S(1)} %get-tuple-element.22.cond_ref, bf16[160,1024]{1,0:T(8,128)(2,1)S(1)} %get-tuple-element.23.a_ref.own_ref.refs_0_.main_ref, bf16[160,1024]{1,0:T(8,128)(2,1)S(1)} %collective-permute-done.b_ref.refs_1_.refs_2_, ...), custom_call_target="tpu_custom_call" | custom-call | tf_op jit(solution)/shard_map/surface/pallas_call | solution.py:400
  32.3 0.1 collective-permute-done.9.near_ref
  32.5 1.4 %collective-permute-done.10.far_ref = bf16[64,1024]{1,0:T(8,128)(2,1)S(1)} collective-permute-done((bf16[64,1024]{1,0:T(8,128)(2,1)S(1)}, bf16[64,1024]{1,0:T(8,128)(2,1)S(1)}, u32[]{:S(2)}, u32[]{:S(2)}) %collective-permute-start.10) | collective-permute-done | bytes 131104 | tf_op jit(solution)/shard_map/ppermute | solution.py:387
  33.9 0.9 %place.1 = (f32[16,1024]{1,0:T(8,128)}, bf16[4,64,1024]{2,1,0:T(8,128)(2,1)}) custom-call(f32[16,128]{1,0:T(8,128)S(1)} %get-tuple-element.22.cond_ref, f32[16,1024]{1,0:T(8,128)S(1)} %surface.1.surface_ref, bf16[64,1024]{1,0:T(8,128)(2,1)S(1)} %get-tuple-element.31.beside_ref, bf16[64,1024]{1,0:T(8,128)(2,1)S(1)} %two.1.two_ref, ...), custom_call_target="tpu_custom_call" | custom-call | tf_op jit(solution)/shard_map/place/pallas_call | solution.py:484
  (1 shorter events, 0.0 us)
Async XLA Ops:
  0.6 11.0 %collective-permute-start.1 = (bf16[128,1024]{1,0:T(8,128)(2,1)}, bf16[128,1024]{1,0:T(8,128)(2,1)S(1)}, u32[]{:S(2)}, u32[]{:S(2)}) collective-permute-start(bf16[128,1024]{1,0:T(8,128)(2,1)} %bitcast.5), channel_id=1, source_target_pairs={{0,24},{4,28},{8,0},{12,4},{16,8},{20,12},{24,16},{28,20},{1,25},{... | collective-permute-start | bytes 786440 | tf_op jit(solution)/shard_map/ppermute | solution.py:383
  7.4 3.4 %collective-permute-start.2 = (bf16[144,128]{1,0:T(8,128)(2,1)S(1)}, bf16[144,128]{1,0:T(8,128)(2,1)S(1)}, u32[]{:S(2)}, u32[]{:S(2)}) collective-permute-start(bf16[144,128]{1,0:T(8,128)(2,1)S(1)} %get-tuple-element.25), channel_id=1, source_target_pairs={{0,1},{1,2},{2,3},{3,0},{4,5},{5,6},{6,7},{7,4},{8,9},{9,10},{10,1... | collective-permute-start | bytes 110600 | tf_op jit(solution)/shard_map/ppermute | solution.py:383
  7.5 3.4 %collective-permute-start.3 = (bf16[144,128]{1,0:T(8,128)(2,1)S(1)}, bf16[144,128]{1,0:T(8,128)(2,1)S(1)}, u32[]{:S(2)}, u32[]{:S(2)}) collective-permute-start(bf16[144,128]{1,0:T(8,128)(2,1)S(1)} %get-tuple-element.26), channel_id=1, source_target_pairs={{0,3},{1,0},{2,1},{3,2},{4,7},{5,4},{6,5},{7,6},{8,11},{9,8},{10,9... | collective-permute-start | bytes 110600 | tf_op jit(solution)/shard_map/ppermute | solution.py:383
  9.2 9.7 %collective-permute-start = (bf16[160,1024]{1,0:T(8,128)(2,1)S(1)}, bf16[160,1024]{1,0:T(8,128)(2,1)S(1)}, u32[]{:S(2)}, u32[]{:S(2)}) collective-permute-start(bf16[160,1024]{1,0:T(8,128)(2,1)S(1)} %get-tuple-element.23.a_ref.own_ref.refs_0_.main_ref), channel_id=1, source_target_pairs={{0,4},{4,0},{8,12},{12,8},{16,20},{20,16},{24,28},{28,24},{1,5},{5... | collective-permute-start | bytes 983048 | tf_op jit(solution)/shard_map/ppermute | solution.py:387
  11.0 6.4 %copy-start = (bf16[512,256]{1,0:T(8,128)(2,1)S(1)}, bf16[512,256]{1,0:T(8,128)(2,1)}, u32[]{:S(2)}) copy-start(bf16[512,256]{1,0:T(8,128)(2,1)} %constant.11.clone.fourth_ref.refs_11_) | copy-start | bytes 786436
  11.0 6.4 %copy-start.1 = (bf16[256,256]{1,0:T(8,128)(2,1)S(1)}, bf16[256,256]{1,0:T(8,128)(2,1)}, u32[]{:S(2)}) copy-start(bf16[256,256]{1,0:T(8,128)(2,1)} %constant.9.clone.second_ref.refs_9_) | copy-start | bytes 393220
  11.0 6.4 %copy-start.2 = (bf16[128,192]{1,0:T(8,128)(2,1)S(1)}, bf16[128,192]{1,0:T(8,128)(2,1)}, u32[]{:S(2)}) copy-start(bf16[128,192]{1,0:T(8,128)(2,1)} %constant.8.clone.first_ref.refs_8_) | copy-start | bytes 147460
  11.0 6.4 %copy-start.3 = (bf16[64,256]{1,0:T(8,128)(2,1)S(1)}, bf16[64,256]{1,0:T(8,128)(2,1)}, u32[]{:S(2)}) copy-start(bf16[64,256]{1,0:T(8,128)(2,1)} %constant.10.clone.third_ref.refs_10_) | copy-start | bytes 98308
  11.6 11.3 %collective-permute-start.4 = (bf16[144,1024]{1,0:T(8,128)(2,1)S(1)}, bf16[144,1024]{1,0:T(8,128)(2,1)S(1)}, u32[]{:S(2)}, u32[]{:S(2)}) collective-permute-start(bf16[144,1024]{1,0:T(8,128)(2,1)S(1)} %join.1), channel_id=1, source_target_pairs={{0,24},{4,28},{8,0},{12,4},{16,8},{20,12},{24,16},{28,20},{1,25},{... | collective-permute-start | bytes 884744 | tf_op jit(solution)/shard_map/ppermute | solution.py:383
  15.9 4.5 %collective-permute-start.7 = (bf16[16,640]{1,0:T(8,128)(2,1)S(1)}, bf16[16,640]{1,0:T(8,128)(2,1)S(1)}, u32[]{:S(2)}, u32[]{:S(2)}) collective-permute-start(bf16[16,640]{1,0:T(8,128)(2,1)S(1)} %halo.1.halo_ref), channel_id=1, source_target_pairs={{0,4},{4,0},{8,12},{12,8},{16,20},{20,16},{24,28},{28,24},{1,5},{5... | collective-permute-start | bytes 61448 | tf_op jit(solution)/shard_map/ppermute | solution.py:387
  17.4 9.3 %collective-permute-start.8 = (bf16[16,640]{1,0:T(8,128)(2,1)S(1)}, bf16[16,640]{1,0:T(8,128)(2,1)S(1)}, u32[]{:S(2)}, u32[]{:S(2)}) collective-permute-start(bf16[16,640]{1,0:T(8,128)(2,1)S(1)} %halo.1.halo_ref), channel_id=1, source_target_pairs={{0,16},{4,20},{8,24},{12,28},{16,0},{20,4},{24,8},{28,12},{1,17},{... | collective-permute-start | bytes 61448 | tf_op jit(solution)/shard_map/ppermute | solution.py:383
  19.2 11.4 %collective-permute-start.6 = (bf16[64,1024]{1,0:T(8,128)(2,1)S(1)}, bf16[64,1024]{1,0:T(8,128)(2,1)S(1)}, u32[]{:S(2)}, u32[]{:S(2)}) collective-permute-start(bf16[64,1024]{1,0:T(8,128)(2,1)S(1)} %candidate.1.earlier_ref), channel_id=1, source_target_pairs={{0,8},{4,12},{8,16},{12,20},{16,24},{20,28},{24,0},{28,4},{1,9},{5... | collective-permute-start | bytes 393224 | tf_op jit(solution)/shard_map/ppermute | solution.py:383
  23.2 7.4 %collective-permute-start.5 = (bf16[64,1024]{1,0:T(8,128)(2,1)S(1)}, bf16[64,1024]{1,0:T(8,128)(2,1)S(1)}, u32[]{:S(2)}, u32[]{:S(2)}) collective-permute-start(bf16[64,1024]{1,0:T(8,128)(2,1)S(1)} %later.1), channel_id=1, source_target_pairs={{0,4},{4,0},{8,12},{12,8},{16,20},{20,16},{24,28},{28,24},{1,5},{5... | collective-permute-start | bytes 393224 | tf_op jit(solution)/shard_map/ppermute | solution.py:387
  26.2 6.3 %collective-permute-start.9 = (bf16[64,1024]{1,0:T(8,128)(2,1)S(1)}, bf16[64,1024]{1,0:T(8,128)(2,1)S(1)}, u32[]{:S(2)}, u32[]{:S(2)}) collective-permute-start(bf16[64,1024]{1,0:T(8,128)(2,1)S(1)} %get-tuple-element.38), channel_id=1, source_target_pairs={{0,4},{4,0},{8,12},{12,8},{16,20},{20,16},{24,28},{28,24},{1,5},{5... | collective-permute-start | bytes 393224 | tf_op jit(solution)/shard_map/ppermute | solution.py:387
  28.0 5.9 %collective-permute-start.10 = (bf16[64,1024]{1,0:T(8,128)(2,1)S(1)}, bf16[64,1024]{1,0:T(8,128)(2,1)S(1)}, u32[]{:S(2)}, u32[]{:S(2)}) collective-permute-start(bf16[64,1024]{1,0:T(8,128)(2,1)S(1)} %get-tuple-element.39), channel_id=1, source_target_pairs={{0,4},{4,0},{8,12},{12,8},{16,20},{20,16},{24,28},{28,24},{1,5},{5... | collective-permute-start | bytes 393224 | tf_op jit(solution)/shard_map/ppermute | solution.py:387

commit v5 on v4

--- a/solution.py
+++ b/solution.py
@@ -39,11 +39,12 @@
     top = 96
     rows = 2 * LANES - top
     step = iota((rows, LANES), 0) + top - iota((rows, LANES), 1) - (LANES - PAD - 3)
-    step = step.astype(F32) - table[TAPS : TAPS + 1, :]
-    out = jnp.zeros((rows, LANES), F32)
+    table = table.astype(BF16)
+    step = step.astype(F32).astype(BF16) - table[TAPS : TAPS + 1, :]
+    out = jnp.zeros((rows, LANES), BF16)
     for tap in range(TAPS):
-        out = jnp.where(step == float(tap), table[tap : tap + 1, :], out)
-    return jnp.concatenate([jnp.zeros((top, LANES), BF16), out.astype(BF16)], axis=0)
+        out = jnp.where(step == jnp.asarray(tap, BF16), table[tap : tap + 1, :], out)
+    return jnp.concatenate([jnp.zeros((top, LANES), BF16), out], axis=0)
 
 
 def amplitude(real, imag):
@@ -95,10 +96,9 @@
     high_ref[0 : 2 * rows, :] = own_ref[0 : 2 * rows, cols - LANES :]
 
 
-def candidate_kernel(first, cond_ref, a_ref, b_ref, amp_ref):
+def candidate_kernel(picks, cond_ref, a_ref, b_ref, amp_ref):
     rows = amp_ref.shape[0]
-    at = PICK + first
-    a, b = cond_ref[at : at + 1, 0:1] > 0.0, cond_ref[at + 1 : at + 2, 0:1] > 0.0
+    a, b = (cond_ref[PICK + k : PICK + k + 1, 0:1] > 0.0 for k in picks)
     value = jnp.where(b, b_ref[0 : 2 * rows, :].astype(F32), a_ref[0 : 2 * rows, :].astype(F32))
     value = amplitude(value[0:rows], value[rows:])
     amp_ref[...] = jnp.where(a | b, value.astype(F32), 0.0).astype(BF16)
@@ -161,9 +161,8 @@
     rows, lanes = field.shape
     base = jnp.concatenate([field, jnp.zeros((8, lanes), F32)], axis=0)
     two = base + pltpu.roll(base, 1, 0)
-    four = two + pltpu.roll(two, 2, 0)
-    five = four + pltpu.roll(base, 4, 0)
-    return pltpu.roll(five, rows + 8 - BOXA // 2, 0)[0:rows]
+    four = two + pltpu.roll(two, rows + 8 - BOXA // 2, 0)
+    return (four + pltpu.roll(base, BOXA // 2, 0))[0:rows]
 
 
 def keep_tile(ext_ref, p, real, imag):
@@ -189,6 +188,11 @@
     rows = own.shape[0]
     re, im = line_box(sums[0:rows]), line_box(sums[rows : 2 * rows])
     return ((re * re + im * im) / (own * partner + 1e-06)).astype(BF16)
+
+
+def late_candidate_kernel(picks, earlier_ref, *refs):
+    del earlier_ref
+    candidate_kernel(picks, *refs)
 
 
 def own_kernel(earlier_ref, main_ref, halo_ref, ext_ref, power_ref, fields_ref):
@@ -420,7 +424,7 @@
     inputs = [pltpu.with_memory_space_constraint(v, pltpu.HBM) for v in inputs]
     own, cond, taps, low, high = pl.pallas_call(
         prep_kernel,
-        out_shape=(sds((2 * rows + 32, cols), BF16), sds((16, LANES), F32), sds((HROWS, LANES), BF16), payload, payload),
+        out_shape=(sds((2 * rows + 16, cols), BF16), sds((16, LANES), F32), sds((HROWS, LANES), BF16), payload, payload),
         in_specs=[pl.BlockSpec(memory_space=pltpu.HBM)] * 4 + [SMEM],
         out_specs=(VMEM,) * 5,
         scratch_shapes=[
@@ -442,12 +446,10 @@
     )
     joined = sds((2 * rows + HROWS, cols), BF16)
     four = shifted(call(join_kernel, "join", joined, (halo, two)), "date", 2)
+    later = call(functools.partial(candidate_kernel, (0, 2)), "later", field, (cond, own, two))
+    across = lax.ppermute(later, "date", [(s, (s - 2) % dates ^ 1) for s in range(dates)])
     beside_halo = swapped(halo, "date", 1)
     four_halo = shifted(halo, "date", 4)
-    amp = call(functools.partial(candidate_kernel, 0), "candidate", field, (cond, own, beside))
-    before = shifted(amp, "date", -2) if dates == 8 else spread(amp, "date")
-    later = call(functools.partial(candidate_kernel, 2), "later", field, (cond, two, four))
-    across = swapped(later, "date", 1)
     first, second, third, fourth = [jnp.asarray(t) for t in surface_tables()]
     spec, energy = call(
         spectrum_kernel,
@@ -458,10 +460,12 @@
     )
     resampled = (sds((2 * rows, cols + LANES), BF16), sds((rows, cols), F32))
     scratch = [[((k * rows, cols + LANES), BF16)] for k in range(4)]
-    own_ext = call(own_kernel, "own", resampled, (amp, own, halo), scratch[1])
+    own_ext = call(own_kernel, "own", resampled, (energy, own, halo), scratch[1])
     *beside_ext, coh_beside = call(
         beside_kernel, "beside", (*resampled, field), (energy, *own_ext, beside, beside_halo), scratch[3]
     )
+    amp = call(functools.partial(late_candidate_kernel, (0, 1)), "candidate", field, (coh_beside, cond, own, beside))
+    before = shifted(amp, "date", -2) if dates == 8 else spread(amp, "date")
     *two_ext, coh_near = call(pair_kernel, "near", (*resampled, field), (*beside_ext, two, four), scratch[3])
     near = swapped(coh_near, "date", 1)
     coh_two = call(again_kernel, "two", field, (*own_ext, *two_ext), scratch[2])

time: 35 us -> 33 us (0.943)
  Pallas kernels: 11.2 us -> 10 us
  waiting for transfers between devices: 4.01 us -> 2.95 us
    ppermute x6, starting transfers between devices: 11.3 us -> 13 us  [shifted(): lax.ppermute(value, axis, [(s, (s - steps) % count) for s in range(count)])]
    ppermute x5 -> x4, starting transfers between devices: 6.82 us -> 5.19 us  [swapped(): lax.ppermute(value, axis, [(s, s ^ step) for s in range(lax.axis_size(axi...]
    ppermute x5 -> x4, waiting for transfers between devices: 2.07 us -> 0.65 us  [swapped(): lax.ppermute(value, axis, [(s, s ^ step) for s in range(lax.axis_size(axi...]
    pallas_call x12, Pallas kernels: 9.26 us -> 8.08 us  [call(): pl.pallas_call(kernel, out_shape=out_shape, in_specs=[VMEM] * len(operand...]
    ppermute x6, waiting for transfers between devices: 1.94 us -> 2.3 us  [shifted(): lax.ppermute(value, axis, [(s, (s - steps) % count) for s in range(count)])]
  transfers between devices with their start and end apart: 11 -> 11, of which waited for: 6 -> 5; matrix products, arithmetic and copies ran while one was open for 0% -> 0% of each run, Pallas kernels for 30% -> 28%
where the time goes in v5:
time: 33 us; the launch traced here: 32.8 us
  starting transfers between devices  18.4 us (56%)
  Pallas kernels  10 us (30%)
  waiting for transfers between devices  2.95 us (9%)
  between operations  1.43 us (4%)
    ppermute x6, starting transfers between devices, shifted(): lax.ppermute(value, axis, [(s, (s - steps) % count) for s in range(count)])  13 us
    pallas_call x12, Pallas kernels, call(): pl.pallas_call(kernel, out_shape=out_shape, in_specs=[VMEM] * len(operand...  8.08 us
    ppermute x4, starting transfers between devices, swapped(): lax.ppermute(value, axis, [(s, s ^ step) for s in range(lax.axis_size(axi...  5.19 us
    ppermute x6, waiting for transfers between devices, shifted(): lax.ppermute(value, axis, [(s, (s - steps) % count) for s in range(count)])  2.3 us
    pallas_call x1, Pallas kernels, body(): pl.pallas_call(prep_kernel, out_shape=(sds((2 * rows + 16, cols), BF16),...  1.03 us
    pallas_call x1, Pallas kernels, body(): pl.pallas_call(place_kernel, out_shape=(sds(surface.shape, F32), sds((SPA...  0.93 us
  transfers between devices with their start and end apart: 11, of which 5 were waited for; matrix products, arithmetic and copies ran while one was open for 0% of the time, Pallas kernels for 28%

profile of v5, /device:TPU:0, one launch (start us, length us, event | category | flops | bytes accessed | tf_op | source)
XLA Modules:
  0.0 32.8 jit_solution(12208703993336915504)
XLA Ops:
  0.6 5.1 %collective-permute-start.1 = (bf16[128,1024]{1,0:T(8,128)(2,1)}, bf16[128,1024]{1,0:T(8,128)(2,1)S(1)}, u32[]{:S(2)}, u32[]{:S(2)}) collective-permute-start(bf16[128,1024]{1,0:T(8,128)(2,1)} %bitcast.5), channel_id=1, source_target_pairs={{0,24},{4,28},{8,0},{12,4},{16,8},{20,12},{24,16},{28,20},{1,25},{... | collective-permute-start | bytes 786440 | tf_op jit(solution)/shard_map/ppermute | solution.py:387
  6.4 1.0 %prepare.1 = (bf16[144,1024]{1,0:T(8,128)(2,1)S(1)}, f32[16,128]{1,0:T(8,128)S(1)}, bf16[16,128]{1,0:T(8,128)(2,1)S(1)}, bf16[144,128]{1,0:T(8,128)(2,1)S(1)}, bf16[144,128]{1,0:T(8,128)(2,1)S(1)}) custom-call(bf16[128,1024]{1,0:T(8,128)(2,1)} %bitcast.6, s32[1,16]{1,0:T(1,128)} %bitcast.7, f32[1,16]{1,0:T(1,128)} %bitcast.8, s32[1,4]{1,0:T(1,128)} %partners_hbm.1, ...), custom_call_target="tpu_custom_call" | custom-call | tf_op jit(solution)/shard_map/prepare/pallas_call | solution.py:425
  7.4 0.1 collective-permute-start.2
  7.5 1.7 %collective-permute-start.3 = (bf16[144,128]{1,0:T(8,128)(2,1)S(1)}, bf16[144,128]{1,0:T(8,128)(2,1)S(1)}, u32[]{:S(2)}, u32[]{:S(2)}) collective-permute-start(bf16[144,128]{1,0:T(8,128)(2,1)S(1)} %get-tuple-element.26), channel_id=1, source_target_pairs={{0,3},{1,0},{2,1},{3,2},{4,7},{5,4},{6,5},{7,6},{8,11},{9,8},{10,9... | collective-permute-start | bytes 110600 | tf_op jit(solution)/shard_map/ppermute | solution.py:387
  9.2 1.5 %collective-permute-start = (bf16[144,1024]{1,0:T(8,128)(2,1)S(1)}, bf16[144,1024]{1,0:T(8,128)(2,1)S(1)}, u32[]{:S(2)}, u32[]{:S(2)}) collective-permute-start(bf16[144,1024]{1,0:T(8,128)(2,1)S(1)} %get-tuple-element.23.a_ref.own_ref.main_ref.refs_1_.refs_0_), channel_id=1, source_target_pairs={{0,4},{4,0},{8,12},{12,8},{16,20},{20,16},{24,28},{28,24},{1,5},{5... | collective-permute-start | bytes 884744 | tf_op jit(solution)/shard_map/ppermute | solution.py:391
  10.7 0.1 collective-permute-done.2.left_ref
  10.9 0.0 collective-permute-done.3.right_ref
  10.9 0.2 halo.1.halo_ref
  11.0 0.0 copy-start
  11.0 0.0 copy-start.1
  11.0 0.0 copy-start.2
  11.0 0.0 copy-start.3
  11.0 0.6 %collective-permute-done.1.main_ref.b_ref.refs_2_ = bf16[128,1024]{1,0:T(8,128)(2,1)S(1)} collective-permute-done((bf16[128,1024]{1,0:T(8,128)(2,1)}, bf16[128,1024]{1,0:T(8,128)(2,1)S(1)}, u32[]{:S(2)}, u32[]{:S(2)}) %collective-permute-start.1) | collective-permute-done | bytes 262176 | tf_op jit(solution)/shard_map/ppermute | solution.py:387
  11.6 4.2 %collective-permute-start.4 = (bf16[144,1024]{1,0:T(8,128)(2,1)S(1)}, bf16[144,1024]{1,0:T(8,128)(2,1)S(1)}, u32[]{:S(2)}, u32[]{:S(2)}) collective-permute-start(bf16[144,1024]{1,0:T(8,128)(2,1)S(1)} %join.1), channel_id=1, source_target_pairs={{0,24},{4,28},{8,0},{12,4},{16,8},{20,12},{24,16},{28,20},{1,25},{... | collective-permute-start | bytes 884744 | tf_op jit(solution)/shard_map/ppermute | solution.py:387
  15.9 1.5 %collective-permute-start.6 = (bf16[16,640]{1,0:T(8,128)(2,1)S(1)}, bf16[16,640]{1,0:T(8,128)(2,1)S(1)}, u32[]{:S(2)}, u32[]{:S(2)}) collective-permute-start(bf16[16,640]{1,0:T(8,128)(2,1)S(1)} %halo.1.halo_ref), channel_id=1, source_target_pairs={{0,4},{4,0},{8,12},{12,8},{16,20},{20,16},{24,28},{28,24},{1,5},{5... | collective-permute-start | bytes 61448 | tf_op jit(solution)/shard_map/ppermute | solution.py:391
  17.4 0.0 collective-permute-start.8
  17.4 0.0 copy-done
  17.4 0.0 copy-done.1
  17.4 0.0 copy-done.2
  17.4 0.0 copy-done.3
  17.4 1.0 %spectrum.1 = (f32[128,1024]{1,0:T(8,128)S(1)}, f32[8,128]{1,0:T(8,128)S(1)}) custom-call(bf16[144,1024]{1,0:T(8,128)(2,1)S(1)} %get-tuple-element.23.a_ref.own_ref.main_ref.refs_1_.refs_0_, bf16[128,192]{1,0:T(8,128)(2,1)S(1)} %copy-done.2, bf16[256,256]{1,0:T(8,128)(2,1)S(1)} %copy-done.1, bf16[64,256]{1,0:T(8,128)(2,1)S(1)} %copy-done.3, ...), custom_call_target="tpu_custom_call" | custom-call | tf_op jit(solution)/shard_map/spectrum/pallas_call | solution.py:404
  18.4 0.8 %own.1 = (bf16[128,1152]{1,0:T(8,128)(2,1)S(1)}, f32[64,1024]{1,0:T(8,128)S(1)}) custom-call(f32[8,128]{1,0:T(8,128)S(1)} %get-tuple-element.27.earlier_ref.refs_7_, bf16[144,1024]{1,0:T(8,128)(2,1)S(1)} %get-tuple-element.23.a_ref.own_ref.main_ref.refs_1_.refs_0_, bf16[16,640]{1,0:T(8,128)(2,1)S(1)} %halo.1.halo_ref), custom_call_target="tpu_custom_call" | custom-call | tf_op jit(solution)/shard_map/own/pallas_call | solution.py:404
  19.2 0.3 later.1
  19.5 0.2 collective-permute-start.5
  19.6 0.0 collective-permute-done.6.refs_3_
  19.7 0.0 collective-permute-done.refs_2_.refs_1_
  19.7 1.0 %beside.1 = (bf16[128,1152]{1,0:T(8,128)(2,1)S(1)}, f32[64,1024]{1,0:T(8,128)S(1)}, bf16[64,1024]{1,0:T(8,128)(2,1)S(1)}) custom-call(f32[8,128]{1,0:T(8,128)S(1)} %get-tuple-element.27.earlier_ref.refs_7_, bf16[128,1152]{1,0:T(8,128)(2,1)S(1)} %get-tuple-element.28.refs_0_.own_ref, f32[64,1024]{1,0:T(8,128)S(1)} %get-tuple-element.29.refs_1_.own_power_ref, ...), custom_call_target="tpu_custom_call" | custom-call | tf_op jit(solution)/shard_map/beside/pallas_call | solution.py:404
  20.7 0.3 candidate.1
  21.0 1.9 %collective-permute-start.7 = (bf16[64,1024]{1,0:T(8,128)(2,1)S(1)}, bf16[64,1024]{1,0:T(8,128)(2,1)S(1)}, u32[]{:S(2)}, u32[]{:S(2)}) collective-permute-start(bf16[64,1024]{1,0:T(8,128)(2,1)S(1)} %candidate.1), channel_id=1, source_target_pairs={{0,8},{4,12},{8,16},{12,20},{16,24},{20,28},{24,0},{28,4},{1,9},{5... | collective-permute-start | bytes 393224 | tf_op jit(solution)/shard_map/ppermute | solution.py:387
  22.8 0.2 collective-permute-done.4.refs_3_.halo_ref.main_ref
  23.0 1.0 %near.1 = (bf16[128,1152]{1,0:T(8,128)(2,1)S(1)}, f32[64,1024]{1,0:T(8,128)S(1)}, bf16[64,1024]{1,0:T(8,128)(2,1)S(1)}) custom-call(bf16[128,1152]{1,0:T(8,128)(2,1)S(1)} %get-tuple-element.32.own_ref, f32[64,1024]{1,0:T(8,128)S(1)} %get-tuple-element.33.own_power_ref, bf16[128,1024]{1,0:T(8,128)(2,1)S(1)} %collective-permute-done.1.main_ref.b_ref.refs_2_, ...), custom_call_target="tpu_custom_call" | custom-call | tf_op jit(solution)/shard_map/near/pallas_call | solution.py:404
  24.0 1.6 %collective-permute-start.9 = (bf16[64,1024]{1,0:T(8,128)(2,1)S(1)}, bf16[64,1024]{1,0:T(8,128)(2,1)S(1)}, u32[]{:S(2)}, u32[]{:S(2)}) collective-permute-start(bf16[64,1024]{1,0:T(8,128)(2,1)S(1)} %get-tuple-element.38), channel_id=1, source_target_pairs={{0,4},{4,0},{8,12},{12,8},{16,20},{20,16},{24,28},{28,24},{1,5},{5... | collective-permute-start | bytes 393224 | tf_op jit(solution)/shard_map/ppermute | solution.py:391
  25.6 0.0 collective-permute-done.8.halo_ref
  25.6 1.0 %far.1 = (bf16[128,1152]{1,0:T(8,128)(2,1)S(1)}, f32[64,1024]{1,0:T(8,128)S(1)}, bf16[64,1024]{1,0:T(8,128)(2,1)S(1)}) custom-call(bf16[128,1152]{1,0:T(8,128)(2,1)S(1)} %get-tuple-element.32.own_ref, f32[64,1024]{1,0:T(8,128)S(1)} %get-tuple-element.33.own_power_ref, bf16[144,1024]{1,0:T(8,128)(2,1)S(1)} %collective-permute-done.4.refs_3_.halo_ref.main_ref, ...), custom_call_target="tpu_custom_call" | custom-call | tf_op jit(solution)/shard_map/far/pallas_call | solution.py:404
  26.6 0.6 %collective-permute-start.10 = (bf16[64,1024]{1,0:T(8,128)(2,1)S(1)}, bf16[64,1024]{1,0:T(8,128)(2,1)S(1)}, u32[]{:S(2)}, u32[]{:S(2)}) collective-permute-start(bf16[64,1024]{1,0:T(8,128)(2,1)S(1)} %get-tuple-element.39), channel_id=1, source_target_pairs={{0,4},{4,0},{8,12},{12,8},{16,20},{20,16},{24,28},{28,24},{1,5},{5... | collective-permute-start | bytes 393224 | tf_op jit(solution)/shard_map/ppermute | solution.py:391
  27.2 0.4 %four.1.four_ref = bf16[64,1024]{1,0:T(8,128)(2,1)S(1)} custom-call(bf16[128,1152]{1,0:T(8,128)(2,1)S(1)} %get-tuple-element.28.refs_0_.own_ref, f32[64,1024]{1,0:T(8,128)S(1)} %get-tuple-element.29.refs_1_.own_power_ref, bf16[128,1152]{1,0:T(8,128)(2,1)S(1)} %get-tuple-element.36.ext_ref, f32[64,1024]{1,0:T(8,128)S(1)} %get-tuple-element.37.power_ref), custom_call_target="tpu_custom_call" | custom-call | tf_op jit(solution)/shard_map/four/pallas_call | solution.py:404
  27.7 0.4 %two.1.two_ref = bf16[64,1024]{1,0:T(8,128)(2,1)S(1)} custom-call(bf16[128,1152]{1,0:T(8,128)(2,1)S(1)} %get-tuple-element.28.refs_0_.own_ref, f32[64,1024]{1,0:T(8,128)S(1)} %get-tuple-element.29.refs_1_.own_power_ref, bf16[128,1152]{1,0:T(8,128)(2,1)S(1)} %get-tuple-element.34.ext_ref, f32[64,1024]{1,0:T(8,128)S(1)} %get-tuple-element.35.power_ref), custom_call_target="tpu_custom_call" | custom-call | tf_op jit(solution)/shard_map/two/pallas_call | solution.py:404
  28.1 0.0 collective-permute-done.5.refs_4_
  28.1 1.4 %collective-permute-done.7.refs_5_ = bf16[64,1024]{1,0:T(8,128)(2,1)S(1)} collective-permute-done((bf16[64,1024]{1,0:T(8,128)(2,1)S(1)}, bf16[64,1024]{1,0:T(8,128)(2,1)S(1)}, u32[]{:S(2)}, u32[]{:S(2)}) %collective-permute-start.7) | collective-permute-done | bytes 131104 | tf_op jit(solution)/shard_map/ppermute | solution.py:387
  29.5 1.7 %surface.1.surface_ref = f32[16,1024]{1,0:T(8,128)S(1)} custom-call(f32[16,128]{1,0:T(8,128)S(1)} %get-tuple-element.22.cond_ref.refs_0_, bf16[144,1024]{1,0:T(8,128)(2,1)S(1)} %get-tuple-element.23.a_ref.own_ref.main_ref.refs_1_.refs_0_, bf16[144,1024]{1,0:T(8,128)(2,1)S(1)} %collective-permute-done.refs_2_.refs_1_, ...), custom_call_target="tpu_custom_call" | custom-call | tf_op jit(solution)/shard_map/surface/pallas_call | solution.py:404
  31.2 0.0 collective-permute-done.9.near_ref
  31.2 0.6 %collective-permute-done.10.far_ref = bf16[64,1024]{1,0:T(8,128)(2,1)S(1)} collective-permute-done((bf16[64,1024]{1,0:T(8,128)(2,1)S(1)}, bf16[64,1024]{1,0:T(8,128)(2,1)S(1)}, u32[]{:S(2)}, u32[]{:S(2)}) %collective-permute-start.10) | collective-permute-done | bytes 131104 | tf_op jit(solution)/shard_map/ppermute | solution.py:391
  31.9 0.9 %place.1 = (f32[16,1024]{1,0:T(8,128)}, bf16[4,64,1024]{2,1,0:T(8,128)(2,1)}) custom-call(f32[16,128]{1,0:T(8,128)S(1)} %get-tuple-element.22.cond_ref.refs_0_, f32[16,1024]{1,0:T(8,128)S(1)} %surface.1.surface_ref, bf16[64,1024]{1,0:T(8,128)(2,1)S(1)} %get-tuple-element.30.earlier_ref.beside_ref, bf16[64,1024]{1,0:T(8,128)(2,1)S(1)} %two.1.two_ref, ...), custom_call_target="tpu_custom_call" | custom-call | tf_op jit(solution)/shard_map/place/pallas_call | solution.py:488
  (1 shorter events, 0.0 us)
Async XLA Ops:
  0.6 11.0 %collective-permute-start.1 = (bf16[128,1024]{1,0:T(8,128)(2,1)}, bf16[128,1024]{1,0:T(8,128)(2,1)S(1)}, u32[]{:S(2)}, u32[]{:S(2)}) collective-permute-start(bf16[128,1024]{1,0:T(8,128)(2,1)} %bitcast.5), channel_id=1, source_target_pairs={{0,24},{4,28},{8,0},{12,4},{16,8},{20,12},{24,16},{28,20},{1,25},{... | collective-permute-start | bytes 786440 | tf_op jit(solution)/shard_map/ppermute | solution.py:387
  7.4 3.4 %collective-permute-start.2 = (bf16[144,128]{1,0:T(8,128)(2,1)S(1)}, bf16[144,128]{1,0:T(8,128)(2,1)S(1)}, u32[]{:S(2)}, u32[]{:S(2)}) collective-permute-start(bf16[144,128]{1,0:T(8,128)(2,1)S(1)} %get-tuple-element.25), channel_id=1, source_target_pairs={{0,1},{1,2},{2,3},{3,0},{4,5},{5,6},{6,7},{7,4},{8,9},{9,10},{10,1... | collective-permute-start | bytes 110600 | tf_op jit(solution)/shard_map/ppermute | solution.py:387
  7.5 3.4 %collective-permute-start.3 = (bf16[144,128]{1,0:T(8,128)(2,1)S(1)}, bf16[144,128]{1,0:T(8,128)(2,1)S(1)}, u32[]{:S(2)}, u32[]{:S(2)}) collective-permute-start(bf16[144,128]{1,0:T(8,128)(2,1)S(1)} %get-tuple-element.26), channel_id=1, source_target_pairs={{0,3},{1,0},{2,1},{3,2},{4,7},{5,4},{6,5},{7,6},{8,11},{9,8},{10,9... | collective-permute-start | bytes 110600 | tf_op jit(solution)/shard_map/ppermute | solution.py:387
  9.2 10.4 %collective-permute-start = (bf16[144,1024]{1,0:T(8,128)(2,1)S(1)}, bf16[144,1024]{1,0:T(8,128)(2,1)S(1)}, u32[]{:S(2)}, u32[]{:S(2)}) collective-permute-start(bf16[144,1024]{1,0:T(8,128)(2,1)S(1)} %get-tuple-element.23.a_ref.own_ref.main_ref.refs_1_.refs_0_), channel_id=1, source_target_pairs={{0,4},{4,0},{8,12},{12,8},{16,20},{20,16},{24,28},{28,24},{1,5},{5... | collective-permute-start | bytes 884744 | tf_op jit(solution)/shard_map/ppermute | solution.py:391
  11.0 6.4 %copy-start = (bf16[512,256]{1,0:T(8,128)(2,1)S(1)}, bf16[512,256]{1,0:T(8,128)(2,1)}, u32[]{:S(2)}) copy-start(bf16[512,256]{1,0:T(8,128)(2,1)} %constant.11.clone.fourth_ref.refs_11_) | copy-start | bytes 786436
  11.0 6.4 %copy-start.1 = (bf16[256,256]{1,0:T(8,128)(2,1)S(1)}, bf16[256,256]{1,0:T(8,128)(2,1)}, u32[]{:S(2)}) copy-start(bf16[256,256]{1,0:T(8,128)(2,1)} %constant.9.clone.second_ref.refs_9_) | copy-start | bytes 393220
  11.0 6.4 %copy-start.2 = (bf16[128,192]{1,0:T(8,128)(2,1)S(1)}, bf16[128,192]{1,0:T(8,128)(2,1)}, u32[]{:S(2)}) copy-start(bf16[128,192]{1,0:T(8,128)(2,1)} %constant.8.clone.first_ref.refs_8_) | copy-start | bytes 147460
  11.0 6.4 %copy-start.3 = (bf16[64,256]{1,0:T(8,128)(2,1)S(1)}, bf16[64,256]{1,0:T(8,128)(2,1)}, u32[]{:S(2)}) copy-start(bf16[64,256]{1,0:T(8,128)(2,1)} %constant.10.clone.third_ref.refs_10_) | copy-start | bytes 98308
  11.6 11.4 %collective-permute-start.4 = (bf16[144,1024]{1,0:T(8,128)(2,1)S(1)}, bf16[144,1024]{1,0:T(8,128)(2,1)S(1)}, u32[]{:S(2)}, u32[]{:S(2)}) collective-permute-start(bf16[144,1024]{1,0:T(8,128)(2,1)S(1)} %join.1), channel_id=1, source_target_pairs={{0,24},{4,28},{8,0},{12,4},{16,8},{20,12},{24,16},{28,20},{1,25},{... | collective-permute-start | bytes 884744 | tf_op jit(solution)/shard_map/ppermute | solution.py:387
  15.9 3.8 %collective-permute-start.6 = (bf16[16,640]{1,0:T(8,128)(2,1)S(1)}, bf16[16,640]{1,0:T(8,128)(2,1)S(1)}, u32[]{:S(2)}, u32[]{:S(2)}) collective-permute-start(bf16[16,640]{1,0:T(8,128)(2,1)S(1)} %halo.1.halo_ref), channel_id=1, source_target_pairs={{0,4},{4,0},{8,12},{12,8},{16,20},{20,16},{24,28},{28,24},{1,5},{5... | collective-permute-start | bytes 61448 | tf_op jit(solution)/shard_map/ppermute | solution.py:391
  17.4 8.2 %collective-permute-start.8 = (bf16[16,640]{1,0:T(8,128)(2,1)S(1)}, bf16[16,640]{1,0:T(8,128)(2,1)S(1)}, u32[]{:S(2)}, u32[]{:S(2)}) collective-permute-start(bf16[16,640]{1,0:T(8,128)(2,1)S(1)} %halo.1.halo_ref), channel_id=1, source_target_pairs={{0,16},{4,20},{8,24},{12,28},{16,0},{20,4},{24,8},{28,12},{1,17},{... | collective-permute-start | bytes 61448 | tf_op jit(solution)/shard_map/ppermute | solution.py:387
  19.5 8.6 %collective-permute-start.5 = (bf16[64,1024]{1,0:T(8,128)(2,1)S(1)}, bf16[64,1024]{1,0:T(8,128)(2,1)S(1)}, u32[]{:S(2)}, u32[]{:S(2)}) collective-permute-start(bf16[64,1024]{1,0:T(8,128)(2,1)S(1)} %later.1), channel_id=1, source_target_pairs={{0,28},{4,24},{8,4},{12,0},{16,12},{20,8},{24,20},{28,16},{1,29},{... | collective-permute-start | bytes 393224 | tf_op jit(solution)/shard_map/ppermute | solution.py:450
  21.0 8.6 %collective-permute-start.7 = (bf16[64,1024]{1,0:T(8,128)(2,1)S(1)}, bf16[64,1024]{1,0:T(8,128)(2,1)S(1)}, u32[]{:S(2)}, u32[]{:S(2)}) collective-permute-start(bf16[64,1024]{1,0:T(8,128)(2,1)S(1)} %candidate.1), channel_id=1, source_target_pairs={{0,8},{4,12},{8,16},{12,20},{16,24},{20,28},{24,0},{28,4},{1,9},{5... | collective-permute-start | bytes 393224 | tf_op jit(solution)/shard_map/ppermute | solution.py:387
  24.0 7.2 %collective-permute-start.9 = (bf16[64,1024]{1,0:T(8,128)(2,1)S(1)}, bf16[64,1024]{1,0:T(8,128)(2,1)S(1)}, u32[]{:S(2)}, u32[]{:S(2)}) collective-permute-start(bf16[64,1024]{1,0:T(8,128)(2,1)S(1)} %get-tuple-element.38), channel_id=1, source_target_pairs={{0,4},{4,0},{8,12},{12,8},{16,20},{20,16},{24,28},{28,24},{1,5},{5... | collective-permute-start | bytes 393224 | tf_op jit(solution)/shard_map/ppermute | solution.py:391
  26.6 5.2 %collective-permute-start.10 = (bf16[64,1024]{1,0:T(8,128)(2,1)S(1)}, bf16[64,1024]{1,0:T(8,128)(2,1)S(1)}, u32[]{:S(2)}, u32[]{:S(2)}) collective-permute-start(bf16[64,1024]{1,0:T(8,128)(2,1)S(1)} %get-tuple-element.39), channel_id=1, source_target_pairs={{0,4},{4,0},{8,12},{12,8},{16,20},{20,16},{24,28},{28,24},{1,5},{5... | collective-permute-start | bytes 393224 | tf_op jit(solution)/shard_map/ppermute | solution.py:391

commit v6 on v5

--- a/solution.py
+++ b/solution.py
@@ -481,7 +481,7 @@
             ((rows, cols), BF16),
             ((tiles, LANES), F32),
             ((2 * rows, cols), F32),
-            ((8 * cols // BLK, LANES), F32),
+            ((8 * cols // BLK + 8, LANES), F32),
         ],
     )
     operands = (cond, surface, coh_beside, coh_two, coh_four, near, far)

time: 33 us -> 33 us (level)
  no operation moved by 1% of the time
where the time goes in v6:
time: 33 us; the launch traced here: 32.8 us
  starting transfers between devices  18.4 us (56%)
  Pallas kernels  10 us (30%)
  waiting for transfers between devices  2.95 us (9%)
  between operations  1.43 us (4%)
    ppermute x6, starting transfers between devices, shifted(): lax.ppermute(value, axis, [(s, (s - steps) % count) for s in range(count)])  13 us
    pallas_call x12, Pallas kernels, call(): pl.pallas_call(kernel, out_shape=out_shape, in_specs=[VMEM] * len(operand...  8.08 us
    ppermute x4, starting transfers between devices, swapped(): lax.ppermute(value, axis, [(s, s ^ step) for s in range(lax.axis_size(axi...  5.19 us
    ppermute x6, waiting for transfers between devices, shifted(): lax.ppermute(value, axis, [(s, (s - steps) % count) for s in range(count)])  2.3 us
    pallas_call x1, Pallas kernels, body(): pl.pallas_call(prep_kernel, out_shape=(sds((2 * rows + 16, cols), BF16),...  1.03 us
    pallas_call x1, Pallas kernels, body(): pl.pallas_call(place_kernel, out_shape=(sds(surface.shape, F32), sds((SPA...  0.93 us
  transfers between devices with their start and end apart: 11, of which 5 were waited for; matrix products, arithmetic and copies ran while one was open for 0% of the time, Pallas kernels for 28%

profile of v6, /device:TPU:0, one launch (start us, length us, event | category | flops | bytes accessed | tf_op | source)
XLA Modules:
  0.0 32.8 jit_solution(3434677728665158993)
XLA Ops:
  0.6 5.1 %collective-permute-start.1 = (bf16[128,1024]{1,0:T(8,128)(2,1)}, bf16[128,1024]{1,0:T(8,128)(2,1)S(1)}, u32[]{:S(2)}, u32[]{:S(2)}) collective-permute-start(bf16[128,1024]{1,0:T(8,128)(2,1)} %bitcast.5), channel_id=1, source_target_pairs={{0,24},{4,28},{8,0},{12,4},{16,8},{20,12},{24,16},{28,20},{1,25},{... | collective-permute-start | bytes 786440 | tf_op jit(solution)/shard_map/ppermute | solution.py:387
  6.4 1.0 %prepare.1 = (bf16[144,1024]{1,0:T(8,128)(2,1)S(1)}, f32[16,128]{1,0:T(8,128)S(1)}, bf16[16,128]{1,0:T(8,128)(2,1)S(1)}, bf16[144,128]{1,0:T(8,128)(2,1)S(1)}, bf16[144,128]{1,0:T(8,128)(2,1)S(1)}) custom-call(bf16[128,1024]{1,0:T(8,128)(2,1)} %bitcast.6, s32[1,16]{1,0:T(1,128)} %bitcast.7, f32[1,16]{1,0:T(1,128)} %bitcast.8, s32[1,4]{1,0:T(1,128)} %partners_hbm.1, ...), custom_call_target="tpu_custom_call" | custom-call | tf_op jit(solution)/shard_map/prepare/pallas_call | solution.py:425
  7.4 0.1 collective-permute-start.2
  7.5 1.7 %collective-permute-start.3 = (bf16[144,128]{1,0:T(8,128)(2,1)S(1)}, bf16[144,128]{1,0:T(8,128)(2,1)S(1)}, u32[]{:S(2)}, u32[]{:S(2)}) collective-permute-start(bf16[144,128]{1,0:T(8,128)(2,1)S(1)} %get-tuple-element.26), channel_id=1, source_target_pairs={{0,3},{1,0},{2,1},{3,2},{4,7},{5,4},{6,5},{7,6},{8,11},{9,8},{10,9... | collective-permute-start | bytes 110600 | tf_op jit(solution)/shard_map/ppermute | solution.py:387
  9.2 1.5 %collective-permute-start = (bf16[144,1024]{1,0:T(8,128)(2,1)S(1)}, bf16[144,1024]{1,0:T(8,128)(2,1)S(1)}, u32[]{:S(2)}, u32[]{:S(2)}) collective-permute-start(bf16[144,1024]{1,0:T(8,128)(2,1)S(1)} %get-tuple-element.23.a_ref.own_ref.main_ref.refs_1_.refs_0_), channel_id=1, source_target_pairs={{0,4},{4,0},{8,12},{12,8},{16,20},{20,16},{24,28},{28,24},{1,5},{5... | collective-permute-start | bytes 884744 | tf_op jit(solution)/shard_map/ppermute | solution.py:391
  10.7 0.1 collective-permute-done.2.left_ref
  10.9 0.0 collective-permute-done.3.right_ref
  10.9 0.2 halo.1.halo_ref
  11.0 0.0 copy-start
  11.0 0.0 copy-start.1
  11.0 0.0 copy-start.2
  11.0 0.0 copy-start.3
  11.0 0.6 %collective-permute-done.1.main_ref.b_ref.refs_2_ = bf16[128,1024]{1,0:T(8,128)(2,1)S(1)} collective-permute-done((bf16[128,1024]{1,0:T(8,128)(2,1)}, bf16[128,1024]{1,0:T(8,128)(2,1)S(1)}, u32[]{:S(2)}, u32[]{:S(2)}) %collective-permute-start.1) | collective-permute-done | bytes 262176 | tf_op jit(solution)/shard_map/ppermute | solution.py:387
  11.6 4.2 %collective-permute-start.4 = (bf16[144,1024]{1,0:T(8,128)(2,1)S(1)}, bf16[144,1024]{1,0:T(8,128)(2,1)S(1)}, u32[]{:S(2)}, u32[]{:S(2)}) collective-permute-start(bf16[144,1024]{1,0:T(8,128)(2,1)S(1)} %join.1), channel_id=1, source_target_pairs={{0,24},{4,28},{8,0},{12,4},{16,8},{20,12},{24,16},{28,20},{1,25},{... | collective-permute-start | bytes 884744 | tf_op jit(solution)/shard_map/ppermute | solution.py:387
  15.9 1.5 %collective-permute-start.6 = (bf16[16,640]{1,0:T(8,128)(2,1)S(1)}, bf16[16,640]{1,0:T(8,128)(2,1)S(1)}, u32[]{:S(2)}, u32[]{:S(2)}) collective-permute-start(bf16[16,640]{1,0:T(8,128)(2,1)S(1)} %halo.1.halo_ref), channel_id=1, source_target_pairs={{0,4},{4,0},{8,12},{12,8},{16,20},{20,16},{24,28},{28,24},{1,5},{5... | collective-permute-start | bytes 61448 | tf_op jit(solution)/shard_map/ppermute | solution.py:391
  17.4 0.0 collective-permute-start.8
  17.4 0.0 copy-done
  17.4 0.0 copy-done.1
  17.4 0.0 copy-done.2
  17.4 0.0 copy-done.3
  17.4 1.0 %spectrum.1 = (f32[128,1024]{1,0:T(8,128)S(1)}, f32[8,128]{1,0:T(8,128)S(1)}) custom-call(bf16[144,1024]{1,0:T(8,128)(2,1)S(1)} %get-tuple-element.23.a_ref.own_ref.main_ref.refs_1_.refs_0_, bf16[128,192]{1,0:T(8,128)(2,1)S(1)} %copy-done.2, bf16[256,256]{1,0:T(8,128)(2,1)S(1)} %copy-done.1, bf16[64,256]{1,0:T(8,128)(2,1)S(1)} %copy-done.3, ...), custom_call_target="tpu_custom_call" | custom-call | tf_op jit(solution)/shard_map/spectrum/pallas_call | solution.py:404
  18.4 0.8 %own.1 = (bf16[128,1152]{1,0:T(8,128)(2,1)S(1)}, f32[64,1024]{1,0:T(8,128)S(1)}) custom-call(f32[8,128]{1,0:T(8,128)S(1)} %get-tuple-element.27.earlier_ref.refs_7_, bf16[144,1024]{1,0:T(8,128)(2,1)S(1)} %get-tuple-element.23.a_ref.own_ref.main_ref.refs_1_.refs_0_, bf16[16,640]{1,0:T(8,128)(2,1)S(1)} %halo.1.halo_ref), custom_call_target="tpu_custom_call" | custom-call | tf_op jit(solution)/shard_map/own/pallas_call | solution.py:404
  19.2 0.3 later.1
  19.5 0.2 collective-permute-start.5
  19.6 0.0 collective-permute-done.6.refs_3_
  19.7 0.0 collective-permute-done.refs_2_.refs_1_
  19.7 1.0 %beside.1 = (bf16[128,1152]{1,0:T(8,128)(2,1)S(1)}, f32[64,1024]{1,0:T(8,128)S(1)}, bf16[64,1024]{1,0:T(8,128)(2,1)S(1)}) custom-call(f32[8,128]{1,0:T(8,128)S(1)} %get-tuple-element.27.earlier_ref.refs_7_, bf16[128,1152]{1,0:T(8,128)(2,1)S(1)} %get-tuple-element.28.refs_0_.own_ref, f32[64,1024]{1,0:T(8,128)S(1)} %get-tuple-element.29.refs_1_.own_power_ref, ...), custom_call_target="tpu_custom_call" | custom-call | tf_op jit(solution)/shard_map/beside/pallas_call | solution.py:404
  20.7 0.3 candidate.1
  21.0 1.9 %collective-permute-start.7 = (bf16[64,1024]{1,0:T(8,128)(2,1)S(1)}, bf16[64,1024]{1,0:T(8,128)(2,1)S(1)}, u32[]{:S(2)}, u32[]{:S(2)}) collective-permute-start(bf16[64,1024]{1,0:T(8,128)(2,1)S(1)} %candidate.1), channel_id=1, source_target_pairs={{0,8},{4,12},{8,16},{12,20},{16,24},{20,28},{24,0},{28,4},{1,9},{5... | collective-permute-start | bytes 393224 | tf_op jit(solution)/shard_map/ppermute | solution.py:387
  22.8 0.2 collective-permute-done.4.refs_3_.halo_ref.main_ref
  23.0 1.0 %near.1 = (bf16[128,1152]{1,0:T(8,128)(2,1)S(1)}, f32[64,1024]{1,0:T(8,128)S(1)}, bf16[64,1024]{1,0:T(8,128)(2,1)S(1)}) custom-call(bf16[128,1152]{1,0:T(8,128)(2,1)S(1)} %get-tuple-element.32.own_ref, f32[64,1024]{1,0:T(8,128)S(1)} %get-tuple-element.33.own_power_ref, bf16[128,1024]{1,0:T(8,128)(2,1)S(1)} %collective-permute-done.1.main_ref.b_ref.refs_2_, ...), custom_call_target="tpu_custom_call" | custom-call | tf_op jit(solution)/shard_map/near/pallas_call | solution.py:404
  24.0 1.6 %collective-permute-start.9 = (bf16[64,1024]{1,0:T(8,128)(2,1)S(1)}, bf16[64,1024]{1,0:T(8,128)(2,1)S(1)}, u32[]{:S(2)}, u32[]{:S(2)}) collective-permute-start(bf16[64,1024]{1,0:T(8,128)(2,1)S(1)} %get-tuple-element.38), channel_id=1, source_target_pairs={{0,4},{4,0},{8,12},{12,8},{16,20},{20,16},{24,28},{28,24},{1,5},{5... | collective-permute-start | bytes 393224 | tf_op jit(solution)/shard_map/ppermute | solution.py:391
  25.6 0.0 collective-permute-done.8.halo_ref
  25.6 1.0 %far.1 = (bf16[128,1152]{1,0:T(8,128)(2,1)S(1)}, f32[64,1024]{1,0:T(8,128)S(1)}, bf16[64,1024]{1,0:T(8,128)(2,1)S(1)}) custom-call(bf16[128,1152]{1,0:T(8,128)(2,1)S(1)} %get-tuple-element.32.own_ref, f32[64,1024]{1,0:T(8,128)S(1)} %get-tuple-element.33.own_power_ref, bf16[144,1024]{1,0:T(8,128)(2,1)S(1)} %collective-permute-done.4.refs_3_.halo_ref.main_ref, ...), custom_call_target="tpu_custom_call" | custom-call | tf_op jit(solution)/shard_map/far/pallas_call | solution.py:404
  26.6 0.6 %collective-permute-start.10 = (bf16[64,1024]{1,0:T(8,128)(2,1)S(1)}, bf16[64,1024]{1,0:T(8,128)(2,1)S(1)}, u32[]{:S(2)}, u32[]{:S(2)}) collective-permute-start(bf16[64,1024]{1,0:T(8,128)(2,1)S(1)} %get-tuple-element.39), channel_id=1, source_target_pairs={{0,4},{4,0},{8,12},{12,8},{16,20},{20,16},{24,28},{28,24},{1,5},{5... | collective-permute-start | bytes 393224 | tf_op jit(solution)/shard_map/ppermute | solution.py:391
  27.2 0.4 %four.1.four_ref = bf16[64,1024]{1,0:T(8,128)(2,1)S(1)} custom-call(bf16[128,1152]{1,0:T(8,128)(2,1)S(1)} %get-tuple-element.28.refs_0_.own_ref, f32[64,1024]{1,0:T(8,128)S(1)} %get-tuple-element.29.refs_1_.own_power_ref, bf16[128,1152]{1,0:T(8,128)(2,1)S(1)} %get-tuple-element.36.ext_ref, f32[64,1024]{1,0:T(8,128)S(1)} %get-tuple-element.37.power_ref), custom_call_target="tpu_custom_call" | custom-call | tf_op jit(solution)/shard_map/four/pallas_call | solution.py:404
  27.7 0.4 %two.1.two_ref = bf16[64,1024]{1,0:T(8,128)(2,1)S(1)} custom-call(bf16[128,1152]{1,0:T(8,128)(2,1)S(1)} %get-tuple-element.28.refs_0_.own_ref, f32[64,1024]{1,0:T(8,128)S(1)} %get-tuple-element.29.refs_1_.own_power_ref, bf16[128,1152]{1,0:T(8,128)(2,1)S(1)} %get-tuple-element.34.ext_ref, f32[64,1024]{1,0:T(8,128)S(1)} %get-tuple-element.35.power_ref), custom_call_target="tpu_custom_call" | custom-call | tf_op jit(solution)/shard_map/two/pallas_call | solution.py:404
  28.1 0.0 collective-permute-done.5.refs_4_
  28.1 1.4 %collective-permute-done.7.refs_5_ = bf16[64,1024]{1,0:T(8,128)(2,1)S(1)} collective-permute-done((bf16[64,1024]{1,0:T(8,128)(2,1)S(1)}, bf16[64,1024]{1,0:T(8,128)(2,1)S(1)}, u32[]{:S(2)}, u32[]{:S(2)}) %collective-permute-start.7) | collective-permute-done | bytes 131104 | tf_op jit(solution)/shard_map/ppermute | solution.py:387
  29.5 1.7 %surface.1.surface_ref = f32[16,1024]{1,0:T(8,128)S(1)} custom-call(f32[16,128]{1,0:T(8,128)S(1)} %get-tuple-element.22.cond_ref.refs_0_, bf16[144,1024]{1,0:T(8,128)(2,1)S(1)} %get-tuple-element.23.a_ref.own_ref.main_ref.refs_1_.refs_0_, bf16[144,1024]{1,0:T(8,128)(2,1)S(1)} %collective-permute-done.refs_2_.refs_1_, ...), custom_call_target="tpu_custom_call" | custom-call | tf_op jit(solution)/shard_map/surface/pallas_call | solution.py:404
  31.2 0.0 collective-permute-done.9.near_ref
  31.2 0.6 %collective-permute-done.10.far_ref = bf16[64,1024]{1,0:T(8,128)(2,1)S(1)} collective-permute-done((bf16[64,1024]{1,0:T(8,128)(2,1)S(1)}, bf16[64,1024]{1,0:T(8,128)(2,1)S(1)}, u32[]{:S(2)}, u32[]{:S(2)}) %collective-permute-start.10) | collective-permute-done | bytes 131104 | tf_op jit(solution)/shard_map/ppermute | solution.py:391
  31.9 0.9 %place.1 = (f32[16,1024]{1,0:T(8,128)}, bf16[4,64,1024]{2,1,0:T(8,128)(2,1)}) custom-call(f32[16,128]{1,0:T(8,128)S(1)} %get-tuple-element.22.cond_ref.refs_0_, f32[16,1024]{1,0:T(8,128)S(1)} %surface.1.surface_ref, bf16[64,1024]{1,0:T(8,128)(2,1)S(1)} %get-tuple-element.30.earlier_ref.beside_ref, bf16[64,1024]{1,0:T(8,128)(2,1)S(1)} %two.1.two_ref, ...), custom_call_target="tpu_custom_call" | custom-call | tf_op jit(solution)/shard_map/place/pallas_call | solution.py:488
  (1 shorter events, 0.0 us)
Async XLA Ops:
  0.6 11.0 %collective-permute-start.1 = (bf16[128,1024]{1,0:T(8,128)(2,1)}, bf16[128,1024]{1,0:T(8,128)(2,1)S(1)}, u32[]{:S(2)}, u32[]{:S(2)}) collective-permute-start(bf16[128,1024]{1,0:T(8,128)(2,1)} %bitcast.5), channel_id=1, source_target_pairs={{0,24},{4,28},{8,0},{12,4},{16,8},{20,12},{24,16},{28,20},{1,25},{... | collective-permute-start | bytes 786440 | tf_op jit(solution)/shard_map/ppermute | solution.py:387
  7.4 3.4 %collective-permute-start.2 = (bf16[144,128]{1,0:T(8,128)(2,1)S(1)}, bf16[144,128]{1,0:T(8,128)(2,1)S(1)}, u32[]{:S(2)}, u32[]{:S(2)}) collective-permute-start(bf16[144,128]{1,0:T(8,128)(2,1)S(1)} %get-tuple-element.25), channel_id=1, source_target_pairs={{0,1},{1,2},{2,3},{3,0},{4,5},{5,6},{6,7},{7,4},{8,9},{9,10},{10,1... | collective-permute-start | bytes 110600 | tf_op jit(solution)/shard_map/ppermute | solution.py:387
  7.5 3.4 %collective-permute-start.3 = (bf16[144,128]{1,0:T(8,128)(2,1)S(1)}, bf16[144,128]{1,0:T(8,128)(2,1)S(1)}, u32[]{:S(2)}, u32[]{:S(2)}) collective-permute-start(bf16[144,128]{1,0:T(8,128)(2,1)S(1)} %get-tuple-element.26), channel_id=1, source_target_pairs={{0,3},{1,0},{2,1},{3,2},{4,7},{5,4},{6,5},{7,6},{8,11},{9,8},{10,9... | collective-permute-start | bytes 110600 | tf_op jit(solution)/shard_map/ppermute | solution.py:387
  9.2 10.4 %collective-permute-start = (bf16[144,1024]{1,0:T(8,128)(2,1)S(1)}, bf16[144,1024]{1,0:T(8,128)(2,1)S(1)}, u32[]{:S(2)}, u32[]{:S(2)}) collective-permute-start(bf16[144,1024]{1,0:T(8,128)(2,1)S(1)} %get-tuple-element.23.a_ref.own_ref.main_ref.refs_1_.refs_0_), channel_id=1, source_target_pairs={{0,4},{4,0},{8,12},{12,8},{16,20},{20,16},{24,28},{28,24},{1,5},{5... | collective-permute-start | bytes 884744 | tf_op jit(solution)/shard_map/ppermute | solution.py:391
  11.0 6.4 %copy-start = (bf16[512,256]{1,0:T(8,128)(2,1)S(1)}, bf16[512,256]{1,0:T(8,128)(2,1)}, u32[]{:S(2)}) copy-start(bf16[512,256]{1,0:T(8,128)(2,1)} %constant.11.clone.fourth_ref.refs_11_) | copy-start | bytes 786436
  11.0 6.4 %copy-start.1 = (bf16[256,256]{1,0:T(8,128)(2,1)S(1)}, bf16[256,256]{1,0:T(8,128)(2,1)}, u32[]{:S(2)}) copy-start(bf16[256,256]{1,0:T(8,128)(2,1)} %constant.9.clone.second_ref.refs_9_) | copy-start | bytes 393220
  11.0 6.4 %copy-start.2 = (bf16[128,192]{1,0:T(8,128)(2,1)S(1)}, bf16[128,192]{1,0:T(8,128)(2,1)}, u32[]{:S(2)}) copy-start(bf16[128,192]{1,0:T(8,128)(2,1)} %constant.8.clone.first_ref.refs_8_) | copy-start | bytes 147460
  11.0 6.4 %copy-start.3 = (bf16[64,256]{1,0:T(8,128)(2,1)S(1)}, bf16[64,256]{1,0:T(8,128)(2,1)}, u32[]{:S(2)}) copy-start(bf16[64,256]{1,0:T(8,128)(2,1)} %constant.10.clone.third_ref.refs_10_) | copy-start | bytes 98308
  11.6 11.4 %collective-permute-start.4 = (bf16[144,1024]{1,0:T(8,128)(2,1)S(1)}, bf16[144,1024]{1,0:T(8,128)(2,1)S(1)}, u32[]{:S(2)}, u32[]{:S(2)}) collective-permute-start(bf16[144,1024]{1,0:T(8,128)(2,1)S(1)} %join.1), channel_id=1, source_target_pairs={{0,24},{4,28},{8,0},{12,4},{16,8},{20,12},{24,16},{28,20},{1,25},{... | collective-permute-start | bytes 884744 | tf_op jit(solution)/shard_map/ppermute | solution.py:387
  15.9 3.8 %collective-permute-start.6 = (bf16[16,640]{1,0:T(8,128)(2,1)S(1)}, bf16[16,640]{1,0:T(8,128)(2,1)S(1)}, u32[]{:S(2)}, u32[]{:S(2)}) collective-permute-start(bf16[16,640]{1,0:T(8,128)(2,1)S(1)} %halo.1.halo_ref), channel_id=1, source_target_pairs={{0,4},{4,0},{8,12},{12,8},{16,20},{20,16},{24,28},{28,24},{1,5},{5... | collective-permute-start | bytes 61448 | tf_op jit(solution)/shard_map/ppermute | solution.py:391
  17.4 8.2 %collective-permute-start.8 = (bf16[16,640]{1,0:T(8,128)(2,1)S(1)}, bf16[16,640]{1,0:T(8,128)(2,1)S(1)}, u32[]{:S(2)}, u32[]{:S(2)}) collective-permute-start(bf16[16,640]{1,0:T(8,128)(2,1)S(1)} %halo.1.halo_ref), channel_id=1, source_target_pairs={{0,16},{4,20},{8,24},{12,28},{16,0},{20,4},{24,8},{28,12},{1,17},{... | collective-permute-start | bytes 61448 | tf_op jit(solution)/shard_map/ppermute | solution.py:387
  19.5 8.6 %collective-permute-start.5 = (bf16[64,1024]{1,0:T(8,128)(2,1)S(1)}, bf16[64,1024]{1,0:T(8,128)(2,1)S(1)}, u32[]{:S(2)}, u32[]{:S(2)}) collective-permute-start(bf16[64,1024]{1,0:T(8,128)(2,1)S(1)} %later.1), channel_id=1, source_target_pairs={{0,28},{4,24},{8,4},{12,0},{16,12},{20,8},{24,20},{28,16},{1,29},{... | collective-permute-start | bytes 393224 | tf_op jit(solution)/shard_map/ppermute | solution.py:450
  21.0 8.6 %collective-permute-start.7 = (bf16[64,1024]{1,0:T(8,128)(2,1)S(1)}, bf16[64,1024]{1,0:T(8,128)(2,1)S(1)}, u32[]{:S(2)}, u32[]{:S(2)}) collective-permute-start(bf16[64,1024]{1,0:T(8,128)(2,1)S(1)} %candidate.1), channel_id=1, source_target_pairs={{0,8},{4,12},{8,16},{12,20},{16,24},{20,28},{24,0},{28,4},{1,9},{5... | collective-permute-start | bytes 393224 | tf_op jit(solution)/shard_map/ppermute | solution.py:387
  24.0 7.2 %collective-permute-start.9 = (bf16[64,1024]{1,0:T(8,128)(2,1)S(1)}, bf16[64,1024]{1,0:T(8,128)(2,1)S(1)}, u32[]{:S(2)}, u32[]{:S(2)}) collective-permute-start(bf16[64,1024]{1,0:T(8,128)(2,1)S(1)} %get-tuple-element.38), channel_id=1, source_target_pairs={{0,4},{4,0},{8,12},{12,8},{16,20},{20,16},{24,28},{28,24},{1,5},{5... | collective-permute-start | bytes 393224 | tf_op jit(solution)/shard_map/ppermute | solution.py:391
  26.6 5.2 %collective-permute-start.10 = (bf16[64,1024]{1,0:T(8,128)(2,1)S(1)}, bf16[64,1024]{1,0:T(8,128)(2,1)S(1)}, u32[]{:S(2)}, u32[]{:S(2)}) collective-permute-start(bf16[64,1024]{1,0:T(8,128)(2,1)S(1)} %get-tuple-element.39), channel_id=1, source_target_pairs={{0,4},{4,0},{8,12},{12,8},{16,20},{20,16},{24,28},{28,24},{1,5},{5... | collective-permute-start | bytes 393224 | tf_op jit(solution)/shard_map/ppermute | solution.py:391

commit v7 on v6

--- a/solution.py
+++ b/solution.py
@@ -233,7 +233,7 @@
     pair_kernel(*refs)
 
 
-def again_kernel(own_ref, own_power_ref, ext_ref, power_ref, out_ref, fields_ref):
+def again_kernel(h, cond_ref, own_ref, own_power_ref, ext_ref, power_ref, out_ref, fields_ref):
     rows, cols = out_ref.shape
     for p in range(cols // LANES + 1):
         lanes = slice(p * LANES, (p + 1) * LANES)
@@ -242,26 +242,28 @@
     for p in range(cols // LANES):
         lanes = slice(p * LANES, (p + 1) * LANES)
         sums = dot(fields_ref[:, p * LANES : (p + 2) * LANES], box)
-        out_ref[:, lanes] = coherence(sums, own_power_ref[:, lanes], power_ref[:, lanes])
+        value = coherence(sums, own_power_ref[:, lanes], power_ref[:, lanes]).astype(F32)
+        out_ref[:, lanes] = (value * cond_ref[h : h + 1, :]).astype(BF16)
+
+
+def one_kernel(cond_ref, beside_ref, near_ref, out_ref):
+    even = cond_ref[EVEN : EVEN + 1, 0:1] > 0.0
+    value = jnp.where(even, beside_ref[...].astype(F32), near_ref[...].astype(F32))
+    out_ref[...] = (value * cond_ref[0:1, 0:1]).astype(BF16)
 
 
 def place_kernel(
-    cond_ref, surface_ref, beside_ref, two_ref, four_ref, near_ref, far_ref, surface_hbm, out_hbm, out_ref, sems
+    cond_ref, surface_ref, one_ref, two_ref, four_ref, near_ref, far_ref, surface_hbm, out_hbm, three_ref, sems
 ):
-    copies = [pltpu.make_async_copy(surface_ref, surface_hbm, sems.at[SPAN])]
-    copies += [pltpu.make_async_copy(out_ref.at[h], out_hbm.at[h], sems.at[h]) for h in range(SPAN)]
-    copies[0].start()
+    sources = (one_ref, two_ref, three_ref, four_ref)
+    copies = [pltpu.make_async_copy(ref, out_hbm.at[h], sems.at[h]) for h, ref in enumerate(sources)]
+    copies.append(pltpu.make_async_copy(surface_ref, surface_hbm, sems.at[SPAN]))
     even = cond_ref[EVEN : EVEN + 1, 0:1] > 0.0
-    near = near_ref[...].astype(F32)
-    fields = [
-        lambda: jnp.where(even, beside_ref[...].astype(F32), near),
-        lambda: two_ref[...].astype(F32),
-        lambda: jnp.where(even, near, far_ref[...].astype(F32)),
-        lambda: four_ref[...].astype(F32),
-    ]
-    for h, value in enumerate(fields):
-        out_ref[h] = (value() * cond_ref[h : h + 1, 0:1]).astype(BF16)
-        copies[1 + h].start()
+    value = jnp.where(even, near_ref[...].astype(F32), far_ref[...].astype(F32))
+    for h in (0, 1, 3, 4):
+        copies[h].start()
+    three_ref[...] = (value * cond_ref[2:3, 0:1]).astype(BF16)
+    copies[2].start()
     for copy in copies:
         copy.wait()
 
@@ -448,6 +450,8 @@
     four = shifted(call(join_kernel, "join", joined, (halo, two)), "date", 2)
     later = call(functools.partial(candidate_kernel, (0, 2)), "later", field, (cond, own, two))
     across = lax.ppermute(later, "date", [(s, (s - 2) % dates ^ 1) for s in range(dates)])
+    amp = call(functools.partial(late_candidate_kernel, (0, 1)), "candidate", field, (later, cond, own, beside))
+    before = shifted(amp, "date", -2) if dates == 8 else spread(amp, "date")
     beside_halo = swapped(halo, "date", 1)
     four_halo = shifted(halo, "date", 4)
     first, second, third, fourth = [jnp.asarray(t) for t in surface_tables()]
@@ -462,16 +466,14 @@
     scratch = [[((k * rows, cols + LANES), BF16)] for k in range(4)]
     own_ext = call(own_kernel, "own", resampled, (energy, own, halo), scratch[1])
     *beside_ext, coh_beside = call(
-        beside_kernel, "beside", (*resampled, field), (energy, *own_ext, beside, beside_halo), scratch[3]
+        beside_kernel, "beside", (*resampled, field), (amp, *own_ext, beside, beside_halo), scratch[3]
     )
-    amp = call(functools.partial(late_candidate_kernel, (0, 1)), "candidate", field, (coh_beside, cond, own, beside))
-    before = shifted(amp, "date", -2) if dates == 8 else spread(amp, "date")
     *two_ext, coh_near = call(pair_kernel, "near", (*resampled, field), (*beside_ext, two, four), scratch[3])
     near = swapped(coh_near, "date", 1)
-    coh_two = call(again_kernel, "two", field, (*own_ext, *two_ext), scratch[2])
+    coh_two = call(functools.partial(again_kernel, 1), "two", field, (cond, *own_ext, *two_ext), scratch[2])
     *four_ext, coh_far = call(pair_kernel, "far", (*resampled, field), (*beside_ext, four, four_halo), scratch[3])
     far = swapped(coh_far, "date", 1)
-    coh_four = call(again_kernel, "four", field, (*own_ext, *four_ext), scratch[2])
+    coh_four = call(functools.partial(again_kernel, 3), "four", field, (cond, *own_ext, *four_ext), scratch[2])
     surface = call(
         surface_kernel,
         "surface",
@@ -484,13 +486,14 @@
             ((8 * cols // BLK + 8, LANES), F32),
         ],
     )
-    operands = (cond, surface, coh_beside, coh_two, coh_four, near, far)
+    coh_one = call(one_kernel, "one", field, (cond, coh_beside, near))
+    operands = (cond, surface, coh_one, coh_two, coh_four, near, far)
     surface, fields = pl.pallas_call(
         place_kernel,
         out_shape=(sds(surface.shape, F32), sds((SPAN, rows, cols), BF16)),
         in_specs=[VMEM] * len(operands),
         out_specs=(pl.BlockSpec(memory_space=pl.ANY),) * 2,
-        scratch_shapes=[pltpu.VMEM((SPAN, rows, cols), BF16), pltpu.SemaphoreType.DMA((SPAN + 1,))],
+        scratch_shapes=[pltpu.VMEM((rows, cols), BF16), pltpu.SemaphoreType.DMA((SPAN + 1,))],
         compiler_params=PARAMS,
         name="place",
     )(*operands)

time: 33 us -> 32.9 us (level)
    ppermute x6, waiting for transfers between devices: 2.3 us -> 1.29 us  [shifted(): lax.ppermute(value, axis, [(s, (s - steps) % count) for s in range(count)])]
    ppermute x4, waiting for transfers between devices: 0.65 us -> 1.54 us  [swapped(): lax.ppermute(value, axis, [(s, s ^ step) for s in range(lax.axis_size(axi...]
    pallas_call x12 -> x13, Pallas kernels: 8.08 us -> 8.19 us  [call(): pl.pallas_call(kernel, out_shape=out_shape, in_specs=[VMEM] * len(operand...]
where the time goes in v7:
time: 32.9 us; the launch traced here: 32.7 us
  starting transfers between devices  18.4 us (56%)
  Pallas kernels  10.1 us (31%)
  waiting for transfers between devices  2.84 us (9%)
  between operations  1.42 us (4%)
    ppermute x6, starting transfers between devices, shifted(): lax.ppermute(value, axis, [(s, (s - steps) % count) for s in range(count)])  13 us
    pallas_call x13, Pallas kernels, call(): pl.pallas_call(kernel, out_shape=out_shape, in_specs=[VMEM] * len(operand...  8.19 us
    ppermute x4, starting transfers between devices, swapped(): lax.ppermute(value, axis, [(s, s ^ step) for s in range(lax.axis_size(axi...  5.2 us
    ppermute x4, waiting for transfers between devices, swapped(): lax.ppermute(value, axis, [(s, s ^ step) for s in range(lax.axis_size(axi...  1.54 us
    ppermute x6, waiting for transfers between devices, shifted(): lax.ppermute(value, axis, [(s, (s - steps) % count) for s in range(count)])  1.29 us
    pallas_call x1, Pallas kernels, body(): pl.pallas_call(prep_kernel, out_shape=(sds((2 * rows + 16, cols), BF16),...  1.03 us
    pallas_call x1, Pallas kernels, body(): pl.pallas_call(place_kernel, out_shape=(sds(surface.shape, F32), sds((SPA...  0.85 us
  transfers between devices with their start and end apart: 11, of which 5 were waited for; matrix products, arithmetic and copies ran while one was open for 0% of the time, Pallas kernels for 28%

profile of v7, /device:TPU:0, one launch (start us, length us, event | category | flops | bytes accessed | tf_op | source)
XLA Modules:
  0.0 32.7 jit_solution(10418242152819297634)
XLA Ops:
  0.6 5.1 %collective-permute-start.1 = (bf16[128,1024]{1,0:T(8,128)(2,1)}, bf16[128,1024]{1,0:T(8,128)(2,1)S(1)}, u32[]{:S(2)}, u32[]{:S(2)}) collective-permute-start(bf16[128,1024]{1,0:T(8,128)(2,1)} %bitcast.5), channel_id=1, source_target_pairs={{0,24},{4,28},{8,0},{12,4},{16,8},{20,12},{24,16},{28,20},{1,25},{... | collective-permute-start | bytes 786440 | tf_op jit(solution)/shard_map/ppermute | solution.py:389
  6.4 1.0 %prepare.1 = (bf16[144,1024]{1,0:T(8,128)(2,1)S(1)}, f32[16,128]{1,0:T(8,128)S(1)}, bf16[16,128]{1,0:T(8,128)(2,1)S(1)}, bf16[144,128]{1,0:T(8,128)(2,1)S(1)}, bf16[144,128]{1,0:T(8,128)(2,1)S(1)}) custom-call(bf16[128,1024]{1,0:T(8,128)(2,1)} %bitcast.6, s32[1,16]{1,0:T(1,128)} %bitcast.7, f32[1,16]{1,0:T(1,128)} %bitcast.8, s32[1,4]{1,0:T(1,128)} %partners_hbm.1, ...), custom_call_target="tpu_custom_call" | custom-call | tf_op jit(solution)/shard_map/prepare/pallas_call | solution.py:427
  7.4 0.1 collective-permute-start.2
  7.5 1.7 %collective-permute-start.3 = (bf16[144,128]{1,0:T(8,128)(2,1)S(1)}, bf16[144,128]{1,0:T(8,128)(2,1)S(1)}, u32[]{:S(2)}, u32[]{:S(2)}) collective-permute-start(bf16[144,128]{1,0:T(8,128)(2,1)S(1)} %get-tuple-element.26), channel_id=1, source_target_pairs={{0,3},{1,0},{2,1},{3,2},{4,7},{5,4},{6,5},{7,6},{8,11},{9,8},{10,9... | collective-permute-start | bytes 110600 | tf_op jit(solution)/shard_map/ppermute | solution.py:389
  9.2 1.5 %collective-permute-start = (bf16[144,1024]{1,0:T(8,128)(2,1)S(1)}, bf16[144,1024]{1,0:T(8,128)(2,1)S(1)}, u32[]{:S(2)}, u32[]{:S(2)}) collective-permute-start(bf16[144,1024]{1,0:T(8,128)(2,1)S(1)} %get-tuple-element.23.a_ref.refs_1_.own_ref.refs_0_.main_ref), channel_id=1, source_target_pairs={{0,4},{4,0},{8,12},{12,8},{16,20},{20,16},{24,28},{28,24},{1,5},{5... | collective-permute-start | bytes 884744 | tf_op jit(solution)/shard_map/ppermute | solution.py:393
  10.7 0.1 collective-permute-done.2.left_ref
  10.9 0.0 collective-permute-done.3.right_ref
  10.9 0.2 halo.1.halo_ref
  11.0 0.0 copy-start
  11.0 0.0 copy-start.1
  11.0 0.0 copy-start.2
  11.0 0.0 copy-start.3
  11.0 0.6 %collective-permute-done.1.main_ref.b_ref.refs_2_ = bf16[128,1024]{1,0:T(8,128)(2,1)S(1)} collective-permute-done((bf16[128,1024]{1,0:T(8,128)(2,1)}, bf16[128,1024]{1,0:T(8,128)(2,1)S(1)}, u32[]{:S(2)}, u32[]{:S(2)}) %collective-permute-start.1) | collective-permute-done | bytes 262176 | tf_op jit(solution)/shard_map/ppermute | solution.py:389
  11.6 4.2 %collective-permute-start.4 = (bf16[144,1024]{1,0:T(8,128)(2,1)S(1)}, bf16[144,1024]{1,0:T(8,128)(2,1)S(1)}, u32[]{:S(2)}, u32[]{:S(2)}) collective-permute-start(bf16[144,1024]{1,0:T(8,128)(2,1)S(1)} %join.1), channel_id=1, source_target_pairs={{0,24},{4,28},{8,0},{12,4},{16,8},{20,12},{24,16},{28,20},{1,25},{... | collective-permute-start | bytes 884744 | tf_op jit(solution)/shard_map/ppermute | solution.py:389
  15.9 1.5 %collective-permute-start.7 = (bf16[16,640]{1,0:T(8,128)(2,1)S(1)}, bf16[16,640]{1,0:T(8,128)(2,1)S(1)}, u32[]{:S(2)}, u32[]{:S(2)}) collective-permute-start(bf16[16,640]{1,0:T(8,128)(2,1)S(1)} %halo.1.halo_ref), channel_id=1, source_target_pairs={{0,4},{4,0},{8,12},{12,8},{16,20},{20,16},{24,28},{28,24},{1,5},{5... | collective-permute-start | bytes 61448 | tf_op jit(solution)/shard_map/ppermute | solution.py:393
  17.4 0.0 collective-permute-start.9
  17.4 0.0 copy-done
  17.4 0.0 copy-done.1
  17.4 0.0 copy-done.2
  17.4 0.0 copy-done.3
  17.4 1.0 %spectrum.1 = (f32[128,1024]{1,0:T(8,128)S(1)}, f32[8,128]{1,0:T(8,128)S(1)}) custom-call(bf16[144,1024]{1,0:T(8,128)(2,1)S(1)} %get-tuple-element.23.a_ref.refs_1_.own_ref.refs_0_.main_ref, bf16[128,192]{1,0:T(8,128)(2,1)S(1)} %copy-done.2, bf16[256,256]{1,0:T(8,128)(2,1)S(1)} %copy-done.1, bf16[64,256]{1,0:T(8,128)(2,1)S(1)} %copy-done.3, ...), custom_call_target="tpu_custom_call" | custom-call | tf_op jit(solution)/shard_map/spectrum/pallas_call | solution.py:406
  18.4 0.8 %own.1 = (bf16[128,1152]{1,0:T(8,128)(2,1)S(1)}, f32[64,1024]{1,0:T(8,128)S(1)}) custom-call(f32[8,128]{1,0:T(8,128)S(1)} %get-tuple-element.28.refs_7_.earlier_ref, bf16[144,1024]{1,0:T(8,128)(2,1)S(1)} %get-tuple-element.23.a_ref.refs_1_.own_ref.refs_0_.main_ref, bf16[16,640]{1,0:T(8,128)(2,1)S(1)} %halo.1.halo_ref), custom_call_target="tpu_custom_call" | custom-call | tf_op jit(solution)/shard_map/own/pallas_call | solution.py:406
  19.2 0.3 later.1.earlier_ref
  19.5 0.2 collective-permute-start.5
  19.6 0.0 collective-permute-done.refs_2_.refs_1_
  19.7 0.3 candidate.1.earlier_ref
  19.9 1.9 %collective-permute-start.6 = (bf16[64,1024]{1,0:T(8,128)(2,1)S(1)}, bf16[64,1024]{1,0:T(8,128)(2,1)S(1)}, u32[]{:S(2)}, u32[]{:S(2)}) collective-permute-start(bf16[64,1024]{1,0:T(8,128)(2,1)S(1)} %candidate.1.earlier_ref), channel_id=1, source_target_pairs={{0,8},{4,12},{8,16},{12,20},{16,24},{20,28},{24,0},{28,4},{1,9},{5... | collective-permute-start | bytes 393224 | tf_op jit(solution)/shard_map/ppermute | solution.py:389
  21.8 0.0 collective-permute-done.7.refs_3_
  21.8 1.0 %beside.1 = (bf16[128,1152]{1,0:T(8,128)(2,1)S(1)}, f32[64,1024]{1,0:T(8,128)S(1)}, bf16[64,1024]{1,0:T(8,128)(2,1)S(1)}) custom-call(bf16[64,1024]{1,0:T(8,128)(2,1)S(1)} %candidate.1.earlier_ref, bf16[128,1152]{1,0:T(8,128)(2,1)S(1)} %get-tuple-element.29.refs_0_.own_ref, f32[64,1024]{1,0:T(8,128)S(1)} %get-tuple-element.30.refs_1_.own_power_ref, ...), custom_call_target="tpu_custom_call" | custom-call | tf_op jit(solution)/shard_map/beside/pallas_call | solution.py:406
  22.8 0.2 collective-permute-done.4.refs_3_.halo_ref.main_ref
  23.0 1.0 %near.1 = (bf16[128,1152]{1,0:T(8,128)(2,1)S(1)}, f32[64,1024]{1,0:T(8,128)S(1)}, bf16[64,1024]{1,0:T(8,128)(2,1)S(1)}) custom-call(bf16[128,1152]{1,0:T(8,128)(2,1)S(1)} %get-tuple-element.32.own_ref, f32[64,1024]{1,0:T(8,128)S(1)} %get-tuple-element.33.own_power_ref, bf16[128,1024]{1,0:T(8,128)(2,1)S(1)} %collective-permute-done.1.main_ref.b_ref.refs_2_, ...), custom_call_target="tpu_custom_call" | custom-call | tf_op jit(solution)/shard_map/near/pallas_call | solution.py:406
  24.0 1.6 %collective-permute-start.8 = (bf16[64,1024]{1,0:T(8,128)(2,1)S(1)}, bf16[64,1024]{1,0:T(8,128)(2,1)S(1)}, u32[]{:S(2)}, u32[]{:S(2)}) collective-permute-start(bf16[64,1024]{1,0:T(8,128)(2,1)S(1)} %get-tuple-element.34), channel_id=1, source_target_pairs={{0,4},{4,0},{8,12},{12,8},{16,20},{20,16},{24,28},{28,24},{1,5},{5... | collective-permute-start | bytes 393224 | tf_op jit(solution)/shard_map/ppermute | solution.py:393
  25.6 0.0 collective-permute-done.9.halo_ref
  25.6 1.0 %far.1 = (bf16[128,1152]{1,0:T(8,128)(2,1)S(1)}, f32[64,1024]{1,0:T(8,128)S(1)}, bf16[64,1024]{1,0:T(8,128)(2,1)S(1)}) custom-call(bf16[128,1152]{1,0:T(8,128)(2,1)S(1)} %get-tuple-element.32.own_ref, f32[64,1024]{1,0:T(8,128)S(1)} %get-tuple-element.33.own_power_ref, bf16[144,1024]{1,0:T(8,128)(2,1)S(1)} %collective-permute-done.4.refs_3_.halo_ref.main_ref, ...), custom_call_target="tpu_custom_call" | custom-call | tf_op jit(solution)/shard_map/far/pallas_call | solution.py:406
  26.6 0.6 %collective-permute-start.10 = (bf16[64,1024]{1,0:T(8,128)(2,1)S(1)}, bf16[64,1024]{1,0:T(8,128)(2,1)S(1)}, u32[]{:S(2)}, u32[]{:S(2)}) collective-permute-start(bf16[64,1024]{1,0:T(8,128)(2,1)S(1)} %get-tuple-element.39), channel_id=1, source_target_pairs={{0,4},{4,0},{8,12},{12,8},{16,20},{20,16},{24,28},{28,24},{1,5},{5... | collective-permute-start | bytes 393224 | tf_op jit(solution)/shard_map/ppermute | solution.py:393
  27.2 0.5 %two.1.two_ref = bf16[64,1024]{1,0:T(8,128)(2,1)S(1)} custom-call(f32[16,128]{1,0:T(8,128)S(1)} %get-tuple-element.22.cond_ref.refs_0_, bf16[128,1152]{1,0:T(8,128)(2,1)S(1)} %get-tuple-element.29.refs_0_.own_ref, f32[64,1024]{1,0:T(8,128)S(1)} %get-tuple-element.30.refs_1_.own_power_ref, bf16[128,1152]{1,0:T(8,128)(2,1)S(1)} %get-tuple-element.35.ext_ref, ...), custom_call_target="tpu_custom_call" | custom-call | tf_op jit(solution)/shard_map/two/pallas_call | solution.py:406
  27.7 0.5 %four.1.four_ref = bf16[64,1024]{1,0:T(8,128)(2,1)S(1)} custom-call(f32[16,128]{1,0:T(8,128)S(1)} %get-tuple-element.22.cond_ref.refs_0_, bf16[128,1152]{1,0:T(8,128)(2,1)S(1)} %get-tuple-element.29.refs_0_.own_ref, f32[64,1024]{1,0:T(8,128)S(1)} %get-tuple-element.30.refs_1_.own_power_ref, bf16[128,1152]{1,0:T(8,128)(2,1)S(1)} %get-tuple-element.37.ext_ref, ...), custom_call_target="tpu_custom_call" | custom-call | tf_op jit(solution)/shard_map/four/pallas_call | solution.py:406
  28.2 0.0 collective-permute-done.5.refs_4_
  28.2 0.4 %collective-permute-done.6.refs_5_ = bf16[64,1024]{1,0:T(8,128)(2,1)S(1)} collective-permute-done((bf16[64,1024]{1,0:T(8,128)(2,1)S(1)}, bf16[64,1024]{1,0:T(8,128)(2,1)S(1)}, u32[]{:S(2)}, u32[]{:S(2)}) %collective-permute-start.6) | collective-permute-done | bytes 131104 | tf_op jit(solution)/shard_map/ppermute | solution.py:389
  28.6 1.7 %surface.1.surface_ref = f32[16,1024]{1,0:T(8,128)S(1)} custom-call(f32[16,128]{1,0:T(8,128)S(1)} %get-tuple-element.22.cond_ref.refs_0_, bf16[144,1024]{1,0:T(8,128)(2,1)S(1)} %get-tuple-element.23.a_ref.refs_1_.own_ref.refs_0_.main_ref, bf16[144,1024]{1,0:T(8,128)(2,1)S(1)} %collective-permute-done.refs_2_.refs_1_, ...), custom_call_target="tpu_custom_call" | custom-call | tf_op jit(solution)/shard_map/surface/pallas_call | solution.py:406
  30.2 0.0 collective-permute-done.8.near_ref
  30.3 0.1 one.1.one_ref
  30.3 1.5 %collective-permute-done.10.far_ref = bf16[64,1024]{1,0:T(8,128)(2,1)S(1)} collective-permute-done((bf16[64,1024]{1,0:T(8,128)(2,1)S(1)}, bf16[64,1024]{1,0:T(8,128)(2,1)S(1)}, u32[]{:S(2)}, u32[]{:S(2)}) %collective-permute-start.10) | collective-permute-done | bytes 131104 | tf_op jit(solution)/shard_map/ppermute | solution.py:393
  31.9 0.9 %place.1 = (f32[16,1024]{1,0:T(8,128)}, bf16[4,64,1024]{2,1,0:T(8,128)(2,1)}) custom-call(f32[16,128]{1,0:T(8,128)S(1)} %get-tuple-element.22.cond_ref.refs_0_, f32[16,1024]{1,0:T(8,128)S(1)} %surface.1.surface_ref, bf16[64,1024]{1,0:T(8,128)(2,1)S(1)} %one.1.one_ref, bf16[64,1024]{1,0:T(8,128)(2,1)S(1)} %two.1.two_ref, bf16[64,1024]{1,0:T(8,128)(2,1)S(1)} %four.1.four_ref, ...), custom_call_target="tpu_custom_call" | custom-call | tf_op jit(solution)/shard_map/place/pallas_call | solution.py:491
  (1 shorter events, 0.0 us)
Async XLA Ops:
  0.6 11.0 %collective-permute-start.1 = (bf16[128,1024]{1,0:T(8,128)(2,1)}, bf16[128,1024]{1,0:T(8,128)(2,1)S(1)}, u32[]{:S(2)}, u32[]{:S(2)}) collective-permute-start(bf16[128,1024]{1,0:T(8,128)(2,1)} %bitcast.5), channel_id=1, source_target_pairs={{0,24},{4,28},{8,0},{12,4},{16,8},{20,12},{24,16},{28,20},{1,25},{... | collective-permute-start | bytes 786440 | tf_op jit(solution)/shard_map/ppermute | solution.py:389
  7.4 3.4 %collective-permute-start.2 = (bf16[144,128]{1,0:T(8,128)(2,1)S(1)}, bf16[144,128]{1,0:T(8,128)(2,1)S(1)}, u32[]{:S(2)}, u32[]{:S(2)}) collective-permute-start(bf16[144,128]{1,0:T(8,128)(2,1)S(1)} %get-tuple-element.25), channel_id=1, source_target_pairs={{0,1},{1,2},{2,3},{3,0},{4,5},{5,6},{6,7},{7,4},{8,9},{9,10},{10,1... | collective-permute-start | bytes 110600 | tf_op jit(solution)/shard_map/ppermute | solution.py:389
  7.5 3.4 %collective-permute-start.3 = (bf16[144,128]{1,0:T(8,128)(2,1)S(1)}, bf16[144,128]{1,0:T(8,128)(2,1)S(1)}, u32[]{:S(2)}, u32[]{:S(2)}) collective-permute-start(bf16[144,128]{1,0:T(8,128)(2,1)S(1)} %get-tuple-element.26), channel_id=1, source_target_pairs={{0,3},{1,0},{2,1},{3,2},{4,7},{5,4},{6,5},{7,6},{8,11},{9,8},{10,9... | collective-permute-start | bytes 110600 | tf_op jit(solution)/shard_map/ppermute | solution.py:389
  9.2 10.4 %collective-permute-start = (bf16[144,1024]{1,0:T(8,128)(2,1)S(1)}, bf16[144,1024]{1,0:T(8,128)(2,1)S(1)}, u32[]{:S(2)}, u32[]{:S(2)}) collective-permute-start(bf16[144,1024]{1,0:T(8,128)(2,1)S(1)} %get-tuple-element.23.a_ref.refs_1_.own_ref.refs_0_.main_ref), channel_id=1, source_target_pairs={{0,4},{4,0},{8,12},{12,8},{16,20},{20,16},{24,28},{28,24},{1,5},{5... | collective-permute-start | bytes 884744 | tf_op jit(solution)/shard_map/ppermute | solution.py:393
  11.0 6.4 %copy-start = (bf16[512,256]{1,0:T(8,128)(2,1)S(1)}, bf16[512,256]{1,0:T(8,128)(2,1)}, u32[]{:S(2)}) copy-start(bf16[512,256]{1,0:T(8,128)(2,1)} %constant.11.clone.fourth_ref.refs_11_) | copy-start | bytes 786436
  11.0 6.4 %copy-start.1 = (bf16[256,256]{1,0:T(8,128)(2,1)S(1)}, bf16[256,256]{1,0:T(8,128)(2,1)}, u32[]{:S(2)}) copy-start(bf16[256,256]{1,0:T(8,128)(2,1)} %constant.9.clone.second_ref.refs_9_) | copy-start | bytes 393220
  11.0 6.4 %copy-start.2 = (bf16[128,192]{1,0:T(8,128)(2,1)S(1)}, bf16[128,192]{1,0:T(8,128)(2,1)}, u32[]{:S(2)}) copy-start(bf16[128,192]{1,0:T(8,128)(2,1)} %constant.8.clone.first_ref.refs_8_) | copy-start | bytes 147460
  11.0 6.4 %copy-start.3 = (bf16[64,256]{1,0:T(8,128)(2,1)S(1)}, bf16[64,256]{1,0:T(8,128)(2,1)}, u32[]{:S(2)}) copy-start(bf16[64,256]{1,0:T(8,128)(2,1)} %constant.10.clone.third_ref.refs_10_) | copy-start | bytes 98308
  11.6 11.4 %collective-permute-start.4 = (bf16[144,1024]{1,0:T(8,128)(2,1)S(1)}, bf16[144,1024]{1,0:T(8,128)(2,1)S(1)}, u32[]{:S(2)}, u32[]{:S(2)}) collective-permute-start(bf16[144,1024]{1,0:T(8,128)(2,1)S(1)} %join.1), channel_id=1, source_target_pairs={{0,24},{4,28},{8,0},{12,4},{16,8},{20,12},{24,16},{28,20},{1,25},{... | collective-permute-start | bytes 884744 | tf_op jit(solution)/shard_map/ppermute | solution.py:389
  15.9 6.0 %collective-permute-start.7 = (bf16[16,640]{1,0:T(8,128)(2,1)S(1)}, bf16[16,640]{1,0:T(8,128)(2,1)S(1)}, u32[]{:S(2)}, u32[]{:S(2)}) collective-permute-start(bf16[16,640]{1,0:T(8,128)(2,1)S(1)} %halo.1.halo_ref), channel_id=1, source_target_pairs={{0,4},{4,0},{8,12},{12,8},{16,20},{20,16},{24,28},{28,24},{1,5},{5... | collective-permute-start | bytes 61448 | tf_op jit(solution)/shard_map/ppermute | solution.py:393
  17.4 8.2 %collective-permute-start.9 = (bf16[16,640]{1,0:T(8,128)(2,1)S(1)}, bf16[16,640]{1,0:T(8,128)(2,1)S(1)}, u32[]{:S(2)}, u32[]{:S(2)}) collective-permute-start(bf16[16,640]{1,0:T(8,128)(2,1)S(1)} %halo.1.halo_ref), channel_id=1, source_target_pairs={{0,16},{4,20},{8,24},{12,28},{16,0},{20,4},{24,8},{28,12},{1,17},{... | collective-permute-start | bytes 61448 | tf_op jit(solution)/shard_map/ppermute | solution.py:389
  19.5 8.7 %collective-permute-start.5 = (bf16[64,1024]{1,0:T(8,128)(2,1)S(1)}, bf16[64,1024]{1,0:T(8,128)(2,1)S(1)}, u32[]{:S(2)}, u32[]{:S(2)}) collective-permute-start(bf16[64,1024]{1,0:T(8,128)(2,1)S(1)} %later.1.earlier_ref), channel_id=1, source_target_pairs={{0,28},{4,24},{8,4},{12,0},{16,12},{20,8},{24,20},{28,16},{1,29},{... | collective-permute-start | bytes 393224 | tf_op jit(solution)/shard_map/ppermute | solution.py:452
  19.9 8.6 %collective-permute-start.6 = (bf16[64,1024]{1,0:T(8,128)(2,1)S(1)}, bf16[64,1024]{1,0:T(8,128)(2,1)S(1)}, u32[]{:S(2)}, u32[]{:S(2)}) collective-permute-start(bf16[64,1024]{1,0:T(8,128)(2,1)S(1)} %candidate.1.earlier_ref), channel_id=1, source_target_pairs={{0,8},{4,12},{8,16},{12,20},{16,24},{20,28},{24,0},{28,4},{1,9},{5... | collective-permute-start | bytes 393224 | tf_op jit(solution)/shard_map/ppermute | solution.py:389
  24.0 6.2 %collective-permute-start.8 = (bf16[64,1024]{1,0:T(8,128)(2,1)S(1)}, bf16[64,1024]{1,0:T(8,128)(2,1)S(1)}, u32[]{:S(2)}, u32[]{:S(2)}) collective-permute-start(bf16[64,1024]{1,0:T(8,128)(2,1)S(1)} %get-tuple-element.34), channel_id=1, source_target_pairs={{0,4},{4,0},{8,12},{12,8},{16,20},{20,16},{24,28},{28,24},{1,5},{5... | collective-permute-start | bytes 393224 | tf_op jit(solution)/shard_map/ppermute | solution.py:393
  26.6 5.2 %collective-permute-start.10 = (bf16[64,1024]{1,0:T(8,128)(2,1)S(1)}, bf16[64,1024]{1,0:T(8,128)(2,1)S(1)}, u32[]{:S(2)}, u32[]{:S(2)}) collective-permute-start(bf16[64,1024]{1,0:T(8,128)(2,1)S(1)} %get-tuple-element.39), channel_id=1, source_target_pairs={{0,4},{4,0},{8,12},{12,8},{16,20},{20,16},{24,28},{28,24},{1,5},{5... | collective-permute-start | bytes 393224 | tf_op jit(solution)/shard_map/ppermute | solution.py:393

commit v8 on v7

--- a/solution.py
+++ b/solution.py
@@ -56,7 +56,7 @@
 
 
 def prep_kernel(
-    own_hbm, off_hbm, frac_hbm, partners_hbm, ref_ref, own_ref, cond_ref, taps_ref, low_ref, high_ref, *scratch
+    own_hbm, off_hbm, frac_hbm, partners_hbm, own_ref, cond_ref, taps_ref, low_ref, high_ref, *scratch
 ):
     off_ref, frac_ref, partners_ref, sems = scratch
     sources = (own_hbm, off_hbm, frac_hbm, partners_hbm)
@@ -72,10 +72,6 @@
     place, places = lax.axis_index("rng"), lax.axis_size("rng")
     values = [jnp.where(date + 1 + h < dates, partners_ref[0, h], 0) for h in range(SPAN)]
     values += [1 - date % 2, (place > 0).astype(jnp.int32), (place < places - 1).astype(jnp.int32), jnp.int32(0)]
-    beside = date + 1 - 2 * (date % 2)
-    held = [date, beside, date + 2, date + 4, beside + 2, beside + 4]
-    found = [(lax.rem(h, dates) == ref_ref[0]).astype(jnp.int32) for h in held]
-    values += found[0:4] + [(found[4] + found[5]) * int(dates == 8)]
     row = iota(cond_ref.shape, 0)
     cond = jnp.zeros(cond_ref.shape, jnp.int32)
     for k, value in enumerate(values):
@@ -111,7 +107,17 @@
     both_ref[rows:, width:] = jnp.zeros((HROWS, both_ref.shape[1] - width), BF16)
 
 
-def halo_kernel(blocks, cond_ref, taps_ref, left_ref, right_ref, out_ref):
+def halo_kernel(blocks, ref_ref, cond_ref, taps_ref, left_ref, right_ref, out_ref, all_ref):
+    date, dates = lax.axis_index("date"), lax.axis_size("date")
+    beside = date + 1 - 2 * (date % 2)
+    held = [date, beside, date + 2, date + 4, beside + 2, beside + 4]
+    found = [(lax.rem(h, dates) == ref_ref[0]).astype(jnp.int32) for h in held]
+    values = found[0:4] + [(found[4] + found[5]) * int(dates == 8)]
+    row = iota(cond_ref.shape, 0)
+    cond = cond_ref[...]
+    for k, value in enumerate(values):
+        cond = jnp.where(row == PICK + k, value.astype(F32), cond)
+    all_ref[...] = cond
     left = jnp.where(cond_ref[LEFT : LEFT + 1, :] > 0.0, left_ref[...].astype(F32), 0.0)
     right = jnp.where(cond_ref[RIGHT : RIGHT + 1, :] > 0.0, right_ref[...].astype(F32), 0.0)
     rows = (left.shape[0] - HROWS) // 2
@@ -402,11 +408,11 @@
     return value
 
 
-def call(kernel, name, out_shape, operands, scratch=()):
+def call(kernel, name, out_shape, operands, scratch=(), smem=0):
     return pl.pallas_call(
         kernel,
         out_shape=out_shape,
-        in_specs=[VMEM] * len(operands),
+        in_specs=[SMEM] * smem + [VMEM] * (len(operands) - smem),
         out_specs=jax.tree.map(lambda _: VMEM, out_shape),
         scratch_shapes=[pltpu.VMEM(*s) for s in scratch],
         compiler_params=PARAMS,
@@ -427,7 +433,7 @@
     own, cond, taps, low, high = pl.pallas_call(
         prep_kernel,
         out_shape=(sds((2 * rows + 16, cols), BF16), sds((16, LANES), F32), sds((HROWS, LANES), BF16), payload, payload),
-        in_specs=[pl.BlockSpec(memory_space=pltpu.HBM)] * 4 + [SMEM],
+        in_specs=[pl.BlockSpec(memory_space=pltpu.HBM)] * 4,
         out_specs=(VMEM,) * 5,
         scratch_shapes=[
             pltpu.VMEM(int_offset.shape[1:], jnp.int32),
@@ -437,21 +443,23 @@
         ],
         compiler_params=PARAMS,
         name="prepare",
-    )(*inputs, ref_date)
+    )(*inputs)
     beside = swapped(own, "date", 1)
     two = shifted(slc.reshape(2 * rows, cols), "date", 2)
     right = shifted(low, "rng", 1)
     left = shifted(high, "rng", -1)
     width = (rows // HROWS + 1) * LANES
-    halo = call(
-        functools.partial(halo_kernel, cols // BLK), "halo", sds((HROWS, width), BF16), (cond, taps, left, right)
+    halo, cond = call(
+        functools.partial(halo_kernel, cols // BLK),
+        "halo",
+        (sds((HROWS, width), BF16), sds(cond.shape, F32)),
+        (ref_date, cond, taps, left, right),
+        smem=1,
     )
     joined = sds((2 * rows + HROWS, cols), BF16)
     four = shifted(call(join_kernel, "join", joined, (halo, two)), "date", 2)
     later = call(functools.partial(candidate_kernel, (0, 2)), "later", field, (cond, own, two))
     across = lax.ppermute(later, "date", [(s, (s - 2) % dates ^ 1) for s in range(dates)])
-    amp = call(functools.partial(late_candidate_kernel, (0, 1)), "candidate", field, (later, cond, own, beside))
-    before = shifted(amp, "date", -2) if dates == 8 else spread(amp, "date")
     beside_halo = swapped(halo, "date", 1)
     four_halo = shifted(halo, "date", 4)
     first, second, third, fourth = [jnp.asarray(t) for t in surface_tables()]
@@ -466,8 +474,10 @@
     scratch = [[((k * rows, cols + LANES), BF16)] for k in range(4)]
     own_ext = call(own_kernel, "own", resampled, (energy, own, halo), scratch[1])
     *beside_ext, coh_beside = call(
-        beside_kernel, "beside", (*resampled, field), (amp, *own_ext, beside, beside_halo), scratch[3]
+        beside_kernel, "beside", (*resampled, field), (energy, *own_ext, beside, beside_halo), scratch[3]
     )
+    amp = call(functools.partial(late_candidate_kernel, (0, 1)), "candidate", field, (coh_beside, cond, own, beside))
+    before = shifted(amp, "date", -2) if dates == 8 else spread(amp, "date")
     *two_ext, coh_near = call(pair_kernel, "near", (*resampled, field), (*beside_ext, two, four), scratch[3])
     near = swapped(coh_near, "date", 1)
     coh_two = call(functools.partial(again_kernel, 1), "two", field, (cond, *own_ext, *two_ext), scratch[2])

time: 32.9 us -> 33.1 us (level)
    ppermute x6, waiting for transfers between devices: 1.29 us -> 1.64 us  [shifted(): lax.ppermute(value, axis, [(s, (s - steps) % count) for s in range(count)])]
  transfers between devices with their start and end apart: 11 -> 11, of which waited for: 5 -> 4; matrix products, arithmetic and copies ran while one was open for 0% -> 0% of each run, Pallas kernels for 28% -> 28%
where the time goes in v8:
time: 33.1 us; the launch traced here: 32.9 us
  starting transfers between devices  18.4 us (56%)
  Pallas kernels  10.1 us (31%)
  waiting for transfers between devices  2.96 us (9%)
  between operations  1.43 us (4%)
    ppermute x6, starting transfers between devices, shifted(): lax.ppermute(value, axis, [(s, (s - steps) % count) for s in range(count)])  12.9 us
    pallas_call x13, Pallas kernels, call(): pl.pallas_call(kernel, out_shape=out_shape, in_specs=[SMEM] * smem + [VME...  8.21 us
    ppermute x4, starting transfers between devices, swapped(): lax.ppermute(value, axis, [(s, s ^ step) for s in range(lax.axis_size(axi...  5.19 us
    ppermute x6, waiting for transfers between devices, shifted(): lax.ppermute(value, axis, [(s, (s - steps) % count) for s in range(count)])  1.64 us
    ppermute x4, waiting for transfers between devices, swapped(): lax.ppermute(value, axis, [(s, s ^ step) for s in range(lax.axis_size(axi...  1.31 us
    pallas_call x1, Pallas kernels, body(): pl.pallas_call(prep_kernel, out_shape=(sds((2 * rows + 16, cols), BF16),...  1.03 us
    pallas_call x1, Pallas kernels, body(): pl.pallas_call(place_kernel, out_shape=(sds(surface.shape, F32), sds((SPA...  0.85 us
  transfers between devices with their start and end apart: 11, of which 4 were waited for; matrix products, arithmetic and copies ran while one was open for 0% of the time, Pallas kernels for 28%

profile of v8, /device:TPU:0, one launch (start us, length us, event | category | flops | bytes accessed | tf_op | source)
XLA Modules:
  0.0 32.9 jit_solution(13396759497387419761)
XLA Ops:
  0.6 5.1 %collective-permute-start.3 = (bf16[128,1024]{1,0:T(8,128)(2,1)}, bf16[128,1024]{1,0:T(8,128)(2,1)S(1)}, u32[]{:S(2)}, u32[]{:S(2)}) collective-permute-start(bf16[128,1024]{1,0:T(8,128)(2,1)} %bitcast.5), channel_id=1, source_target_pairs={{0,24},{4,28},{8,0},{12,4},{16,8},{20,12},{24,16},{28,20},{1,25},{... | collective-permute-start | bytes 786440 | tf_op jit(solution)/shard_map/ppermute | solution.py:395
  5.7 1.0 %prepare.1 = (bf16[144,1024]{1,0:T(8,128)(2,1)S(1)}, f32[16,128]{1,0:T(8,128)S(1)}, bf16[16,128]{1,0:T(8,128)(2,1)S(1)}, bf16[144,128]{1,0:T(8,128)(2,1)S(1)}, bf16[144,128]{1,0:T(8,128)(2,1)S(1)}) custom-call(bf16[128,1024]{1,0:T(8,128)(2,1)} %bitcast.6, s32[1,16]{1,0:T(1,128)} %bitcast.7, f32[1,16]{1,0:T(1,128)} %bitcast.8, s32[1,4]{1,0:T(1,128)} %partners_hbm.1), custom_call_target="tpu_custom_call" | custom-call | tf_op jit(solution)/shard_map/prepare/pallas_call | solution.py:433
  6.8 0.1 collective-permute-start
  6.8 1.7 %collective-permute-start.1 = (bf16[144,128]{1,0:T(8,128)(2,1)S(1)}, bf16[144,128]{1,0:T(8,128)(2,1)S(1)}, u32[]{:S(2)}, u32[]{:S(2)}) collective-permute-start(bf16[144,128]{1,0:T(8,128)(2,1)S(1)} %get-tuple-element.27), channel_id=1, source_target_pairs={{0,3},{1,0},{2,1},{3,2},{4,7},{5,4},{6,5},{7,6},{8,11},{9,8},{10,9... | collective-permute-start | bytes 110600 | tf_op jit(solution)/shard_map/ppermute | solution.py:395
  8.6 1.5 %collective-permute-start.2 = (bf16[144,1024]{1,0:T(8,128)(2,1)S(1)}, bf16[144,1024]{1,0:T(8,128)(2,1)S(1)}, u32[]{:S(2)}, u32[]{:S(2)}) collective-permute-start(bf16[144,1024]{1,0:T(8,128)(2,1)S(1)} %get-tuple-element.29.a_ref.own_ref.main_ref.refs_1_.refs_0_), channel_id=1, source_target_pairs={{0,4},{4,0},{8,12},{12,8},{16,20},{20,16},{24,28},{28,24},{1,5},{5... | collective-permute-start | bytes 884744 | tf_op jit(solution)/shard_map/ppermute | solution.py:399
  10.7 0.0 collective-permute-done.left_ref
  10.8 0.0 collective-permute-done.1.right_ref
  10.8 0.2 halo.1
  10.9 0.7 %collective-permute-done.3.main_ref.b_ref.refs_2_ = bf16[128,1024]{1,0:T(8,128)(2,1)S(1)} collective-permute-done((bf16[128,1024]{1,0:T(8,128)(2,1)}, bf16[128,1024]{1,0:T(8,128)(2,1)S(1)}, u32[]{:S(2)}, u32[]{:S(2)}) %collective-permute-start.3) | collective-permute-done | bytes 262176 | tf_op jit(solution)/shard_map/ppermute | solution.py:395
  11.6 0.0 copy-start
  11.6 0.0 copy-start.1
  11.6 0.0 copy-start.2
  11.6 0.0 copy-start.3
  11.6 4.2 %collective-permute-start.4 = (bf16[144,1024]{1,0:T(8,128)(2,1)S(1)}, bf16[144,1024]{1,0:T(8,128)(2,1)S(1)}, u32[]{:S(2)}, u32[]{:S(2)}) collective-permute-start(bf16[144,1024]{1,0:T(8,128)(2,1)S(1)} %join.1), channel_id=1, source_target_pairs={{0,24},{4,28},{8,0},{12,4},{16,8},{20,12},{24,16},{28,20},{1,25},{... | collective-permute-start | bytes 884744 | tf_op jit(solution)/shard_map/ppermute | solution.py:395
  15.9 1.5 %collective-permute-start.6 = (bf16[16,640]{1,0:T(8,128)(2,1)S(1)}, bf16[16,640]{1,0:T(8,128)(2,1)S(1)}, u32[]{:S(2)}, u32[]{:S(2)}) collective-permute-start(bf16[16,640]{1,0:T(8,128)(2,1)S(1)} %get-tuple-element.30.halo_ref), channel_id=1, source_target_pairs={{0,4},{4,0},{8,12},{12,8},{16,20},{20,16},{24,28},{28,24},{1,5},{5... | collective-permute-start | bytes 61448 | tf_op jit(solution)/shard_map/ppermute | solution.py:399
  17.4 0.0 collective-permute-start.9
  17.4 0.0 copy-done
  17.4 0.0 copy-done.1
  17.4 0.0 copy-done.2
  17.4 0.0 copy-done.3
  17.4 1.0 %spectrum.1 = (f32[128,1024]{1,0:T(8,128)S(1)}, f32[8,128]{1,0:T(8,128)S(1)}) custom-call(bf16[144,1024]{1,0:T(8,128)(2,1)S(1)} %get-tuple-element.29.a_ref.own_ref.main_ref.refs_1_.refs_0_, bf16[128,192]{1,0:T(8,128)(2,1)S(1)} %copy-done.2, bf16[256,256]{1,0:T(8,128)(2,1)S(1)} %copy-done.1, bf16[64,256]{1,0:T(8,128)(2,1)S(1)} %copy-done.3, ...), custom_call_target="tpu_custom_call" | custom-call | tf_op jit(solution)/shard_map/spectrum/pallas_call | solution.py:412
  18.4 0.8 %own.1 = (bf16[128,1152]{1,0:T(8,128)(2,1)S(1)}, f32[64,1024]{1,0:T(8,128)S(1)}) custom-call(f32[8,128]{1,0:T(8,128)S(1)} %get-tuple-element.31.earlier_ref.refs_7_, bf16[144,1024]{1,0:T(8,128)(2,1)S(1)} %get-tuple-element.29.a_ref.own_ref.main_ref.refs_1_.refs_0_, bf16[16,640]{1,0:T(8,128)(2,1)S(1)} %get-tuple-element.30.halo_ref), custom_call_target="tpu_custom_call" | custom-call | tf_op jit(solution)/shard_map/own/pallas_call | solution.py:412
  19.2 0.3 later.1
  19.5 0.4 %collective-permute-start.5 = (bf16[64,1024]{1,0:T(8,128)(2,1)S(1)}, bf16[64,1024]{1,0:T(8,128)(2,1)S(1)}, u32[]{:S(2)}, u32[]{:S(2)}) collective-permute-start(bf16[64,1024]{1,0:T(8,128)(2,1)S(1)} %later.1), channel_id=1, source_target_pairs={{0,28},{4,24},{8,4},{12,0},{16,12},{20,8},{24,20},{28,16},{1,29},{... | collective-permute-start | bytes 393224 | tf_op jit(solution)/shard_map/ppermute | solution.py:462
  19.8 0.0 collective-permute-done.6.refs_3_
  19.8 0.0 collective-permute-done.2.refs_2_.refs_1_
  19.8 1.0 %beside.1 = (bf16[128,1152]{1,0:T(8,128)(2,1)S(1)}, f32[64,1024]{1,0:T(8,128)S(1)}, bf16[64,1024]{1,0:T(8,128)(2,1)S(1)}) custom-call(f32[8,128]{1,0:T(8,128)S(1)} %get-tuple-element.31.earlier_ref.refs_7_, bf16[128,1152]{1,0:T(8,128)(2,1)S(1)} %get-tuple-element.32.refs_0_.own_ref, f32[64,1024]{1,0:T(8,128)S(1)} %get-tuple-element.33.refs_1_.own_power_ref, ...), custom_call_target="tpu_custom_call" | custom-call | tf_op jit(solution)/shard_map/beside/pallas_call | solution.py:412
  20.9 0.3 candidate.1
  21.1 1.7 %collective-permute-start.7 = (bf16[64,1024]{1,0:T(8,128)(2,1)S(1)}, bf16[64,1024]{1,0:T(8,128)(2,1)S(1)}, u32[]{:S(2)}, u32[]{:S(2)}) collective-permute-start(bf16[64,1024]{1,0:T(8,128)(2,1)S(1)} %candidate.1), channel_id=1, source_target_pairs={{0,8},{4,12},{8,16},{12,20},{16,24},{20,28},{24,0},{28,4},{1,9},{5... | collective-permute-start | bytes 393224 | tf_op jit(solution)/shard_map/ppermute | solution.py:395
  22.9 0.5 %collective-permute-done.4.refs_3_.halo_ref.main_ref = bf16[144,1024]{1,0:T(8,128)(2,1)S(1)} collective-permute-done((bf16[144,1024]{1,0:T(8,128)(2,1)S(1)}, bf16[144,1024]{1,0:T(8,128)(2,1)S(1)}, u32[]{:S(2)}, u32[]{:S(2)}) %collective-permute-start.4) | collective-permute-done | bytes 294944 | tf_op jit(solution)/shard_map/ppermute | solution.py:395
  23.4 1.0 %near.1 = (bf16[128,1152]{1,0:T(8,128)(2,1)S(1)}, f32[64,1024]{1,0:T(8,128)S(1)}, bf16[64,1024]{1,0:T(8,128)(2,1)S(1)}) custom-call(bf16[128,1152]{1,0:T(8,128)(2,1)S(1)} %get-tuple-element.36.own_ref, f32[64,1024]{1,0:T(8,128)S(1)} %get-tuple-element.37.own_power_ref, bf16[128,1024]{1,0:T(8,128)(2,1)S(1)} %collective-permute-done.3.main_ref.b_ref.refs_2_, ...), custom_call_target="tpu_custom_call" | custom-call | tf_op jit(solution)/shard_map/near/pallas_call | solution.py:412
  24.4 1.6 %collective-permute-start.8 = (bf16[64,1024]{1,0:T(8,128)(2,1)S(1)}, bf16[64,1024]{1,0:T(8,128)(2,1)S(1)}, u32[]{:S(2)}, u32[]{:S(2)}) collective-permute-start(bf16[64,1024]{1,0:T(8,128)(2,1)S(1)} %get-tuple-element.38), channel_id=1, source_target_pairs={{0,4},{4,0},{8,12},{12,8},{16,20},{20,16},{24,28},{28,24},{1,5},{5... | collective-permute-start | bytes 393224 | tf_op jit(solution)/shard_map/ppermute | solution.py:399
  26.0 0.0 collective-permute-done.9.halo_ref
  26.0 1.0 %far.1 = (bf16[128,1152]{1,0:T(8,128)(2,1)S(1)}, f32[64,1024]{1,0:T(8,128)S(1)}, bf16[64,1024]{1,0:T(8,128)(2,1)S(1)}) custom-call(bf16[128,1152]{1,0:T(8,128)(2,1)S(1)} %get-tuple-element.36.own_ref, f32[64,1024]{1,0:T(8,128)S(1)} %get-tuple-element.37.own_power_ref, bf16[144,1024]{1,0:T(8,128)(2,1)S(1)} %collective-permute-done.4.refs_3_.halo_ref.main_ref, ...), custom_call_target="tpu_custom_call" | custom-call | tf_op jit(solution)/shard_map/far/pallas_call | solution.py:412
  27.0 0.6 %collective-permute-start.10 = (bf16[64,1024]{1,0:T(8,128)(2,1)S(1)}, bf16[64,1024]{1,0:T(8,128)(2,1)S(1)}, u32[]{:S(2)}, u32[]{:S(2)}) collective-permute-start(bf16[64,1024]{1,0:T(8,128)(2,1)S(1)} %get-tuple-element.43), channel_id=1, source_target_pairs={{0,4},{4,0},{8,12},{12,8},{16,20},{20,16},{24,28},{28,24},{1,5},{5... | collective-permute-start | bytes 393224 | tf_op jit(solution)/shard_map/ppermute | solution.py:399
  27.6 0.5 %four.1.four_ref = bf16[64,1024]{1,0:T(8,128)(2,1)S(1)} custom-call(f32[16,128]{1,0:T(8,128)S(1)} %get-tuple-element.28.cond_ref.refs_0_, bf16[128,1152]{1,0:T(8,128)(2,1)S(1)} %get-tuple-element.32.refs_0_.own_ref, f32[64,1024]{1,0:T(8,128)S(1)} %get-tuple-element.33.refs_1_.own_power_ref, bf16[128,1152]{1,0:T(8,128)(2,1)S(1)} %get-tuple-element.41.ext_ref, ...), custom_call_target="tpu_custom_call" | custom-call | tf_op jit(solution)/shard_map/four/pallas_call | solution.py:412
  28.0 0.5 %two.1.two_ref = bf16[64,1024]{1,0:T(8,128)(2,1)S(1)} custom-call(f32[16,128]{1,0:T(8,128)S(1)} %get-tuple-element.28.cond_ref.refs_0_, bf16[128,1152]{1,0:T(8,128)(2,1)S(1)} %get-tuple-element.32.refs_0_.own_ref, f32[64,1024]{1,0:T(8,128)S(1)} %get-tuple-element.33.refs_1_.own_power_ref, bf16[128,1152]{1,0:T(8,128)(2,1)S(1)} %get-tuple-element.39.ext_ref, ...), custom_call_target="tpu_custom_call" | custom-call | tf_op jit(solution)/shard_map/two/pallas_call | solution.py:412
  28.5 0.0 collective-permute-done.5.refs_4_
  28.5 0.4 %collective-permute-done.7.refs_5_ = bf16[64,1024]{1,0:T(8,128)(2,1)S(1)} collective-permute-done((bf16[64,1024]{1,0:T(8,128)(2,1)S(1)}, bf16[64,1024]{1,0:T(8,128)(2,1)S(1)}, u32[]{:S(2)}, u32[]{:S(2)}) %collective-permute-start.7) | collective-permute-done | bytes 131104 | tf_op jit(solution)/shard_map/ppermute | solution.py:395
  29.0 1.7 %surface.1.surface_ref = f32[16,1024]{1,0:T(8,128)S(1)} custom-call(f32[16,128]{1,0:T(8,128)S(1)} %get-tuple-element.28.cond_ref.refs_0_, bf16[144,1024]{1,0:T(8,128)(2,1)S(1)} %get-tuple-element.29.a_ref.own_ref.main_ref.refs_1_.refs_0_, bf16[144,1024]{1,0:T(8,128)(2,1)S(1)} %collective-permute-done.2.refs_2_.refs_1_, ...), custom_call_target="tpu_custom_call" | custom-call | tf_op jit(solution)/shard_map/surface/pallas_call | solution.py:412
  30.6 0.0 collective-permute-done.8.near_ref
  30.6 0.1 one.1.one_ref
  30.7 1.3 %collective-permute-done.10.far_ref = bf16[64,1024]{1,0:T(8,128)(2,1)S(1)} collective-permute-done((bf16[64,1024]{1,0:T(8,128)(2,1)S(1)}, bf16[64,1024]{1,0:T(8,128)(2,1)S(1)}, u32[]{:S(2)}, u32[]{:S(2)}) %collective-permute-start.10) | collective-permute-done | bytes 131104 | tf_op jit(solution)/shard_map/ppermute | solution.py:399
  32.0 0.9 %place.1 = (f32[16,1024]{1,0:T(8,128)}, bf16[4,64,1024]{2,1,0:T(8,128)(2,1)}) custom-call(f32[16,128]{1,0:T(8,128)S(1)} %get-tuple-element.28.cond_ref.refs_0_, f32[16,1024]{1,0:T(8,128)S(1)} %surface.1.surface_ref, bf16[64,1024]{1,0:T(8,128)(2,1)S(1)} %one.1.one_ref, bf16[64,1024]{1,0:T(8,128)(2,1)S(1)} %two.1.two_ref, bf16[64,1024]{1,0:T(8,128)(2,1)S(1)} %four.1.four_ref, ...), custom_call_target="tpu_custom_call" | custom-call | tf_op jit(solution)/shard_map/place/pallas_call | solution.py:501
  (1 shorter events, 0.0 us)
Async XLA Ops:
  0.6 11.0 %collective-permute-start.3 = (bf16[128,1024]{1,0:T(8,128)(2,1)}, bf16[128,1024]{1,0:T(8,128)(2,1)S(1)}, u32[]{:S(2)}, u32[]{:S(2)}) collective-permute-start(bf16[128,1024]{1,0:T(8,128)(2,1)} %bitcast.5), channel_id=1, source_target_pairs={{0,24},{4,28},{8,0},{12,4},{16,8},{20,12},{24,16},{28,20},{1,25},{... | collective-permute-start | bytes 786440 | tf_op jit(solution)/shard_map/ppermute | solution.py:395
  6.8 4.0 %collective-permute-start = (bf16[144,128]{1,0:T(8,128)(2,1)S(1)}, bf16[144,128]{1,0:T(8,128)(2,1)S(1)}, u32[]{:S(2)}, u32[]{:S(2)}) collective-permute-start(bf16[144,128]{1,0:T(8,128)(2,1)S(1)} %get-tuple-element.26), channel_id=1, source_target_pairs={{0,1},{1,2},{2,3},{3,0},{4,5},{5,6},{6,7},{7,4},{8,9},{9,10},{10,1... | collective-permute-start | bytes 110600 | tf_op jit(solution)/shard_map/ppermute | solution.py:395
  6.8 3.9 %collective-permute-start.1 = (bf16[144,128]{1,0:T(8,128)(2,1)S(1)}, bf16[144,128]{1,0:T(8,128)(2,1)S(1)}, u32[]{:S(2)}, u32[]{:S(2)}) collective-permute-start(bf16[144,128]{1,0:T(8,128)(2,1)S(1)} %get-tuple-element.27), channel_id=1, source_target_pairs={{0,3},{1,0},{2,1},{3,2},{4,7},{5,4},{6,5},{7,6},{8,11},{9,8},{10,9... | collective-permute-start | bytes 110600 | tf_op jit(solution)/shard_map/ppermute | solution.py:395
  8.6 11.3 %collective-permute-start.2 = (bf16[144,1024]{1,0:T(8,128)(2,1)S(1)}, bf16[144,1024]{1,0:T(8,128)(2,1)S(1)}, u32[]{:S(2)}, u32[]{:S(2)}) collective-permute-start(bf16[144,1024]{1,0:T(8,128)(2,1)S(1)} %get-tuple-element.29.a_ref.own_ref.main_ref.refs_1_.refs_0_), channel_id=1, source_target_pairs={{0,4},{4,0},{8,12},{12,8},{16,20},{20,16},{24,28},{28,24},{1,5},{5... | collective-permute-start | bytes 884744 | tf_op jit(solution)/shard_map/ppermute | solution.py:399
  11.6 5.8 %copy-start = (bf16[512,256]{1,0:T(8,128)(2,1)S(1)}, bf16[512,256]{1,0:T(8,128)(2,1)}, u32[]{:S(2)}) copy-start(bf16[512,256]{1,0:T(8,128)(2,1)} %constant.11.clone.fourth_ref.refs_11_) | copy-start | bytes 786436
  11.6 5.8 %copy-start.1 = (bf16[256,256]{1,0:T(8,128)(2,1)S(1)}, bf16[256,256]{1,0:T(8,128)(2,1)}, u32[]{:S(2)}) copy-start(bf16[256,256]{1,0:T(8,128)(2,1)} %constant.9.clone.second_ref.refs_9_) | copy-start | bytes 393220
  11.6 5.8 %copy-start.2 = (bf16[128,192]{1,0:T(8,128)(2,1)S(1)}, bf16[128,192]{1,0:T(8,128)(2,1)}, u32[]{:S(2)}) copy-start(bf16[128,192]{1,0:T(8,128)(2,1)} %constant.8.clone.first_ref.refs_8_) | copy-start | bytes 147460
  11.6 5.8 %copy-start.3 = (bf16[64,256]{1,0:T(8,128)(2,1)S(1)}, bf16[64,256]{1,0:T(8,128)(2,1)}, u32[]{:S(2)}) copy-start(bf16[64,256]{1,0:T(8,128)(2,1)} %constant.10.clone.third_ref.refs_10_) | copy-start | bytes 98308
  11.6 11.7 %collective-permute-start.4 = (bf16[144,1024]{1,0:T(8,128)(2,1)S(1)}, bf16[144,1024]{1,0:T(8,128)(2,1)S(1)}, u32[]{:S(2)}, u32[]{:S(2)}) collective-permute-start(bf16[144,1024]{1,0:T(8,128)(2,1)S(1)} %join.1), channel_id=1, source_target_pairs={{0,24},{4,28},{8,0},{12,4},{16,8},{20,12},{24,16},{28,20},{1,25},{... | collective-permute-start | bytes 884744 | tf_op jit(solution)/shard_map/ppermute | solution.py:395
  15.9 4.0 %collective-permute-start.6 = (bf16[16,640]{1,0:T(8,128)(2,1)S(1)}, bf16[16,640]{1,0:T(8,128)(2,1)S(1)}, u32[]{:S(2)}, u32[]{:S(2)}) collective-permute-start(bf16[16,640]{1,0:T(8,128)(2,1)S(1)} %get-tuple-element.30.halo_ref), channel_id=1, source_target_pairs={{0,4},{4,0},{8,12},{12,8},{16,20},{20,16},{24,28},{28,24},{1,5},{5... | collective-permute-start | bytes 61448 | tf_op jit(solution)/shard_map/ppermute | solution.py:399
  17.4 8.6 %collective-permute-start.9 = (bf16[16,640]{1,0:T(8,128)(2,1)S(1)}, bf16[16,640]{1,0:T(8,128)(2,1)S(1)}, u32[]{:S(2)}, u32[]{:S(2)}) collective-permute-start(bf16[16,640]{1,0:T(8,128)(2,1)S(1)} %get-tuple-element.30.halo_ref), channel_id=1, source_target_pairs={{0,16},{4,20},{8,24},{12,28},{16,0},{20,4},{24,8},{28,12},{1,17},{... | collective-permute-start | bytes 61448 | tf_op jit(solution)/shard_map/ppermute | solution.py:395
  19.5 9.0 %collective-permute-start.5 = (bf16[64,1024]{1,0:T(8,128)(2,1)S(1)}, bf16[64,1024]{1,0:T(8,128)(2,1)S(1)}, u32[]{:S(2)}, u32[]{:S(2)}) collective-permute-start(bf16[64,1024]{1,0:T(8,128)(2,1)S(1)} %later.1), channel_id=1, source_target_pairs={{0,28},{4,24},{8,4},{12,0},{16,12},{20,8},{24,20},{28,16},{1,29},{... | collective-permute-start | bytes 393224 | tf_op jit(solution)/shard_map/ppermute | solution.py:462
  21.1 7.8 %collective-permute-start.7 = (bf16[64,1024]{1,0:T(8,128)(2,1)S(1)}, bf16[64,1024]{1,0:T(8,128)(2,1)S(1)}, u32[]{:S(2)}, u32[]{:S(2)}) collective-permute-start(bf16[64,1024]{1,0:T(8,128)(2,1)S(1)} %candidate.1), channel_id=1, source_target_pairs={{0,8},{4,12},{8,16},{12,20},{16,24},{20,28},{24,0},{28,4},{1,9},{5... | collective-permute-start | bytes 393224 | tf_op jit(solution)/shard_map/ppermute | solution.py:395
  24.4 6.2 %collective-permute-start.8 = (bf16[64,1024]{1,0:T(8,128)(2,1)S(1)}, bf16[64,1024]{1,0:T(8,128)(2,1)S(1)}, u32[]{:S(2)}, u32[]{:S(2)}) collective-permute-start(bf16[64,1024]{1,0:T(8,128)(2,1)S(1)} %get-tuple-element.38), channel_id=1, source_target_pairs={{0,4},{4,0},{8,12},{12,8},{16,20},{20,16},{24,28},{28,24},{1,5},{5... | collective-permute-start | bytes 393224 | tf_op jit(solution)/shard_map/ppermute | solution.py:399
  27.0 5.0 %collective-permute-start.10 = (bf16[64,1024]{1,0:T(8,128)(2,1)S(1)}, bf16[64,1024]{1,0:T(8,128)(2,1)S(1)}, u32[]{:S(2)}, u32[]{:S(2)}) collective-permute-start(bf16[64,1024]{1,0:T(8,128)(2,1)S(1)} %get-tuple-element.43), channel_id=1, source_target_pairs={{0,4},{4,0},{8,12},{12,8},{16,20},{20,16},{24,28},{28,24},{1,5},{5... | collective-permute-start | bytes 393224 | tf_op jit(solution)/shard_map/ppermute | solution.py:399

commit v9 on v6

--- a/solution.py
+++ b/solution.py
@@ -462,9 +462,9 @@
     scratch = [[((k * rows, cols + LANES), BF16)] for k in range(4)]
     own_ext = call(own_kernel, "own", resampled, (energy, own, halo), scratch[1])
     *beside_ext, coh_beside = call(
-        beside_kernel, "beside", (*resampled, field), (energy, *own_ext, beside, beside_halo), scratch[3]
+        beside_kernel, "beside", (*resampled, field), (later, *own_ext, beside, beside_halo), scratch[3]
     )
-    amp = call(functools.partial(late_candidate_kernel, (0, 1)), "candidate", field, (coh_beside, cond, own, beside))
+    amp = call(functools.partial(candidate_kernel, (0, 1)), "candidate", field, (cond, own, beside))
     before = shifted(amp, "date", -2) if dates == 8 else spread(amp, "date")
     *two_ext, coh_near = call(pair_kernel, "near", (*resampled, field), (*beside_ext, two, four), scratch[3])
     near = swapped(coh_near, "date", 1)

time: 33 us -> 33 us (level)
    ppermute x4, waiting for transfers between devices: 0.65 us -> 1.63 us  [swapped(): lax.ppermute(value, axis, [(s, s ^ step) for s in range(lax.axis_size(axi...]
    ppermute x6, waiting for transfers between devices: 2.3 us -> 1.34 us  [shifted(): lax.ppermute(value, axis, [(s, (s - steps) % count) for s in range(count)])]
where the time goes in v9:
time: 33 us; the launch traced here: 32.8 us
  starting transfers between devices  18.4 us (56%)
  Pallas kernels  10 us (30%)
  waiting for transfers between devices  2.98 us (9%)
  between operations  1.43 us (4%)
    ppermute x6, starting transfers between devices, shifted(): lax.ppermute(value, axis, [(s, (s - steps) % count) for s in range(count)])  13 us
    pallas_call x12, Pallas kernels, call(): pl.pallas_call(kernel, out_shape=out_shape, in_specs=[VMEM] * len(operand...  8.06 us
    ppermute x4, starting transfers between devices, swapped(): lax.ppermute(value, axis, [(s, s ^ step) for s in range(lax.axis_size(axi...  5.19 us
    ppermute x4, waiting for transfers between devices, swapped(): lax.ppermute(value, axis, [(s, s ^ step) for s in range(lax.axis_size(axi...  1.63 us
    ppermute x6, waiting for transfers between devices, shifted(): lax.ppermute(value, axis, [(s, (s - steps) % count) for s in range(count)])  1.34 us
    pallas_call x1, Pallas kernels, body(): pl.pallas_call(prep_kernel, out_shape=(sds((2 * rows + 16, cols), BF16),...  1.03 us
    pallas_call x1, Pallas kernels, body(): pl.pallas_call(place_kernel, out_shape=(sds(surface.shape, F32), sds((SPA...  0.93 us
  transfers between devices with their start and end apart: 11, of which 5 were waited for; matrix products, arithmetic and copies ran while one was open for 0% of the time, Pallas kernels for 28%

profile of v9, /device:TPU:0, one launch (start us, length us, event | category | flops | bytes accessed | tf_op | source)
XLA Modules:
  0.0 32.8 jit_solution(12781495221809500722)
XLA Ops:
  0.6 5.1 %collective-permute-start.1 = (bf16[128,1024]{1,0:T(8,128)(2,1)}, bf16[128,1024]{1,0:T(8,128)(2,1)S(1)}, u32[]{:S(2)}, u32[]{:S(2)}) collective-permute-start(bf16[128,1024]{1,0:T(8,128)(2,1)} %bitcast.5), channel_id=1, source_target_pairs={{0,24},{4,28},{8,0},{12,4},{16,8},{20,12},{24,16},{28,20},{1,25},{... | collective-permute-start | bytes 786440 | tf_op jit(solution)/shard_map/ppermute | solution.py:387
  6.4 1.0 %prepare.1 = (bf16[144,1024]{1,0:T(8,128)(2,1)S(1)}, f32[16,128]{1,0:T(8,128)S(1)}, bf16[16,128]{1,0:T(8,128)(2,1)S(1)}, bf16[144,128]{1,0:T(8,128)(2,1)S(1)}, bf16[144,128]{1,0:T(8,128)(2,1)S(1)}) custom-call(bf16[128,1024]{1,0:T(8,128)(2,1)} %bitcast.6, s32[1,16]{1,0:T(1,128)} %bitcast.7, f32[1,16]{1,0:T(1,128)} %bitcast.8, s32[1,4]{1,0:T(1,128)} %partners_hbm.1, ...), custom_call_target="tpu_custom_call" | custom-call | tf_op jit(solution)/shard_map/prepare/pallas_call | solution.py:425
  7.4 0.1 collective-permute-start.2
  7.5 1.7 %collective-permute-start.3 = (bf16[144,128]{1,0:T(8,128)(2,1)S(1)}, bf16[144,128]{1,0:T(8,128)(2,1)S(1)}, u32[]{:S(2)}, u32[]{:S(2)}) collective-permute-start(bf16[144,128]{1,0:T(8,128)(2,1)S(1)} %get-tuple-element.26), channel_id=1, source_target_pairs={{0,3},{1,0},{2,1},{3,2},{4,7},{5,4},{6,5},{7,6},{8,11},{9,8},{10,9... | collective-permute-start | bytes 110600 | tf_op jit(solution)/shard_map/ppermute | solution.py:387
  9.2 1.5 %collective-permute-start = (bf16[144,1024]{1,0:T(8,128)(2,1)S(1)}, bf16[144,1024]{1,0:T(8,128)(2,1)S(1)}, u32[]{:S(2)}, u32[]{:S(2)}) collective-permute-start(bf16[144,1024]{1,0:T(8,128)(2,1)S(1)} %get-tuple-element.23.a_ref.own_ref.refs_0_.main_ref), channel_id=1, source_target_pairs={{0,4},{4,0},{8,12},{12,8},{16,20},{20,16},{24,28},{28,24},{1,5},{5... | collective-permute-start | bytes 884744 | tf_op jit(solution)/shard_map/ppermute | solution.py:391
  10.7 0.1 collective-permute-done.2.left_ref
  10.9 0.0 collective-permute-done.3.right_ref
  10.9 0.2 halo.1.halo_ref
  11.0 0.0 copy-start
  11.0 0.0 copy-start.1
  11.0 0.0 copy-start.2
  11.0 0.0 copy-start.3
  11.0 0.6 %collective-permute-done.1.main_ref.b_ref.refs_2_ = bf16[128,1024]{1,0:T(8,128)(2,1)S(1)} collective-permute-done((bf16[128,1024]{1,0:T(8,128)(2,1)}, bf16[128,1024]{1,0:T(8,128)(2,1)S(1)}, u32[]{:S(2)}, u32[]{:S(2)}) %collective-permute-start.1) | collective-permute-done | bytes 262176 | tf_op jit(solution)/shard_map/ppermute | solution.py:387
  11.6 4.2 %collective-permute-start.4 = (bf16[144,1024]{1,0:T(8,128)(2,1)S(1)}, bf16[144,1024]{1,0:T(8,128)(2,1)S(1)}, u32[]{:S(2)}, u32[]{:S(2)}) collective-permute-start(bf16[144,1024]{1,0:T(8,128)(2,1)S(1)} %join.1), channel_id=1, source_target_pairs={{0,24},{4,28},{8,0},{12,4},{16,8},{20,12},{24,16},{28,20},{1,25},{... | collective-permute-start | bytes 884744 | tf_op jit(solution)/shard_map/ppermute | solution.py:387
  15.9 1.5 %collective-permute-start.7 = (bf16[16,640]{1,0:T(8,128)(2,1)S(1)}, bf16[16,640]{1,0:T(8,128)(2,1)S(1)}, u32[]{:S(2)}, u32[]{:S(2)}) collective-permute-start(bf16[16,640]{1,0:T(8,128)(2,1)S(1)} %halo.1.halo_ref), channel_id=1, source_target_pairs={{0,4},{4,0},{8,12},{12,8},{16,20},{20,16},{24,28},{28,24},{1,5},{5... | collective-permute-start | bytes 61448 | tf_op jit(solution)/shard_map/ppermute | solution.py:391
  17.4 0.0 collective-permute-start.8
  17.4 0.0 copy-done
  17.4 0.0 copy-done.1
  17.4 0.0 copy-done.2
  17.4 0.0 copy-done.3
  17.4 1.0 %spectrum.1 = (f32[128,1024]{1,0:T(8,128)S(1)}, f32[8,128]{1,0:T(8,128)S(1)}) custom-call(bf16[144,1024]{1,0:T(8,128)(2,1)S(1)} %get-tuple-element.23.a_ref.own_ref.refs_0_.main_ref, bf16[128,192]{1,0:T(8,128)(2,1)S(1)} %copy-done.2, bf16[256,256]{1,0:T(8,128)(2,1)S(1)} %copy-done.1, bf16[64,256]{1,0:T(8,128)(2,1)S(1)} %copy-done.3, bf16[512,256]{1,0:T(8,128)(2,1)S(1)} %copy-done), custom_call_target="tpu_custom_call" | custom-call | tf_op jit(solution)/shard_map/spectrum/pallas_call | solution.py:404
  18.4 0.8 %own.1 = (bf16[128,1152]{1,0:T(8,128)(2,1)S(1)}, f32[64,1024]{1,0:T(8,128)S(1)}) custom-call(f32[8,128]{1,0:T(8,128)S(1)} %get-tuple-element.28.refs_7_.earlier_ref, bf16[144,1024]{1,0:T(8,128)(2,1)S(1)} %get-tuple-element.23.a_ref.own_ref.refs_0_.main_ref, bf16[16,640]{1,0:T(8,128)(2,1)S(1)} %halo.1.halo_ref), custom_call_target="tpu_custom_call" | custom-call | tf_op jit(solution)/shard_map/own/pallas_call | solution.py:404
  19.2 0.3 later.1.earlier_ref
  19.5 0.2 collective-permute-start.5
  19.6 0.0 collective-permute-done.b_ref.refs_1_.refs_2_
  19.7 0.3 candidate.1
  19.9 1.9 %collective-permute-start.6 = (bf16[64,1024]{1,0:T(8,128)(2,1)S(1)}, bf16[64,1024]{1,0:T(8,128)(2,1)S(1)}, u32[]{:S(2)}, u32[]{:S(2)}) collective-permute-start(bf16[64,1024]{1,0:T(8,128)(2,1)S(1)} %candidate.1), channel_id=1, source_target_pairs={{0,8},{4,12},{8,16},{12,20},{16,24},{20,28},{24,0},{28,4},{1,9},{5... | collective-permute-start | bytes 393224 | tf_op jit(solution)/shard_map/ppermute | solution.py:387
  21.8 0.0 collective-permute-done.7.refs_3_
  21.8 1.0 %beside.1 = (bf16[128,1152]{1,0:T(8,128)(2,1)S(1)}, f32[64,1024]{1,0:T(8,128)S(1)}, bf16[64,1024]{1,0:T(8,128)(2,1)S(1)}) custom-call(bf16[64,1024]{1,0:T(8,128)(2,1)S(1)} %later.1.earlier_ref, bf16[128,1152]{1,0:T(8,128)(2,1)S(1)} %get-tuple-element.29.refs_0_.own_ref, f32[64,1024]{1,0:T(8,128)S(1)} %get-tuple-element.30.refs_1_.own_power_ref, ...), custom_call_target="tpu_custom_call" | custom-call | tf_op jit(solution)/shard_map/beside/pallas_call | solution.py:404
  22.8 0.2 collective-permute-done.4.refs_3_.halo_ref.main_ref
  23.0 1.0 %near.1 = (bf16[128,1152]{1,0:T(8,128)(2,1)S(1)}, f32[64,1024]{1,0:T(8,128)S(1)}, bf16[64,1024]{1,0:T(8,128)(2,1)S(1)}) custom-call(bf16[128,1152]{1,0:T(8,128)(2,1)S(1)} %get-tuple-element.32.own_ref, f32[64,1024]{1,0:T(8,128)S(1)} %get-tuple-element.33.own_power_ref, bf16[128,1024]{1,0:T(8,128)(2,1)S(1)} %collective-permute-done.1.main_ref.b_ref.refs_2_, ...), custom_call_target="tpu_custom_call" | custom-call | tf_op jit(solution)/shard_map/near/pallas_call | solution.py:404
  24.0 1.6 %collective-permute-start.9 = (bf16[64,1024]{1,0:T(8,128)(2,1)S(1)}, bf16[64,1024]{1,0:T(8,128)(2,1)S(1)}, u32[]{:S(2)}, u32[]{:S(2)}) collective-permute-start(bf16[64,1024]{1,0:T(8,128)(2,1)S(1)} %get-tuple-element.38), channel_id=1, source_target_pairs={{0,4},{4,0},{8,12},{12,8},{16,20},{20,16},{24,28},{28,24},{1,5},{5... | collective-permute-start | bytes 393224 | tf_op jit(solution)/shard_map/ppermute | solution.py:391
  25.6 0.0 collective-permute-done.8.halo_ref
  25.6 1.0 %far.1 = (bf16[128,1152]{1,0:T(8,128)(2,1)S(1)}, f32[64,1024]{1,0:T(8,128)S(1)}, bf16[64,1024]{1,0:T(8,128)(2,1)S(1)}) custom-call(bf16[128,1152]{1,0:T(8,128)(2,1)S(1)} %get-tuple-element.32.own_ref, f32[64,1024]{1,0:T(8,128)S(1)} %get-tuple-element.33.own_power_ref, bf16[144,1024]{1,0:T(8,128)(2,1)S(1)} %collective-permute-done.4.refs_3_.halo_ref.main_ref, ...), custom_call_target="tpu_custom_call" | custom-call | tf_op jit(solution)/shard_map/far/pallas_call | solution.py:404
  26.6 0.6 %collective-permute-start.10 = (bf16[64,1024]{1,0:T(8,128)(2,1)S(1)}, bf16[64,1024]{1,0:T(8,128)(2,1)S(1)}, u32[]{:S(2)}, u32[]{:S(2)}) collective-permute-start(bf16[64,1024]{1,0:T(8,128)(2,1)S(1)} %get-tuple-element.39), channel_id=1, source_target_pairs={{0,4},{4,0},{8,12},{12,8},{16,20},{20,16},{24,28},{28,24},{1,5},{5... | collective-permute-start | bytes 393224 | tf_op jit(solution)/shard_map/ppermute | solution.py:391
  27.2 0.4 %two.1.two_ref = bf16[64,1024]{1,0:T(8,128)(2,1)S(1)} custom-call(bf16[128,1152]{1,0:T(8,128)(2,1)S(1)} %get-tuple-element.29.refs_0_.own_ref, f32[64,1024]{1,0:T(8,128)S(1)} %get-tuple-element.30.refs_1_.own_power_ref, bf16[128,1152]{1,0:T(8,128)(2,1)S(1)} %get-tuple-element.34.ext_ref, f32[64,1024]{1,0:T(8,128)S(1)} %get-tuple-element.35.power_ref), custom_call_target="tpu_custom_call" | custom-call | tf_op jit(solution)/shard_map/two/pallas_call | solution.py:404
  27.7 0.4 %four.1.four_ref = bf16[64,1024]{1,0:T(8,128)(2,1)S(1)} custom-call(bf16[128,1152]{1,0:T(8,128)(2,1)S(1)} %get-tuple-element.29.refs_0_.own_ref, f32[64,1024]{1,0:T(8,128)S(1)} %get-tuple-element.30.refs_1_.own_power_ref, bf16[128,1152]{1,0:T(8,128)(2,1)S(1)} %get-tuple-element.36.ext_ref, f32[64,1024]{1,0:T(8,128)S(1)} %get-tuple-element.37.power_ref), custom_call_target="tpu_custom_call" | custom-call | tf_op jit(solution)/shard_map/four/pallas_call | solution.py:404
  28.1 0.0 collective-permute-done.5.refs_4_
  28.1 0.4 %collective-permute-done.6.refs_5_ = bf16[64,1024]{1,0:T(8,128)(2,1)S(1)} collective-permute-done((bf16[64,1024]{1,0:T(8,128)(2,1)S(1)}, bf16[64,1024]{1,0:T(8,128)(2,1)S(1)}, u32[]{:S(2)}, u32[]{:S(2)}) %collective-permute-start.6) | collective-permute-done | bytes 131104 | tf_op jit(solution)/shard_map/ppermute | solution.py:387
  28.6 1.7 %surface.1.surface_ref = f32[16,1024]{1,0:T(8,128)S(1)} custom-call(f32[16,128]{1,0:T(8,128)S(1)} %get-tuple-element.22.cond_ref, bf16[144,1024]{1,0:T(8,128)(2,1)S(1)} %get-tuple-element.23.a_ref.own_ref.refs_0_.main_ref, bf16[144,1024]{1,0:T(8,128)(2,1)S(1)} %collective-permute-done.b_ref.refs_1_.refs_2_, ...), custom_call_target="tpu_custom_call" | custom-call | tf_op jit(solution)/shard_map/surface/pallas_call | solution.py:404
  30.2 0.0 collective-permute-done.9.near_ref
  30.3 1.6 %collective-permute-done.10.far_ref = bf16[64,1024]{1,0:T(8,128)(2,1)S(1)} collective-permute-done((bf16[64,1024]{1,0:T(8,128)(2,1)S(1)}, bf16[64,1024]{1,0:T(8,128)(2,1)S(1)}, u32[]{:S(2)}, u32[]{:S(2)}) %collective-permute-start.10) | collective-permute-done | bytes 131104 | tf_op jit(solution)/shard_map/ppermute | solution.py:391
  31.9 0.9 %place.1 = (f32[16,1024]{1,0:T(8,128)}, bf16[4,64,1024]{2,1,0:T(8,128)(2,1)}) custom-call(f32[16,128]{1,0:T(8,128)S(1)} %get-tuple-element.22.cond_ref, f32[16,1024]{1,0:T(8,128)S(1)} %surface.1.surface_ref, bf16[64,1024]{1,0:T(8,128)(2,1)S(1)} %get-tuple-element.31.beside_ref, bf16[64,1024]{1,0:T(8,128)(2,1)S(1)} %two.1.two_ref, ...), custom_call_target="tpu_custom_call" | custom-call | tf_op jit(solution)/shard_map/place/pallas_call | solution.py:488
  (1 shorter events, 0.0 us)
Async XLA Ops:
  0.6 11.0 %collective-permute-start.1 = (bf16[128,1024]{1,0:T(8,128)(2,1)}, bf16[128,1024]{1,0:T(8,128)(2,1)S(1)}, u32[]{:S(2)}, u32[]{:S(2)}) collective-permute-start(bf16[128,1024]{1,0:T(8,128)(2,1)} %bitcast.5), channel_id=1, source_target_pairs={{0,24},{4,28},{8,0},{12,4},{16,8},{20,12},{24,16},{28,20},{1,25},{... | collective-permute-start | bytes 786440 | tf_op jit(solution)/shard_map/ppermute | solution.py:387
  7.4 3.4 %collective-permute-start.2 = (bf16[144,128]{1,0:T(8,128)(2,1)S(1)}, bf16[144,128]{1,0:T(8,128)(2,1)S(1)}, u32[]{:S(2)}, u32[]{:S(2)}) collective-permute-start(bf16[144,128]{1,0:T(8,128)(2,1)S(1)} %get-tuple-element.25), channel_id=1, source_target_pairs={{0,1},{1,2},{2,3},{3,0},{4,5},{5,6},{6,7},{7,4},{8,9},{9,10},{10,1... | collective-permute-start | bytes 110600 | tf_op jit(solution)/shard_map/ppermute | solution.py:387
  7.5 3.4 %collective-permute-start.3 = (bf16[144,128]{1,0:T(8,128)(2,1)S(1)}, bf16[144,128]{1,0:T(8,128)(2,1)S(1)}, u32[]{:S(2)}, u32[]{:S(2)}) collective-permute-start(bf16[144,128]{1,0:T(8,128)(2,1)S(1)} %get-tuple-element.26), channel_id=1, source_target_pairs={{0,3},{1,0},{2,1},{3,2},{4,7},{5,4},{6,5},{7,6},{8,11},{9,8},{10,9... | collective-permute-start | bytes 110600 | tf_op jit(solution)/shard_map/ppermute | solution.py:387
  9.2 10.4 %collective-permute-start = (bf16[144,1024]{1,0:T(8,128)(2,1)S(1)}, bf16[144,1024]{1,0:T(8,128)(2,1)S(1)}, u32[]{:S(2)}, u32[]{:S(2)}) collective-permute-start(bf16[144,1024]{1,0:T(8,128)(2,1)S(1)} %get-tuple-element.23.a_ref.own_ref.refs_0_.main_ref), channel_id=1, source_target_pairs={{0,4},{4,0},{8,12},{12,8},{16,20},{20,16},{24,28},{28,24},{1,5},{5... | collective-permute-start | bytes 884744 | tf_op jit(solution)/shard_map/ppermute | solution.py:391
  11.0 6.4 %copy-start = (bf16[512,256]{1,0:T(8,128)(2,1)S(1)}, bf16[512,256]{1,0:T(8,128)(2,1)}, u32[]{:S(2)}) copy-start(bf16[512,256]{1,0:T(8,128)(2,1)} %constant.11.clone.fourth_ref.refs_11_) | copy-start | bytes 786436
  11.0 6.4 %copy-start.1 = (bf16[256,256]{1,0:T(8,128)(2,1)S(1)}, bf16[256,256]{1,0:T(8,128)(2,1)}, u32[]{:S(2)}) copy-start(bf16[256,256]{1,0:T(8,128)(2,1)} %constant.9.clone.second_ref.refs_9_) | copy-start | bytes 393220
  11.0 6.4 %copy-start.2 = (bf16[128,192]{1,0:T(8,128)(2,1)S(1)}, bf16[128,192]{1,0:T(8,128)(2,1)}, u32[]{:S(2)}) copy-start(bf16[128,192]{1,0:T(8,128)(2,1)} %constant.8.clone.first_ref.refs_8_) | copy-start | bytes 147460
  11.0 6.4 %copy-start.3 = (bf16[64,256]{1,0:T(8,128)(2,1)S(1)}, bf16[64,256]{1,0:T(8,128)(2,1)}, u32[]{:S(2)}) copy-start(bf16[64,256]{1,0:T(8,128)(2,1)} %constant.10.clone.third_ref.refs_10_) | copy-start | bytes 98308
  11.6 11.4 %collective-permute-start.4 = (bf16[144,1024]{1,0:T(8,128)(2,1)S(1)}, bf16[144,1024]{1,0:T(8,128)(2,1)S(1)}, u32[]{:S(2)}, u32[]{:S(2)}) collective-permute-start(bf16[144,1024]{1,0:T(8,128)(2,1)S(1)} %join.1), channel_id=1, source_target_pairs={{0,24},{4,28},{8,0},{12,4},{16,8},{20,12},{24,16},{28,20},{1,25},{... | collective-permute-start | bytes 884744 | tf_op jit(solution)/shard_map/ppermute | solution.py:387
  15.9 6.0 %collective-permute-start.7 = (bf16[16,640]{1,0:T(8,128)(2,1)S(1)}, bf16[16,640]{1,0:T(8,128)(2,1)S(1)}, u32[]{:S(2)}, u32[]{:S(2)}) collective-permute-start(bf16[16,640]{1,0:T(8,128)(2,1)S(1)} %halo.1.halo_ref), channel_id=1, source_target_pairs={{0,4},{4,0},{8,12},{12,8},{16,20},{20,16},{24,28},{28,24},{1,5},{5... | collective-permute-start | bytes 61448 | tf_op jit(solution)/shard_map/ppermute | solution.py:391
  17.4 8.2 %collective-permute-start.8 = (bf16[16,640]{1,0:T(8,128)(2,1)S(1)}, bf16[16,640]{1,0:T(8,128)(2,1)S(1)}, u32[]{:S(2)}, u32[]{:S(2)}) collective-permute-start(bf16[16,640]{1,0:T(8,128)(2,1)S(1)} %halo.1.halo_ref), channel_id=1, source_target_pairs={{0,16},{4,20},{8,24},{12,28},{16,0},{20,4},{24,8},{28,12},{1,17},{... | collective-permute-start | bytes 61448 | tf_op jit(solution)/shard_map/ppermute | solution.py:387
  19.5 8.7 %collective-permute-start.5 = (bf16[64,1024]{1,0:T(8,128)(2,1)S(1)}, bf16[64,1024]{1,0:T(8,128)(2,1)S(1)}, u32[]{:S(2)}, u32[]{:S(2)}) collective-permute-start(bf16[64,1024]{1,0:T(8,128)(2,1)S(1)} %later.1.earlier_ref), channel_id=1, source_target_pairs={{0,28},{4,24},{8,4},{12,0},{16,12},{20,8},{24,20},{28,16},{1,29},{... | collective-permute-start | bytes 393224 | tf_op jit(solution)/shard_map/ppermute | solution.py:450
  19.9 8.6 %collective-permute-start.6 = (bf16[64,1024]{1,0:T(8,128)(2,1)S(1)}, bf16[64,1024]{1,0:T(8,128)(2,1)S(1)}, u32[]{:S(2)}, u32[]{:S(2)}) collective-permute-start(bf16[64,1024]{1,0:T(8,128)(2,1)S(1)} %candidate.1), channel_id=1, source_target_pairs={{0,8},{4,12},{8,16},{12,20},{16,24},{20,28},{24,0},{28,4},{1,9},{5... | collective-permute-start | bytes 393224 | tf_op jit(solution)/shard_map/ppermute | solution.py:387
  24.0 6.2 %collective-permute-start.9 = (bf16[64,1024]{1,0:T(8,128)(2,1)S(1)}, bf16[64,1024]{1,0:T(8,128)(2,1)S(1)}, u32[]{:S(2)}, u32[]{:S(2)}) collective-permute-start(bf16[64,1024]{1,0:T(8,128)(2,1)S(1)} %get-tuple-element.38), channel_id=1, source_target_pairs={{0,4},{4,0},{8,12},{12,8},{16,20},{20,16},{24,28},{28,24},{1,5},{5... | collective-permute-start | bytes 393224 | tf_op jit(solution)/shard_map/ppermute | solution.py:391
  26.6 5.2 %collective-permute-start.10 = (bf16[64,1024]{1,0:T(8,128)(2,1)S(1)}, bf16[64,1024]{1,0:T(8,128)(2,1)S(1)}, u32[]{:S(2)}, u32[]{:S(2)}) collective-permute-start(bf16[64,1024]{1,0:T(8,128)(2,1)S(1)} %get-tuple-element.39), channel_id=1, source_target_pairs={{0,4},{4,0},{8,12},{12,8},{16,20},{20,16},{24,28},{28,24},{1,5},{5... | collective-permute-start | bytes 393224 | tf_op jit(solution)/shard_map/ppermute | solution.py:391

commit v10 on v7

--- a/solution.py
+++ b/solution.py
@@ -450,8 +450,6 @@
     four = shifted(call(join_kernel, "join", joined, (halo, two)), "date", 2)
     later = call(functools.partial(candidate_kernel, (0, 2)), "later", field, (cond, own, two))
     across = lax.ppermute(later, "date", [(s, (s - 2) % dates ^ 1) for s in range(dates)])
-    amp = call(functools.partial(late_candidate_kernel, (0, 1)), "candidate", field, (later, cond, own, beside))
-    before = shifted(amp, "date", -2) if dates == 8 else spread(amp, "date")
     beside_halo = swapped(halo, "date", 1)
     four_halo = shifted(halo, "date", 4)
     first, second, third, fourth = [jnp.asarray(t) for t in surface_tables()]
@@ -466,8 +464,10 @@
     scratch = [[((k * rows, cols + LANES), BF16)] for k in range(4)]
     own_ext = call(own_kernel, "own", resampled, (energy, own, halo), scratch[1])
     *beside_ext, coh_beside = call(
-        beside_kernel, "beside", (*resampled, field), (amp, *own_ext, beside, beside_halo), scratch[3]
+        beside_kernel, "beside", (*resampled, field), (energy, *own_ext, beside, beside_halo), scratch[3]
     )
+    amp = call(functools.partial(late_candidate_kernel, (0, 1)), "candidate", field, (coh_beside, cond, own, beside))
+    before = shifted(amp, "date", -2) if dates == 8 else spread(amp, "date")
     *two_ext, coh_near = call(pair_kernel, "near", (*resampled, field), (*beside_ext, two, four), scratch[3])
     near = swapped(coh_near, "date", 1)
     coh_two = call(functools.partial(again_kernel, 1), "two", field, (cond, *own_ext, *two_ext), scratch[2])

time: 32.9 us -> 32.9 us (level)
    ppermute x4, waiting for transfers between devices: 1.54 us -> 0.55 us  [swapped(): lax.ppermute(value, axis, [(s, s ^ step) for s in range(lax.axis_size(axi...]
    ppermute x6, waiting for transfers between devices: 1.29 us -> 2.25 us  [shifted(): lax.ppermute(value, axis, [(s, (s - steps) % count) for s in range(count)])]
where the time goes in v10:
time: 32.9 us; the launch traced here: 32.7 us
  starting transfers between devices  18.4 us (56%)
  Pallas kernels  10.1 us (31%)
  waiting for transfers between devices  2.81 us (9%)
  between operations  1.42 us (4%)
    ppermute x6, starting transfers between devices, shifted(): lax.ppermute(value, axis, [(s, (s - steps) % count) for s in range(count)])  13 us
    pallas_call x13, Pallas kernels, call(): pl.pallas_call(kernel, out_shape=out_shape, in_specs=[VMEM] * len(operand...  8.21 us
    ppermute x4, starting transfers between devices, swapped(): lax.ppermute(value, axis, [(s, s ^ step) for s in range(lax.axis_size(axi...  5.19 us
    ppermute x6, waiting for transfers between devices, shifted(): lax.ppermute(value, axis, [(s, (s - steps) % count) for s in range(count)])  2.25 us
    pallas_call x1, Pallas kernels, body(): pl.pallas_call(prep_kernel, out_shape=(sds((2 * rows + 16, cols), BF16),...  1.03 us
    pallas_call x1, Pallas kernels, body(): pl.pallas_call(place_kernel, out_shape=(sds(surface.shape, F32), sds((SPA...  0.85 us
  transfers between devices with their start and end apart: 11, of which 5 were waited for; matrix products, arithmetic and copies ran while one was open for 0% of the time, Pallas kernels for 28%

profile of v10, /device:TPU:0, one launch (start us, length us, event | category | flops | bytes accessed | tf_op | source)
XLA Modules:
  0.0 32.7 jit_solution(1677249505339295031)
XLA Ops:
  0.6 5.1 %collective-permute-start.1 = (bf16[128,1024]{1,0:T(8,128)(2,1)}, bf16[128,1024]{1,0:T(8,128)(2,1)S(1)}, u32[]{:S(2)}, u32[]{:S(2)}) collective-permute-start(bf16[128,1024]{1,0:T(8,128)(2,1)} %bitcast.5), channel_id=1, source_target_pairs={{0,24},{4,28},{8,0},{12,4},{16,8},{20,12},{24,16},{28,20},{1,25},{... | collective-permute-start | bytes 786440 | tf_op jit(solution)/shard_map/ppermute | solution.py:389
  6.4 1.0 %prepare.1 = (bf16[144,1024]{1,0:T(8,128)(2,1)S(1)}, f32[16,128]{1,0:T(8,128)S(1)}, bf16[16,128]{1,0:T(8,128)(2,1)S(1)}, bf16[144,128]{1,0:T(8,128)(2,1)S(1)}, bf16[144,128]{1,0:T(8,128)(2,1)S(1)}) custom-call(bf16[128,1024]{1,0:T(8,128)(2,1)} %bitcast.6, s32[1,16]{1,0:T(1,128)} %bitcast.7, f32[1,16]{1,0:T(1,128)} %bitcast.8, s32[1,4]{1,0:T(1,128)} %partners_hbm.1, ...), custom_call_target="tpu_custom_call" | custom-call | tf_op jit(solution)/shard_map/prepare/pallas_call | solution.py:427
  7.4 0.1 collective-permute-start.2
  7.5 1.7 %collective-permute-start.3 = (bf16[144,128]{1,0:T(8,128)(2,1)S(1)}, bf16[144,128]{1,0:T(8,128)(2,1)S(1)}, u32[]{:S(2)}, u32[]{:S(2)}) collective-permute-start(bf16[144,128]{1,0:T(8,128)(2,1)S(1)} %get-tuple-element.26), channel_id=1, source_target_pairs={{0,3},{1,0},{2,1},{3,2},{4,7},{5,4},{6,5},{7,6},{8,11},{9,8},{10,9... | collective-permute-start | bytes 110600 | tf_op jit(solution)/shard_map/ppermute | solution.py:389
  9.2 1.5 %collective-permute-start = (bf16[144,1024]{1,0:T(8,128)(2,1)S(1)}, bf16[144,1024]{1,0:T(8,128)(2,1)S(1)}, u32[]{:S(2)}, u32[]{:S(2)}) collective-permute-start(bf16[144,1024]{1,0:T(8,128)(2,1)S(1)} %get-tuple-element.23.a_ref.own_ref.main_ref.refs_1_.refs_0_), channel_id=1, source_target_pairs={{0,4},{4,0},{8,12},{12,8},{16,20},{20,16},{24,28},{28,24},{1,5},{5... | collective-permute-start | bytes 884744 | tf_op jit(solution)/shard_map/ppermute | solution.py:393
  10.7 0.1 collective-permute-done.2.left_ref
  10.9 0.0 collective-permute-done.3.right_ref
  10.9 0.2 halo.1.halo_ref
  11.0 0.0 copy-start
  11.0 0.0 copy-start.1
  11.0 0.0 copy-start.2
  11.0 0.0 copy-start.3
  11.0 0.6 %collective-permute-done.1.main_ref.b_ref.refs_2_ = bf16[128,1024]{1,0:T(8,128)(2,1)S(1)} collective-permute-done((bf16[128,1024]{1,0:T(8,128)(2,1)}, bf16[128,1024]{1,0:T(8,128)(2,1)S(1)}, u32[]{:S(2)}, u32[]{:S(2)}) %collective-permute-start.1) | collective-permute-done | bytes 262176 | tf_op jit(solution)/shard_map/ppermute | solution.py:389
  11.6 4.2 %collective-permute-start.4 = (bf16[144,1024]{1,0:T(8,128)(2,1)S(1)}, bf16[144,1024]{1,0:T(8,128)(2,1)S(1)}, u32[]{:S(2)}, u32[]{:S(2)}) collective-permute-start(bf16[144,1024]{1,0:T(8,128)(2,1)S(1)} %join.1), channel_id=1, source_target_pairs={{0,24},{4,28},{8,0},{12,4},{16,8},{20,12},{24,16},{28,20},{1,25},{... | collective-permute-start | bytes 884744 | tf_op jit(solution)/shard_map/ppermute | solution.py:389
  15.9 1.5 %collective-permute-start.6 = (bf16[16,640]{1,0:T(8,128)(2,1)S(1)}, bf16[16,640]{1,0:T(8,128)(2,1)S(1)}, u32[]{:S(2)}, u32[]{:S(2)}) collective-permute-start(bf16[16,640]{1,0:T(8,128)(2,1)S(1)} %halo.1.halo_ref), channel_id=1, source_target_pairs={{0,4},{4,0},{8,12},{12,8},{16,20},{20,16},{24,28},{28,24},{1,5},{5... | collective-permute-start | bytes 61448 | tf_op jit(solution)/shard_map/ppermute | solution.py:393
  17.4 0.0 collective-permute-start.9
  17.4 0.0 copy-done
  17.4 0.0 copy-done.1
  17.4 0.0 copy-done.2
  17.4 0.0 copy-done.3
  17.4 1.0 %spectrum.1 = (f32[128,1024]{1,0:T(8,128)S(1)}, f32[8,128]{1,0:T(8,128)S(1)}) custom-call(bf16[144,1024]{1,0:T(8,128)(2,1)S(1)} %get-tuple-element.23.a_ref.own_ref.main_ref.refs_1_.refs_0_, bf16[128,192]{1,0:T(8,128)(2,1)S(1)} %copy-done.2, bf16[256,256]{1,0:T(8,128)(2,1)S(1)} %copy-done.1, bf16[64,256]{1,0:T(8,128)(2,1)S(1)} %copy-done.3, ...), custom_call_target="tpu_custom_call" | custom-call | tf_op jit(solution)/shard_map/spectrum/pallas_call | solution.py:406
  18.4 0.8 %own.1 = (bf16[128,1152]{1,0:T(8,128)(2,1)S(1)}, f32[64,1024]{1,0:T(8,128)S(1)}) custom-call(f32[8,128]{1,0:T(8,128)S(1)} %get-tuple-element.27.earlier_ref.refs_7_, bf16[144,1024]{1,0:T(8,128)(2,1)S(1)} %get-tuple-element.23.a_ref.own_ref.main_ref.refs_1_.refs_0_, bf16[16,640]{1,0:T(8,128)(2,1)S(1)} %halo.1.halo_ref), custom_call_target="tpu_custom_call" | custom-call | tf_op jit(solution)/shard_map/own/pallas_call | solution.py:406
  19.2 0.3 later.1
  19.5 0.2 collective-permute-start.5
  19.6 0.0 collective-permute-done.6.refs_3_
  19.7 0.0 collective-permute-done.refs_2_.refs_1_
  19.7 1.0 %beside.1 = (bf16[128,1152]{1,0:T(8,128)(2,1)S(1)}, f32[64,1024]{1,0:T(8,128)S(1)}, bf16[64,1024]{1,0:T(8,128)(2,1)S(1)}) custom-call(f32[8,128]{1,0:T(8,128)S(1)} %get-tuple-element.27.earlier_ref.refs_7_, bf16[128,1152]{1,0:T(8,128)(2,1)S(1)} %get-tuple-element.28.refs_0_.own_ref, f32[64,1024]{1,0:T(8,128)S(1)} %get-tuple-element.29.refs_1_.own_power_ref, ...), custom_call_target="tpu_custom_call" | custom-call | tf_op jit(solution)/shard_map/beside/pallas_call | solution.py:406
  20.7 0.3 candidate.1
  21.0 1.9 %collective-permute-start.7 = (bf16[64,1024]{1,0:T(8,128)(2,1)S(1)}, bf16[64,1024]{1,0:T(8,128)(2,1)S(1)}, u32[]{:S(2)}, u32[]{:S(2)}) collective-permute-start(bf16[64,1024]{1,0:T(8,128)(2,1)S(1)} %candidate.1), channel_id=1, source_target_pairs={{0,8},{4,12},{8,16},{12,20},{16,24},{20,28},{24,0},{28,4},{1,9},{5... | collective-permute-start | bytes 393224 | tf_op jit(solution)/shard_map/ppermute | solution.py:389
  22.8 0.2 collective-permute-done.4.refs_3_.halo_ref.main_ref
  23.0 1.0 %near.1 = (bf16[128,1152]{1,0:T(8,128)(2,1)S(1)}, f32[64,1024]{1,0:T(8,128)S(1)}, bf16[64,1024]{1,0:T(8,128)(2,1)S(1)}) custom-call(bf16[128,1152]{1,0:T(8,128)(2,1)S(1)} %get-tuple-element.32.own_ref, f32[64,1024]{1,0:T(8,128)S(1)} %get-tuple-element.33.own_power_ref, bf16[128,1024]{1,0:T(8,128)(2,1)S(1)} %collective-permute-done.1.main_ref.b_ref.refs_2_, ...), custom_call_target="tpu_custom_call" | custom-call | tf_op jit(solution)/shard_map/near/pallas_call | solution.py:406
  24.0 1.6 %collective-permute-start.8 = (bf16[64,1024]{1,0:T(8,128)(2,1)S(1)}, bf16[64,1024]{1,0:T(8,128)(2,1)S(1)}, u32[]{:S(2)}, u32[]{:S(2)}) collective-permute-start(bf16[64,1024]{1,0:T(8,128)(2,1)S(1)} %get-tuple-element.34), channel_id=1, source_target_pairs={{0,4},{4,0},{8,12},{12,8},{16,20},{20,16},{24,28},{28,24},{1,5},{5... | collective-permute-start | bytes 393224 | tf_op jit(solution)/shard_map/ppermute | solution.py:393
  25.6 0.0 collective-permute-done.9.halo_ref
  25.6 1.0 %far.1 = (bf16[128,1152]{1,0:T(8,128)(2,1)S(1)}, f32[64,1024]{1,0:T(8,128)S(1)}, bf16[64,1024]{1,0:T(8,128)(2,1)S(1)}) custom-call(bf16[128,1152]{1,0:T(8,128)(2,1)S(1)} %get-tuple-element.32.own_ref, f32[64,1024]{1,0:T(8,128)S(1)} %get-tuple-element.33.own_power_ref, bf16[144,1024]{1,0:T(8,128)(2,1)S(1)} %collective-permute-done.4.refs_3_.halo_ref.main_ref, ...), custom_call_target="tpu_custom_call" | custom-call | tf_op jit(solution)/shard_map/far/pallas_call | solution.py:406
  26.6 0.6 %collective-permute-start.10 = (bf16[64,1024]{1,0:T(8,128)(2,1)S(1)}, bf16[64,1024]{1,0:T(8,128)(2,1)S(1)}, u32[]{:S(2)}, u32[]{:S(2)}) collective-permute-start(bf16[64,1024]{1,0:T(8,128)(2,1)S(1)} %get-tuple-element.39), channel_id=1, source_target_pairs={{0,4},{4,0},{8,12},{12,8},{16,20},{20,16},{24,28},{28,24},{1,5},{5... | collective-permute-start | bytes 393224 | tf_op jit(solution)/shard_map/ppermute | solution.py:393
  27.2 0.5 %four.1.four_ref = bf16[64,1024]{1,0:T(8,128)(2,1)S(1)} custom-call(f32[16,128]{1,0:T(8,128)S(1)} %get-tuple-element.22.cond_ref.refs_0_, bf16[128,1152]{1,0:T(8,128)(2,1)S(1)} %get-tuple-element.28.refs_0_.own_ref, f32[64,1024]{1,0:T(8,128)S(1)} %get-tuple-element.29.refs_1_.own_power_ref, bf16[128,1152]{1,0:T(8,128)(2,1)S(1)} %get-tuple-element.37.ext_ref, ...), custom_call_target="tpu_custom_call" | custom-call | tf_op jit(solution)/shard_map/four/pallas_call | solution.py:406
  27.7 0.5 %two.1.two_ref = bf16[64,1024]{1,0:T(8,128)(2,1)S(1)} custom-call(f32[16,128]{1,0:T(8,128)S(1)} %get-tuple-element.22.cond_ref.refs_0_, bf16[128,1152]{1,0:T(8,128)(2,1)S(1)} %get-tuple-element.28.refs_0_.own_ref, f32[64,1024]{1,0:T(8,128)S(1)} %get-tuple-element.29.refs_1_.own_power_ref, bf16[128,1152]{1,0:T(8,128)(2,1)S(1)} %get-tuple-element.35.ext_ref, ...), custom_call_target="tpu_custom_call" | custom-call | tf_op jit(solution)/shard_map/two/pallas_call | solution.py:406
  28.1 0.0 collective-permute-done.5.refs_4_
  28.2 1.4 %collective-permute-done.7.refs_5_ = bf16[64,1024]{1,0:T(8,128)(2,1)S(1)} collective-permute-done((bf16[64,1024]{1,0:T(8,128)(2,1)S(1)}, bf16[64,1024]{1,0:T(8,128)(2,1)S(1)}, u32[]{:S(2)}, u32[]{:S(2)}) %collective-permute-start.7) | collective-permute-done | bytes 131104 | tf_op jit(solution)/shard_map/ppermute | solution.py:389
  29.5 1.7 %surface.1.surface_ref = f32[16,1024]{1,0:T(8,128)S(1)} custom-call(f32[16,128]{1,0:T(8,128)S(1)} %get-tuple-element.22.cond_ref.refs_0_, bf16[144,1024]{1,0:T(8,128)(2,1)S(1)} %get-tuple-element.23.a_ref.own_ref.main_ref.refs_1_.refs_0_, bf16[144,1024]{1,0:T(8,128)(2,1)S(1)} %collective-permute-done.refs_2_.refs_1_, ...), custom_call_target="tpu_custom_call" | custom-call | tf_op jit(solution)/shard_map/surface/pallas_call | solution.py:406
  31.2 0.0 collective-permute-done.8.near_ref
  31.2 0.1 one.1.one_ref
  31.3 0.5 %collective-permute-done.10.far_ref = bf16[64,1024]{1,0:T(8,128)(2,1)S(1)} collective-permute-done((bf16[64,1024]{1,0:T(8,128)(2,1)S(1)}, bf16[64,1024]{1,0:T(8,128)(2,1)S(1)}, u32[]{:S(2)}, u32[]{:S(2)}) %collective-permute-start.10) | collective-permute-done | bytes 131104 | tf_op jit(solution)/shard_map/ppermute | solution.py:393
  31.9 0.9 %place.1 = (f32[16,1024]{1,0:T(8,128)}, bf16[4,64,1024]{2,1,0:T(8,128)(2,1)}) custom-call(f32[16,128]{1,0:T(8,128)S(1)} %get-tuple-element.22.cond_ref.refs_0_, f32[16,1024]{1,0:T(8,128)S(1)} %surface.1.surface_ref, bf16[64,1024]{1,0:T(8,128)(2,1)S(1)} %one.1.one_ref, bf16[64,1024]{1,0:T(8,128)(2,1)S(1)} %two.1.two_ref, bf16[64,1024]{1,0:T(8,128)(2,1)S(1)} %four.1.four_ref, ...), custom_call_target="tpu_custom_call" | custom-call | tf_op jit(solution)/shard_map/place/pallas_call | solution.py:491
  (1 shorter events, 0.0 us)
Async XLA Ops:
  0.6 11.0 %collective-permute-start.1 = (bf16[128,1024]{1,0:T(8,128)(2,1)}, bf16[128,1024]{1,0:T(8,128)(2,1)S(1)}, u32[]{:S(2)}, u32[]{:S(2)}) collective-permute-start(bf16[128,1024]{1,0:T(8,128)(2,1)} %bitcast.5), channel_id=1, source_target_pairs={{0,24},{4,28},{8,0},{12,4},{16,8},{20,12},{24,16},{28,20},{1,25},{... | collective-permute-start | bytes 786440 | tf_op jit(solution)/shard_map/ppermute | solution.py:389
  7.4 3.4 %collective-permute-start.2 = (bf16[144,128]{1,0:T(8,128)(2,1)S(1)}, bf16[144,128]{1,0:T(8,128)(2,1)S(1)}, u32[]{:S(2)}, u32[]{:S(2)}) collective-permute-start(bf16[144,128]{1,0:T(8,128)(2,1)S(1)} %get-tuple-element.25), channel_id=1, source_target_pairs={{0,1},{1,2},{2,3},{3,0},{4,5},{5,6},{6,7},{7,4},{8,9},{9,10},{10,1... | collective-permute-start | bytes 110600 | tf_op jit(solution)/shard_map/ppermute | solution.py:389
  7.5 3.4 %collective-permute-start.3 = (bf16[144,128]{1,0:T(8,128)(2,1)S(1)}, bf16[144,128]{1,0:T(8,128)(2,1)S(1)}, u32[]{:S(2)}, u32[]{:S(2)}) collective-permute-start(bf16[144,128]{1,0:T(8,128)(2,1)S(1)} %get-tuple-element.26), channel_id=1, source_target_pairs={{0,3},{1,0},{2,1},{3,2},{4,7},{5,4},{6,5},{7,6},{8,11},{9,8},{10,9... | collective-permute-start | bytes 110600 | tf_op jit(solution)/shard_map/ppermute | solution.py:389
  9.2 10.4 %collective-permute-start = (bf16[144,1024]{1,0:T(8,128)(2,1)S(1)}, bf16[144,1024]{1,0:T(8,128)(2,1)S(1)}, u32[]{:S(2)}, u32[]{:S(2)}) collective-permute-start(bf16[144,1024]{1,0:T(8,128)(2,1)S(1)} %get-tuple-element.23.a_ref.own_ref.main_ref.refs_1_.refs_0_), channel_id=1, source_target_pairs={{0,4},{4,0},{8,12},{12,8},{16,20},{20,16},{24,28},{28,24},{1,5},{5... | collective-permute-start | bytes 884744 | tf_op jit(solution)/shard_map/ppermute | solution.py:393
  11.0 6.4 %copy-start = (bf16[512,256]{1,0:T(8,128)(2,1)S(1)}, bf16[512,256]{1,0:T(8,128)(2,1)}, u32[]{:S(2)}) copy-start(bf16[512,256]{1,0:T(8,128)(2,1)} %constant.11.clone.fourth_ref.refs_11_) | copy-start | bytes 786436
  11.0 6.4 %copy-start.1 = (bf16[256,256]{1,0:T(8,128)(2,1)S(1)}, bf16[256,256]{1,0:T(8,128)(2,1)}, u32[]{:S(2)}) copy-start(bf16[256,256]{1,0:T(8,128)(2,1)} %constant.9.clone.second_ref.refs_9_) | copy-start | bytes 393220
  11.0 6.4 %copy-start.2 = (bf16[128,192]{1,0:T(8,128)(2,1)S(1)}, bf16[128,192]{1,0:T(8,128)(2,1)}, u32[]{:S(2)}) copy-start(bf16[128,192]{1,0:T(8,128)(2,1)} %constant.8.clone.first_ref.refs_8_) | copy-start | bytes 147460
  11.0 6.4 %copy-start.3 = (bf16[64,256]{1,0:T(8,128)(2,1)S(1)}, bf16[64,256]{1,0:T(8,128)(2,1)}, u32[]{:S(2)}) copy-start(bf16[64,256]{1,0:T(8,128)(2,1)} %constant.10.clone.third_ref.refs_10_) | copy-start | bytes 98308
  11.6 11.4 %collective-permute-start.4 = (bf16[144,1024]{1,0:T(8,128)(2,1)S(1)}, bf16[144,1024]{1,0:T(8,128)(2,1)S(1)}, u32[]{:S(2)}, u32[]{:S(2)}) collective-permute-start(bf16[144,1024]{1,0:T(8,128)(2,1)S(1)} %join.1), channel_id=1, source_target_pairs={{0,24},{4,28},{8,0},{12,4},{16,8},{20,12},{24,16},{28,20},{1,25},{... | collective-permute-start | bytes 884744 | tf_op jit(solution)/shard_map/ppermute | solution.py:389
  15.9 3.8 %collective-permute-start.6 = (bf16[16,640]{1,0:T(8,128)(2,1)S(1)}, bf16[16,640]{1,0:T(8,128)(2,1)S(1)}, u32[]{:S(2)}, u32[]{:S(2)}) collective-permute-start(bf16[16,640]{1,0:T(8,128)(2,1)S(1)} %halo.1.halo_ref), channel_id=1, source_target_pairs={{0,4},{4,0},{8,12},{12,8},{16,20},{20,16},{24,28},{28,24},{1,5},{5... | collective-permute-start | bytes 61448 | tf_op jit(solution)/shard_map/ppermute | solution.py:393
  17.4 8.2 %collective-permute-start.9 = (bf16[16,640]{1,0:T(8,128)(2,1)S(1)}, bf16[16,640]{1,0:T(8,128)(2,1)S(1)}, u32[]{:S(2)}, u32[]{:S(2)}) collective-permute-start(bf16[16,640]{1,0:T(8,128)(2,1)S(1)} %halo.1.halo_ref), channel_id=1, source_target_pairs={{0,16},{4,20},{8,24},{12,28},{16,0},{20,4},{24,8},{28,12},{1,17},{... | collective-permute-start | bytes 61448 | tf_op jit(solution)/shard_map/ppermute | solution.py:389
  19.5 8.7 %collective-permute-start.5 = (bf16[64,1024]{1,0:T(8,128)(2,1)S(1)}, bf16[64,1024]{1,0:T(8,128)(2,1)S(1)}, u32[]{:S(2)}, u32[]{:S(2)}) collective-permute-start(bf16[64,1024]{1,0:T(8,128)(2,1)S(1)} %later.1), channel_id=1, source_target_pairs={{0,28},{4,24},{8,4},{12,0},{16,12},{20,8},{24,20},{28,16},{1,29},{... | collective-permute-start | bytes 393224 | tf_op jit(solution)/shard_map/ppermute | solution.py:452
  21.0 8.6 %collective-permute-start.7 = (bf16[64,1024]{1,0:T(8,128)(2,1)S(1)}, bf16[64,1024]{1,0:T(8,128)(2,1)S(1)}, u32[]{:S(2)}, u32[]{:S(2)}) collective-permute-start(bf16[64,1024]{1,0:T(8,128)(2,1)S(1)} %candidate.1), channel_id=1, source_target_pairs={{0,8},{4,12},{8,16},{12,20},{16,24},{20,28},{24,0},{28,4},{1,9},{5... | collective-permute-start | bytes 393224 | tf_op jit(solution)/shard_map/ppermute | solution.py:389
  24.0 7.2 %collective-permute-start.8 = (bf16[64,1024]{1,0:T(8,128)(2,1)S(1)}, bf16[64,1024]{1,0:T(8,128)(2,1)S(1)}, u32[]{:S(2)}, u32[]{:S(2)}) collective-permute-start(bf16[64,1024]{1,0:T(8,128)(2,1)S(1)} %get-tuple-element.34), channel_id=1, source_target_pairs={{0,4},{4,0},{8,12},{12,8},{16,20},{20,16},{24,28},{28,24},{1,5},{5... | collective-permute-start | bytes 393224 | tf_op jit(solution)/shard_map/ppermute | solution.py:393
  26.6 5.2 %collective-permute-start.10 = (bf16[64,1024]{1,0:T(8,128)(2,1)S(1)}, bf16[64,1024]{1,0:T(8,128)(2,1)S(1)}, u32[]{:S(2)}, u32[]{:S(2)}) collective-permute-start(bf16[64,1024]{1,0:T(8,128)(2,1)S(1)} %get-tuple-element.39), channel_id=1, source_target_pairs={{0,4},{4,0},{8,12},{12,8},{16,20},{20,16},{24,28},{28,24},{1,5},{5... | collective-permute-start | bytes 393224 | tf_op jit(solution)/shard_map/ppermute | solution.py:393
